TPU v7x, 32 devices: a whole 2x2x4 slice. The times are simulated.
32 devices in a mesh: ctx: 8 (over z, y), tp: 4 (over x, core).
Axes of the slice: x: 2, y: 2, z: 4, core: 2. Of those that a mesh axis runs over, the one named last changes fastest.
Arguments:
- query_heads: bfloat16 [1024, 32, 128], P('ctx', 'tp'), may hold values from -5 to 5
- key_heads: bfloat16 [1024, 4, 128], P('ctx', 'tp'), may hold values from -5 to 5
- value_heads: bfloat16 [1024, 4, 128], P('ctx', 'tp'), may hold values from -6 to 6
- parents: int32 [8], replicated, may hold values from -1 to 6, as said below
- out_weight: bfloat16 [4096, 4096], P('tp'), may hold values from -1 to 1
Outputs:
- projected: bfloat16 [1024, 4096], P('ctx', 'tp')
Inputs may be any that keep to these rules, and one draw needn't show every extreme that they name: parents[0] is -1 and every other block's parent is an earlier block; block 7 has parent 8 - 2.
All inputs are finite; a program needn't handle non-finite values.
Results may differ from a plain program's by a relative error of at most 0.015.
Values may be sent and summed in bfloat16 or wider, within the bound.
No kernel may reach another device: no remote copies, remote signals or barrier semaphores. Data moves between devices by JAX's collectives and lax.ppermute only.
A program may use at most 128 MiB of HBM per device.

v0:
```python
import math

import jax
import jax.numpy as jnp
from jax import lax
from jax.sharding import PartitionSpec as P

HEAD_DIM = 128
BLOCK = 128


FLOOR = -1e30


def lineage_table(parents):
    width_blocks = parents.shape[0]
    block_ids = jnp.arange(width_blocks, dtype=jnp.int32)
    lineage = (parents[:, None] == block_ids[None, :]).astype(jnp.int32)
    lineage = lineage + (block_ids[:, None] == block_ids[None, :]).astype(jnp.int32)
    for squaring in range(max(width_blocks - 1, 1).bit_length()):
        lineage = jnp.minimum(jnp.dot(lineage, lineage, preferred_element_type=jnp.int32), 1)
    return lineage


def shards(query_heads, key_heads, value_heads, parents, out_weight):
    tok_rows, local_heads, head_dim = query_heads.shape
    local_kv = key_heads.shape[1]
    group_size = local_heads // local_kv
    score_scale = 1.0 / math.sqrt(HEAD_DIM)
    grouped = query_heads.reshape(tok_rows, local_kv, group_size, head_dim)
    lineage = lineage_table(parents)
    first_block = lax.axis_index("ctx") * (tok_rows // BLOCK)
    own_rows = lax.dynamic_slice_in_dim(lineage, first_block, tok_rows // BLOCK, 0)
    token_rows = jnp.repeat(own_rows, BLOCK, axis=0)
    query_ids = lax.axis_index("ctx") * tok_rows + jnp.arange(tok_rows, dtype=jnp.int32)
    block_ids = jnp.arange(parents.shape[0], dtype=jnp.int32)

    def absorb_block(carry_state, key_block, value_block, offset):
        sub_span = key_block.shape[0]
        key_ids = offset + jnp.arange(sub_span, dtype=jnp.int32)
        onehot = ((key_ids // BLOCK)[:, None] == block_ids[None, :]).astype(jnp.int32)
        reached = jnp.dot(token_rows, onehot.T, preferred_element_type=jnp.int32)
        visible_mask = (reached > 0) & (key_ids[None, :] <= query_ids[:, None])
        running_max, running_sum, weighted = carry_state
        scores = (
            jnp.einsum("tgjd,sgd->gjts", grouped, key_block, preferred_element_type=jnp.float32)
            * score_scale
        )
        scores = jnp.where(visible_mask, scores, FLOOR)
        new_max = jnp.maximum(running_max, jnp.max(scores, axis=-1))
        weights = jnp.where(visible_mask, jnp.exp(scores - new_max[..., None]), 0.0)
        factor = jnp.exp(running_max - new_max)
        running_sum = running_sum * factor + jnp.sum(weights, axis=-1)
        weighted = weighted * factor[..., None] + jnp.einsum(
            "gjts,sgd->gjtd",
            weights.astype(jnp.bfloat16),
            value_block,
            preferred_element_type=jnp.float32,
        )
        return (new_max, running_sum, weighted)

    starting = (
        jnp.full((local_kv, group_size, tok_rows), FLOOR, jnp.float32),
        jnp.zeros((local_kv, group_size, tok_rows), jnp.float32),
        jnp.zeros((local_kv, group_size, tok_rows, head_dim), jnp.float32),
    )
    carry_state = starting
    key_piece = lax.all_gather(key_heads, "ctx", axis=0, tiled=True)
    value_piece = lax.all_gather(value_heads, "ctx", axis=0, tiled=True)
    piece_rows = key_piece.shape[0]
    sub_span = math.gcd(piece_rows, 512)
    repeats = piece_rows // sub_span
    key_split = key_piece.reshape(repeats, sub_span, local_kv, head_dim)
    value_split = value_piece.reshape(repeats, sub_span, local_kv, head_dim)
    starts = sub_span * jnp.arange(repeats, dtype=jnp.int32)

    def visit(state_in, inputs):
        key_block, value_block, block_start = inputs
        return (absorb_block(state_in, key_block, value_block, block_start), None)

    carry_state, unused = lax.scan(visit, carry_state, (key_split, value_split, starts))
    running_max, running_sum, weighted = carry_state
    normalized = weighted / running_sum[..., None]
    attended = (
        jnp.transpose(normalized, (2, 0, 1, 3))
        .reshape(tok_rows, local_heads * head_dim)
        .astype(jnp.bfloat16)
    )
    partial_value = jnp.dot(attended, out_weight, preferred_element_type=jnp.float32)
    projected = lax.psum_scatter(
        partial_value.astype(jnp.bfloat16), "tp", scatter_dimension=1, tiled=True
    )
    return projected


def solution(mesh):
    return jax.shard_map(
        shards,
        mesh=mesh,
        in_specs=(
            P("ctx", "tp", None),
            P("ctx", "tp", None),
            P("ctx", "tp", None),
            P(),
            P("tp", None),
        ),
        out_specs=P("ctx", "tp"),
        check_vma=False,
    )
```

profile of v0, /device:TPU:0, one launch (start us, length us, event | category | flops | bytes accessed | tf_op | source)
XLA Modules:
  0.0 118.2 jit_solution(1036365636583127662)
XLA Ops:
  6.5 0.0 reduce-scatter.2.cloned.1.call-start
  6.5 0.9 convolution_minimum_fusion.2
  7.5 0.3 convolution_minimum_fusion
  7.8 32.7 %all_gather.6 = bf16[1024,1,128]{2,0,1:T(8,128)(2,1)S(1)} all-gather(bf16[128,1,128]{2,0,1:T(8,128)(2,1)} %param.8), channel_id=1, replica_groups=mesh['ctx'=8,'tp'=4] {'ctx'}, dimensions={0}, use_global_device_ids=true | all-gather | bytes 294912 | tf_op jit(solution)/shard_map/all_gather | solution.py:68
  40.5 30.9 %all_gather.7 = bf16[1024,1,128]{2,0,1:T(8,128)(2,1)S(1)} all-gather(bf16[128,1,128]{2,0,1:T(8,128)(2,1)} %param.9), channel_id=1, replica_groups=mesh['ctx'=8,'tp'=4] {'ctx'}, dimensions={0}, use_global_device_ids=true | all-gather | bytes 294912 | tf_op jit(solution)/shard_map/all_gather | solution.py:69
  71.5 1.0 copy.13
  72.5 6.9 %while.17 = (s32[]{:T(128)}, f32[1,8,128]{2,1,0:T(8,128)S(1)}, f32[1,8,128]{2,1,0:T(8,128)S(1)}, f32[1,8,128,128]{3,2,1,0:T(8,128)S(1)}, s32[2]{0:T(128)S(1)}, /...) while((s32[]{:T(128)}, f32[1,8,128]{2,1,0:T(8,128)S(1)}, ...), condition=%wide.region_3.4_spmd.clone, body=%wide.region_0.3_spmd.clone.sunk | while | flops 276908160 | bytes 8201405 | solution.py:81
  72.5 0.6 dynamic_slice.46
  73.1 0.6 add_select_fusion.2
  73.6 0.4 fusion.57
  74.0 0.5 fusion.58
  74.5 0.8 fusion.61
  75.4 0.5 fusion.60
  75.9 0.6 dynamic_slice.46
  76.5 0.6 add_select_fusion.2
  77.1 0.4 fusion.57
  77.5 0.5 fusion.58
  77.9 0.8 fusion.61
  78.8 0.5 fusion.60
  79.3 0.2 copy.10
  79.6 0.1 divide_convert_fusion
  79.6 5.7 %convolution_convert_fusion = bf16[128,4096]{1,0:T(8,128)(2,1)} fusion(bf16[128,1024]{0,1:T(8,128)(2,1)S(1)} %bitcast.95, bf16[1024,4096]{1,0:T(8,128)(2,1)} %param.11), kind=kOutput, calls=%fused_computation.49 | convolution fusion | flops 1074266112 | bytes 9699328 | tf_op jit(solution)/shard_map/dot_general | solution.py:89
  85.3 0.0 reduce-scatter.2.cloned.1.call-update
  85.3 26.0 %reduce-scatter.2.cloned.1.call-done = bf16[128,1024]{1,0:T(8,128)(2,1)} async-done(((bf16[128,4096]{1,0:T(8,128)(2,1)}), bf16[128,1024]{1,0:T(8,128)(2,1)}) %reduce-scatter.2.cloned.1.call-update) | async-done | bytes 262160 | tf_op jit(solution)/shard_map/reduce_scatter | solution.py:90
  (13 shorter events, 0.1 us)
Async XLA Ops:
  6.5 104.8 %reduce-scatter.2.cloned.1.call-start = ((), (), s32[]{:S(2)}) async-start(), calls=%async_computation.1 | async-start | bytes 1310720 | tf_op jit(solution)/shard_map/reduce_scatter | solution.py:90
Sparse Core Ops, SparseCore 0:
  85.4 25.8 reduce-scatter.1
where the time goes:
time: 118 us
  blocking collectives  63.7 us (54%)
  waiting for transfers between devices  26 us (22%)
  between operations  13.4 us (11%)
  matrix products  10.2 us (9%)
  local copies, waits for them, and re-layouts  2.36 us (2%)
  other arithmetic  2.28 us (2%)
    all_gather x1, blocking collectives, shards(): key_piece = lax.all_gather(key_heads, 'ctx', axis=0, tiled=True)  32.7 us
    all_gather x1, blocking collectives, shards(): value_piece = lax.all_gather(value_heads, 'ctx', axis=0, tiled=True)  30.9 us
    reduce_scatter x1, waiting for transfers between devices, shards(): lax.psum_scatter(partial_value.astype(jnp.bfloat16), 'tp', scatter_dimens...  26 us
    dot_general x1, matrix products, shards(): jnp.dot(attended, out_weight, preferred_element_type=jnp.float32)  5.67 us
  transfers between devices with their start and end apart: 1, of which 1 were waited for; matrix products, arithmetic and copies ran while one was open for 0% of the time, Pallas kernels for 0%

commit v1 on v0

v1 whole, which is shorter than its diff:
```python
import functools
import math

import jax
import jax.numpy as jnp
from jax import lax
from jax.experimental import pallas as pl
from jax.experimental.pallas import tpu as pltpu
from jax.sharding import PartitionSpec as P

BLOCK = 128
DIRECT_MOST = 8


def attend_project_kernel(n_pieces, gathered, tp_size, parents_ref, q_ref, *refs):
    kv_refs = refs[:n_pieces]
    w_hbm, keep_ref, send_ref, w_ref, m_ref, l_ref, acc_ref, att_ref, w_sem = refs[n_pieces:]
    rows, head_dim = q_ref.shape
    group = rows // BLOCK
    width = keep_ref.shape[2]
    scale = math.log2(math.e) / math.sqrt(head_dim)
    me = lax.axis_index("ctx")
    mine = lax.axis_index("tp")

    w_copy = pltpu.make_async_copy(w_hbm, w_ref, w_sem)
    w_copy.start()

    def scores_of(k):
        return lax.dot_general(k, q_ref[...], (((1,), (1,)), ((), ())), preferred_element_type=jnp.float32)

    def weighted(v, p):
        return lax.dot_general(v, p.astype(jnp.bfloat16), (((0,), (0,)), ((), ())), preferred_element_type=jnp.float32)

    own = kv_refs[0]
    s = scores_of(own[0:BLOCK, :])
    key_at = lax.broadcasted_iota(jnp.int32, s.shape, 0)
    query_at = lax.broadcasted_iota(jnp.int32, s.shape, 1) & (BLOCK - 1)
    s = jnp.where(key_at <= query_at, s, -1e30)
    m = jnp.max(s, axis=0, keepdims=True)
    p = jnp.exp2((s - m) * scale)
    m_ref[...] = m
    l_ref[...] = jnp.sum(p, axis=0, keepdims=True)
    acc_ref[...] = weighted(own[BLOCK:, :], p)

    def absorb(k, v):
        s = scores_of(k)
        m_old = m_ref[...]
        m_new = jnp.maximum(m_old, jnp.max(s, axis=0, keepdims=True))
        p = jnp.exp2((s - m_new) * scale)
        factor = jnp.exp2((m_old - m_new) * scale)
        m_ref[...] = m_new
        l_ref[...] = l_ref[...] * factor + jnp.sum(p, axis=0, keepdims=True)
        acc_ref[...] = acc_ref[...] * factor + weighted(v, p)

    ancestor = parents_ref[me]
    if gathered:
        piece = kv_refs[1]

        def visit(step, wanted):
            block = me - step
            hit = (block >= 0) & (block == wanted)

            @pl.when(hit)
            def _():
                start = pl.multiple_of(block * 2 * BLOCK, 2 * BLOCK)
                absorb(piece[pl.ds(start, BLOCK), :], piece[pl.ds(start + BLOCK, BLOCK), :])

            return jnp.where(hit, parents_ref[jnp.maximum(block, 0)], wanted)

        lax.fori_loop(1, parents_ref.shape[0], visit, ancestor)
    else:
        for step in range(1, n_pieces):
            block = me - step
            hit = (block >= 0) & (block == ancestor)

            @pl.when(hit)
            def _():
                absorb(kv_refs[step][0:BLOCK, :], kv_refs[step][BLOCK:, :])

            ancestor = jnp.where(hit, parents_ref[jnp.maximum(block, 0)], ancestor)

    for head in range(group):
        at = slice(head * BLOCK, (head + 1) * BLOCK)
        part = acc_ref[:, at] / l_ref[:, at]
        att_ref[:, head * head_dim:(head + 1) * head_dim] = part.T.astype(jnp.bfloat16)

    w_copy.wait()

    def project(block):
        start = pl.multiple_of(block * width, 128)
        return jnp.dot(att_ref[...], w_ref[:, pl.ds(start, width)], preferred_element_type=jnp.float32)

    if tp_size == 4:
        far = mine ^ 2
        send_ref[0] = project(far ^ 1).astype(jnp.bfloat16)
        send_ref[1] = project(mine ^ 1).astype(jnp.bfloat16)
        keep_ref[0] = project(far)
        keep_ref[1] = project(mine)
    else:
        for block in range(tp_size):
            send_ref[block] = project(block).astype(jnp.bfloat16)
        keep_ref[...] = jnp.zeros_like(keep_ref)


def shards(ctx_size, tp_size, query_heads, key_heads, value_heads, parents, out_weight):
    tok_rows, local_heads, head_dim = query_heads.shape
    assert tok_rows == BLOCK and key_heads.shape[1] == 1 and parents.shape[0] == ctx_size
    width = out_weight.shape[1] // tp_size
    rows = local_heads * tok_rows

    kv = jnp.concatenate([key_heads[:, 0, :], value_heads[:, 0, :]], axis=0)
    pieces = [kv]
    gathered = ctx_size > DIRECT_MOST
    if gathered:
        pieces.append(lax.all_gather(kv, "ctx", axis=0, tiled=True))
    else:
        for step in range(1, ctx_size):
            pieces.append(lax.ppermute(kv, "ctx", [(i, i + step) for i in range(ctx_size - step)]))
    q = jnp.transpose(query_heads, (1, 0, 2)).reshape(rows, head_dim)

    vmem = pl.BlockSpec(memory_space=pltpu.VMEM)
    n_send = 2 if tp_size == 4 else tp_size
    keep, send = pl.pallas_call(
        functools.partial(attend_project_kernel, len(pieces), gathered, tp_size),
        out_shape=(
            jax.ShapeDtypeStruct((2, tok_rows, width), jnp.float32),
            jax.ShapeDtypeStruct((n_send, tok_rows, width), jnp.bfloat16),
        ),
        in_specs=[pl.BlockSpec(memory_space=pltpu.SMEM), vmem] + [vmem] * len(pieces) + [pl.BlockSpec(memory_space=pl.ANY)],
        out_specs=(vmem, vmem),
        scratch_shapes=[
            pltpu.VMEM(out_weight.shape, jnp.bfloat16),
            pltpu.VMEM((1, rows), jnp.float32),
            pltpu.VMEM((1, rows), jnp.float32),
            pltpu.VMEM((head_dim, rows), jnp.float32),
            pltpu.VMEM((tok_rows, local_heads * head_dim), jnp.bfloat16),
            pltpu.SemaphoreType.DMA,
        ],
        compiler_params=pltpu.CompilerParams(vmem_limit_bytes=32 * 1024 * 1024),
        cost_estimate=pl.CostEstimate(flops=1_600_000_000, bytes_accessed=12_000_000, transcendentals=1_000_000),
    )(parents, q, *pieces, out_weight)

    if tp_size != 4:
        flat = jnp.transpose(send, (1, 0, 2)).reshape(tok_rows, tp_size * width)
        return lax.psum_scatter(flat, "tp", scatter_dimension=1, tiled=True)
    near_pairs = [(i, i ^ 1) for i in range(4)]
    far_pairs = [(i, i ^ 2) for i in range(4)]
    far_in = lax.ppermute(send[0], "tp", near_pairs)
    near_in = lax.ppermute(send[1], "tp", near_pairs)
    far_sum = (keep[0] + far_in.astype(jnp.float32)).astype(jnp.bfloat16)
    from_far = lax.ppermute(far_sum, "tp", far_pairs)
    return (keep[1] + near_in.astype(jnp.float32) + from_far.astype(jnp.float32)).astype(jnp.bfloat16)


def solution(mesh):
    return jax.shard_map(
        functools.partial(shards, mesh.shape["ctx"], mesh.shape["tp"]),
        mesh=mesh,
        in_specs=(
            P("ctx", "tp", None),
            P("ctx", "tp", None),
            P("ctx", "tp", None),
            P(),
            P("tp", None),
        ),
        out_specs=P("ctx", "tp"),
        check_vma=False,
    )
```

time: 118 us -> 40.5 us (0.34)
  the two profiles are of different devices: /device:TPU:0 before, /device:TPU:18 now
where the time goes in v1:
time: 40.5 us
  starting transfers between devices  17.5 us (43%)
  waiting for transfers between devices  11.6 us (29%)
  local copies, waits for them, and re-layouts  5.06 us (12%)
  Pallas kernels  4.59 us (11%)
  other arithmetic  1.63 us (4%)
    ppermute x7, starting transfers between devices, shards(): lax.ppermute(kv, 'ctx', [(i, i + step) for i in range(ctx_size - step)])  16.3 us
    ppermute x1, waiting for transfers between devices, shards(): from_far = lax.ppermute(far_sum, 'tp', far_pairs)  7.82 us
    pallas_call x1, Pallas kernels, shards(): pl.pallas_call(functools.partial(attend_project_kernel, len(pieces), gath...  4.59 us
    unnamed x4, local copies, waits for them, and re-layouts  4.04 us
    ppermute x7, waiting for transfers between devices, shards(): lax.ppermute(kv, 'ctx', [(i, i + step) for i in range(ctx_size - step)])  2.8 us
    ppermute x1, waiting for transfers between devices, shards(): far_in = lax.ppermute(send[0], 'tp', near_pairs)  1.02 us
    transpose x1, local copies, waits for them, and re-layouts, shards(): q = jnp.transpose(query_heads, (1, 0, 2)).reshape(rows, head_dim)  0.99 us
  transfers between devices with their start and end apart: 10, of which 4 were waited for; matrix products, arithmetic and copies ran while one was open for 3% of the time, Pallas kernels for 0%

profile of v1, /device:TPU:18, one launch (start us, length us, event | category | flops | bytes accessed | tf_op | source)
XLA Modules:
  0.0 40.5 jit_solution(3396869794562638368)
XLA Ops:
  0.0 0.8 %pad_maximum_fusion.refs_0_ = bf16[256,128]{1,0:T(8,128)(2,1)S(1)} fusion(bf16[128,128]{1,0:T(8,128)(2,1)} %bitcast.20, bf16[128,128]{1,0:T(8,128)(2,1)} %bitcast.21), kind=kLoop, calls=%fused_computation.7 | loop fusion | flops 131072 | bytes 131072 | tf_op jit(solution)/shard_map/concatenate | solution.py:111
  0.8 0.7 %collective-permute-start.6 = (bf16[256,128]{1,0:T(8,128)(2,1)S(1)}, bf16[256,128]{1,0:T(8,128)(2,1)S(1)}, u32[]{:S(2)}, u32[]{:S(2)}) collective-permute-start(bf16[256,128]{1,0:T(8,128)(2,1)S(1)} %pad_maximum_fusion.refs_0_), channel_id=1, source_target_pairs={{0,28},{1,29},{2,30},{3,31}} | collective-permute-start | bytes 196616 | tf_op jit(solution)/shard_map/ppermute | solution.py:118
  1.4 0.7 %collective-permute-start.5 = (bf16[256,128]{1,0:T(8,128)(2,1)S(1)}, bf16[256,128]{1,0:T(8,128)(2,1)S(1)}, u32[]{:S(2)}, u32[]{:S(2)}) collective-permute-start(bf16[256,128]{1,0:T(8,128)(2,1)S(1)} %pad_maximum_fusion.refs_0_), channel_id=1, source_target_pairs={{0,24},{4,28},{1,25},{5,29},{2,26},{6,30},{3,27},{7,31}} | collective-permute-start | bytes 196616 | tf_op jit(solution)/shard_map/ppermute | solution.py:118
  2.1 0.7 %collective-permute-start.4 = (bf16[256,128]{1,0:T(8,128)(2,1)S(1)}, bf16[256,128]{1,0:T(8,128)(2,1)S(1)}, u32[]{:S(2)}, u32[]{:S(2)}) collective-permute-start(bf16[256,128]{1,0:T(8,128)(2,1)S(1)} %pad_maximum_fusion.refs_0_), channel_id=1, source_target_pairs={{0,20},{4,24},{8,28},{1,21},{5,25},{9,29},{2,22},{6,26},{10,30},{3... | collective-permute-start | bytes 196616 | tf_op jit(solution)/shard_map/ppermute | solution.py:118
  2.8 1.3 %collective-permute-start.3 = (bf16[256,128]{1,0:T(8,128)(2,1)S(1)}, bf16[256,128]{1,0:T(8,128)(2,1)S(1)}, u32[]{:S(2)}, u32[]{:S(2)}) collective-permute-start(bf16[256,128]{1,0:T(8,128)(2,1)S(1)} %pad_maximum_fusion.refs_0_), channel_id=1, source_target_pairs={{0,16},{4,20},{8,24},{12,28},{1,17},{5,21},{9,25},{13,29},{2,18},{... | collective-permute-start | bytes 196616 | tf_op jit(solution)/shard_map/ppermute | solution.py:118
  4.1 6.3 %collective-permute-start.2 = (bf16[256,128]{1,0:T(8,128)(2,1)S(1)}, bf16[256,128]{1,0:T(8,128)(2,1)S(1)}, u32[]{:S(2)}, u32[]{:S(2)}) collective-permute-start(bf16[256,128]{1,0:T(8,128)(2,1)S(1)} %pad_maximum_fusion.refs_0_), channel_id=1, source_target_pairs={{0,12},{4,16},{8,20},{12,24},{16,28},{1,13},{5,17},{9,21},{13,25},... | collective-permute-start | bytes 196616 | tf_op jit(solution)/shard_map/ppermute | solution.py:118
  10.4 0.0 collective-permute-done.6.refs_7_
  10.4 1.9 %collective-permute-start.1 = (bf16[256,128]{1,0:T(8,128)(2,1)S(1)}, bf16[256,128]{1,0:T(8,128)(2,1)S(1)}, u32[]{:S(2)}, u32[]{:S(2)}) collective-permute-start(bf16[256,128]{1,0:T(8,128)(2,1)S(1)} %pad_maximum_fusion.refs_0_), channel_id=1, source_target_pairs={{0,8},{4,12},{8,16},{12,20},{16,24},{20,28},{1,9},{5,13},{9,17},{1... | collective-permute-start | bytes 196616 | tf_op jit(solution)/shard_map/ppermute | solution.py:118
  12.4 0.0 collective-permute-done.5.refs_6_
  12.4 4.8 %collective-permute-start = (bf16[256,128]{1,0:T(8,128)(2,1)S(1)}, bf16[256,128]{1,0:T(8,128)(2,1)S(1)}, u32[]{:S(2)}, u32[]{:S(2)}) collective-permute-start(bf16[256,128]{1,0:T(8,128)(2,1)S(1)} %pad_maximum_fusion.refs_0_), channel_id=1, source_target_pairs={{0,4},{4,8},{8,12},{12,16},{16,20},{20,24},{24,28},{1,5},{5,9},{9,... | collective-permute-start | bytes 196616 | tf_op jit(solution)/shard_map/ppermute | solution.py:118
  17.2 1.0 %copy.6 = bf16[8,128,128]{2,1,0:T(8,128)(2,1)S(1)} copy(bf16[8,128,128]{2,0,1:T(8,128)(2,1)} %bitcast.19) | data formatting | bytes 524288 | tf_op jit(solution)/shard_map/transpose | solution.py:119
  18.1 0.0 collective-permute-done.4.refs_5_
  18.2 0.0 collective-permute-done.3.refs_4_
  18.2 0.0 collective-permute-done.2.refs_3_
  18.2 1.5 %collective-permute-done.1.refs_2_ = bf16[256,128]{1,0:T(8,128)(2,1)S(1)} collective-permute-done((bf16[256,128]{1,0:T(8,128)(2,1)S(1)}, bf16[256,128]{1,0:T(8,128)(2,1)S(1)}, u32[]{:S(2)}, u32[]{:S(2)}) %collective-permute-start.1) | collective-permute-done | bytes 65568 | tf_op jit(solution)/shard_map/ppermute | solution.py:118
  19.7 1.3 %collective-permute-done.refs_1_ = bf16[256,128]{1,0:T(8,128)(2,1)S(1)} collective-permute-done((bf16[256,128]{1,0:T(8,128)(2,1)S(1)}, bf16[256,128]{1,0:T(8,128)(2,1)S(1)}, u32[]{:S(2)}, u32[]{:S(2)}) %collective-permute-start) | collective-permute-done | bytes 65568 | tf_op jit(solution)/shard_map/ppermute | solution.py:118
  21.0 0.0 copy-start
  21.0 3.4 %copy-done = bf16[1024,4096]{1,0:T(8,128)(2,1)S(1)} copy-done((bf16[1024,4096]{1,0:T(8,128)(2,1)S(1)}, bf16[1024,4096]{1,0:T(8,128)(2,1)}, u32[]{:S(2)}) %copy-start) | copy-done | bytes 8388632
  24.4 0.0 copy-start.1
  24.4 0.7 %copy-done.1 = s32[8]{0:T(128)S(1)} copy-done((s32[8]{0:T(128)S(1)}, s32[8]{0:T(128)}, u32[]{:S(2)}) %copy-start.1) | copy-done | bytes 56
  25.0 4.6 %shard_map.55 = (f32[2,128,1024]{2,1,0:T(8,128)S(1)}, bf16[2,128,1024]{2,1,0:T(8,128)(2,1)S(1)}) custom-call(s32[8]{0:T(128)S(1)} %copy-done.1, bf16[1024,128]{1,0:T(8,128)(2,1)S(1)} %bitcast.18, bf16[256,128]{1,0:T(8,128)(2,1)S(1)} %pad_maximum_fusion.refs_0_, bf16[256,128]{1,0:T(8,128)(2,1)S(1)} %collective-permute-done.refs_1_, ...), custom_call_target="tpu_custom_call" | custom-call | flops 1600000000 | bytes 12000000 | tf_op jit(solution)/shard_map/pallas_call | solution.py:123
  29.6 0.1 collective-permute-start.8
  29.7 0.5 %collective-permute-start.7 = (bf16[128,1024]{1,0:T(8,128)(2,1)S(1)}, bf16[128,1024]{1,0:T(8,128)(2,1)S(1)}, u32[]{:S(2)}, u32[]{:S(2)}) collective-permute-start(bf16[128,1024]{1,0:T(8,128)(2,1)S(1)} %get-tuple-element.9), channel_id=1, source_target_pairs={{0,1},{1,0},{2,3},{3,2},{4,5},{5,4},{6,7},{7,6},{8,9},{9,8},{10,11... | collective-permute-start | bytes 786440 | tf_op jit(solution)/shard_map/ppermute | solution.py:149
  30.2 1.0 %collective-permute-done.8 = bf16[128,1024]{1,0:T(8,128)(2,1)S(1)} collective-permute-done((bf16[128,1024]{1,0:T(8,128)(2,1)S(1)}, bf16[128,1024]{1,0:T(8,128)(2,1)S(1)}, u32[]{:S(2)}, u32[]{:S(2)}) %collective-permute-start.8) | collective-permute-done | bytes 262176 | tf_op jit(solution)/shard_map/ppermute | solution.py:148
  31.2 0.1 fusion
  31.3 0.6 %collective-permute-start.9 = (bf16[128,1024]{1,0:T(8,128)(2,1)S(1)}, bf16[128,1024]{1,0:T(8,128)(2,1)S(1)}, u32[]{:S(2)}, u32[]{:S(2)}) collective-permute-start(bf16[128,1024]{1,0:T(8,128)(2,1)S(1)} %fusion), channel_id=1, source_target_pairs={{0,2},{1,3},{2,0},{3,1},{4,6},{5,7},{6,4},{7,5},{8,10},{9,11},{10,... | collective-permute-start | bytes 786440 | tf_op jit(solution)/shard_map/ppermute | solution.py:151
  31.9 0.0 collective-permute-done.7
  31.9 7.8 %collective-permute-done.9 = bf16[128,1024]{1,0:T(8,128)(2,1)S(1)} collective-permute-done((bf16[128,1024]{1,0:T(8,128)(2,1)S(1)}, bf16[128,1024]{1,0:T(8,128)(2,1)S(1)}, u32[]{:S(2)}, u32[]{:S(2)}) %collective-permute-start.9) | collective-permute-done | bytes 262176 | tf_op jit(solution)/shard_map/ppermute | solution.py:151
  39.7 0.8 %fusion.2 = bf16[128,1024]{1,0:T(8,128)(2,1)} fusion(bf16[128,1024]{1,0:T(8,128)(2,1)S(1)} %collective-permute-done.9, bf16[128,1024]{1,0:T(8,128)(2,1)S(1)} %collective-permute-done.7, f32[2,128,1024]{2,1,0:T(8,128)S(1)} %get-tuple-element.7), kind=kLoop, calls=%fused_computation.4 | loop fusion | flops 655360 | bytes 1310720 | tf_op jit(solution)/shard_map/convert_element_type | solution.py:152
  (1 shorter events, 0.0 us)
Async XLA Ops:
  0.8 9.6 %collective-permute-start.6 = (bf16[256,128]{1,0:T(8,128)(2,1)S(1)}, bf16[256,128]{1,0:T(8,128)(2,1)S(1)}, u32[]{:S(2)}, u32[]{:S(2)}) collective-permute-start(bf16[256,128]{1,0:T(8,128)(2,1)S(1)} %pad_maximum_fusion.refs_0_), channel_id=1, source_target_pairs={{0,28},{1,29},{2,30},{3,31}} | collective-permute-start | bytes 196616 | tf_op jit(solution)/shard_map/ppermute | solution.py:118
  1.4 10.9 %collective-permute-start.5 = (bf16[256,128]{1,0:T(8,128)(2,1)S(1)}, bf16[256,128]{1,0:T(8,128)(2,1)S(1)}, u32[]{:S(2)}, u32[]{:S(2)}) collective-permute-start(bf16[256,128]{1,0:T(8,128)(2,1)S(1)} %pad_maximum_fusion.refs_0_), channel_id=1, source_target_pairs={{0,24},{4,28},{1,25},{5,29},{2,26},{6,30},{3,27},{7,31}} | collective-permute-start | bytes 196616 | tf_op jit(solution)/shard_map/ppermute | solution.py:118
  2.1 16.0 %collective-permute-start.4 = (bf16[256,128]{1,0:T(8,128)(2,1)S(1)}, bf16[256,128]{1,0:T(8,128)(2,1)S(1)}, u32[]{:S(2)}, u32[]{:S(2)}) collective-permute-start(bf16[256,128]{1,0:T(8,128)(2,1)S(1)} %pad_maximum_fusion.refs_0_), channel_id=1, source_target_pairs={{0,20},{4,24},{8,28},{1,21},{5,25},{9,29},{2,22},{6,26},{10,30},{3... | collective-permute-start | bytes 196616 | tf_op jit(solution)/shard_map/ppermute | solution.py:118
  2.8 15.4 %collective-permute-start.3 = (bf16[256,128]{1,0:T(8,128)(2,1)S(1)}, bf16[256,128]{1,0:T(8,128)(2,1)S(1)}, u32[]{:S(2)}, u32[]{:S(2)}) collective-permute-start(bf16[256,128]{1,0:T(8,128)(2,1)S(1)} %pad_maximum_fusion.refs_0_), channel_id=1, source_target_pairs={{0,16},{4,20},{8,24},{12,28},{1,17},{5,21},{9,25},{13,29},{2,18},{... | collective-permute-start | bytes 196616 | tf_op jit(solution)/shard_map/ppermute | solution.py:118
  4.1 14.1 %collective-permute-start.2 = (bf16[256,128]{1,0:T(8,128)(2,1)S(1)}, bf16[256,128]{1,0:T(8,128)(2,1)S(1)}, u32[]{:S(2)}, u32[]{:S(2)}) collective-permute-start(bf16[256,128]{1,0:T(8,128)(2,1)S(1)} %pad_maximum_fusion.refs_0_), channel_id=1, source_target_pairs={{0,12},{4,16},{8,20},{12,24},{16,28},{1,13},{5,17},{9,21},{13,25},... | collective-permute-start | bytes 196616 | tf_op jit(solution)/shard_map/ppermute | solution.py:118
  10.4 9.2 %collective-permute-start.1 = (bf16[256,128]{1,0:T(8,128)(2,1)S(1)}, bf16[256,128]{1,0:T(8,128)(2,1)S(1)}, u32[]{:S(2)}, u32[]{:S(2)}) collective-permute-start(bf16[256,128]{1,0:T(8,128)(2,1)S(1)} %pad_maximum_fusion.refs_0_), channel_id=1, source_target_pairs={{0,8},{4,12},{8,16},{12,20},{16,24},{20,28},{1,9},{5,13},{9,17},{1... | collective-permute-start | bytes 196616 | tf_op jit(solution)/shard_map/ppermute | solution.py:118
  12.4 8.6 %collective-permute-start = (bf16[256,128]{1,0:T(8,128)(2,1)S(1)}, bf16[256,128]{1,0:T(8,128)(2,1)S(1)}, u32[]{:S(2)}, u32[]{:S(2)}) collective-permute-start(bf16[256,128]{1,0:T(8,128)(2,1)S(1)} %pad_maximum_fusion.refs_0_), channel_id=1, source_target_pairs={{0,4},{4,8},{8,12},{12,16},{16,20},{20,24},{24,28},{1,5},{5,9},{9,... | collective-permute-start | bytes 196616 | tf_op jit(solution)/shard_map/ppermute | solution.py:118
  21.0 3.4 %copy-start = (bf16[1024,4096]{1,0:T(8,128)(2,1)S(1)}, bf16[1024,4096]{1,0:T(8,128)(2,1)}, u32[]{:S(2)}) copy-start(bf16[1024,4096]{1,0:T(8,128)(2,1)} %refs_8_.1) | copy-start | bytes 25165828
  24.4 0.7 %copy-start.1 = (s32[8]{0:T(128)S(1)}, s32[8]{0:T(128)}, u32[]{:S(2)}) copy-start(s32[8]{0:T(128)} %parents_ref.1) | copy-start | bytes 100
  29.6 1.6 %collective-permute-start.8 = (bf16[128,1024]{1,0:T(8,128)(2,1)S(1)}, bf16[128,1024]{1,0:T(8,128)(2,1)S(1)}, u32[]{:S(2)}, u32[]{:S(2)}) collective-permute-start(bf16[128,1024]{1,0:T(8,128)(2,1)S(1)} %get-tuple-element.10), channel_id=1, source_target_pairs={{0,1},{1,0},{2,3},{3,2},{4,5},{5,4},{6,7},{7,6},{8,9},{9,8},{10,11... | collective-permute-start | bytes 786440 | tf_op jit(solution)/shard_map/ppermute | solution.py:148
  29.7 2.2 %collective-permute-start.7 = (bf16[128,1024]{1,0:T(8,128)(2,1)S(1)}, bf16[128,1024]{1,0:T(8,128)(2,1)S(1)}, u32[]{:S(2)}, u32[]{:S(2)}) collective-permute-start(bf16[128,1024]{1,0:T(8,128)(2,1)S(1)} %get-tuple-element.9), channel_id=1, source_target_pairs={{0,1},{1,0},{2,3},{3,2},{4,5},{5,4},{6,7},{7,6},{8,9},{9,8},{10,11... | collective-permute-start | bytes 786440 | tf_op jit(solution)/shard_map/ppermute | solution.py:149
  31.3 8.4 %collective-permute-start.9 = (bf16[128,1024]{1,0:T(8,128)(2,1)S(1)}, bf16[128,1024]{1,0:T(8,128)(2,1)S(1)}, u32[]{:S(2)}, u32[]{:S(2)}) collective-permute-start(bf16[128,1024]{1,0:T(8,128)(2,1)S(1)} %fusion), channel_id=1, source_target_pairs={{0,2},{1,3},{2,0},{3,1},{4,6},{5,7},{6,4},{7,5},{8,10},{9,11},{10,... | collective-permute-start | bytes 786440 | tf_op jit(solution)/shard_map/ppermute | solution.py:151

commit v2 on v1

v2 whole, which is shorter than its diff:
```python
import functools
import math

import jax
import jax.numpy as jnp
from jax import lax
from jax.experimental import pallas as pl
from jax.experimental.pallas import tpu as pltpu
from jax.sharding import PartitionSpec as P

BLOCK = 128
DIRECT_SIZE = 8
VMEM_LIMIT = 32 * 1024 * 1024


def scores_of(k, q):
    return lax.dot_general(k, q, (((1,), (1,)), ((), ())), preferred_element_type=jnp.float32)


def weighted(v, p):
    return lax.dot_general(v, p.astype(jnp.bfloat16), (((0,), (0,)), ((), ())), preferred_element_type=jnp.float32)


def exponent_scale(head_dim):
    return math.log2(math.e) / math.sqrt(head_dim)


def own_block_kernel(q_ref, kv_ref, w_hbm, m_ref, l_ref, acc_ref, w_ref, w_sem):
    w_copy = pltpu.make_async_copy(w_hbm, w_ref, w_sem)
    w_copy.start()
    scale = exponent_scale(q_ref.shape[1])
    s = scores_of(kv_ref[0:BLOCK, :], q_ref[...])
    key_at = lax.broadcasted_iota(jnp.int32, s.shape, 0)
    query_at = lax.broadcasted_iota(jnp.int32, s.shape, 1) & (BLOCK - 1)
    s = jnp.where(key_at <= query_at, s, -1e30)
    m = jnp.max(s, axis=0, keepdims=True)
    p = jnp.exp2((s - m) * scale)
    m_ref[...] = m
    l_ref[...] = jnp.sum(p, axis=0, keepdims=True)
    acc_ref[...] = weighted(kv_ref[BLOCK:, :], p)
    w_copy.wait()


def project(att, w_ref, block, width):
    start = pl.multiple_of(block * width, 128)
    return jnp.dot(att, w_ref[:, pl.ds(start, width)], preferred_element_type=jnp.float32)


def others_kernel(xors, parents_ref, q_ref, m_in, l_in, acc_in, *refs):
    kv_refs = refs[:max(len(xors), 1)]
    w_ref, att_ref, send_ref, keep_ref, m_ref, l_ref, acc_ref = refs[len(kv_refs):]
    rows, head_dim = q_ref.shape
    group = rows // BLOCK
    width = keep_ref.shape[1]
    scale = exponent_scale(head_dim)
    me = lax.axis_index("ctx")
    far = lax.axis_index("tp") ^ 2

    m_ref[...] = m_in[...]
    l_ref[...] = l_in[...]
    acc_ref[...] = acc_in[...]

    def absorb(k, v):
        s = scores_of(k, q_ref[...])
        m_old = m_ref[...]
        m_new = jnp.maximum(m_old, jnp.max(s, axis=0, keepdims=True))
        p = jnp.exp2((s - m_new) * scale)
        factor = jnp.exp2((m_old - m_new) * scale)
        m_ref[...] = m_new
        l_ref[...] = l_ref[...] * factor + jnp.sum(p, axis=0, keepdims=True)
        acc_ref[...] = acc_ref[...] * factor + weighted(v, p)

    if xors:
        wanted = parents_ref[me]
        reached = jnp.int32(0)
        for step in range(1, len(xors) + 1):
            block = me - step
            hit = (block >= 0) & (block == wanted)
            block = jnp.maximum(block, 0)
            reached = jnp.where(hit, reached | lax.shift_left(jnp.int32(1), block), reached)
            wanted = jnp.where(hit, parents_ref[block], wanted)
        for other, kv_ref in zip(xors, kv_refs):
            @pl.when((lax.shift_right_logical(reached, me ^ other) & 1) == 1)
            def _():
                absorb(kv_ref[0:BLOCK, :], kv_ref[BLOCK:, :])
    else:
        piece = kv_refs[0]

        def visit(step, wanted):
            block = me - step
            hit = (block >= 0) & (block == wanted)
            block = jnp.maximum(block, 0)

            @pl.when(hit)
            def _():
                start = pl.multiple_of(block * 2 * BLOCK, 2 * BLOCK)
                absorb(piece[pl.ds(start, BLOCK), :], piece[pl.ds(start + BLOCK, BLOCK), :])

            return jnp.where(hit, parents_ref[block], wanted)

        lax.fori_loop(1, parents_ref.shape[0], visit, parents_ref[me])

    for head in range(group):
        at = slice(head * BLOCK, (head + 1) * BLOCK)
        part = acc_ref[:, at] / l_ref[:, at]
        att_ref[:, head * head_dim:(head + 1) * head_dim] = part.T.astype(jnp.bfloat16)

    att = att_ref[...]
    send_ref[...] = project(att, w_ref, far ^ 1, width).astype(jnp.bfloat16)
    keep_ref[...] = project(att, w_ref, far, width)


def near_kernel(att_ref, w_ref, send_ref, keep_ref):
    mine = lax.axis_index("tp")
    width = keep_ref.shape[1]
    att = att_ref[...]
    send_ref[...] = project(att, w_ref, mine ^ 1, width).astype(jnp.bfloat16)
    keep_ref[...] = project(att, w_ref, mine, width)


def shards(ctx_size, tp_size, query_heads, key_heads, value_heads, parents, out_weight):
    tok_rows, local_heads, head_dim = query_heads.shape
    assert tok_rows == BLOCK and key_heads.shape[1] == 1 and parents.shape[0] == ctx_size and tp_size == 4
    width = out_weight.shape[1] // tp_size
    rows = local_heads * tok_rows
    params = pltpu.CompilerParams(vmem_limit_bytes=VMEM_LIMIT)
    vmem = pl.BlockSpec(memory_space=pltpu.VMEM)
    hbm = pl.BlockSpec(memory_space=pltpu.HBM)
    smem = pl.BlockSpec(memory_space=pltpu.SMEM)

    def swap(x, axis, size, other):
        return lax.ppermute(x, axis, [(i, i ^ other) for i in range(size)])

    kv = jnp.concatenate([key_heads[:, 0, :], value_heads[:, 0, :]], axis=0)
    if ctx_size == DIRECT_SIZE:
        columns = [swap(kv, "ctx", ctx_size, other) for other in (2, 4, 6)]
        beside = swap(kv, "ctx", ctx_size, 1)
    q = jnp.transpose(query_heads, (1, 0, 2)).reshape(rows, head_dim)

    m, l, acc, w = pl.pallas_call(
        own_block_kernel,
        out_shape=(
            jax.ShapeDtypeStruct((1, rows), jnp.float32),
            jax.ShapeDtypeStruct((1, rows), jnp.float32),
            jax.ShapeDtypeStruct((head_dim, rows), jnp.float32),
            jax.ShapeDtypeStruct(out_weight.shape, out_weight.dtype),
        ),
        in_specs=[vmem, vmem, hbm],
        out_specs=(vmem, vmem, vmem, vmem),
        scratch_shapes=[pltpu.SemaphoreType.DMA],
        compiler_params=params,
        cost_estimate=pl.CostEstimate(flops=67_000_000, bytes_accessed=9_000_000, transcendentals=130_000),
    )(q, kv, pltpu.with_memory_space_constraint(out_weight, pltpu.HBM))

    if ctx_size == DIRECT_SIZE:
        pairs = []
        for at in range(3):
            columns[at], m = lax.optimization_barrier((columns[at], m))
            pairs.append(swap(columns[at], "ctx", ctx_size, 1))
        pieces = columns + pairs + [beside]
        xors = (2, 4, 6, 3, 5, 7, 1)
    else:
        xors = ()
        pieces = [lax.all_gather(kv, "ctx", axis=0, tiled=True)]

    att, send_far, keep_far = pl.pallas_call(
        functools.partial(others_kernel, xors),
        out_shape=(
            jax.ShapeDtypeStruct((tok_rows, local_heads * head_dim), jnp.bfloat16),
            jax.ShapeDtypeStruct((tok_rows, width), jnp.bfloat16),
            jax.ShapeDtypeStruct((tok_rows, width), jnp.float32),
        ),
        in_specs=[smem] + [vmem] * (5 + len(pieces)),
        out_specs=(vmem, vmem, vmem),
        scratch_shapes=[
            pltpu.VMEM((1, rows), jnp.float32),
            pltpu.VMEM((1, rows), jnp.float32),
            pltpu.VMEM((head_dim, rows), jnp.float32),
        ],
        compiler_params=params,
        cost_estimate=pl.CostEstimate(flops=1_000_000_000, bytes_accessed=10_000_000, transcendentals=1_000_000),
    )(parents, q, m, l, acc, *pieces, w)

    far_in = swap(send_far, "tp", tp_size, 1)
    send_near, keep_near = pl.pallas_call(
        near_kernel,
        out_shape=(
            jax.ShapeDtypeStruct((tok_rows, width), jnp.bfloat16),
            jax.ShapeDtypeStruct((tok_rows, width), jnp.float32),
        ),
        in_specs=[vmem, vmem],
        out_specs=(vmem, vmem),
        compiler_params=params,
        cost_estimate=pl.CostEstimate(flops=540_000_000, bytes_accessed=4_000_000, transcendentals=0),
    )(att, w)
    near_in = swap(send_near, "tp", tp_size, 1)
    far_sum = (keep_far + far_in.astype(jnp.float32)).astype(jnp.bfloat16)
    from_far = swap(far_sum, "tp", tp_size, 2)
    return (keep_near + near_in.astype(jnp.float32) + from_far.astype(jnp.float32)).astype(jnp.bfloat16)


def solution(mesh):
    return jax.shard_map(
        functools.partial(shards, mesh.shape["ctx"], mesh.shape["tp"]),
        mesh=mesh,
        in_specs=(
            P("ctx", "tp", None),
            P("ctx", "tp", None),
            P("ctx", "tp", None),
            P(),
            P("tp", None),
        ),
        out_specs=P("ctx", "tp"),
        check_vma=False,
    )
```

time: 40.5 us -> 31.6 us (0.78)
  the two profiles are of different devices: /device:TPU:18 before, /device:TPU:0 now
where the time goes in v2:
time: 31.6 us; the launch traced here: 31.3 us
  starting transfers between devices  13 us (41%)
  waiting for transfers between devices  10 us (32%)
  Pallas kernels  5.55 us (18%)
  other arithmetic  1.67 us (5%)
  local copies, waits for them, and re-layouts  0.99 us (3%)
    ppermute x10, starting transfers between devices, swap(): return lax.ppermute(x, axis, [(i, i ^ other) for i in range(size)])  13 us
    ppermute x10, waiting for transfers between devices, swap(): return lax.ppermute(x, axis, [(i, i ^ other) for i in range(size)])  10 us
    pallas_call x1, Pallas kernels, shards(): pl.pallas_call(own_block_kernel, out_shape=(jax.ShapeDtypeStruct((1, rows...  3.39 us
    pallas_call x1, Pallas kernels, shards(): pl.pallas_call(functools.partial(others_kernel, xors), out_shape=(jax.Sha...  1.42 us
    transpose x1, local copies, waits for them, and re-layouts, shards(): q = jnp.transpose(query_heads, (1, 0, 2)).reshape(rows, head_dim)  0.99 us
    convert_element_type x1, other arithmetic, shards(): (keep_near + near_in.astype(jnp.float32) + from_far.astype(jnp.float32))....  0.81 us
    concatenate x1, other arithmetic, shards(): kv = jnp.concatenate([key_heads[:, 0, :], value_heads[:, 0, :]], axis=0)  0.79 us
    pallas_call x1, Pallas kernels, shards(): pl.pallas_call(near_kernel, out_shape=(jax.ShapeDtypeStruct((tok_rows, wi...  0.73 us
  transfers between devices with their start and end apart: 10, of which 5 were waited for; matrix products, arithmetic and copies ran while one was open for 3% of the time, Pallas kernels for 13%

profile of v2, /device:TPU:0, one launch (start us, length us, event | category | flops | bytes accessed | tf_op | source)
XLA Modules:
  0.0 31.3 jit_solution(17161182071715707875)
XLA Ops:
  0.0 0.0 copy-start
  0.0 0.8 %pad_maximum_fusion.kv_ref = bf16[256,128]{1,0:T(8,128)(2,1)S(1)} fusion(bf16[128,128]{1,0:T(8,128)(2,1)} %bitcast.7, bf16[128,128]{1,0:T(8,128)(2,1)} %bitcast.8), kind=kLoop, calls=%fused_computation.2 | loop fusion | flops 131072 | bytes 131072 | tf_op jit(solution)/shard_map/concatenate | solution.py:134
  0.8 3.0 %collective-permute-start.2 = (bf16[256,128]{1,0:T(8,128)(2,1)S(1)}, bf16[256,128]{1,0:T(8,128)(2,1)S(1)}, u32[]{:S(2)}, u32[]{:S(2)}) collective-permute-start(bf16[256,128]{1,0:T(8,128)(2,1)S(1)} %pad_maximum_fusion.kv_ref), channel_id=1, source_target_pairs={{0,8},{4,12},{8,0},{12,4},{16,24},{20,28},{24,16},{28,20},{1,9},{5... | collective-permute-start | bytes 196616 | tf_op jit(solution)/shard_map/ppermute | solution.py:132
  3.8 2.6 %collective-permute-start.1 = (bf16[256,128]{1,0:T(8,128)(2,1)S(1)}, bf16[256,128]{1,0:T(8,128)(2,1)S(1)}, u32[]{:S(2)}, u32[]{:S(2)}) collective-permute-start(bf16[256,128]{1,0:T(8,128)(2,1)S(1)} %pad_maximum_fusion.kv_ref), channel_id=1, source_target_pairs={{0,16},{4,20},{8,24},{12,28},{16,0},{20,4},{24,8},{28,12},{1,17},{... | collective-permute-start | bytes 196616 | tf_op jit(solution)/shard_map/ppermute | solution.py:132
  6.4 0.0 collective-permute-start
  6.4 1.7 %collective-permute-start.6 = (bf16[256,128]{1,0:T(8,128)(2,1)S(1)}, bf16[256,128]{1,0:T(8,128)(2,1)S(1)}, u32[]{:S(2)}, u32[]{:S(2)}) collective-permute-start(bf16[256,128]{1,0:T(8,128)(2,1)S(1)} %pad_maximum_fusion.kv_ref), channel_id=1, source_target_pairs={{0,4},{4,0},{8,12},{12,8},{16,20},{20,16},{24,28},{28,24},{1,5},{5... | collective-permute-start | bytes 196616 | tf_op jit(solution)/shard_map/ppermute | solution.py:132
  8.2 1.0 %copy.6 = bf16[8,128,128]{2,1,0:T(8,128)(2,1)S(1)} copy(bf16[8,128,128]{2,0,1:T(8,128)(2,1)} %bitcast.6) | data formatting | bytes 524288 | tf_op jit(solution)/shard_map/transpose | solution.py:138
  9.1 3.4 %shard_map.55 = (f32[1,1024]{1,0:T(1,128)S(1)}, f32[1,1024]{1,0:T(1,128)S(1)}, f32[128,1024]{1,0:T(8,128)S(1)}, bf16[1024,4096]{1,0:T(8,128)(2,1)S(1)}) custom-call(bf16[1024,128]{1,0:T(8,128)(2,1)S(1)} %bitcast.4, bf16[256,128]{1,0:T(8,128)(2,1)S(1)} %pad_maximum_fusion.kv_ref, bf16[1024,4096]{1,0:T(8,128)(2,1)} %w_hbm.1), custom_call_target="tpu_custom_call" | custom-call | flops 67000000 | bytes 9000000 | tf_op jit(solution)/shard_map/pallas_call | solution.py:140
  12.5 0.0 collective-permute-done.2.refs_0_
  12.6 0.0 collective-permute-done.1.refs_1_
  12.6 0.0 collective-permute-done.refs_2_
  12.6 1.4 %collective-permute-start.5 = (bf16[256,128]{1,0:T(8,128)(2,1)S(1)}, bf16[256,128]{1,0:T(8,128)(2,1)S(1)}, u32[]{:S(2)}, u32[]{:S(2)}) collective-permute-start(bf16[256,128]{1,0:T(8,128)(2,1)S(1)} %collective-permute-done.refs_2_), channel_id=1, source_target_pairs={{0,4},{4,0},{8,12},{12,8},{16,20},{20,16},{24,28},{28,24},{1,5},{5... | collective-permute-start | bytes 196616 | tf_op jit(solution)/shard_map/ppermute | solution.py:132
  14.0 0.7 %collective-permute-start.4 = (bf16[256,128]{1,0:T(8,128)(2,1)S(1)}, bf16[256,128]{1,0:T(8,128)(2,1)S(1)}, u32[]{:S(2)}, u32[]{:S(2)}) collective-permute-start(bf16[256,128]{1,0:T(8,128)(2,1)S(1)} %collective-permute-done.1.refs_1_), channel_id=1, source_target_pairs={{0,4},{4,0},{8,12},{12,8},{16,20},{20,16},{24,28},{28,24},{1,5},{5... | collective-permute-start | bytes 196616 | tf_op jit(solution)/shard_map/ppermute | solution.py:132
  14.7 1.4 %collective-permute-start.3 = (bf16[256,128]{1,0:T(8,128)(2,1)S(1)}, bf16[256,128]{1,0:T(8,128)(2,1)S(1)}, u32[]{:S(2)}, u32[]{:S(2)}) collective-permute-start(bf16[256,128]{1,0:T(8,128)(2,1)S(1)} %collective-permute-done.2.refs_0_), channel_id=1, source_target_pairs={{0,4},{4,0},{8,12},{12,8},{16,20},{20,16},{24,28},{28,24},{1,5},{5... | collective-permute-start | bytes 196616 | tf_op jit(solution)/shard_map/ppermute | solution.py:132
  16.0 0.0 collective-permute-done.6.refs_6_
  16.0 0.9 %collective-permute-done.5.refs_5_ = bf16[256,128]{1,0:T(8,128)(2,1)S(1)} collective-permute-done((bf16[256,128]{1,0:T(8,128)(2,1)S(1)}, bf16[256,128]{1,0:T(8,128)(2,1)S(1)}, u32[]{:S(2)}, u32[]{:S(2)}) %collective-permute-start.5) | collective-permute-done | bytes 65568 | tf_op jit(solution)/shard_map/ppermute | solution.py:132
  16.9 1.4 %collective-permute-done.4.refs_4_ = bf16[256,128]{1,0:T(8,128)(2,1)S(1)} collective-permute-done((bf16[256,128]{1,0:T(8,128)(2,1)S(1)}, bf16[256,128]{1,0:T(8,128)(2,1)S(1)}, u32[]{:S(2)}, u32[]{:S(2)}) %collective-permute-start.4) | collective-permute-done | bytes 65568 | tf_op jit(solution)/shard_map/ppermute | solution.py:132
  18.3 0.7 %collective-permute-done.3.refs_3_ = bf16[256,128]{1,0:T(8,128)(2,1)S(1)} collective-permute-done((bf16[256,128]{1,0:T(8,128)(2,1)S(1)}, bf16[256,128]{1,0:T(8,128)(2,1)S(1)}, u32[]{:S(2)}, u32[]{:S(2)}) %collective-permute-start.3) | collective-permute-done | bytes 65568 | tf_op jit(solution)/shard_map/ppermute | solution.py:132
  19.0 0.0 copy-done
  19.0 1.4 %shard_map.56 = (bf16[128,1024]{1,0:T(8,128)(2,1)S(1)}, bf16[128,1024]{1,0:T(8,128)(2,1)S(1)}, f32[128,1024]{1,0:T(8,128)S(1)}) custom-call(s32[8]{0:T(128)S(1)} %copy-done, bf16[1024,128]{1,0:T(8,128)(2,1)S(1)} %bitcast.5, f32[1,1024]{1,0:T(1,128)S(1)} %get-tuple-element.23.m_in, f32[1,1024]{1,0:T(1,128)S(1)} %get-tuple-element.24.l_in, ...), custom_call_target="tpu_custom_call" | custom-call | flops 1000000000 | bytes 10000000 | tf_op jit(solution)/shard_map/pallas_call | solution.py:166
  20.4 0.1 collective-permute-start.8
  20.5 0.7 %shard_map.57 = (bf16[128,1024]{1,0:T(8,128)(2,1)S(1)}, f32[128,1024]{1,0:T(8,128)S(1)}) custom-call(bf16[128,1024]{1,0:T(8,128)(2,1)S(1)} %get-tuple-element.30.att_ref, bf16[1024,4096]{1,0:T(8,128)(2,1)S(1)} %get-tuple-element.29.refs_7_.w_ref), custom_call_target="tpu_custom_call" | custom-call | flops 540000000 | bytes 4000000 | tf_op jit(solution)/shard_map/pallas_call | solution.py:185
  21.2 0.6 %collective-permute-start.7 = (bf16[128,1024]{1,0:T(8,128)(2,1)S(1)}, bf16[128,1024]{1,0:T(8,128)(2,1)S(1)}, u32[]{:S(2)}, u32[]{:S(2)}) collective-permute-start(bf16[128,1024]{1,0:T(8,128)(2,1)S(1)} %get-tuple-element.32), channel_id=1, source_target_pairs={{0,1},{1,0},{2,3},{3,2},{4,5},{5,4},{6,7},{7,6},{8,9},{9,8},{10,11... | collective-permute-start | bytes 786440 | tf_op jit(solution)/shard_map/ppermute | solution.py:132
  21.8 0.2 collective-permute-done.8
  22.0 0.1 add_convert_fusion.1
  22.1 1.5 %collective-permute-start.9 = (bf16[128,1024]{1,0:T(8,128)(2,1)S(1)}, bf16[128,1024]{1,0:T(8,128)(2,1)S(1)}, u32[]{:S(2)}, u32[]{:S(2)}) collective-permute-start(bf16[128,1024]{1,0:T(8,128)(2,1)S(1)} %add_convert_fusion.1), channel_id=1, source_target_pairs={{0,2},{1,3},{2,0},{3,1},{4,6},{5,7},{6,4},{7,5},{8,10},{9,11},{10,... | collective-permute-start | bytes 786440 | tf_op jit(solution)/shard_map/ppermute | solution.py:132
  23.6 0.0 collective-permute-done.7
  23.6 6.9 %collective-permute-done.9 = bf16[128,1024]{1,0:T(8,128)(2,1)S(1)} collective-permute-done((bf16[128,1024]{1,0:T(8,128)(2,1)S(1)}, bf16[128,1024]{1,0:T(8,128)(2,1)S(1)}, u32[]{:S(2)}, u32[]{:S(2)}) %collective-permute-start.9) | collective-permute-done | bytes 262176 | tf_op jit(solution)/shard_map/ppermute | solution.py:132
  30.5 0.8 %add_convert_fusion = bf16[128,1024]{1,0:T(8,128)(2,1)} fusion(bf16[128,1024]{1,0:T(8,128)(2,1)S(1)} %collective-permute-done.9, f32[128,1024]{1,0:T(8,128)S(1)} %get-tuple-element.31, bf16[128,1024]{1,0:T(8,128)(2,1)S(1)} %collective-permute-done.7), kind=kLoop, calls=%fused_computation | loop fusion | flops 655360 | bytes 1310720 | tf_op jit(solution)/shard_map/convert_element_type | solution.py:199
Async XLA Ops:
  0.0 19.0 %copy-start = (s32[8]{0:T(128)S(1)}, s32[8]{0:T(128)}, u32[]{:S(2)}) copy-start(s32[8]{0:T(128)} %parents_ref.1) | copy-start | bytes 100
  0.8 11.7 %collective-permute-start.2 = (bf16[256,128]{1,0:T(8,128)(2,1)S(1)}, bf16[256,128]{1,0:T(8,128)(2,1)S(1)}, u32[]{:S(2)}, u32[]{:S(2)}) collective-permute-start(bf16[256,128]{1,0:T(8,128)(2,1)S(1)} %pad_maximum_fusion.kv_ref), channel_id=1, source_target_pairs={{0,8},{4,12},{8,0},{12,4},{16,24},{20,28},{24,16},{28,20},{1,9},{5... | collective-permute-start | bytes 196616 | tf_op jit(solution)/shard_map/ppermute | solution.py:132
  3.8 8.7 %collective-permute-start.1 = (bf16[256,128]{1,0:T(8,128)(2,1)S(1)}, bf16[256,128]{1,0:T(8,128)(2,1)S(1)}, u32[]{:S(2)}, u32[]{:S(2)}) collective-permute-start(bf16[256,128]{1,0:T(8,128)(2,1)S(1)} %pad_maximum_fusion.kv_ref), channel_id=1, source_target_pairs={{0,16},{4,20},{8,24},{12,28},{16,0},{20,4},{24,8},{28,12},{1,17},{... | collective-permute-start | bytes 196616 | tf_op jit(solution)/shard_map/ppermute | solution.py:132
  6.4 6.2 %collective-permute-start = (bf16[256,128]{1,0:T(8,128)(2,1)S(1)}, bf16[256,128]{1,0:T(8,128)(2,1)S(1)}, u32[]{:S(2)}, u32[]{:S(2)}) collective-permute-start(bf16[256,128]{1,0:T(8,128)(2,1)S(1)} %pad_maximum_fusion.kv_ref), channel_id=1, source_target_pairs={{0,24},{4,28},{8,16},{12,20},{16,8},{20,12},{24,0},{28,4},{1,25},{... | collective-permute-start | bytes 196616 | tf_op jit(solution)/shard_map/ppermute | solution.py:132
  6.4 9.6 %collective-permute-start.6 = (bf16[256,128]{1,0:T(8,128)(2,1)S(1)}, bf16[256,128]{1,0:T(8,128)(2,1)S(1)}, u32[]{:S(2)}, u32[]{:S(2)}) collective-permute-start(bf16[256,128]{1,0:T(8,128)(2,1)S(1)} %pad_maximum_fusion.kv_ref), channel_id=1, source_target_pairs={{0,4},{4,0},{8,12},{12,8},{16,20},{20,16},{24,28},{28,24},{1,5},{5... | collective-permute-start | bytes 196616 | tf_op jit(solution)/shard_map/ppermute | solution.py:132
  12.6 4.3 %collective-permute-start.5 = (bf16[256,128]{1,0:T(8,128)(2,1)S(1)}, bf16[256,128]{1,0:T(8,128)(2,1)S(1)}, u32[]{:S(2)}, u32[]{:S(2)}) collective-permute-start(bf16[256,128]{1,0:T(8,128)(2,1)S(1)} %collective-permute-done.refs_2_), channel_id=1, source_target_pairs={{0,4},{4,0},{8,12},{12,8},{16,20},{20,16},{24,28},{28,24},{1,5},{5... | collective-permute-start | bytes 196616 | tf_op jit(solution)/shard_map/ppermute | solution.py:132
  14.0 4.3 %collective-permute-start.4 = (bf16[256,128]{1,0:T(8,128)(2,1)S(1)}, bf16[256,128]{1,0:T(8,128)(2,1)S(1)}, u32[]{:S(2)}, u32[]{:S(2)}) collective-permute-start(bf16[256,128]{1,0:T(8,128)(2,1)S(1)} %collective-permute-done.1.refs_1_), channel_id=1, source_target_pairs={{0,4},{4,0},{8,12},{12,8},{16,20},{20,16},{24,28},{28,24},{1,5},{5... | collective-permute-start | bytes 196616 | tf_op jit(solution)/shard_map/ppermute | solution.py:132
  14.7 4.3 %collective-permute-start.3 = (bf16[256,128]{1,0:T(8,128)(2,1)S(1)}, bf16[256,128]{1,0:T(8,128)(2,1)S(1)}, u32[]{:S(2)}, u32[]{:S(2)}) collective-permute-start(bf16[256,128]{1,0:T(8,128)(2,1)S(1)} %collective-permute-done.2.refs_0_), channel_id=1, source_target_pairs={{0,4},{4,0},{8,12},{12,8},{16,20},{20,16},{24,28},{28,24},{1,5},{5... | collective-permute-start | bytes 196616 | tf_op jit(solution)/shard_map/ppermute | solution.py:132
  20.4 1.6 %collective-permute-start.8 = (bf16[128,1024]{1,0:T(8,128)(2,1)S(1)}, bf16[128,1024]{1,0:T(8,128)(2,1)S(1)}, u32[]{:S(2)}, u32[]{:S(2)}) collective-permute-start(bf16[128,1024]{1,0:T(8,128)(2,1)S(1)} %get-tuple-element.34), channel_id=1, source_target_pairs={{0,1},{1,0},{2,3},{3,2},{4,5},{5,4},{6,7},{7,6},{8,9},{9,8},{10,11... | collective-permute-start | bytes 786440 | tf_op jit(solution)/shard_map/ppermute | solution.py:132
  21.2 2.4 %collective-permute-start.7 = (bf16[128,1024]{1,0:T(8,128)(2,1)S(1)}, bf16[128,1024]{1,0:T(8,128)(2,1)S(1)}, u32[]{:S(2)}, u32[]{:S(2)}) collective-permute-start(bf16[128,1024]{1,0:T(8,128)(2,1)S(1)} %get-tuple-element.32), channel_id=1, source_target_pairs={{0,1},{1,0},{2,3},{3,2},{4,5},{5,4},{6,7},{7,6},{8,9},{9,8},{10,11... | collective-permute-start | bytes 786440 | tf_op jit(solution)/shard_map/ppermute | solution.py:132
  22.1 8.4 %collective-permute-start.9 = (bf16[128,1024]{1,0:T(8,128)(2,1)S(1)}, bf16[128,1024]{1,0:T(8,128)(2,1)S(1)}, u32[]{:S(2)}, u32[]{:S(2)}) collective-permute-start(bf16[128,1024]{1,0:T(8,128)(2,1)S(1)} %add_convert_fusion.1), channel_id=1, source_target_pairs={{0,2},{1,3},{2,0},{3,1},{4,6},{5,7},{6,4},{7,5},{8,10},{9,11},{10,... | collective-permute-start | bytes 786440 | tf_op jit(solution)/shard_map/ppermute | solution.py:132

commit v3 on v2

v3 whole, which is shorter than its diff:
```python
import functools
import math

import jax
import jax.numpy as jnp
from jax import lax
from jax.experimental import pallas as pl
from jax.experimental.pallas import tpu as pltpu
from jax.sharding import PartitionSpec as P

BLOCK = 128
DIRECT_SIZE = 8
VMEM_LIMIT = 32 * 1024 * 1024


def scores_of(k, q):
    return lax.dot_general(k, q, (((1,), (1,)), ((), ())), preferred_element_type=jnp.float32)


def weighted(v, p):
    return lax.dot_general(v, p.astype(jnp.bfloat16), (((0,), (0,)), ((), ())), preferred_element_type=jnp.float32)


def exponent_scale(head_dim):
    return math.log2(math.e) / math.sqrt(head_dim)


def pack_kernel(k_hbm, v_hbm, kv_ref, sems):
    k_copy = pltpu.make_async_copy(k_hbm, kv_ref.at[0:BLOCK, :], sems.at[0])
    v_copy = pltpu.make_async_copy(v_hbm, kv_ref.at[BLOCK:2 * BLOCK, :], sems.at[1])
    k_copy.start()
    v_copy.start()
    k_copy.wait()
    v_copy.wait()


def own_block_kernel(q_ref, kv_ref, m_ref, l_ref, acc_ref):
    scale = exponent_scale(q_ref.shape[1])
    s = scores_of(kv_ref[0:BLOCK, :], q_ref[...])
    key_at = lax.broadcasted_iota(jnp.int32, s.shape, 0)
    query_at = lax.broadcasted_iota(jnp.int32, s.shape, 1) & (BLOCK - 1)
    s = jnp.where(key_at <= query_at, s, -1e30)
    m = jnp.max(s, axis=0, keepdims=True)
    p = jnp.exp2((s - m) * scale)
    m_ref[...] = m
    l_ref[...] = jnp.sum(p, axis=0, keepdims=True)
    acc_ref[...] = weighted(kv_ref[BLOCK:, :], p)


def project(att, w_ref, block, width):
    start = pl.multiple_of(block * width, 128)
    return jnp.dot(att, w_ref[:, pl.ds(start, width)], preferred_element_type=jnp.float32)


def absorb(scale, q_ref, k, v, m_ref, l_ref, acc_ref):
    s = scores_of(k, q_ref[...])
    m_old = m_ref[...]
    m_new = jnp.maximum(m_old, jnp.max(s, axis=0, keepdims=True))
    p = jnp.exp2((s - m_new) * scale)
    factor = jnp.exp2((m_old - m_new) * scale)
    m_ref[...] = m_new
    l_ref[...] = l_ref[...] * factor + jnp.sum(p, axis=0, keepdims=True)
    acc_ref[...] = acc_ref[...] * factor + weighted(v, p)


def absorb_reached(xors, parents_ref, q_ref, kv_refs, state):
    scale = exponent_scale(q_ref.shape[1])
    me = lax.axis_index("ctx")
    wanted = parents_ref[me]
    reached = jnp.int32(0)
    for step in range(1, DIRECT_SIZE):
        block = me - step
        hit = (block >= 0) & (block == wanted)
        block = jnp.maximum(block, 0)
        reached = jnp.where(hit, reached | lax.shift_left(jnp.int32(1), block), reached)
        wanted = jnp.where(hit, parents_ref[block], wanted)
    for other, kv_ref in zip(xors, kv_refs):
        @pl.when((lax.shift_right_logical(reached, me ^ other) & 1) == 1)
        def _():
            absorb(scale, q_ref, kv_ref[0:BLOCK, :], kv_ref[BLOCK:, :], *state)


def absorb_walk(parents_ref, q_ref, piece, state):
    scale = exponent_scale(q_ref.shape[1])
    me = lax.axis_index("ctx")

    def visit(step, wanted):
        block = me - step
        hit = (block >= 0) & (block == wanted)
        block = jnp.maximum(block, 0)

        @pl.when(hit)
        def _():
            start = pl.multiple_of(block * 2 * BLOCK, 2 * BLOCK)
            absorb(scale, q_ref, piece[pl.ds(start, BLOCK), :], piece[pl.ds(start + BLOCK, BLOCK), :], *state)

        return jnp.where(hit, parents_ref[block], wanted)

    lax.fori_loop(1, parents_ref.shape[0], visit, parents_ref[me])


def first_others_kernel(xors, parents_ref, q_ref, m_in, l_in, acc_in, *refs):
    state = refs[len(xors):]
    absorb_reached(xors, parents_ref, q_ref, refs[:len(xors)], state)


def last_others_kernel(xors, parents_ref, q_ref, m_in, l_in, acc_in, *refs):
    kv_refs = refs[:max(len(xors), 1)]
    w_ref, att_ref, send_ref, keep_ref, *state = refs[len(kv_refs):]
    rows, head_dim = q_ref.shape
    group = rows // BLOCK
    width = keep_ref.shape[1]
    far = lax.axis_index("tp") ^ 2
    if xors:
        absorb_reached(xors, parents_ref, q_ref, kv_refs, state)
    else:
        absorb_walk(parents_ref, q_ref, kv_refs[0], state)
    m_ref, l_ref, acc_ref = state

    for head in range(group):
        at = slice(head * BLOCK, (head + 1) * BLOCK)
        part = acc_ref[:, at] / l_ref[:, at]
        att_ref[:, head * head_dim:(head + 1) * head_dim] = part.T.astype(jnp.bfloat16)

    att = att_ref[...]
    send_ref[...] = project(att, w_ref, far ^ 1, width).astype(jnp.bfloat16)
    keep_ref[...] = project(att, w_ref, far, width)


def near_kernel(att_ref, w_ref, send_ref, keep_ref):
    mine = lax.axis_index("tp")
    width = keep_ref.shape[1]
    att = att_ref[...]
    send_ref[...] = project(att, w_ref, mine ^ 1, width).astype(jnp.bfloat16)
    keep_ref[...] = project(att, w_ref, mine, width)


def shards(ctx_size, tp_size, query_heads, key_heads, value_heads, parents, out_weight):
    tok_rows, local_heads, head_dim = query_heads.shape
    assert tok_rows == BLOCK and key_heads.shape[1] == 1 and parents.shape[0] == ctx_size and tp_size == 4
    width = out_weight.shape[1] // tp_size
    rows = local_heads * tok_rows
    params = pltpu.CompilerParams(vmem_limit_bytes=VMEM_LIMIT)
    vmem = pl.BlockSpec(memory_space=pltpu.VMEM)
    hbm = pl.BlockSpec(memory_space=pltpu.HBM)
    smem = pl.BlockSpec(memory_space=pltpu.SMEM)

    def in_hbm(x):
        return pltpu.with_memory_space_constraint(x, pltpu.HBM)

    def swap(x, axis, size, other):
        return lax.ppermute(x, axis, [(i, i ^ other) for i in range(size)])

    kv = pl.pallas_call(
        pack_kernel,
        out_shape=jax.ShapeDtypeStruct((2 * tok_rows, head_dim), jnp.bfloat16),
        in_specs=[hbm, hbm],
        out_specs=vmem,
        scratch_shapes=[pltpu.SemaphoreType.DMA((2,))],
        compiler_params=params,
        cost_estimate=pl.CostEstimate(flops=8_000_000_000, bytes_accessed=130_000, transcendentals=0),
    )(in_hbm(key_heads[:, 0, :]), in_hbm(value_heads[:, 0, :]))
    if ctx_size == DIRECT_SIZE:
        columns = [swap(kv, "ctx", ctx_size, other) for other in (6, 4, 2)]
    q = jnp.transpose(query_heads, (1, 0, 2)).reshape(rows, head_dim)

    m, l, acc = pl.pallas_call(
        own_block_kernel,
        out_shape=(
            jax.ShapeDtypeStruct((1, rows), jnp.float32),
            jax.ShapeDtypeStruct((1, rows), jnp.float32),
            jax.ShapeDtypeStruct((head_dim, rows), jnp.float32),
        ),
        in_specs=[vmem, vmem],
        out_specs=(vmem, vmem, vmem),
        compiler_params=params,
        cost_estimate=pl.CostEstimate(flops=67_000_000, bytes_accessed=1_000_000, transcendentals=130_000),
    )(q, kv)

    state = (m, l, acc)
    state_shapes = tuple(jax.ShapeDtypeStruct(x.shape, x.dtype) for x in state)
    if ctx_size == DIRECT_SIZE:
        late, m = lax.optimization_barrier((kv, m))
        state = (m, l, acc)
        beside = swap(late, "ctx", ctx_size, 1)
        pieces = [swap(x, "ctx", ctx_size, 1) for x in columns]
        xors = (6, 4, 2, 1)
        state = pl.pallas_call(
            functools.partial(first_others_kernel, xors),
            out_shape=state_shapes,
            in_specs=[smem] + [vmem] * (4 + len(xors)),
            out_specs=(vmem,) * 3,
            input_output_aliases={2: 0, 3: 1, 4: 2},
            compiler_params=params,
            cost_estimate=pl.CostEstimate(flops=270_000_000, bytes_accessed=1_000_000, transcendentals=500_000),
        )(parents, q, *state, *columns, beside)
        xors = (7, 5, 3)
    else:
        xors = ()
        pieces = [lax.all_gather(kv, "ctx", axis=0, tiled=True)]

    att, send_far, keep_far, *_ = pl.pallas_call(
        functools.partial(last_others_kernel, xors),
        out_shape=(
            jax.ShapeDtypeStruct((tok_rows, local_heads * head_dim), jnp.bfloat16),
            jax.ShapeDtypeStruct((tok_rows, width), jnp.bfloat16),
            jax.ShapeDtypeStruct((tok_rows, width), jnp.float32),
        ) + state_shapes,
        in_specs=[smem] + [vmem] * (5 + len(pieces)),
        out_specs=(vmem,) * 6,
        input_output_aliases={2: 3, 3: 4, 4: 5},
        compiler_params=params,
        cost_estimate=pl.CostEstimate(flops=1_000_000_000, bytes_accessed=10_000_000, transcendentals=1_000_000),
    )(parents, q, *state, *pieces, out_weight)

    far_in = swap(send_far, "tp", tp_size, 1)
    send_near, keep_near = pl.pallas_call(
        near_kernel,
        out_shape=(
            jax.ShapeDtypeStruct((tok_rows, width), jnp.bfloat16),
            jax.ShapeDtypeStruct((tok_rows, width), jnp.float32),
        ),
        in_specs=[vmem, vmem],
        out_specs=(vmem, vmem),
        compiler_params=params,
        cost_estimate=pl.CostEstimate(flops=540_000_000, bytes_accessed=4_000_000, transcendentals=0),
    )(att, out_weight)
    near_in = swap(send_near, "tp", tp_size, 1)
    far_sum = (keep_far + far_in.astype(jnp.float32)).astype(jnp.bfloat16)
    from_far = swap(far_sum, "tp", tp_size, 2)
    return (keep_near + near_in.astype(jnp.float32) + from_far.astype(jnp.float32)).astype(jnp.bfloat16)


def solution(mesh):
    return jax.shard_map(
        functools.partial(shards, mesh.shape["ctx"], mesh.shape["tp"]),
        mesh=mesh,
        in_specs=(
            P("ctx", "tp", None),
            P("ctx", "tp", None),
            P("ctx", "tp", None),
            P(),
            P("tp", None),
        ),
        out_specs=P("ctx", "tp"),
        check_vma=False,
    )
```

time: 31.6 us -> 29.5 us (0.934)
  Pallas kernels: 5.55 us -> 4.15 us
  waiting for transfers between devices: 10 us -> 11.3 us
  local copies, waits for them, and re-layouts: 0.99 us -> 0.05 us
  other arithmetic: 1.67 us -> 0.86 us
    pallas_call x1, Pallas kernels: 3.39 us -> 0.51 us  [shards(): pl.pallas_call(own_block_kernel, out_shape=(jax.ShapeDtypeStruct((1, rows...]
    pallas_call x1 -> x3, Pallas kernels: 1.42 us -> 2.91 us  [the longest x1 1.37 us: shards(): pl.pallas_call(functools.partial(last_others_kernel, xors), out_shape=(ja...]
    ppermute x10, waiting for transfers between devices: 10 us -> 11.3 us  [swap(): return lax.ppermute(x, axis, [(i, i ^ other) for i in range(size)])]
    transpose x1, local copies, waits for them, and re-layouts: 0.99 us -> 0.04 us  [shards(): q = jnp.transpose(query_heads, (1, 0, 2)).reshape(rows, head_dim)]
    concatenate x1 -> x0, other arithmetic: 0.79 us -> none  [shards(): kv = jnp.concatenate([key_heads[:, 0, :], value_heads[:, 0, :]], axis=0)]
  transfers between devices with their start and end apart: 10 -> 10, of which waited for: 5 -> 5; matrix products, arithmetic and copies ran while one was open for 3% -> 0% of each run, Pallas kernels for 13% -> 6%
where the time goes in v3:
time: 29.5 us; the launch traced here: 29.4 us
  starting transfers between devices  12.9 us (44%)
  waiting for transfers between devices  11.3 us (38%)
  Pallas kernels  4.15 us (14%)
  other arithmetic  0.86 us (3%)
    ppermute x10, starting transfers between devices, swap(): return lax.ppermute(x, axis, [(i, i ^ other) for i in range(size)])  12.9 us
    ppermute x10, waiting for transfers between devices, swap(): return lax.ppermute(x, axis, [(i, i ^ other) for i in range(size)])  11.3 us
    pallas_call x1, Pallas kernels, shards(): pl.pallas_call(functools.partial(last_others_kernel, xors), out_shape=(ja...  1.37 us
    pallas_call x1, Pallas kernels, shards(): pl.pallas_call(pack_kernel, out_shape=jax.ShapeDtypeStruct((2 * tok_rows,...  0.94 us
    convert_element_type x1, other arithmetic, shards(): (keep_near + near_in.astype(jnp.float32) + from_far.astype(jnp.float32))....  0.81 us
    pallas_call x1, Pallas kernels, shards(): pl.pallas_call(near_kernel, out_shape=(jax.ShapeDtypeStruct((tok_rows, wi...  0.73 us
    pallas_call x1, Pallas kernels, shards(): pl.pallas_call(functools.partial(first_others_kernel, xors), out_shape=st...  0.6 us
  transfers between devices with their start and end apart: 10, of which 5 were waited for; matrix products, arithmetic and copies ran while one was open for 0% of the time, Pallas kernels for 6%

profile of v3, /device:TPU:0, one launch (start us, length us, event | category | flops | bytes accessed | tf_op | source)
XLA Modules:
  0.0 29.4 jit_solution(10105056124790720350)
XLA Ops:
  0.0 0.0 copy-start.2
  0.0 0.0 copy-start.1
  0.0 0.0 copy-start
  0.0 0.9 %shard_map.55.kv_ref = bf16[256,128]{1,0:T(8,128)(2,1)S(1)} custom-call(bf16[128,128]{1,0:T(8,128)(2,1)} %bitcast.8, bf16[128,128]{1,0:T(8,128)(2,1)} %bitcast.9), custom_call_target="tpu_custom_call" | custom-call | flops 8000000000 | bytes 130000 | tf_op jit(solution)/shard_map/pallas_call | solution.py:154
  1.0 3.1 %collective-permute-start.2 = (bf16[256,128]{1,0:T(8,128)(2,1)S(1)}, bf16[256,128]{1,0:T(8,128)(2,1)S(1)}, u32[]{:S(2)}, u32[]{:S(2)}) collective-permute-start(bf16[256,128]{1,0:T(8,128)(2,1)S(1)} %shard_map.55.kv_ref), channel_id=1, source_target_pairs={{0,8},{4,12},{8,0},{12,4},{16,24},{20,28},{24,16},{28,20},{1,9},{5... | collective-permute-start | bytes 196616 | tf_op jit(solution)/shard_map/ppermute | solution.py:152
  4.0 2.6 %collective-permute-start.1 = (bf16[256,128]{1,0:T(8,128)(2,1)S(1)}, bf16[256,128]{1,0:T(8,128)(2,1)S(1)}, u32[]{:S(2)}, u32[]{:S(2)}) collective-permute-start(bf16[256,128]{1,0:T(8,128)(2,1)S(1)} %shard_map.55.kv_ref), channel_id=1, source_target_pairs={{0,16},{4,20},{8,24},{12,28},{16,0},{20,4},{24,8},{28,12},{1,17},{... | collective-permute-start | bytes 196616 | tf_op jit(solution)/shard_map/ppermute | solution.py:152
  6.6 0.0 collective-permute-start
  6.6 0.0 copy-done.2
  6.7 0.5 %shard_map.56 = (f32[1,1024]{1,0:T(1,128)S(1)}, f32[1,1024]{1,0:T(1,128)S(1)}, f32[128,1024]{1,0:T(8,128)S(1)}) custom-call(bf16[1024,128]{1,0:T(8,128)(2,1)S(1)} %bitcast.4, bf16[256,128]{1,0:T(8,128)(2,1)S(1)} %shard_map.55.kv_ref), custom_call_target="tpu_custom_call" | custom-call | flops 67000000 | bytes 1000000 | tf_op jit(solution)/shard_map/pallas_call | solution.py:167
  7.2 1.8 %collective-permute-start.3 = (bf16[256,128]{1,0:T(8,128)(2,1)S(1)}, bf16[256,128]{1,0:T(8,128)(2,1)S(1)}, u32[]{:S(2)}, u32[]{:S(2)}) collective-permute-start(bf16[256,128]{1,0:T(8,128)(2,1)S(1)} %shard_map.55.kv_ref), channel_id=1, source_target_pairs={{0,4},{4,0},{8,12},{12,8},{16,20},{20,16},{24,28},{28,24},{1,5},{5... | collective-permute-start | bytes 196616 | tf_op jit(solution)/shard_map/ppermute | solution.py:152
  9.0 0.0 collective-permute-done.2.refs_2_
  9.0 0.3 collective-permute-start.6
  9.3 2.0 %collective-permute-done.1.refs_1_ = bf16[256,128]{1,0:T(8,128)(2,1)S(1)} collective-permute-done((bf16[256,128]{1,0:T(8,128)(2,1)S(1)}, bf16[256,128]{1,0:T(8,128)(2,1)S(1)}, u32[]{:S(2)}, u32[]{:S(2)}) %collective-permute-start.1) | collective-permute-done | bytes 65568 | tf_op jit(solution)/shard_map/ppermute | solution.py:152
  11.3 1.5 %collective-permute-start.5 = (bf16[256,128]{1,0:T(8,128)(2,1)S(1)}, bf16[256,128]{1,0:T(8,128)(2,1)S(1)}, u32[]{:S(2)}, u32[]{:S(2)}) collective-permute-start(bf16[256,128]{1,0:T(8,128)(2,1)S(1)} %collective-permute-done.1.refs_1_), channel_id=1, source_target_pairs={{0,4},{4,0},{8,12},{12,8},{16,20},{20,16},{24,28},{28,24},{1,5},{5... | collective-permute-start | bytes 196616 | tf_op jit(solution)/shard_map/ppermute | solution.py:152
  12.8 0.0 collective-permute-done.refs_0_
  12.8 1.4 %collective-permute-start.4 = (bf16[256,128]{1,0:T(8,128)(2,1)S(1)}, bf16[256,128]{1,0:T(8,128)(2,1)S(1)}, u32[]{:S(2)}, u32[]{:S(2)}) collective-permute-start(bf16[256,128]{1,0:T(8,128)(2,1)S(1)} %collective-permute-done.refs_0_), channel_id=1, source_target_pairs={{0,4},{4,0},{8,12},{12,8},{16,20},{20,16},{24,28},{28,24},{1,5},{5... | collective-permute-start | bytes 196616 | tf_op jit(solution)/shard_map/ppermute | solution.py:152
  14.2 0.0 collective-permute-done.3.refs_3_
  14.2 0.0 copy-done.1
  14.2 0.6 %shard_map.57 = (f32[1,1024]{1,0:T(1,128)S(1)}, f32[1,1024]{1,0:T(1,128)S(1)}, f32[128,1024]{1,0:T(8,128)S(1)}) custom-call(s32[8]{0:T(128)S(1)} %copy-done.1, bf16[1024,128]{1,0:T(8,128)(2,1)S(1)} %bitcast.5, f32[1,1024]{1,0:T(1,128)S(1)} %get-tuple-element.19.m_in, ...), custom_call_target="tpu_custom_call", output_to_operand_aliasing={{0}: (2, {}), {1}: (3, {}), {2}: (4, {})} | custom-call | flops 270000000 | bytes 1000000 | tf_op jit(solution)/shard_map/pallas_call | solution.py:188
  14.8 0.0 collective-permute-done.6.refs_2_
  14.9 0.7 %collective-permute-done.5.refs_1_ = bf16[256,128]{1,0:T(8,128)(2,1)S(1)} collective-permute-done((bf16[256,128]{1,0:T(8,128)(2,1)S(1)}, bf16[256,128]{1,0:T(8,128)(2,1)S(1)}, u32[]{:S(2)}, u32[]{:S(2)}) %collective-permute-start.5) | collective-permute-done | bytes 65568 | tf_op jit(solution)/shard_map/ppermute | solution.py:152
  15.6 1.5 %collective-permute-done.4.refs_0_ = bf16[256,128]{1,0:T(8,128)(2,1)S(1)} collective-permute-done((bf16[256,128]{1,0:T(8,128)(2,1)S(1)}, bf16[256,128]{1,0:T(8,128)(2,1)S(1)}, u32[]{:S(2)}, u32[]{:S(2)}) %collective-permute-start.4) | collective-permute-done | bytes 65568 | tf_op jit(solution)/shard_map/ppermute | solution.py:152
  17.1 0.0 copy-done
  17.1 1.4 %shard_map.58 = (bf16[128,1024]{1,0:T(8,128)(2,1)S(1)}, bf16[128,1024]{1,0:T(8,128)(2,1)S(1)}, f32[128,1024]{1,0:T(8,128)S(1)}, f32[1,1024]{1,0:T(1,128)S(1)}, f...) custom-call(s32[8]{0:T(128)S(1)} %copy-done.1, ...), custom_call_target="tpu_custom_call", output_to_operand_aliasing={{3}: (2, {}), {4}: (3, {}), {5}: (4, {})} | custom-call | flops 1000000000 | bytes 10000000 | tf_op jit(solution)/shard_map/pallas_call | solution.py:202
  18.5 0.1 collective-permute-start.8
  18.6 0.7 %shard_map.59 = (bf16[128,1024]{1,0:T(8,128)(2,1)S(1)}, f32[128,1024]{1,0:T(8,128)S(1)}) custom-call(bf16[128,1024]{1,0:T(8,128)(2,1)S(1)} %get-tuple-element.26.att_ref, bf16[1024,4096]{1,0:T(8,128)(2,1)S(1)} %copy-done), custom_call_target="tpu_custom_call" | custom-call | flops 540000000 | bytes 4000000 | tf_op jit(solution)/shard_map/pallas_call | solution.py:217
  19.3 0.6 %collective-permute-start.7 = (bf16[128,1024]{1,0:T(8,128)(2,1)S(1)}, bf16[128,1024]{1,0:T(8,128)(2,1)S(1)}, u32[]{:S(2)}, u32[]{:S(2)}) collective-permute-start(bf16[128,1024]{1,0:T(8,128)(2,1)S(1)} %get-tuple-element.28), channel_id=1, source_target_pairs={{0,1},{1,0},{2,3},{3,2},{4,5},{5,4},{6,7},{7,6},{8,9},{9,8},{10,11... | collective-permute-start | bytes 786440 | tf_op jit(solution)/shard_map/ppermute | solution.py:152
  19.9 0.2 collective-permute-done.8
  20.1 0.1 add_convert_fusion.1
  20.1 1.6 %collective-permute-start.9 = (bf16[128,1024]{1,0:T(8,128)(2,1)S(1)}, bf16[128,1024]{1,0:T(8,128)(2,1)S(1)}, u32[]{:S(2)}, u32[]{:S(2)}) collective-permute-start(bf16[128,1024]{1,0:T(8,128)(2,1)S(1)} %add_convert_fusion.1), channel_id=1, source_target_pairs={{0,2},{1,3},{2,0},{3,1},{4,6},{5,7},{6,4},{7,5},{8,10},{9,11},{10,... | collective-permute-start | bytes 786440 | tf_op jit(solution)/shard_map/ppermute | solution.py:152
  21.7 0.0 collective-permute-done.7
  21.7 6.8 %collective-permute-done.9 = bf16[128,1024]{1,0:T(8,128)(2,1)S(1)} collective-permute-done((bf16[128,1024]{1,0:T(8,128)(2,1)S(1)}, bf16[128,1024]{1,0:T(8,128)(2,1)S(1)}, u32[]{:S(2)}, u32[]{:S(2)}) %collective-permute-start.9) | collective-permute-done | bytes 262176 | tf_op jit(solution)/shard_map/ppermute | solution.py:152
  28.6 0.8 %add_convert_fusion = bf16[128,1024]{1,0:T(8,128)(2,1)} fusion(bf16[128,1024]{1,0:T(8,128)(2,1)S(1)} %collective-permute-done.9, f32[128,1024]{1,0:T(8,128)S(1)} %get-tuple-element.27, bf16[128,1024]{1,0:T(8,128)(2,1)S(1)} %collective-permute-done.7), kind=kLoop, calls=%fused_computation | loop fusion | flops 655360 | bytes 1310720 | tf_op jit(solution)/shard_map/convert_element_type | solution.py:231
  (1 shorter events, 0.0 us)
Async XLA Ops:
  0.0 6.6 %copy-start.2 = (bf16[128,8,128]{2,1,0:T(8,128)(2,1)S(1)}, bf16[128,8,128]{2,1,0:T(8,128)(2,1)}, u32[]{:S(2)}) copy-start(bf16[128,8,128]{2,1,0:T(8,128)(2,1)} %param.5) | copy-start | bytes 786436
  0.0 14.2 %copy-start.1 = (s32[8]{0:T(128)S(1)}, s32[8]{0:T(128)}, u32[]{:S(2)}) copy-start(s32[8]{0:T(128)} %parents_ref.3) | copy-start | bytes 100
  0.0 17.1 %copy-start = (bf16[1024,4096]{1,0:T(8,128)(2,1)S(1)}, bf16[1024,4096]{1,0:T(8,128)(2,1)}, u32[]{:S(2)}) copy-start(bf16[1024,4096]{1,0:T(8,128)(2,1)} %w_ref.1) | copy-start | bytes 25165828
  1.0 8.1 %collective-permute-start.2 = (bf16[256,128]{1,0:T(8,128)(2,1)S(1)}, bf16[256,128]{1,0:T(8,128)(2,1)S(1)}, u32[]{:S(2)}, u32[]{:S(2)}) collective-permute-start(bf16[256,128]{1,0:T(8,128)(2,1)S(1)} %shard_map.55.kv_ref), channel_id=1, source_target_pairs={{0,8},{4,12},{8,0},{12,4},{16,24},{20,28},{24,16},{28,20},{1,9},{5... | collective-permute-start | bytes 196616 | tf_op jit(solution)/shard_map/ppermute | solution.py:152
  4.0 7.3 %collective-permute-start.1 = (bf16[256,128]{1,0:T(8,128)(2,1)S(1)}, bf16[256,128]{1,0:T(8,128)(2,1)S(1)}, u32[]{:S(2)}, u32[]{:S(2)}) collective-permute-start(bf16[256,128]{1,0:T(8,128)(2,1)S(1)} %shard_map.55.kv_ref), channel_id=1, source_target_pairs={{0,16},{4,20},{8,24},{12,28},{16,0},{20,4},{24,8},{28,12},{1,17},{... | collective-permute-start | bytes 196616 | tf_op jit(solution)/shard_map/ppermute | solution.py:152
  6.6 6.2 %collective-permute-start = (bf16[256,128]{1,0:T(8,128)(2,1)S(1)}, bf16[256,128]{1,0:T(8,128)(2,1)S(1)}, u32[]{:S(2)}, u32[]{:S(2)}) collective-permute-start(bf16[256,128]{1,0:T(8,128)(2,1)S(1)} %shard_map.55.kv_ref), channel_id=1, source_target_pairs={{0,24},{4,28},{8,16},{12,20},{16,8},{20,12},{24,0},{28,4},{1,25},{... | collective-permute-start | bytes 196616 | tf_op jit(solution)/shard_map/ppermute | solution.py:152
  7.2 7.0 %collective-permute-start.3 = (bf16[256,128]{1,0:T(8,128)(2,1)S(1)}, bf16[256,128]{1,0:T(8,128)(2,1)S(1)}, u32[]{:S(2)}, u32[]{:S(2)}) collective-permute-start(bf16[256,128]{1,0:T(8,128)(2,1)S(1)} %shard_map.55.kv_ref), channel_id=1, source_target_pairs={{0,4},{4,0},{8,12},{12,8},{16,20},{20,16},{24,28},{28,24},{1,5},{5... | collective-permute-start | bytes 196616 | tf_op jit(solution)/shard_map/ppermute | solution.py:152
  9.0 5.8 %collective-permute-start.6 = (bf16[256,128]{1,0:T(8,128)(2,1)S(1)}, bf16[256,128]{1,0:T(8,128)(2,1)S(1)}, u32[]{:S(2)}, u32[]{:S(2)}) collective-permute-start(bf16[256,128]{1,0:T(8,128)(2,1)S(1)} %collective-permute-done.2.refs_2_), channel_id=1, source_target_pairs={{0,4},{4,0},{8,12},{12,8},{16,20},{20,16},{24,28},{28,24},{1,5},{5... | collective-permute-start | bytes 196616 | tf_op jit(solution)/shard_map/ppermute | solution.py:152
  11.3 4.3 %collective-permute-start.5 = (bf16[256,128]{1,0:T(8,128)(2,1)S(1)}, bf16[256,128]{1,0:T(8,128)(2,1)S(1)}, u32[]{:S(2)}, u32[]{:S(2)}) collective-permute-start(bf16[256,128]{1,0:T(8,128)(2,1)S(1)} %collective-permute-done.1.refs_1_), channel_id=1, source_target_pairs={{0,4},{4,0},{8,12},{12,8},{16,20},{20,16},{24,28},{28,24},{1,5},{5... | collective-permute-start | bytes 196616 | tf_op jit(solution)/shard_map/ppermute | solution.py:152
  12.8 4.3 %collective-permute-start.4 = (bf16[256,128]{1,0:T(8,128)(2,1)S(1)}, bf16[256,128]{1,0:T(8,128)(2,1)S(1)}, u32[]{:S(2)}, u32[]{:S(2)}) collective-permute-start(bf16[256,128]{1,0:T(8,128)(2,1)S(1)} %collective-permute-done.refs_0_), channel_id=1, source_target_pairs={{0,4},{4,0},{8,12},{12,8},{16,20},{20,16},{24,28},{28,24},{1,5},{5... | collective-permute-start | bytes 196616 | tf_op jit(solution)/shard_map/ppermute | solution.py:152
  18.5 1.6 %collective-permute-start.8 = (bf16[128,1024]{1,0:T(8,128)(2,1)S(1)}, bf16[128,1024]{1,0:T(8,128)(2,1)S(1)}, u32[]{:S(2)}, u32[]{:S(2)}) collective-permute-start(bf16[128,1024]{1,0:T(8,128)(2,1)S(1)} %get-tuple-element.30), channel_id=1, source_target_pairs={{0,1},{1,0},{2,3},{3,2},{4,5},{5,4},{6,7},{7,6},{8,9},{9,8},{10,11... | collective-permute-start | bytes 786440 | tf_op jit(solution)/shard_map/ppermute | solution.py:152
  19.3 2.4 %collective-permute-start.7 = (bf16[128,1024]{1,0:T(8,128)(2,1)S(1)}, bf16[128,1024]{1,0:T(8,128)(2,1)S(1)}, u32[]{:S(2)}, u32[]{:S(2)}) collective-permute-start(bf16[128,1024]{1,0:T(8,128)(2,1)S(1)} %get-tuple-element.28), channel_id=1, source_target_pairs={{0,1},{1,0},{2,3},{3,2},{4,5},{5,4},{6,7},{7,6},{8,9},{9,8},{10,11... | collective-permute-start | bytes 786440 | tf_op jit(solution)/shard_map/ppermute | solution.py:152
  20.1 8.4 %collective-permute-start.9 = (bf16[128,1024]{1,0:T(8,128)(2,1)S(1)}, bf16[128,1024]{1,0:T(8,128)(2,1)S(1)}, u32[]{:S(2)}, u32[]{:S(2)}) collective-permute-start(bf16[128,1024]{1,0:T(8,128)(2,1)S(1)} %add_convert_fusion.1), channel_id=1, source_target_pairs={{0,2},{1,3},{2,0},{3,1},{4,6},{5,7},{6,4},{7,5},{8,10},{9,11},{10,... | collective-permute-start | bytes 786440 | tf_op jit(solution)/shard_map/ppermute | solution.py:152

commit v4 on v3

--- a/solution.py
+++ b/solution.py
@@ -99,12 +99,12 @@
     lax.fori_loop(1, parents_ref.shape[0], visit, parents_ref[me])
 
 
-def first_others_kernel(xors, parents_ref, q_ref, m_in, l_in, acc_in, *refs):
+def others_kernel(xors, parents_ref, q_ref, m_in, l_in, acc_in, *refs):
     state = refs[len(xors):]
     absorb_reached(xors, parents_ref, q_ref, refs[:len(xors)], state)
 
 
-def last_others_kernel(xors, parents_ref, q_ref, m_in, l_in, acc_in, *refs):
+def last_kernel(xors, parents_ref, q_ref, m_in, l_in, acc_in, *refs):
     kv_refs = refs[:max(len(xors), 1)]
     w_ref, att_ref, send_ref, keep_ref, *state = refs[len(kv_refs):]
     rows, head_dim = q_ref.shape
@@ -161,7 +161,7 @@
         cost_estimate=pl.CostEstimate(flops=8_000_000_000, bytes_accessed=130_000, transcendentals=0),
     )(in_hbm(key_heads[:, 0, :]), in_hbm(value_heads[:, 0, :]))
     if ctx_size == DIRECT_SIZE:
-        columns = [swap(kv, "ctx", ctx_size, other) for other in (6, 4, 2)]
+        columns = [swap(kv, "ctx", ctx_size, other) for other in (4, 2, 6)]
     q = jnp.transpose(query_heads, (1, 0, 2)).reshape(rows, head_dim)
 
     m, l, acc = pl.pallas_call(
@@ -183,24 +183,28 @@
         late, m = lax.optimization_barrier((kv, m))
         state = (m, l, acc)
         beside = swap(late, "ctx", ctx_size, 1)
-        pieces = [swap(x, "ctx", ctx_size, 1) for x in columns]
-        xors = (6, 4, 2, 1)
-        state = pl.pallas_call(
-            functools.partial(first_others_kernel, xors),
-            out_shape=state_shapes,
-            in_specs=[smem] + [vmem] * (4 + len(xors)),
-            out_specs=(vmem,) * 3,
-            input_output_aliases={2: 0, 3: 1, 4: 2},
-            compiler_params=params,
-            cost_estimate=pl.CostEstimate(flops=270_000_000, bytes_accessed=1_000_000, transcendentals=500_000),
-        )(parents, q, *state, *columns, beside)
-        xors = (7, 5, 3)
+        pairs = [swap(x, "ctx", ctx_size, 1) for x in columns]
+
+        def absorbed(state, xors, arrived):
+            return pl.pallas_call(
+                functools.partial(others_kernel, xors),
+                out_shape=state_shapes,
+                in_specs=[smem] + [vmem] * (4 + len(xors)),
+                out_specs=(vmem,) * 3,
+                input_output_aliases={2: 0, 3: 1, 4: 2},
+                compiler_params=params,
+                cost_estimate=pl.CostEstimate(flops=270_000_000, bytes_accessed=1_000_000, transcendentals=500_000),
+            )(parents, q, *state, *arrived)
+
+        state = absorbed(state, (4, 2, 6, 1), [*columns, beside])
+        state = absorbed(state, (3, 7), pairs[1:])
+        xors, pieces = (5,), pairs[:1]
     else:
         xors = ()
         pieces = [lax.all_gather(kv, "ctx", axis=0, tiled=True)]
 
     att, send_far, keep_far, *_ = pl.pallas_call(
-        functools.partial(last_others_kernel, xors),
+        functools.partial(last_kernel, xors),
         out_shape=(
             jax.ShapeDtypeStruct((tok_rows, local_heads * head_dim), jnp.bfloat16),
             jax.ShapeDtypeStruct((tok_rows, width), jnp.bfloat16),
@@ -225,9 +229,10 @@
         compiler_params=params,
         cost_estimate=pl.CostEstimate(flops=540_000_000, bytes_accessed=4_000_000, transcendentals=0),
     )(att, out_weight)
-    near_in = swap(send_near, "tp", tp_size, 1)
     far_sum = (keep_far + far_in.astype(jnp.float32)).astype(jnp.bfloat16)
     from_far = swap(far_sum, "tp", tp_size, 2)
+    send_near, _ = lax.optimization_barrier((send_near, far_sum))
+    near_in = swap(send_near, "tp", tp_size, 1)
     return (keep_near + near_in.astype(jnp.float32) + from_far.astype(jnp.float32)).astype(jnp.bfloat16)
 
 

time: 29.5 us -> 29.1 us (0.986)
  waiting for transfers between devices: 11.3 us -> 10.1 us
  Pallas kernels: 4.15 us -> 4.72 us
    ppermute x10, waiting for transfers between devices: 11.3 us -> 10.1 us  [swap(): return lax.ppermute(x, axis, [(i, i ^ other) for i in range(size)])]
    pallas_call x2 -> x3, Pallas kernels: 1.97 us -> 2.54 us  [the longest x1 1.35 us: shards(): pl.pallas_call(functools.partial(last_kernel, xors), out_shape=(jax.Shape...]
  transfers between devices with their start and end apart: 10 -> 10, of which waited for: 5 -> 5; matrix products, arithmetic and copies ran while one was open for 0% -> 0% of each run, Pallas kernels for 6% -> 8%
where the time goes in v4:
time: 29.1 us; the launch traced here: 28.9 us
  starting transfers between devices  13.1 us (45%)
  waiting for transfers between devices  10.1 us (35%)
  Pallas kernels  4.72 us (16%)
  other arithmetic  0.87 us (3%)
    ppermute x10, starting transfers between devices, swap(): return lax.ppermute(x, axis, [(i, i ^ other) for i in range(size)])  13.1 us
    ppermute x10, waiting for transfers between devices, swap(): return lax.ppermute(x, axis, [(i, i ^ other) for i in range(size)])  10.1 us
    pallas_call x1, Pallas kernels, shards(): pl.pallas_call(functools.partial(last_kernel, xors), out_shape=(jax.Shape...  1.35 us
    pallas_call x2, Pallas kernels, absorbed(): pl.pallas_call(functools.partial(others_kernel, xors), out_shape=state_sh...  1.18 us
    pallas_call x1, Pallas kernels, shards(): pl.pallas_call(pack_kernel, out_shape=jax.ShapeDtypeStruct((2 * tok_rows,...  0.94 us
    convert_element_type x1, other arithmetic, shards(): (keep_near + near_in.astype(jnp.float32) + from_far.astype(jnp.float32))....  0.81 us
    pallas_call x1, Pallas kernels, shards(): pl.pallas_call(near_kernel, out_shape=(jax.ShapeDtypeStruct((tok_rows, wi...  0.73 us
  transfers between devices with their start and end apart: 10, of which 5 were waited for; matrix products, arithmetic and copies ran while one was open for 0% of the time, Pallas kernels for 8%

profile of v4, /device:TPU:0, one launch (start us, length us, event | category | flops | bytes accessed | tf_op | source)
XLA Modules:
  0.0 28.9 jit_solution(10518654510711179376)
XLA Ops:
  0.0 0.0 slice-start
  0.0 0.0 copy-start.1
  0.0 0.0 copy-start
  0.0 0.0 slice-start.1
  0.0 0.9 %shard_map.55.kv_ref = bf16[256,128]{1,0:T(8,128)(2,1)S(1)} custom-call(bf16[128,128]{1,0:T(8,128)(2,1)} %bitcast.11, bf16[128,128]{1,0:T(8,128)(2,1)} %bitcast.12), custom_call_target="tpu_custom_call" | custom-call | flops 8000000000 | bytes 130000 | tf_op jit(solution)/shard_map/pallas_call | solution.py:154
  1.0 5.1 %collective-permute-start.2 = (bf16[256,128]{1,0:T(8,128)(2,1)S(1)}, bf16[256,128]{1,0:T(8,128)(2,1)S(1)}, u32[]{:S(2)}, u32[]{:S(2)}) collective-permute-start(bf16[256,128]{1,0:T(8,128)(2,1)S(1)} %shard_map.55.kv_ref), channel_id=1, source_target_pairs={{0,24},{4,28},{8,16},{12,20},{16,8},{20,12},{24,0},{28,4},{1,25},{... | collective-permute-start | bytes 196616 | tf_op jit(solution)/shard_map/ppermute | solution.py:152
  6.1 0.0 collective-permute-start.1
  6.1 0.6 %collective-permute-start = (bf16[256,128]{1,0:T(8,128)(2,1)S(1)}, bf16[256,128]{1,0:T(8,128)(2,1)S(1)}, u32[]{:S(2)}, u32[]{:S(2)}) collective-permute-start(bf16[256,128]{1,0:T(8,128)(2,1)S(1)} %shard_map.55.kv_ref), channel_id=1, source_target_pairs={{0,16},{4,20},{8,24},{12,28},{16,0},{20,4},{24,8},{28,12},{1,17},{... | collective-permute-start | bytes 196616 | tf_op jit(solution)/shard_map/ppermute | solution.py:152
  6.7 0.0 copy-done.1
  6.8 0.5 %shard_map.56 = (f32[1,1024]{1,0:T(1,128)S(1)}, f32[1,1024]{1,0:T(1,128)S(1)}, f32[128,1024]{1,0:T(8,128)S(1)}) custom-call(bf16[1024,128]{1,0:T(8,128)(2,1)S(1)} %bitcast.6, bf16[256,128]{1,0:T(8,128)(2,1)S(1)} %shard_map.55.kv_ref), custom_call_target="tpu_custom_call" | custom-call | flops 67000000 | bytes 1000000 | tf_op jit(solution)/shard_map/pallas_call | solution.py:167
  7.3 1.7 %collective-permute-start.3 = (bf16[256,128]{1,0:T(8,128)(2,1)S(1)}, bf16[256,128]{1,0:T(8,128)(2,1)S(1)}, u32[]{:S(2)}, u32[]{:S(2)}) collective-permute-start(bf16[256,128]{1,0:T(8,128)(2,1)S(1)} %shard_map.55.kv_ref), channel_id=1, source_target_pairs={{0,4},{4,0},{8,12},{12,8},{16,20},{20,16},{24,28},{28,24},{1,5},{5... | collective-permute-start | bytes 196616 | tf_op jit(solution)/shard_map/ppermute | solution.py:152
  9.0 0.0 collective-permute-done.2.refs_2_
  9.0 1.5 %collective-permute-start.5 = (bf16[256,128]{1,0:T(8,128)(2,1)S(1)}, bf16[256,128]{1,0:T(8,128)(2,1)S(1)}, u32[]{:S(2)}, u32[]{:S(2)}) collective-permute-start(bf16[256,128]{1,0:T(8,128)(2,1)S(1)} %collective-permute-done.2.refs_2_), channel_id=1, source_target_pairs={{0,4},{4,0},{8,12},{12,8},{16,20},{20,16},{24,28},{28,24},{1,5},{5... | collective-permute-start | bytes 196616 | tf_op jit(solution)/shard_map/ppermute | solution.py:152
  10.5 0.2 collective-permute-done.1.refs_1_
  10.7 1.7 %collective-permute-start.4 = (bf16[256,128]{1,0:T(8,128)(2,1)S(1)}, bf16[256,128]{1,0:T(8,128)(2,1)S(1)}, u32[]{:S(2)}, u32[]{:S(2)}) collective-permute-start(bf16[256,128]{1,0:T(8,128)(2,1)S(1)} %collective-permute-done.1.refs_1_), channel_id=1, source_target_pairs={{0,4},{4,0},{8,12},{12,8},{16,20},{20,16},{24,28},{28,24},{1,5},{5... | collective-permute-start | bytes 196616 | tf_op jit(solution)/shard_map/ppermute | solution.py:152
  12.4 0.0 collective-permute-done.refs_0_
  12.4 0.8 %collective-permute-start.6 = (bf16[256,128]{1,0:T(8,128)(2,1)S(1)}, bf16[256,128]{1,0:T(8,128)(2,1)S(1)}, u32[]{:S(2)}, u32[]{:S(2)}) collective-permute-start(bf16[256,128]{1,0:T(8,128)(2,1)S(1)} %collective-permute-done.refs_0_), channel_id=1, source_target_pairs={{0,4},{4,0},{8,12},{12,8},{16,20},{20,16},{24,28},{28,24},{1,5},{5... | collective-permute-start | bytes 196616 | tf_op jit(solution)/shard_map/ppermute | solution.py:152
  13.2 0.0 collective-permute-done.3.refs_3_
  13.2 0.0 copy-done
  13.2 0.6 %shard_map.57 = (f32[1,1024]{1,0:T(1,128)S(1)}, f32[1,1024]{1,0:T(1,128)S(1)}, f32[128,1024]{1,0:T(8,128)S(1)}) custom-call(s32[8]{0:T(128)S(1)} %copy-done, bf16[1024,128]{1,0:T(8,128)(2,1)S(1)} %bitcast.7, f32[1,1024]{1,0:T(1,128)S(1)} %get-tuple-element.23.m_in, ...), custom_call_target="tpu_custom_call", output_to_operand_aliasing={{0}: (2, {}), {1}: (3, {}), {2}: (4, {})} | custom-call | flops 270000000 | bytes 1000000 | tf_op jit(solution)/shard_map/pallas_call | solution.py:189
  13.9 0.0 collective-permute-done.5.refs_1_
  13.9 1.8 %collective-permute-done.4.refs_0_ = bf16[256,128]{1,0:T(8,128)(2,1)S(1)} collective-permute-done((bf16[256,128]{1,0:T(8,128)(2,1)S(1)}, bf16[256,128]{1,0:T(8,128)(2,1)S(1)}, u32[]{:S(2)}, u32[]{:S(2)}) %collective-permute-start.4) | collective-permute-done | bytes 65568 | tf_op jit(solution)/shard_map/ppermute | solution.py:152
  15.7 0.6 %shard_map.58 = (f32[1,1024]{1,0:T(1,128)S(1)}, f32[1,1024]{1,0:T(1,128)S(1)}, f32[128,1024]{1,0:T(8,128)S(1)}) custom-call(s32[8]{0:T(128)S(1)} %copy-done, bf16[1024,128]{1,0:T(8,128)(2,1)S(1)} %bitcast.8, f32[1,1024]{1,0:T(1,128)S(1)} %get-tuple-element.27.m_in, ...), custom_call_target="tpu_custom_call", output_to_operand_aliasing={{0}: (2, {}), {1}: (3, {}), {2}: (4, {})} | custom-call | flops 270000000 | bytes 1000000 | tf_op jit(solution)/shard_map/pallas_call | solution.py:189
  16.3 0.4 %collective-permute-done.6.refs_0_ = bf16[256,128]{1,0:T(8,128)(2,1)S(1)} collective-permute-done((bf16[256,128]{1,0:T(8,128)(2,1)S(1)}, bf16[256,128]{1,0:T(8,128)(2,1)S(1)}, u32[]{:S(2)}, u32[]{:S(2)}) %collective-permute-start.6) | collective-permute-done | bytes 65568 | tf_op jit(solution)/shard_map/ppermute | solution.py:152
  16.7 0.0 slice-done
  16.7 0.0 slice-done.1
  16.7 1.4 %shard_map.59 = (bf16[128,1024]{1,0:T(8,128)(2,1)S(1)}, bf16[128,1024]{1,0:T(8,128)(2,1)S(1)}, f32[128,1024]{1,0:T(8,128)S(1)}, f32[1,1024]{1,0:T(1,128)S(1)}, f...) custom-call(s32[8]{0:T(128)S(1)} %copy-done, ...), custom_call_target="tpu_custom_call", output_to_operand_aliasing={{3}: (2, {}), {4}: (3, {}), {5}: (4, {})} | custom-call | flops 1000000000 | bytes 10000000 | tf_op jit(solution)/shard_map/pallas_call | solution.py:206
  18.0 0.1 collective-permute-start.7
  18.1 0.7 %shard_map.60 = (bf16[128,1024]{1,0:T(8,128)(2,1)S(1)}, f32[128,1024]{1,0:T(8,128)S(1)}) custom-call(bf16[128,1024]{1,0:T(8,128)(2,1)S(1)} %get-tuple-element.33.att_ref, bf16[1024,4096]{1,0:T(8,128)(2,1)S(1)} %bitcast.5), custom_call_target="tpu_custom_call" | custom-call | flops 540000000 | bytes 4000000 | tf_op jit(solution)/shard_map/pallas_call | solution.py:221
  18.9 0.8 %collective-permute-done.7 = bf16[128,1024]{1,0:T(8,128)(2,1)S(1)} collective-permute-done((bf16[128,1024]{1,0:T(8,128)(2,1)S(1)}, bf16[128,1024]{1,0:T(8,128)(2,1)S(1)}, u32[]{:S(2)}, u32[]{:S(2)}) %collective-permute-start.7) | collective-permute-done | bytes 262176 | tf_op jit(solution)/shard_map/ppermute | solution.py:152
  19.6 0.1 add_convert_fusion.1
  19.7 1.6 %collective-permute-start.9 = (bf16[128,1024]{1,0:T(8,128)(2,1)S(1)}, bf16[128,1024]{1,0:T(8,128)(2,1)S(1)}, u32[]{:S(2)}, u32[]{:S(2)}) collective-permute-start(bf16[128,1024]{1,0:T(8,128)(2,1)S(1)} %add_convert_fusion.1), channel_id=1, source_target_pairs={{0,2},{1,3},{2,0},{3,1},{4,6},{5,7},{6,4},{7,5},{8,10},{9,11},{10,... | collective-permute-start | bytes 786440 | tf_op jit(solution)/shard_map/ppermute | solution.py:152
  21.3 0.0 collective-permute-start.8
  21.3 6.8 %collective-permute-done.9 = bf16[128,1024]{1,0:T(8,128)(2,1)S(1)} collective-permute-done((bf16[128,1024]{1,0:T(8,128)(2,1)S(1)}, bf16[128,1024]{1,0:T(8,128)(2,1)S(1)}, u32[]{:S(2)}, u32[]{:S(2)}) %collective-permute-start.9) | collective-permute-done | bytes 262176 | tf_op jit(solution)/shard_map/ppermute | solution.py:152
  28.1 0.0 collective-permute-done.8
  28.1 0.8 %add_convert_fusion = bf16[128,1024]{1,0:T(8,128)(2,1)} fusion(bf16[128,1024]{1,0:T(8,128)(2,1)S(1)} %collective-permute-done.9, f32[128,1024]{1,0:T(8,128)S(1)} %get-tuple-element.34, bf16[128,1024]{1,0:T(8,128)(2,1)S(1)} %collective-permute-done.8), kind=kLoop, calls=%fused_computation | loop fusion | flops 655360 | bytes 1310720 | tf_op jit(solution)/shard_map/convert_element_type | solution.py:236
  (2 shorter events, 0.0 us)
Async XLA Ops:
  0.0 16.7 %slice-start = ((s8[8388608]{0:T(1024)(128)(4,1)}), s8[4194304]{0:T(1024)(128)(4,1)S(1)}, s32[]{:S(2)}) async-start(s8[8388608]{0:T(1024)(128)(4,1)} %bitcast.4), calls=%async_computation | async-start | bytes 8388608
  0.0 6.7 %copy-start.1 = (bf16[128,8,128]{2,1,0:T(8,128)(2,1)S(1)}, bf16[128,8,128]{2,1,0:T(8,128)(2,1)}, u32[]{:S(2)}) copy-start(bf16[128,8,128]{2,1,0:T(8,128)(2,1)} %param.5) | copy-start | bytes 786436
  0.0 13.2 %copy-start = (s32[8]{0:T(128)S(1)}, s32[8]{0:T(128)}, u32[]{:S(2)}) copy-start(s32[8]{0:T(128)} %parents_ref.5) | copy-start | bytes 100
  0.0 16.7 %slice-start.1 = ((s8[8388608]{0:T(1024)(128)(4,1)}), s8[4194304]{0:T(1024)(128)(4,1)S(1)}, s32[]{:S(2)}) async-start(s8[8388608]{0:T(1024)(128)(4,1)} %bitcast.4), calls=%async_computation.1 | async-start | bytes 8388608
  1.0 8.1 %collective-permute-start.2 = (bf16[256,128]{1,0:T(8,128)(2,1)S(1)}, bf16[256,128]{1,0:T(8,128)(2,1)S(1)}, u32[]{:S(2)}, u32[]{:S(2)}) collective-permute-start(bf16[256,128]{1,0:T(8,128)(2,1)S(1)} %shard_map.55.kv_ref), channel_id=1, source_target_pairs={{0,24},{4,28},{8,16},{12,20},{16,8},{20,12},{24,0},{28,4},{1,25},{... | collective-permute-start | bytes 196616 | tf_op jit(solution)/shard_map/ppermute | solution.py:152
  6.1 4.7 %collective-permute-start.1 = (bf16[256,128]{1,0:T(8,128)(2,1)S(1)}, bf16[256,128]{1,0:T(8,128)(2,1)S(1)}, u32[]{:S(2)}, u32[]{:S(2)}) collective-permute-start(bf16[256,128]{1,0:T(8,128)(2,1)S(1)} %shard_map.55.kv_ref), channel_id=1, source_target_pairs={{0,8},{4,12},{8,0},{12,4},{16,24},{20,28},{24,16},{28,20},{1,9},{5... | collective-permute-start | bytes 196616 | tf_op jit(solution)/shard_map/ppermute | solution.py:152
  6.1 6.3 %collective-permute-start = (bf16[256,128]{1,0:T(8,128)(2,1)S(1)}, bf16[256,128]{1,0:T(8,128)(2,1)S(1)}, u32[]{:S(2)}, u32[]{:S(2)}) collective-permute-start(bf16[256,128]{1,0:T(8,128)(2,1)S(1)} %shard_map.55.kv_ref), channel_id=1, source_target_pairs={{0,16},{4,20},{8,24},{12,28},{16,0},{20,4},{24,8},{28,12},{1,17},{... | collective-permute-start | bytes 196616 | tf_op jit(solution)/shard_map/ppermute | solution.py:152
  7.3 6.0 %collective-permute-start.3 = (bf16[256,128]{1,0:T(8,128)(2,1)S(1)}, bf16[256,128]{1,0:T(8,128)(2,1)S(1)}, u32[]{:S(2)}, u32[]{:S(2)}) collective-permute-start(bf16[256,128]{1,0:T(8,128)(2,1)S(1)} %shard_map.55.kv_ref), channel_id=1, source_target_pairs={{0,4},{4,0},{8,12},{12,8},{16,20},{20,16},{24,28},{28,24},{1,5},{5... | collective-permute-start | bytes 196616 | tf_op jit(solution)/shard_map/ppermute | solution.py:152
  9.0 4.8 %collective-permute-start.5 = (bf16[256,128]{1,0:T(8,128)(2,1)S(1)}, bf16[256,128]{1,0:T(8,128)(2,1)S(1)}, u32[]{:S(2)}, u32[]{:S(2)}) collective-permute-start(bf16[256,128]{1,0:T(8,128)(2,1)S(1)} %collective-permute-done.2.refs_2_), channel_id=1, source_target_pairs={{0,4},{4,0},{8,12},{12,8},{16,20},{20,16},{24,28},{28,24},{1,5},{5... | collective-permute-start | bytes 196616 | tf_op jit(solution)/shard_map/ppermute | solution.py:152
  10.7 5.0 %collective-permute-start.4 = (bf16[256,128]{1,0:T(8,128)(2,1)S(1)}, bf16[256,128]{1,0:T(8,128)(2,1)S(1)}, u32[]{:S(2)}, u32[]{:S(2)}) collective-permute-start(bf16[256,128]{1,0:T(8,128)(2,1)S(1)} %collective-permute-done.1.refs_1_), channel_id=1, source_target_pairs={{0,4},{4,0},{8,12},{12,8},{16,20},{20,16},{24,28},{28,24},{1,5},{5... | collective-permute-start | bytes 196616 | tf_op jit(solution)/shard_map/ppermute | solution.py:152
  12.4 4.3 %collective-permute-start.6 = (bf16[256,128]{1,0:T(8,128)(2,1)S(1)}, bf16[256,128]{1,0:T(8,128)(2,1)S(1)}, u32[]{:S(2)}, u32[]{:S(2)}) collective-permute-start(bf16[256,128]{1,0:T(8,128)(2,1)S(1)} %collective-permute-done.refs_0_), channel_id=1, source_target_pairs={{0,4},{4,0},{8,12},{12,8},{16,20},{20,16},{24,28},{28,24},{1,5},{5... | collective-permute-start | bytes 196616 | tf_op jit(solution)/shard_map/ppermute | solution.py:152
  18.0 1.6 %collective-permute-start.7 = (bf16[128,1024]{1,0:T(8,128)(2,1)S(1)}, bf16[128,1024]{1,0:T(8,128)(2,1)S(1)}, u32[]{:S(2)}, u32[]{:S(2)}) collective-permute-start(bf16[128,1024]{1,0:T(8,128)(2,1)S(1)} %get-tuple-element.37), channel_id=1, source_target_pairs={{0,1},{1,0},{2,3},{3,2},{4,5},{5,4},{6,7},{7,6},{8,9},{9,8},{10,11... | collective-permute-start | bytes 786440 | tf_op jit(solution)/shard_map/ppermute | solution.py:152
  19.7 8.4 %collective-permute-start.9 = (bf16[128,1024]{1,0:T(8,128)(2,1)S(1)}, bf16[128,1024]{1,0:T(8,128)(2,1)S(1)}, u32[]{:S(2)}, u32[]{:S(2)}) collective-permute-start(bf16[128,1024]{1,0:T(8,128)(2,1)S(1)} %add_convert_fusion.1), channel_id=1, source_target_pairs={{0,2},{1,3},{2,0},{3,1},{4,6},{5,7},{6,4},{7,5},{8,10},{9,11},{10,... | collective-permute-start | bytes 786440 | tf_op jit(solution)/shard_map/ppermute | solution.py:152
  21.3 6.9 %collective-permute-start.8 = (bf16[128,1024]{1,0:T(8,128)(2,1)S(1)}, bf16[128,1024]{1,0:T(8,128)(2,1)S(1)}, u32[]{:S(2)}, u32[]{:S(2)}) collective-permute-start(bf16[128,1024]{1,0:T(8,128)(2,1)S(1)} %get-tuple-element.38), channel_id=1, source_target_pairs={{0,1},{1,0},{2,3},{3,2},{4,5},{5,4},{6,7},{7,6},{8,9},{9,8},{10,11... | collective-permute-start | bytes 786440 | tf_op jit(solution)/shard_map/ppermute | solution.py:152

commit v5 on v4

--- a/solution.py
+++ b/solution.py
@@ -34,7 +34,20 @@
     v_copy.wait()
 
 
-def own_block_kernel(q_ref, kv_ref, m_ref, l_ref, acc_ref):
+def reached_mask(parents_ref):
+    me = lax.axis_index("ctx")
+    wanted = parents_ref[me]
+    reached = jnp.int32(0)
+    for step in range(1, DIRECT_SIZE):
+        block = me - step
+        hit = (block >= 0) & (block == wanted)
+        block = jnp.maximum(block, 0)
+        reached = jnp.where(hit, reached | lax.shift_left(jnp.int32(1), block), reached)
+        wanted = jnp.where(hit, parents_ref[block], wanted)
+    return reached
+
+
+def own_block_kernel(parents_ref, q_ref, kv_ref, reached_ref, m_ref, l_ref, acc_ref):
     scale = exponent_scale(q_ref.shape[1])
     s = scores_of(kv_ref[0:BLOCK, :], q_ref[...])
     key_at = lax.broadcasted_iota(jnp.int32, s.shape, 0)
@@ -45,10 +58,11 @@
     m_ref[...] = m
     l_ref[...] = jnp.sum(p, axis=0, keepdims=True)
     acc_ref[...] = weighted(kv_ref[BLOCK:, :], p)
-
-
-def project(att, w_ref, block, width):
-    start = pl.multiple_of(block * width, 128)
+    reached_ref[...] = jnp.full(reached_ref.shape, reached_mask(parents_ref), jnp.int32)
+
+
+def project(att, w_ref, start, width):
+    start = pl.multiple_of(start, 128)
     return jnp.dot(att, w_ref[:, pl.ds(start, width)], preferred_element_type=jnp.float32)
 
 
@@ -63,17 +77,10 @@
     acc_ref[...] = acc_ref[...] * factor + weighted(v, p)
 
 
-def absorb_reached(xors, parents_ref, q_ref, kv_refs, state):
+def absorb_reached(xors, reached_ref, q_ref, kv_refs, state):
     scale = exponent_scale(q_ref.shape[1])
     me = lax.axis_index("ctx")
-    wanted = parents_ref[me]
-    reached = jnp.int32(0)
-    for step in range(1, DIRECT_SIZE):
-        block = me - step
-        hit = (block >= 0) & (block == wanted)
-        block = jnp.maximum(block, 0)
-        reached = jnp.where(hit, reached | lax.shift_left(jnp.int32(1), block), reached)
-        wanted = jnp.where(hit, parents_ref[block], wanted)
+    reached = jnp.max(reached_ref[...])
     for other, kv_ref in zip(xors, kv_refs):
         @pl.when((lax.shift_right_logical(reached, me ^ other) & 1) == 1)
         def _():
@@ -99,40 +106,36 @@
     lax.fori_loop(1, parents_ref.shape[0], visit, parents_ref[me])
 
 
-def others_kernel(xors, parents_ref, q_ref, m_in, l_in, acc_in, *refs):
+def others_kernel(xors, reached_ref, q_ref, m_in, l_in, acc_in, *refs):
     state = refs[len(xors):]
-    absorb_reached(xors, parents_ref, q_ref, refs[:len(xors)], state)
-
-
-def last_kernel(xors, parents_ref, q_ref, m_in, l_in, acc_in, *refs):
+    absorb_reached(xors, reached_ref, q_ref, refs[:len(xors)], state)
+
+
+def last_kernel(xors, tree_ref, q_ref, m_in, l_in, acc_in, *refs):
     kv_refs = refs[:max(len(xors), 1)]
     w_ref, att_ref, send_ref, keep_ref, *state = refs[len(kv_refs):]
     rows, head_dim = q_ref.shape
-    group = rows // BLOCK
-    width = keep_ref.shape[1]
-    far = lax.axis_index("tp") ^ 2
     if xors:
-        absorb_reached(xors, parents_ref, q_ref, kv_refs, state)
+        absorb_reached(xors, tree_ref, q_ref, kv_refs, state)
     else:
-        absorb_walk(parents_ref, q_ref, kv_refs[0], state)
+        absorb_walk(tree_ref, q_ref, kv_refs[0], state)
     m_ref, l_ref, acc_ref = state
 
-    for head in range(group):
+    for head in range(rows // BLOCK):
         at = slice(head * BLOCK, (head + 1) * BLOCK)
         part = acc_ref[:, at] / l_ref[:, at]
         att_ref[:, head * head_dim:(head + 1) * head_dim] = part.T.astype(jnp.bfloat16)
 
+    project_pair(2, 0, att_ref, w_ref, send_ref, keep_ref)
+
+
+def project_pair(flip, half, att_ref, w_ref, send_ref, keep_ref):
+    target = lax.axis_index("tp") ^ flip
+    width = w_ref.shape[1] // 4
+    cols = keep_ref.shape[1]
     att = att_ref[...]
-    send_ref[...] = project(att, w_ref, far ^ 1, width).astype(jnp.bfloat16)
-    keep_ref[...] = project(att, w_ref, far, width)
-
-
-def near_kernel(att_ref, w_ref, send_ref, keep_ref):
-    mine = lax.axis_index("tp")
-    width = keep_ref.shape[1]
-    att = att_ref[...]
-    send_ref[...] = project(att, w_ref, mine ^ 1, width).astype(jnp.bfloat16)
-    keep_ref[...] = project(att, w_ref, mine, width)
+    send_ref[...] = project(att, w_ref, (target ^ 1) * width + half * cols, cols).astype(jnp.bfloat16)
+    keep_ref[...] = project(att, w_ref, target * width + half * cols, cols)
 
 
 def shards(ctx_size, tp_size, query_heads, key_heads, value_heads, parents, out_weight):
@@ -164,19 +167,23 @@
         columns = [swap(kv, "ctx", ctx_size, other) for other in (4, 2, 6)]
     q = jnp.transpose(query_heads, (1, 0, 2)).reshape(rows, head_dim)
 
-    m, l, acc = pl.pallas_call(
+    reached, m, l, acc = pl.pallas_call(
         own_block_kernel,
         out_shape=(
+            jax.ShapeDtypeStruct((8, 128), jnp.int32),
             jax.ShapeDtypeStruct((1, rows), jnp.float32),
             jax.ShapeDtypeStruct((1, rows), jnp.float32),
             jax.ShapeDtypeStruct((head_dim, rows), jnp.float32),
         ),
-        in_specs=[vmem, vmem],
-        out_specs=(vmem, vmem, vmem),
+        in_specs=[smem, vmem, vmem],
+        out_specs=(vmem,) * 4,
         compiler_params=params,
         cost_estimate=pl.CostEstimate(flops=67_000_000, bytes_accessed=1_000_000, transcendentals=130_000),
-    )(q, kv)
-
+    )(parents, q, kv)
+
+    if ctx_size == DIRECT_SIZE:
+        late, m = lax.optimization_barrier((kv, m))
+        beside = swap(late, "ctx", ctx_size, 1)
     state = (m, l, acc)
     state_shapes = tuple(jax.ShapeDtypeStruct(x.shape, x.dtype) for x in state)
     if ctx_size == DIRECT_SIZE:
@@ -189,51 +196,64 @@
             return pl.pallas_call(
                 functools.partial(others_kernel, xors),
                 out_shape=state_shapes,
-                in_specs=[smem] + [vmem] * (4 + len(xors)),
+                in_specs=[vmem] * (5 + len(xors)),
                 out_specs=(vmem,) * 3,
                 input_output_aliases={2: 0, 3: 1, 4: 2},
                 compiler_params=params,
                 cost_estimate=pl.CostEstimate(flops=270_000_000, bytes_accessed=1_000_000, transcendentals=500_000),
-            )(parents, q, *state, *arrived)
+            )(reached, q, *state, *arrived)
 
         state = absorbed(state, (4, 2, 6, 1), [*columns, beside])
         state = absorbed(state, (3, 7), pairs[1:])
-        xors, pieces = (5,), pairs[:1]
+        xors, pieces, tree, tree_spec = (5,), pairs[:1], reached, vmem
     else:
-        xors = ()
-        pieces = [lax.all_gather(kv, "ctx", axis=0, tiled=True)]
-
-    att, send_far, keep_far, *_ = pl.pallas_call(
+        xors, pieces, tree, tree_spec = (), [lax.all_gather(kv, "ctx", axis=0, tiled=True)], parents, smem
+
+    half = width // 2
+    pair_shapes = (
+        jax.ShapeDtypeStruct((tok_rows, half), jnp.bfloat16),
+        jax.ShapeDtypeStruct((tok_rows, half), jnp.float32),
+    )
+    att, send_a, keep_a, *_ = pl.pallas_call(
         functools.partial(last_kernel, xors),
-        out_shape=(
-            jax.ShapeDtypeStruct((tok_rows, local_heads * head_dim), jnp.bfloat16),
-            jax.ShapeDtypeStruct((tok_rows, width), jnp.bfloat16),
-            jax.ShapeDtypeStruct((tok_rows, width), jnp.float32),
-        ) + state_shapes,
-        in_specs=[smem] + [vmem] * (5 + len(pieces)),
+        out_shape=(jax.ShapeDtypeStruct((tok_rows, local_heads * head_dim), jnp.bfloat16),) + pair_shapes + state_shapes,
+        in_specs=[tree_spec] + [vmem] * (5 + len(pieces)),
         out_specs=(vmem,) * 6,
         input_output_aliases={2: 3, 3: 4, 4: 5},
         compiler_params=params,
         cost_estimate=pl.CostEstimate(flops=1_000_000_000, bytes_accessed=10_000_000, transcendentals=1_000_000),
-    )(parents, q, *state, *pieces, out_weight)
-
-    far_in = swap(send_far, "tp", tp_size, 1)
-    send_near, keep_near = pl.pallas_call(
-        near_kernel,
-        out_shape=(
-            jax.ShapeDtypeStruct((tok_rows, width), jnp.bfloat16),
-            jax.ShapeDtypeStruct((tok_rows, width), jnp.float32),
-        ),
-        in_specs=[vmem, vmem],
-        out_specs=(vmem, vmem),
-        compiler_params=params,
-        cost_estimate=pl.CostEstimate(flops=540_000_000, bytes_accessed=4_000_000, transcendentals=0),
-    )(att, out_weight)
-    far_sum = (keep_far + far_in.astype(jnp.float32)).astype(jnp.bfloat16)
-    from_far = swap(far_sum, "tp", tp_size, 2)
-    send_near, _ = lax.optimization_barrier((send_near, far_sum))
+    )(tree, q, *state, *pieces, out_weight)
+
+    def projected(flip, part, shapes, att):
+        return pl.pallas_call(
+            functools.partial(project_pair, flip, part),
+            out_shape=shapes,
+            in_specs=[vmem, vmem],
+            out_specs=(vmem, vmem),
+            compiler_params=params,
+            cost_estimate=pl.CostEstimate(flops=540_000_000, bytes_accessed=4_000_000, transcendentals=0),
+        )(att, out_weight)
+
+    def added(keep, arrived):
+        return (keep + arrived.astype(jnp.float32)).astype(jnp.bfloat16)
+
+    in_a = swap(send_a, "tp", tp_size, 1)
+    send_b, keep_b = projected(2, 1, pair_shapes, att)
+    in_b = swap(send_b, "tp", tp_size, 1)
+    far_a = added(keep_a, in_a)
+    from_a = swap(far_a, "tp", tp_size, 2)
+    far_b = added(keep_b, in_b)
+    from_b = swap(far_b, "tp", tp_size, 2)
+    att, _ = lax.optimization_barrier((att, far_a))
+    send_near, keep_near = projected(
+        0,
+        0,
+        (jax.ShapeDtypeStruct((tok_rows, width), jnp.bfloat16), jax.ShapeDtypeStruct((tok_rows, width), jnp.float32)),
+        att,
+    )
     near_in = swap(send_near, "tp", tp_size, 1)
-    return (keep_near + near_in.astype(jnp.float32) + from_far.astype(jnp.float32)).astype(jnp.bfloat16)
+    from_far = jnp.concatenate([from_a, from_b], axis=1).astype(jnp.float32)
+    return (keep_near + near_in.astype(jnp.float32) + from_far).astype(jnp.bfloat16)
 
 
 def solution(mesh):

time: 29.1 us -> 28.2 us (0.969)
  waiting for transfers between devices: 10.1 us -> 8.94 us
  starting transfers between devices: 13.1 us -> 13.8 us
  Pallas kernels: 4.72 us -> 4.31 us
    ppermute x10 -> x12, waiting for transfers between devices: 10.1 us -> 8.94 us  [swap(): return lax.ppermute(x, axis, [(i, i ^ other) for i in range(size)])]
    pallas_call x2 -> x3, Pallas kernels: 1.24 us -> 2.24 us  [the longest x2 1.19 us: projected(): pl.pallas_call(functools.partial(project_pair, flip, part), out_shape=sha...]
    pallas_call x2, Pallas kernels: 1.18 us -> 0.43 us  [absorbed(): pl.pallas_call(functools.partial(others_kernel, xors), out_shape=state_sh...]
    ppermute x10 -> x12, starting transfers between devices: 13.1 us -> 13.8 us  [swap(): return lax.ppermute(x, axis, [(i, i ^ other) for i in range(size)])]
    pallas_call x1, Pallas kernels: 1.35 us -> 0.7 us  [shards(): pl.pallas_call(functools.partial(last_kernel, xors), out_shape=(jax.Shape...]
    convert_element_type x2 -> x3, other arithmetic: 0.86 us -> 0.85 us  [the longest x1 0.79 us: shards(): (keep_near + near_in.astype(jnp.float32) + from_far).astype(jnp.bfloat16)]
  transfers between devices with their start and end apart: 10 -> 12, of which waited for: 5 -> 7; matrix products, arithmetic and copies ran while one was open for 0% -> 0% of each run, Pallas kernels for 8% -> 10%
where the time goes in v5:
time: 28.2 us; the launch traced here: 28.1 us
  starting transfers between devices  13.8 us (49%)
  waiting for transfers between devices  8.94 us (32%)
  Pallas kernels  4.31 us (15%)
  other arithmetic  0.85 us (3%)
    ppermute x12, starting transfers between devices, swap(): return lax.ppermute(x, axis, [(i, i ^ other) for i in range(size)])  13.8 us
    ppermute x12, waiting for transfers between devices, swap(): return lax.ppermute(x, axis, [(i, i ^ other) for i in range(size)])  8.94 us
    pallas_call x2, Pallas kernels, projected(): pl.pallas_call(functools.partial(project_pair, flip, part), out_shape=sha...  1.19 us
    pallas_call x1, Pallas kernels, shards(): pl.pallas_call(own_block_kernel, out_shape=(jax.ShapeDtypeStruct((8, 128)...  1.05 us
    pallas_call x1, Pallas kernels, shards(): pl.pallas_call(pack_kernel, out_shape=jax.ShapeDtypeStruct((2 * tok_rows,...  0.94 us
    convert_element_type x1, other arithmetic, shards(): (keep_near + near_in.astype(jnp.float32) + from_far).astype(jnp.bfloat16)  0.79 us
    pallas_call x1, Pallas kernels, shards(): pl.pallas_call(functools.partial(last_kernel, xors), out_shape=(jax.Shape...  0.7 us
  transfers between devices with their start and end apart: 12, of which 7 were waited for; matrix products, arithmetic and copies ran while one was open for 0% of the time, Pallas kernels for 10%

profile of v5, /device:TPU:0, one launch (start us, length us, event | category | flops | bytes accessed | tf_op | source)
XLA Modules:
  0.0 28.1 jit_solution(359060943280765513)
XLA Ops:
  0.0 0.0 slice-start
  0.0 0.0 copy-start.1
  0.0 0.0 copy-start
  0.0 0.0 slice-start.1
  0.0 0.9 %shard_map.55.kv_ref = bf16[256,128]{1,0:T(8,128)(2,1)S(1)} custom-call(bf16[128,128]{1,0:T(8,128)(2,1)} %bitcast.11, bf16[128,128]{1,0:T(8,128)(2,1)} %bitcast.12), custom_call_target="tpu_custom_call" | custom-call | flops 8000000000 | bytes 130000 | tf_op jit(solution)/shard_map/pallas_call | solution.py:157
  1.0 5.1 %collective-permute-start.2 = (bf16[256,128]{1,0:T(8,128)(2,1)S(1)}, bf16[256,128]{1,0:T(8,128)(2,1)S(1)}, u32[]{:S(2)}, u32[]{:S(2)}) collective-permute-start(bf16[256,128]{1,0:T(8,128)(2,1)S(1)} %shard_map.55.kv_ref), channel_id=1, source_target_pairs={{0,24},{4,28},{8,16},{12,20},{16,8},{20,12},{24,0},{28,4},{1,25},{... | collective-permute-start | bytes 196616 | tf_op jit(solution)/shard_map/ppermute | solution.py:155
  6.1 0.0 collective-permute-start.1
  6.1 0.6 %collective-permute-start = (bf16[256,128]{1,0:T(8,128)(2,1)S(1)}, bf16[256,128]{1,0:T(8,128)(2,1)S(1)}, u32[]{:S(2)}, u32[]{:S(2)}) collective-permute-start(bf16[256,128]{1,0:T(8,128)(2,1)S(1)} %shard_map.55.kv_ref), channel_id=1, source_target_pairs={{0,16},{4,20},{8,24},{12,28},{16,0},{20,4},{24,8},{28,12},{1,17},{... | collective-permute-start | bytes 196616 | tf_op jit(solution)/shard_map/ppermute | solution.py:155
  6.7 0.0 copy-done.1
  6.8 0.0 copy-done
  6.8 1.0 %shard_map.56 = (s32[8,128]{1,0:T(8,128)S(1)}, f32[1,1024]{1,0:T(1,128)S(1)}, f32[1,1024]{1,0:T(1,128)S(1)}, f32[128,1024]{1,0:T(8,128)S(1)}) custom-call(s32[8]{0:T(128)S(1)} %copy-done, bf16[1024,128]{1,0:T(8,128)(2,1)S(1)} %bitcast.6, bf16[256,128]{1,0:T(8,128)(2,1)S(1)} %shard_map.55.kv_ref), custom_call_target="tpu_custom_call" | custom-call | flops 67000000 | bytes 1000000 | tf_op jit(solution)/shard_map/pallas_call | solution.py:170
  7.8 1.7 %collective-permute-start.3 = (bf16[256,128]{1,0:T(8,128)(2,1)S(1)}, bf16[256,128]{1,0:T(8,128)(2,1)S(1)}, u32[]{:S(2)}, u32[]{:S(2)}) collective-permute-start(bf16[256,128]{1,0:T(8,128)(2,1)S(1)} %shard_map.55.kv_ref), channel_id=1, source_target_pairs={{0,4},{4,0},{8,12},{12,8},{16,20},{20,16},{24,28},{28,24},{1,5},{5... | collective-permute-start | bytes 196616 | tf_op jit(solution)/shard_map/ppermute | solution.py:155
  9.6 0.0 collective-permute-done.2.refs_2_
  9.6 0.9 %collective-permute-start.5 = (bf16[256,128]{1,0:T(8,128)(2,1)S(1)}, bf16[256,128]{1,0:T(8,128)(2,1)S(1)}, u32[]{:S(2)}, u32[]{:S(2)}) collective-permute-start(bf16[256,128]{1,0:T(8,128)(2,1)S(1)} %collective-permute-done.2.refs_2_), channel_id=1, source_target_pairs={{0,4},{4,0},{8,12},{12,8},{16,20},{20,16},{24,28},{28,24},{1,5},{5... | collective-permute-start | bytes 196616 | tf_op jit(solution)/shard_map/ppermute | solution.py:155
  10.5 0.2 collective-permute-done.1.refs_1_
  10.7 1.7 %collective-permute-start.4 = (bf16[256,128]{1,0:T(8,128)(2,1)S(1)}, bf16[256,128]{1,0:T(8,128)(2,1)S(1)}, u32[]{:S(2)}, u32[]{:S(2)}) collective-permute-start(bf16[256,128]{1,0:T(8,128)(2,1)S(1)} %collective-permute-done.1.refs_1_), channel_id=1, source_target_pairs={{0,4},{4,0},{8,12},{12,8},{16,20},{20,16},{24,28},{28,24},{1,5},{5... | collective-permute-start | bytes 196616 | tf_op jit(solution)/shard_map/ppermute | solution.py:155
  12.4 0.0 collective-permute-done.refs_0_
  12.4 0.8 %collective-permute-start.6 = (bf16[256,128]{1,0:T(8,128)(2,1)S(1)}, bf16[256,128]{1,0:T(8,128)(2,1)S(1)}, u32[]{:S(2)}, u32[]{:S(2)}) collective-permute-start(bf16[256,128]{1,0:T(8,128)(2,1)S(1)} %collective-permute-done.refs_0_), channel_id=1, source_target_pairs={{0,4},{4,0},{8,12},{12,8},{16,20},{20,16},{24,28},{28,24},{1,5},{5... | collective-permute-start | bytes 196616 | tf_op jit(solution)/shard_map/ppermute | solution.py:155
  13.2 0.0 collective-permute-done.3.refs_3_
  13.2 0.2 shard_map.57
  13.5 0.8 %collective-permute-done.5.refs_1_ = bf16[256,128]{1,0:T(8,128)(2,1)S(1)} collective-permute-done((bf16[256,128]{1,0:T(8,128)(2,1)S(1)}, bf16[256,128]{1,0:T(8,128)(2,1)S(1)}, u32[]{:S(2)}, u32[]{:S(2)}) %collective-permute-start.5) | collective-permute-done | bytes 65568 | tf_op jit(solution)/shard_map/ppermute | solution.py:155
  14.2 1.5 %collective-permute-done.4.refs_0_ = bf16[256,128]{1,0:T(8,128)(2,1)S(1)} collective-permute-done((bf16[256,128]{1,0:T(8,128)(2,1)S(1)}, bf16[256,128]{1,0:T(8,128)(2,1)S(1)}, u32[]{:S(2)}, u32[]{:S(2)}) %collective-permute-start.4) | collective-permute-done | bytes 65568 | tf_op jit(solution)/shard_map/ppermute | solution.py:155
  15.7 0.2 shard_map.58
  15.9 0.7 %collective-permute-done.6.refs_0_ = bf16[256,128]{1,0:T(8,128)(2,1)S(1)} collective-permute-done((bf16[256,128]{1,0:T(8,128)(2,1)S(1)}, bf16[256,128]{1,0:T(8,128)(2,1)S(1)}, u32[]{:S(2)}, u32[]{:S(2)}) %collective-permute-start.6) | collective-permute-done | bytes 65568 | tf_op jit(solution)/shard_map/ppermute | solution.py:155
  16.7 0.0 slice-done
  16.7 0.0 slice-done.1
  16.7 0.7 %shard_map.59 = (bf16[128,1024]{1,0:T(8,128)(2,1)S(1)}, bf16[128,512]{1,0:T(8,128)(2,1)S(1)}, f32[128,512]{1,0:T(8,128)S(1)}, f32[1,1024]{1,0:T(1,128)S(1)}, f32...) custom-call(s32[8,128]{1,0:T(8,128)S(1)} %get-tuple-element.26.reached_ref, ...), custom_call_target="tpu_custom_call", output_to_operand_aliasing={{3}: (2, {}), {4}: (3, {}), {5}: (4, {})} | custom-call | flops 1000000000 | bytes 10000000 | tf_op jit(solution)/shard_map/pallas_call | solution.py:217
  17.4 0.1 collective-permute-start.7
  17.5 0.5 %shard_map.61 = (bf16[128,512]{1,0:T(8,128)(2,1)S(1)}, f32[128,512]{1,0:T(8,128)S(1)}) custom-call(bf16[128,1024]{1,0:T(8,128)(2,1)S(1)} %get-tuple-element.42.att_ref, bf16[1024,4096]{1,0:T(8,128)(2,1)S(1)} %bitcast.5), custom_call_target="tpu_custom_call" | custom-call | flops 540000000 | bytes 4000000 | tf_op jit(solution)/shard_map/pallas_call | solution.py:228
  17.9 0.6 %collective-permute-start.10 = (bf16[128,512]{1,0:T(8,128)(2,1)S(1)}, bf16[128,512]{1,0:T(8,128)(2,1)S(1)}, u32[]{:S(2)}, u32[]{:S(2)}) collective-permute-start(bf16[128,512]{1,0:T(8,128)(2,1)S(1)} %get-tuple-element.46), channel_id=1, source_target_pairs={{0,1},{1,0},{2,3},{3,2},{4,5},{5,4},{6,7},{7,6},{8,9},{9,8},{10,11... | collective-permute-start | bytes 393224 | tf_op jit(solution)/shard_map/ppermute | solution.py:155
  18.5 0.3 %collective-permute-done.7 = bf16[128,512]{1,0:T(8,128)(2,1)S(1)} collective-permute-done((bf16[128,512]{1,0:T(8,128)(2,1)S(1)}, bf16[128,512]{1,0:T(8,128)(2,1)S(1)}, u32[]{:S(2)}, u32[]{:S(2)}) %collective-permute-start.7) | collective-permute-done | bytes 131104 | tf_op jit(solution)/shard_map/ppermute | solution.py:155
  18.8 1.6 %collective-permute-start.9 = (bf16[128,512]{1,0:T(8,128)(2,1)S(1)}, bf16[128,512]{1,0:T(8,128)(2,1)S(1)}, u32[]{:S(2)}, u32[]{:S(2)}) collective-permute-start(bf16[128,512]{1,0:T(8,128)(2,1)S(1)} %add_convert_fusion.2), channel_id=1, source_target_pairs={{0,2},{1,3},{2,0},{3,1},{4,6},{5,7},{6,4},{7,5},{8,10},{9,11},{10,... | collective-permute-start | bytes 393224 | tf_op jit(solution)/shard_map/ppermute | solution.py:155
  20.4 0.7 %shard_map.60 = (bf16[128,1024]{1,0:T(8,128)(2,1)S(1)}, f32[128,1024]{1,0:T(8,128)S(1)}) custom-call(bf16[128,1024]{1,0:T(8,128)(2,1)S(1)} %get-tuple-element.42.att_ref, bf16[1024,4096]{1,0:T(8,128)(2,1)S(1)} %bitcast.5), custom_call_target="tpu_custom_call" | custom-call | flops 540000000 | bytes 4000000 | tf_op jit(solution)/shard_map/pallas_call | solution.py:228
  21.1 0.1 collective-permute-start.8
  21.2 0.0 collective-permute-done.10
  21.3 0.6 %collective-permute-start.11 = (bf16[128,512]{1,0:T(8,128)(2,1)S(1)}, bf16[128,512]{1,0:T(8,128)(2,1)S(1)}, u32[]{:S(2)}, u32[]{:S(2)}) collective-permute-start(bf16[128,512]{1,0:T(8,128)(2,1)S(1)} %add_convert_fusion.1), channel_id=1, source_target_pairs={{0,2},{1,3},{2,0},{3,1},{4,6},{5,7},{6,4},{7,5},{8,10},{9,11},{10,... | collective-permute-start | bytes 393224 | tf_op jit(solution)/shard_map/ppermute | solution.py:155
  21.9 2.6 %collective-permute-done.9 = bf16[128,512]{1,0:T(8,128)(2,1)S(1)} collective-permute-done((bf16[128,512]{1,0:T(8,128)(2,1)S(1)}, bf16[128,512]{1,0:T(8,128)(2,1)S(1)}, u32[]{:S(2)}, u32[]{:S(2)}) %collective-permute-start.9) | collective-permute-done | bytes 131104 | tf_op jit(solution)/shard_map/ppermute | solution.py:155
  24.5 2.8 %collective-permute-done.11 = bf16[128,512]{1,0:T(8,128)(2,1)S(1)} collective-permute-done((bf16[128,512]{1,0:T(8,128)(2,1)S(1)}, bf16[128,512]{1,0:T(8,128)(2,1)S(1)}, u32[]{:S(2)}, u32[]{:S(2)}) %collective-permute-start.11) | collective-permute-done | bytes 131104 | tf_op jit(solution)/shard_map/ppermute | solution.py:155
  27.3 0.0 collective-permute-done.8
  27.3 0.8 %add_convert_fusion = bf16[128,1024]{1,0:T(8,128)(2,1)} fusion(f32[128,1024]{1,0:T(8,128)S(1)} %get-tuple-element.43, bf16[128,1024]{1,0:T(8,128)(2,1)S(1)} %collective-permute-done.8, bf16[128,512]{1,0:T(8,128)(2,1)S(1)} %collective-permute-done.11, bf16[128,512]{1,0:T(8,128)(2,1)S(1)} %collective-permute-done.9), kind=kLoop, calls=%fused_computation | loop fusion | flops 1048576 | bytes 1310720 | tf_op jit(solution)/shard_map/convert_element_type | solution.py:256
  (4 shorter events, 0.1 us)
Async XLA Ops:
  0.0 16.7 %slice-start = ((s8[8388608]{0:T(1024)(128)(4,1)}), s8[4194304]{0:T(1024)(128)(4,1)S(1)}, s32[]{:S(2)}) async-start(s8[8388608]{0:T(1024)(128)(4,1)} %bitcast.4), calls=%async_computation | async-start | bytes 8388608
  0.0 6.7 %copy-start.1 = (bf16[128,8,128]{2,1,0:T(8,128)(2,1)S(1)}, bf16[128,8,128]{2,1,0:T(8,128)(2,1)}, u32[]{:S(2)}) copy-start(bf16[128,8,128]{2,1,0:T(8,128)(2,1)} %param.5) | copy-start | bytes 786436
  0.0 6.8 %copy-start = (s32[8]{0:T(128)S(1)}, s32[8]{0:T(128)}, u32[]{:S(2)}) copy-start(s32[8]{0:T(128)} %parents_ref.1) | copy-start | bytes 100
  0.0 16.7 %slice-start.1 = ((s8[8388608]{0:T(1024)(128)(4,1)}), s8[4194304]{0:T(1024)(128)(4,1)S(1)}, s32[]{:S(2)}) async-start(s8[8388608]{0:T(1024)(128)(4,1)} %bitcast.4), calls=%async_computation.1 | async-start | bytes 8388608
  1.0 8.6 %collective-permute-start.2 = (bf16[256,128]{1,0:T(8,128)(2,1)S(1)}, bf16[256,128]{1,0:T(8,128)(2,1)S(1)}, u32[]{:S(2)}, u32[]{:S(2)}) collective-permute-start(bf16[256,128]{1,0:T(8,128)(2,1)S(1)} %shard_map.55.kv_ref), channel_id=1, source_target_pairs={{0,24},{4,28},{8,16},{12,20},{16,8},{20,12},{24,0},{28,4},{1,25},{... | collective-permute-start | bytes 196616 | tf_op jit(solution)/shard_map/ppermute | solution.py:155
  6.1 4.7 %collective-permute-start.1 = (bf16[256,128]{1,0:T(8,128)(2,1)S(1)}, bf16[256,128]{1,0:T(8,128)(2,1)S(1)}, u32[]{:S(2)}, u32[]{:S(2)}) collective-permute-start(bf16[256,128]{1,0:T(8,128)(2,1)S(1)} %shard_map.55.kv_ref), channel_id=1, source_target_pairs={{0,8},{4,12},{8,0},{12,4},{16,24},{20,28},{24,16},{28,20},{1,9},{5... | collective-permute-start | bytes 196616 | tf_op jit(solution)/shard_map/ppermute | solution.py:155
  6.1 6.3 %collective-permute-start = (bf16[256,128]{1,0:T(8,128)(2,1)S(1)}, bf16[256,128]{1,0:T(8,128)(2,1)S(1)}, u32[]{:S(2)}, u32[]{:S(2)}) collective-permute-start(bf16[256,128]{1,0:T(8,128)(2,1)S(1)} %shard_map.55.kv_ref), channel_id=1, source_target_pairs={{0,16},{4,20},{8,24},{12,28},{16,0},{20,4},{24,8},{28,12},{1,17},{... | collective-permute-start | bytes 196616 | tf_op jit(solution)/shard_map/ppermute | solution.py:155
  7.8 5.4 %collective-permute-start.3 = (bf16[256,128]{1,0:T(8,128)(2,1)S(1)}, bf16[256,128]{1,0:T(8,128)(2,1)S(1)}, u32[]{:S(2)}, u32[]{:S(2)}) collective-permute-start(bf16[256,128]{1,0:T(8,128)(2,1)S(1)} %shard_map.55.kv_ref), channel_id=1, source_target_pairs={{0,4},{4,0},{8,12},{12,8},{16,20},{20,16},{24,28},{28,24},{1,5},{5... | collective-permute-start | bytes 196616 | tf_op jit(solution)/shard_map/ppermute | solution.py:155
  9.6 4.7 %collective-permute-start.5 = (bf16[256,128]{1,0:T(8,128)(2,1)S(1)}, bf16[256,128]{1,0:T(8,128)(2,1)S(1)}, u32[]{:S(2)}, u32[]{:S(2)}) collective-permute-start(bf16[256,128]{1,0:T(8,128)(2,1)S(1)} %collective-permute-done.2.refs_2_), channel_id=1, source_target_pairs={{0,4},{4,0},{8,12},{12,8},{16,20},{20,16},{24,28},{28,24},{1,5},{5... | collective-permute-start | bytes 196616 | tf_op jit(solution)/shard_map/ppermute | solution.py:155
  10.7 5.0 %collective-permute-start.4 = (bf16[256,128]{1,0:T(8,128)(2,1)S(1)}, bf16[256,128]{1,0:T(8,128)(2,1)S(1)}, u32[]{:S(2)}, u32[]{:S(2)}) collective-permute-start(bf16[256,128]{1,0:T(8,128)(2,1)S(1)} %collective-permute-done.1.refs_1_), channel_id=1, source_target_pairs={{0,4},{4,0},{8,12},{12,8},{16,20},{20,16},{24,28},{28,24},{1,5},{5... | collective-permute-start | bytes 196616 | tf_op jit(solution)/shard_map/ppermute | solution.py:155
  12.4 4.3 %collective-permute-start.6 = (bf16[256,128]{1,0:T(8,128)(2,1)S(1)}, bf16[256,128]{1,0:T(8,128)(2,1)S(1)}, u32[]{:S(2)}, u32[]{:S(2)}) collective-permute-start(bf16[256,128]{1,0:T(8,128)(2,1)S(1)} %collective-permute-done.refs_0_), channel_id=1, source_target_pairs={{0,4},{4,0},{8,12},{12,8},{16,20},{20,16},{24,28},{28,24},{1,5},{5... | collective-permute-start | bytes 196616 | tf_op jit(solution)/shard_map/ppermute | solution.py:155
  17.4 1.4 %collective-permute-start.7 = (bf16[128,512]{1,0:T(8,128)(2,1)S(1)}, bf16[128,512]{1,0:T(8,128)(2,1)S(1)}, u32[]{:S(2)}, u32[]{:S(2)}) collective-permute-start(bf16[128,512]{1,0:T(8,128)(2,1)S(1)} %get-tuple-element.41), channel_id=1, source_target_pairs={{0,1},{1,0},{2,3},{3,2},{4,5},{5,4},{6,7},{7,6},{8,9},{9,8},{10,11... | collective-permute-start | bytes 393224 | tf_op jit(solution)/shard_map/ppermute | solution.py:155
  17.9 3.3 %collective-permute-start.10 = (bf16[128,512]{1,0:T(8,128)(2,1)S(1)}, bf16[128,512]{1,0:T(8,128)(2,1)S(1)}, u32[]{:S(2)}, u32[]{:S(2)}) collective-permute-start(bf16[128,512]{1,0:T(8,128)(2,1)S(1)} %get-tuple-element.46), channel_id=1, source_target_pairs={{0,1},{1,0},{2,3},{3,2},{4,5},{5,4},{6,7},{7,6},{8,9},{9,8},{10,11... | collective-permute-start | bytes 393224 | tf_op jit(solution)/shard_map/ppermute | solution.py:155
  18.8 5.6 %collective-permute-start.9 = (bf16[128,512]{1,0:T(8,128)(2,1)S(1)}, bf16[128,512]{1,0:T(8,128)(2,1)S(1)}, u32[]{:S(2)}, u32[]{:S(2)}) collective-permute-start(bf16[128,512]{1,0:T(8,128)(2,1)S(1)} %add_convert_fusion.2), channel_id=1, source_target_pairs={{0,2},{1,3},{2,0},{3,1},{4,6},{5,7},{6,4},{7,5},{8,10},{9,11},{10,... | collective-permute-start | bytes 393224 | tf_op jit(solution)/shard_map/ppermute | solution.py:155
  21.1 6.1 %collective-permute-start.8 = (bf16[128,1024]{1,0:T(8,128)(2,1)S(1)}, bf16[128,1024]{1,0:T(8,128)(2,1)S(1)}, u32[]{:S(2)}, u32[]{:S(2)}) collective-permute-start(bf16[128,1024]{1,0:T(8,128)(2,1)S(1)} %get-tuple-element.44), channel_id=1, source_target_pairs={{0,1},{1,0},{2,3},{3,2},{4,5},{5,4},{6,7},{7,6},{8,9},{9,8},{10,11... | collective-permute-start | bytes 786440 | tf_op jit(solution)/shard_map/ppermute | solution.py:155
  21.3 6.0 %collective-permute-start.11 = (bf16[128,512]{1,0:T(8,128)(2,1)S(1)}, bf16[128,512]{1,0:T(8,128)(2,1)S(1)}, u32[]{:S(2)}, u32[]{:S(2)}) collective-permute-start(bf16[128,512]{1,0:T(8,128)(2,1)S(1)} %add_convert_fusion.1), channel_id=1, source_target_pairs={{0,2},{1,3},{2,0},{3,1},{4,6},{5,7},{6,4},{7,5},{8,10},{9,11},{10,... | collective-permute-start | bytes 393224 | tf_op jit(solution)/shard_map/ppermute | solution.py:155

commit v6 on v5

--- a/solution.py
+++ b/solution.py
@@ -23,15 +23,6 @@
 
 def exponent_scale(head_dim):
     return math.log2(math.e) / math.sqrt(head_dim)
-
-
-def pack_kernel(k_hbm, v_hbm, kv_ref, sems):
-    k_copy = pltpu.make_async_copy(k_hbm, kv_ref.at[0:BLOCK, :], sems.at[0])
-    v_copy = pltpu.make_async_copy(v_hbm, kv_ref.at[BLOCK:2 * BLOCK, :], sems.at[1])
-    k_copy.start()
-    v_copy.start()
-    k_copy.wait()
-    v_copy.wait()
 
 
 def reached_mask(parents_ref):
@@ -47,7 +38,69 @@
     return reached
 
 
-def own_block_kernel(parents_ref, q_ref, kv_ref, reached_ref, m_ref, l_ref, acc_ref):
+def pack_kernel(walk, k_hbm, v_hbm, parents_hbm, kv_ref, reached_ref, parents_ref, sems):
+    copies = [
+        pltpu.make_async_copy(parents_hbm, parents_ref, sems.at[0]),
+        pltpu.make_async_copy(k_hbm, kv_ref.at[0:BLOCK, :], sems.at[1]),
+        pltpu.make_async_copy(v_hbm, kv_ref.at[BLOCK:2 * BLOCK, :], sems.at[2]),
+    ]
+    for copy in copies:
+        copy.start()
+    copies[0].wait()
+    reached = reached_mask(parents_ref) if walk else jnp.int32(0)
+    reached_ref[...] = jnp.full(reached_ref.shape, reached, jnp.int32)
+    copies[1].wait()
+    copies[2].wait()
+
+
+def project(att, w_ref, start, width):
+    start = pl.multiple_of(start, 128)
+    return jnp.dot(att, w_ref[:, pl.ds(start, width)], preferred_element_type=jnp.float32)
+
+
+def absorb(scale, q_ref, k, v, m_ref, l_ref, acc_ref):
+    s = scores_of(k, q_ref[...])
+    m_old = m_ref[...]
+    m_new = jnp.maximum(m_old, jnp.max(s, axis=0, keepdims=True))
+    p = jnp.exp2((s - m_new) * scale)
+    factor = jnp.exp2((m_old - m_new) * scale)
+    m_ref[...] = m_new
+    l_ref[...] = l_ref[...] * factor + jnp.sum(p, axis=0, keepdims=True)
+    acc_ref[...] = acc_ref[...] * factor + weighted(v, p)
+
+
+def absorb_reached(xors, reached_ref, q_ref, kv_refs, state):
+    scale = exponent_scale(q_ref.shape[1])
+    me = lax.axis_index("ctx")
+    reached = jnp.max(reached_ref[...])
+    for other, kv_ref in zip(xors, kv_refs):
+        @pl.when((lax.shift_right_logical(reached, me ^ other) & 1) == 1)
+        def _():
+            absorb(scale, q_ref, kv_ref[0:BLOCK, :], kv_ref[BLOCK:, :], *state)
+
+
+def absorb_walk(parents_ref, q_ref, piece, state):
+    scale = exponent_scale(q_ref.shape[1])
+    me = lax.axis_index("ctx")
+
+    def visit(step, wanted):
+        block = me - step
+        hit = (block >= 0) & (block == wanted)
+        block = jnp.maximum(block, 0)
+
+        @pl.when(hit)
+        def _():
+            start = pl.multiple_of(block * 2 * BLOCK, 2 * BLOCK)
+            absorb(scale, q_ref, piece[pl.ds(start, BLOCK), :], piece[pl.ds(start + BLOCK, BLOCK), :], *state)
+
+        return jnp.where(hit, parents_ref[block], wanted)
+
+    lax.fori_loop(1, parents_ref.shape[0], visit, parents_ref[me])
+
+
+def own_block_kernel(xors, reached_ref, q_ref, kv_ref, *refs):
+    state = refs[len(xors):]
+    m_ref, l_ref, acc_ref = state
     scale = exponent_scale(q_ref.shape[1])
     s = scores_of(kv_ref[0:BLOCK, :], q_ref[...])
     key_at = lax.broadcasted_iota(jnp.int32, s.shape, 0)
@@ -58,52 +111,7 @@
     m_ref[...] = m
     l_ref[...] = jnp.sum(p, axis=0, keepdims=True)
     acc_ref[...] = weighted(kv_ref[BLOCK:, :], p)
-    reached_ref[...] = jnp.full(reached_ref.shape, reached_mask(parents_ref), jnp.int32)
-
-
-def project(att, w_ref, start, width):
-    start = pl.multiple_of(start, 128)
-    return jnp.dot(att, w_ref[:, pl.ds(start, width)], preferred_element_type=jnp.float32)
-
-
-def absorb(scale, q_ref, k, v, m_ref, l_ref, acc_ref):
-    s = scores_of(k, q_ref[...])
-    m_old = m_ref[...]
-    m_new = jnp.maximum(m_old, jnp.max(s, axis=0, keepdims=True))
-    p = jnp.exp2((s - m_new) * scale)
-    factor = jnp.exp2((m_old - m_new) * scale)
-    m_ref[...] = m_new
-    l_ref[...] = l_ref[...] * factor + jnp.sum(p, axis=0, keepdims=True)
-    acc_ref[...] = acc_ref[...] * factor + weighted(v, p)
-
-
-def absorb_reached(xors, reached_ref, q_ref, kv_refs, state):
-    scale = exponent_scale(q_ref.shape[1])
-    me = lax.axis_index("ctx")
-    reached = jnp.max(reached_ref[...])
-    for other, kv_ref in zip(xors, kv_refs):
-        @pl.when((lax.shift_right_logical(reached, me ^ other) & 1) == 1)
-        def _():
-            absorb(scale, q_ref, kv_ref[0:BLOCK, :], kv_ref[BLOCK:, :], *state)
-
-
-def absorb_walk(parents_ref, q_ref, piece, state):
-    scale = exponent_scale(q_ref.shape[1])
-    me = lax.axis_index("ctx")
-
-    def visit(step, wanted):
-        block = me - step
-        hit = (block >= 0) & (block == wanted)
-        block = jnp.maximum(block, 0)
-
-        @pl.when(hit)
-        def _():
-            start = pl.multiple_of(block * 2 * BLOCK, 2 * BLOCK)
-            absorb(scale, q_ref, piece[pl.ds(start, BLOCK), :], piece[pl.ds(start + BLOCK, BLOCK), :], *state)
-
-        return jnp.where(hit, parents_ref[block], wanted)
-
-    lax.fori_loop(1, parents_ref.shape[0], visit, parents_ref[me])
+    absorb_reached(xors, reached_ref, q_ref, refs[:len(xors)], state)
 
 
 def others_kernel(xors, reached_ref, q_ref, m_in, l_in, acc_in, *refs):
@@ -154,36 +162,39 @@
     def swap(x, axis, size, other):
         return lax.ppermute(x, axis, [(i, i ^ other) for i in range(size)])
 
-    kv = pl.pallas_call(
-        pack_kernel,
-        out_shape=jax.ShapeDtypeStruct((2 * tok_rows, head_dim), jnp.bfloat16),
-        in_specs=[hbm, hbm],
-        out_specs=vmem,
-        scratch_shapes=[pltpu.SemaphoreType.DMA((2,))],
+    kv, reached = pl.pallas_call(
+        functools.partial(pack_kernel, ctx_size == DIRECT_SIZE),
+        out_shape=(
+            jax.ShapeDtypeStruct((2 * tok_rows, head_dim), jnp.bfloat16),
+            jax.ShapeDtypeStruct((8, 128), jnp.int32),
+        ),
+        in_specs=[hbm, hbm, hbm],
+        out_specs=(vmem, vmem),
+        scratch_shapes=[pltpu.SMEM(parents.shape, jnp.int32), pltpu.SemaphoreType.DMA((3,))],
         compiler_params=params,
         cost_estimate=pl.CostEstimate(flops=8_000_000_000, bytes_accessed=130_000, transcendentals=0),
-    )(in_hbm(key_heads[:, 0, :]), in_hbm(value_heads[:, 0, :]))
+    )(in_hbm(key_heads[:, 0, :]), in_hbm(value_heads[:, 0, :]), in_hbm(parents))
+    early = []
     if ctx_size == DIRECT_SIZE:
         columns = [swap(kv, "ctx", ctx_size, other) for other in (4, 2, 6)]
+        early = [swap(kv, "ctx", ctx_size, 1)]
     q = jnp.transpose(query_heads, (1, 0, 2)).reshape(rows, head_dim)
 
-    reached, m, l, acc = pl.pallas_call(
-        own_block_kernel,
+    m, l, acc = pl.pallas_call(
+        functools.partial(own_block_kernel, (1,) * len(early)),
         out_shape=(
-            jax.ShapeDtypeStruct((8, 128), jnp.int32),
             jax.ShapeDtypeStruct((1, rows), jnp.float32),
             jax.ShapeDtypeStruct((1, rows), jnp.float32),
             jax.ShapeDtypeStruct((head_dim, rows), jnp.float32),
         ),
-        in_specs=[smem, vmem, vmem],
-        out_specs=(vmem,) * 4,
+        in_specs=[vmem] * (3 + len(early)),
+        out_specs=(vmem,) * 3,
         compiler_params=params,
-        cost_estimate=pl.CostEstimate(flops=67_000_000, bytes_accessed=1_000_000, transcendentals=130_000),
-    )(parents, q, kv)
+        cost_estimate=pl.CostEstimate(flops=130_000_000, bytes_accessed=1_000_000, transcendentals=260_000),
+    )(reached, q, kv, *early)
 
     if ctx_size == DIRECT_SIZE:
-        late, m = lax.optimization_barrier((kv, m))
-        beside = swap(late, "ctx", ctx_size, 1)
+        columns[0], m = lax.optimization_barrier((columns[0], m))
     state = (m, l, acc)
     state_shapes = tuple(jax.ShapeDtypeStruct(x.shape, x.dtype) for x in state)
     if ctx_size == DIRECT_SIZE:
@@ -203,7 +214,7 @@
                 cost_estimate=pl.CostEstimate(flops=270_000_000, bytes_accessed=1_000_000, transcendentals=500_000),
             )(reached, q, *state, *arrived)
 
-        state = absorbed(state, (4, 2, 6, 1), [*columns, beside])
+        state = absorbed(state, (4, 2, 6), columns)
         state = absorbed(state, (3, 7), pairs[1:])
         xors, pieces, tree, tree_spec = (5,), pairs[:1], reached, vmem
     else:

time: 28.2 us -> 28.8 us (1.021)
  starting transfers between devices: 13.8 us -> 14.4 us
  waiting for transfers between devices: 8.94 us -> 9.49 us
  Pallas kernels: 4.31 us -> 3.78 us
    ppermute x12, starting transfers between devices: 13.8 us -> 14.4 us  [swap(): return lax.ppermute(x, axis, [(i, i ^ other) for i in range(size)])]
    ppermute x12, waiting for transfers between devices: 8.94 us -> 9.49 us  [swap(): return lax.ppermute(x, axis, [(i, i ^ other) for i in range(size)])]
    pallas_call x2, Pallas kernels: 1.99 us -> 1.47 us  [the longest x1 0.95 us: shards(): pl.pallas_call(functools.partial(pack_kernel, ctx_size == DIRECT_SIZE), o...]
  transfers between devices with their start and end apart: 12 -> 12, of which waited for: 7 -> 6; matrix products, arithmetic and copies ran while one was open for 0% -> 0% of each run, Pallas kernels for 10% -> 7%
where the time goes in v6:
time: 28.8 us; the launch traced here: 28.7 us
  starting transfers between devices  14.4 us (50%)
  waiting for transfers between devices  9.49 us (33%)
  Pallas kernels  3.78 us (13%)
  other arithmetic  0.86 us (3%)
    ppermute x12, starting transfers between devices, swap(): return lax.ppermute(x, axis, [(i, i ^ other) for i in range(size)])  14.4 us
    ppermute x12, waiting for transfers between devices, swap(): return lax.ppermute(x, axis, [(i, i ^ other) for i in range(size)])  9.49 us
    pallas_call x2, Pallas kernels, projected(): pl.pallas_call(functools.partial(project_pair, flip, part), out_shape=sha...  1.18 us
    pallas_call x1, Pallas kernels, shards(): pl.pallas_call(functools.partial(pack_kernel, ctx_size == DIRECT_SIZE), o...  0.95 us
    convert_element_type x1, other arithmetic, shards(): (keep_near + near_in.astype(jnp.float32) + from_far).astype(jnp.bfloat16)  0.8 us
    pallas_call x1, Pallas kernels, shards(): pl.pallas_call(functools.partial(last_kernel, xors), out_shape=(jax.Shape...  0.7 us
  transfers between devices with their start and end apart: 12, of which 6 were waited for; matrix products, arithmetic and copies ran while one was open for 0% of the time, Pallas kernels for 7%

profile of v6, /device:TPU:0, one launch (start us, length us, event | category | flops | bytes accessed | tf_op | source)
XLA Modules:
  0.0 28.7 jit_solution(132551482017652435)
XLA Ops:
  0.0 0.0 slice-start
  0.0 0.0 copy-start
  0.0 0.0 slice-start.1
  0.0 1.0 %shard_map.55 = (bf16[256,128]{1,0:T(8,128)(2,1)S(1)}, s32[8,128]{1,0:T(8,128)S(1)}) custom-call(bf16[128,128]{1,0:T(8,128)(2,1)} %bitcast.11, bf16[128,128]{1,0:T(8,128)(2,1)} %bitcast.12, s32[8]{0:T(128)} %parents_hbm.1), custom_call_target="tpu_custom_call" | custom-call | flops 8000000000 | bytes 130000 | tf_op jit(solution)/shard_map/pallas_call | solution.py:165
  1.0 5.1 %collective-permute-start.3 = (bf16[256,128]{1,0:T(8,128)(2,1)S(1)}, bf16[256,128]{1,0:T(8,128)(2,1)S(1)}, u32[]{:S(2)}, u32[]{:S(2)}) collective-permute-start(bf16[256,128]{1,0:T(8,128)(2,1)S(1)} %get-tuple-element.28.kv_ref), channel_id=1, source_target_pairs={{0,24},{4,28},{8,16},{12,20},{16,8},{20,12},{24,0},{28,4},{1,25},{... | collective-permute-start | bytes 196616 | tf_op jit(solution)/shard_map/ppermute | solution.py:163
  6.1 0.0 collective-permute-start.2
  6.1 1.5 %collective-permute-start.1 = (bf16[256,128]{1,0:T(8,128)(2,1)S(1)}, bf16[256,128]{1,0:T(8,128)(2,1)S(1)}, u32[]{:S(2)}, u32[]{:S(2)}) collective-permute-start(bf16[256,128]{1,0:T(8,128)(2,1)S(1)} %get-tuple-element.28.kv_ref), channel_id=1, source_target_pairs={{0,4},{4,0},{8,12},{12,8},{16,20},{20,16},{24,28},{28,24},{1,5},{5... | collective-permute-start | bytes 196616 | tf_op jit(solution)/shard_map/ppermute | solution.py:163
  7.6 0.8 %collective-permute-start = (bf16[256,128]{1,0:T(8,128)(2,1)S(1)}, bf16[256,128]{1,0:T(8,128)(2,1)S(1)}, u32[]{:S(2)}, u32[]{:S(2)}) collective-permute-start(bf16[256,128]{1,0:T(8,128)(2,1)S(1)} %get-tuple-element.28.kv_ref), channel_id=1, source_target_pairs={{0,16},{4,20},{8,24},{12,28},{16,0},{20,4},{24,8},{28,12},{1,17},{... | collective-permute-start | bytes 196616 | tf_op jit(solution)/shard_map/ppermute | solution.py:163
  8.4 0.6 %collective-permute-done.3.refs_2_ = bf16[256,128]{1,0:T(8,128)(2,1)S(1)} collective-permute-done((bf16[256,128]{1,0:T(8,128)(2,1)S(1)}, bf16[256,128]{1,0:T(8,128)(2,1)S(1)}, u32[]{:S(2)}, u32[]{:S(2)}) %collective-permute-start.3) | collective-permute-done | bytes 65568 | tf_op jit(solution)/shard_map/ppermute | solution.py:163
  9.0 1.5 %collective-permute-start.5 = (bf16[256,128]{1,0:T(8,128)(2,1)S(1)}, bf16[256,128]{1,0:T(8,128)(2,1)S(1)}, u32[]{:S(2)}, u32[]{:S(2)}) collective-permute-start(bf16[256,128]{1,0:T(8,128)(2,1)S(1)} %collective-permute-done.3.refs_2_), channel_id=1, source_target_pairs={{0,4},{4,0},{8,12},{12,8},{16,20},{20,16},{24,28},{28,24},{1,5},{5... | collective-permute-start | bytes 196616 | tf_op jit(solution)/shard_map/ppermute | solution.py:163
  10.5 0.0 collective-permute-done.2.refs_1_
  10.5 1.9 %collective-permute-start.4 = (bf16[256,128]{1,0:T(8,128)(2,1)S(1)}, bf16[256,128]{1,0:T(8,128)(2,1)S(1)}, u32[]{:S(2)}, u32[]{:S(2)}) collective-permute-start(bf16[256,128]{1,0:T(8,128)(2,1)S(1)} %collective-permute-done.2.refs_1_), channel_id=1, source_target_pairs={{0,4},{4,0},{8,12},{12,8},{16,20},{20,16},{24,28},{28,24},{1,5},{5... | collective-permute-start | bytes 196616 | tf_op jit(solution)/shard_map/ppermute | solution.py:163
  12.4 0.0 copy-done
  12.4 0.0 collective-permute-done.1.refs_0_
  12.4 0.5 %shard_map.56 = (f32[1,1024]{1,0:T(1,128)S(1)}, f32[1,1024]{1,0:T(1,128)S(1)}, f32[128,1024]{1,0:T(8,128)S(1)}) custom-call(s32[8,128]{1,0:T(8,128)S(1)} %get-tuple-element.27.reached_ref.tree_ref, bf16[1024,128]{1,0:T(8,128)(2,1)S(1)} %bitcast.6, bf16[256,128]{1,0:T(8,128)(2,1)S(1)} %get-tuple-element.28.kv_ref, ...), custom_call_target="tpu_custom_call" | custom-call | flops 130000000 | bytes 1000000 | tf_op jit(solution)/shard_map/pallas_call | solution.py:183
  13.0 0.0 collective-permute-done.refs_0_
  13.0 0.7 %collective-permute-start.6 = (bf16[256,128]{1,0:T(8,128)(2,1)S(1)}, bf16[256,128]{1,0:T(8,128)(2,1)S(1)}, u32[]{:S(2)}, u32[]{:S(2)}) collective-permute-start(bf16[256,128]{1,0:T(8,128)(2,1)S(1)} %collective-permute-done.refs_0_), channel_id=1, source_target_pairs={{0,4},{4,0},{8,12},{12,8},{16,20},{20,16},{24,28},{28,24},{1,5},{5... | collective-permute-start | bytes 196616 | tf_op jit(solution)/shard_map/ppermute | solution.py:163
  13.7 0.2 shard_map.57
  13.9 0.0 collective-permute-done.5.refs_1_
  13.9 0.9 %collective-permute-done.4.refs_0_ = bf16[256,128]{1,0:T(8,128)(2,1)S(1)} collective-permute-done((bf16[256,128]{1,0:T(8,128)(2,1)S(1)}, bf16[256,128]{1,0:T(8,128)(2,1)S(1)}, u32[]{:S(2)}, u32[]{:S(2)}) %collective-permute-start.4) | collective-permute-done | bytes 65568 | tf_op jit(solution)/shard_map/ppermute | solution.py:163
  14.9 0.2 shard_map.58
  15.1 2.2 %collective-permute-done.6.refs_0_ = bf16[256,128]{1,0:T(8,128)(2,1)S(1)} collective-permute-done((bf16[256,128]{1,0:T(8,128)(2,1)S(1)}, bf16[256,128]{1,0:T(8,128)(2,1)S(1)}, u32[]{:S(2)}, u32[]{:S(2)}) %collective-permute-start.6) | collective-permute-done | bytes 65568 | tf_op jit(solution)/shard_map/ppermute | solution.py:163
  17.3 0.0 slice-done
  17.3 0.0 slice-done.1
  17.3 0.7 %shard_map.59 = (bf16[128,1024]{1,0:T(8,128)(2,1)S(1)}, bf16[128,512]{1,0:T(8,128)(2,1)S(1)}, f32[128,512]{1,0:T(8,128)S(1)}, f32[1,1024]{1,0:T(1,128)S(1)}, f32...) custom-call(s32[8,128]{1,0:T(8,128)S(1)} %get-tuple-element.27.reached_ref, ...), custom_call_target="tpu_custom_call", output_to_operand_aliasing={{3}: (2, {}), {4}: (3, {}), {5}: (4, {})} | custom-call | flops 1000000000 | bytes 10000000 | tf_op jit(solution)/shard_map/pallas_call | solution.py:228
  18.0 0.1 collective-permute-start.7
  18.1 0.5 %shard_map.61 = (bf16[128,512]{1,0:T(8,128)(2,1)S(1)}, f32[128,512]{1,0:T(8,128)S(1)}) custom-call(bf16[128,1024]{1,0:T(8,128)(2,1)S(1)} %get-tuple-element.44.att_ref, bf16[1024,4096]{1,0:T(8,128)(2,1)S(1)} %bitcast.5), custom_call_target="tpu_custom_call" | custom-call | flops 540000000 | bytes 4000000 | tf_op jit(solution)/shard_map/pallas_call | solution.py:239
  18.6 0.6 %collective-permute-start.10 = (bf16[128,512]{1,0:T(8,128)(2,1)S(1)}, bf16[128,512]{1,0:T(8,128)(2,1)S(1)}, u32[]{:S(2)}, u32[]{:S(2)}) collective-permute-start(bf16[128,512]{1,0:T(8,128)(2,1)S(1)} %get-tuple-element.48), channel_id=1, source_target_pairs={{0,1},{1,0},{2,3},{3,2},{4,5},{5,4},{6,7},{7,6},{8,9},{9,8},{10,11... | collective-permute-start | bytes 393224 | tf_op jit(solution)/shard_map/ppermute | solution.py:163
  19.1 0.3 %collective-permute-done.7 = bf16[128,512]{1,0:T(8,128)(2,1)S(1)} collective-permute-done((bf16[128,512]{1,0:T(8,128)(2,1)S(1)}, bf16[128,512]{1,0:T(8,128)(2,1)S(1)}, u32[]{:S(2)}, u32[]{:S(2)}) %collective-permute-start.7) | collective-permute-done | bytes 131104 | tf_op jit(solution)/shard_map/ppermute | solution.py:163
  19.5 1.6 %collective-permute-start.9 = (bf16[128,512]{1,0:T(8,128)(2,1)S(1)}, bf16[128,512]{1,0:T(8,128)(2,1)S(1)}, u32[]{:S(2)}, u32[]{:S(2)}) collective-permute-start(bf16[128,512]{1,0:T(8,128)(2,1)S(1)} %add_convert_fusion.2), channel_id=1, source_target_pairs={{0,2},{1,3},{2,0},{3,1},{4,6},{5,7},{6,4},{7,5},{8,10},{9,11},{10,... | collective-permute-start | bytes 393224 | tf_op jit(solution)/shard_map/ppermute | solution.py:163
  21.0 0.7 %shard_map.60 = (bf16[128,1024]{1,0:T(8,128)(2,1)S(1)}, f32[128,1024]{1,0:T(8,128)S(1)}) custom-call(bf16[128,1024]{1,0:T(8,128)(2,1)S(1)} %get-tuple-element.44.att_ref, bf16[1024,4096]{1,0:T(8,128)(2,1)S(1)} %bitcast.5), custom_call_target="tpu_custom_call" | custom-call | flops 540000000 | bytes 4000000 | tf_op jit(solution)/shard_map/pallas_call | solution.py:239
  21.7 0.1 collective-permute-start.8
  21.8 0.0 collective-permute-done.10
  21.9 0.6 %collective-permute-start.11 = (bf16[128,512]{1,0:T(8,128)(2,1)S(1)}, bf16[128,512]{1,0:T(8,128)(2,1)S(1)}, u32[]{:S(2)}, u32[]{:S(2)}) collective-permute-start(bf16[128,512]{1,0:T(8,128)(2,1)S(1)} %add_convert_fusion.1), channel_id=1, source_target_pairs={{0,2},{1,3},{2,0},{3,1},{4,6},{5,7},{6,4},{7,5},{8,10},{9,11},{10,... | collective-permute-start | bytes 393224 | tf_op jit(solution)/shard_map/ppermute | solution.py:163
  22.5 2.6 %collective-permute-done.9 = bf16[128,512]{1,0:T(8,128)(2,1)S(1)} collective-permute-done((bf16[128,512]{1,0:T(8,128)(2,1)S(1)}, bf16[128,512]{1,0:T(8,128)(2,1)S(1)}, u32[]{:S(2)}, u32[]{:S(2)}) %collective-permute-start.9) | collective-permute-done | bytes 131104 | tf_op jit(solution)/shard_map/ppermute | solution.py:163
  25.1 2.8 %collective-permute-done.11 = bf16[128,512]{1,0:T(8,128)(2,1)S(1)} collective-permute-done((bf16[128,512]{1,0:T(8,128)(2,1)S(1)}, bf16[128,512]{1,0:T(8,128)(2,1)S(1)}, u32[]{:S(2)}, u32[]{:S(2)}) %collective-permute-start.11) | collective-permute-done | bytes 131104 | tf_op jit(solution)/shard_map/ppermute | solution.py:163
  27.9 0.0 collective-permute-done.8
  27.9 0.8 %add_convert_fusion = bf16[128,1024]{1,0:T(8,128)(2,1)} fusion(f32[128,1024]{1,0:T(8,128)S(1)} %get-tuple-element.45, bf16[128,1024]{1,0:T(8,128)(2,1)S(1)} %collective-permute-done.8, bf16[128,512]{1,0:T(8,128)(2,1)S(1)} %collective-permute-done.11, bf16[128,512]{1,0:T(8,128)(2,1)S(1)} %collective-permute-done.9), kind=kLoop, calls=%fused_computation | loop fusion | flops 1048576 | bytes 1310720 | tf_op jit(solution)/shard_map/convert_element_type | solution.py:267
  (4 shorter events, 0.1 us)
Async XLA Ops:
  0.0 17.3 %slice-start = ((s8[8388608]{0:T(1024)(128)(4,1)}), s8[4194304]{0:T(1024)(128)(4,1)S(1)}, s32[]{:S(2)}) async-start(s8[8388608]{0:T(1024)(128)(4,1)} %bitcast.4), calls=%async_computation | async-start | bytes 8388608
  0.0 12.4 %copy-start = (bf16[128,8,128]{2,1,0:T(8,128)(2,1)S(1)}, bf16[128,8,128]{2,1,0:T(8,128)(2,1)}, u32[]{:S(2)}) copy-start(bf16[128,8,128]{2,1,0:T(8,128)(2,1)} %param.5) | copy-start | bytes 786436
  0.0 17.3 %slice-start.1 = ((s8[8388608]{0:T(1024)(128)(4,1)}), s8[4194304]{0:T(1024)(128)(4,1)S(1)}, s32[]{:S(2)}) async-start(s8[8388608]{0:T(1024)(128)(4,1)} %bitcast.4), calls=%async_computation.1 | async-start | bytes 8388608
  1.0 8.0 %collective-permute-start.3 = (bf16[256,128]{1,0:T(8,128)(2,1)S(1)}, bf16[256,128]{1,0:T(8,128)(2,1)S(1)}, u32[]{:S(2)}, u32[]{:S(2)}) collective-permute-start(bf16[256,128]{1,0:T(8,128)(2,1)S(1)} %get-tuple-element.28.kv_ref), channel_id=1, source_target_pairs={{0,24},{4,28},{8,16},{12,20},{16,8},{20,12},{24,0},{28,4},{1,25},{... | collective-permute-start | bytes 196616 | tf_op jit(solution)/shard_map/ppermute | solution.py:163
  6.1 4.4 %collective-permute-start.2 = (bf16[256,128]{1,0:T(8,128)(2,1)S(1)}, bf16[256,128]{1,0:T(8,128)(2,1)S(1)}, u32[]{:S(2)}, u32[]{:S(2)}) collective-permute-start(bf16[256,128]{1,0:T(8,128)(2,1)S(1)} %get-tuple-element.28.kv_ref), channel_id=1, source_target_pairs={{0,8},{4,12},{8,0},{12,4},{16,24},{20,28},{24,16},{28,20},{1,9},{5... | collective-permute-start | bytes 196616 | tf_op jit(solution)/shard_map/ppermute | solution.py:163
  6.1 6.3 %collective-permute-start.1 = (bf16[256,128]{1,0:T(8,128)(2,1)S(1)}, bf16[256,128]{1,0:T(8,128)(2,1)S(1)}, u32[]{:S(2)}, u32[]{:S(2)}) collective-permute-start(bf16[256,128]{1,0:T(8,128)(2,1)S(1)} %get-tuple-element.28.kv_ref), channel_id=1, source_target_pairs={{0,4},{4,0},{8,12},{12,8},{16,20},{20,16},{24,28},{28,24},{1,5},{5... | collective-permute-start | bytes 196616 | tf_op jit(solution)/shard_map/ppermute | solution.py:163
  7.6 5.4 %collective-permute-start = (bf16[256,128]{1,0:T(8,128)(2,1)S(1)}, bf16[256,128]{1,0:T(8,128)(2,1)S(1)}, u32[]{:S(2)}, u32[]{:S(2)}) collective-permute-start(bf16[256,128]{1,0:T(8,128)(2,1)S(1)} %get-tuple-element.28.kv_ref), channel_id=1, source_target_pairs={{0,16},{4,20},{8,24},{12,28},{16,0},{20,4},{24,8},{28,12},{1,17},{... | collective-permute-start | bytes 196616 | tf_op jit(solution)/shard_map/ppermute | solution.py:163
  9.0 4.9 %collective-permute-start.5 = (bf16[256,128]{1,0:T(8,128)(2,1)S(1)}, bf16[256,128]{1,0:T(8,128)(2,1)S(1)}, u32[]{:S(2)}, u32[]{:S(2)}) collective-permute-start(bf16[256,128]{1,0:T(8,128)(2,1)S(1)} %collective-permute-done.3.refs_2_), channel_id=1, source_target_pairs={{0,4},{4,0},{8,12},{12,8},{16,20},{20,16},{24,28},{28,24},{1,5},{5... | collective-permute-start | bytes 196616 | tf_op jit(solution)/shard_map/ppermute | solution.py:163
  10.5 4.3 %collective-permute-start.4 = (bf16[256,128]{1,0:T(8,128)(2,1)S(1)}, bf16[256,128]{1,0:T(8,128)(2,1)S(1)}, u32[]{:S(2)}, u32[]{:S(2)}) collective-permute-start(bf16[256,128]{1,0:T(8,128)(2,1)S(1)} %collective-permute-done.2.refs_1_), channel_id=1, source_target_pairs={{0,4},{4,0},{8,12},{12,8},{16,20},{20,16},{24,28},{28,24},{1,5},{5... | collective-permute-start | bytes 196616 | tf_op jit(solution)/shard_map/ppermute | solution.py:163
  13.0 4.3 %collective-permute-start.6 = (bf16[256,128]{1,0:T(8,128)(2,1)S(1)}, bf16[256,128]{1,0:T(8,128)(2,1)S(1)}, u32[]{:S(2)}, u32[]{:S(2)}) collective-permute-start(bf16[256,128]{1,0:T(8,128)(2,1)S(1)} %collective-permute-done.refs_0_), channel_id=1, source_target_pairs={{0,4},{4,0},{8,12},{12,8},{16,20},{20,16},{24,28},{28,24},{1,5},{5... | collective-permute-start | bytes 196616 | tf_op jit(solution)/shard_map/ppermute | solution.py:163
  18.0 1.4 %collective-permute-start.7 = (bf16[128,512]{1,0:T(8,128)(2,1)S(1)}, bf16[128,512]{1,0:T(8,128)(2,1)S(1)}, u32[]{:S(2)}, u32[]{:S(2)}) collective-permute-start(bf16[128,512]{1,0:T(8,128)(2,1)S(1)} %get-tuple-element.43), channel_id=1, source_target_pairs={{0,1},{1,0},{2,3},{3,2},{4,5},{5,4},{6,7},{7,6},{8,9},{9,8},{10,11... | collective-permute-start | bytes 393224 | tf_op jit(solution)/shard_map/ppermute | solution.py:163
  18.6 3.3 %collective-permute-start.10 = (bf16[128,512]{1,0:T(8,128)(2,1)S(1)}, bf16[128,512]{1,0:T(8,128)(2,1)S(1)}, u32[]{:S(2)}, u32[]{:S(2)}) collective-permute-start(bf16[128,512]{1,0:T(8,128)(2,1)S(1)} %get-tuple-element.48), channel_id=1, source_target_pairs={{0,1},{1,0},{2,3},{3,2},{4,5},{5,4},{6,7},{7,6},{8,9},{9,8},{10,11... | collective-permute-start | bytes 393224 | tf_op jit(solution)/shard_map/ppermute | solution.py:163
  19.5 5.6 %collective-permute-start.9 = (bf16[128,512]{1,0:T(8,128)(2,1)S(1)}, bf16[128,512]{1,0:T(8,128)(2,1)S(1)}, u32[]{:S(2)}, u32[]{:S(2)}) collective-permute-start(bf16[128,512]{1,0:T(8,128)(2,1)S(1)} %add_convert_fusion.2), channel_id=1, source_target_pairs={{0,2},{1,3},{2,0},{3,1},{4,6},{5,7},{6,4},{7,5},{8,10},{9,11},{10,... | collective-permute-start | bytes 393224 | tf_op jit(solution)/shard_map/ppermute | solution.py:163
  21.7 6.1 %collective-permute-start.8 = (bf16[128,1024]{1,0:T(8,128)(2,1)S(1)}, bf16[128,1024]{1,0:T(8,128)(2,1)S(1)}, u32[]{:S(2)}, u32[]{:S(2)}) collective-permute-start(bf16[128,1024]{1,0:T(8,128)(2,1)S(1)} %get-tuple-element.46), channel_id=1, source_target_pairs={{0,1},{1,0},{2,3},{3,2},{4,5},{5,4},{6,7},{7,6},{8,9},{9,8},{10,11... | collective-permute-start | bytes 786440 | tf_op jit(solution)/shard_map/ppermute | solution.py:163
  21.9 6.0 %collective-permute-start.11 = (bf16[128,512]{1,0:T(8,128)(2,1)S(1)}, bf16[128,512]{1,0:T(8,128)(2,1)S(1)}, u32[]{:S(2)}, u32[]{:S(2)}) collective-permute-start(bf16[128,512]{1,0:T(8,128)(2,1)S(1)} %add_convert_fusion.1), channel_id=1, source_target_pairs={{0,2},{1,3},{2,0},{3,1},{4,6},{5,7},{6,4},{7,5},{8,10},{9,11},{10,... | collective-permute-start | bytes 393224 | tf_op jit(solution)/shard_map/ppermute | solution.py:163

commit v7 on v6

--- a/solution.py
+++ b/solution.py
@@ -174,14 +174,17 @@
         compiler_params=params,
         cost_estimate=pl.CostEstimate(flops=8_000_000_000, bytes_accessed=130_000, transcendentals=0),
     )(in_hbm(key_heads[:, 0, :]), in_hbm(value_heads[:, 0, :]), in_hbm(parents))
-    early = []
     if ctx_size == DIRECT_SIZE:
         columns = [swap(kv, "ctx", ctx_size, other) for other in (4, 2, 6)]
-        early = [swap(kv, "ctx", ctx_size, 1)]
+        beside = swap(kv, "ctx", ctx_size, 1)
+        pairs = [swap(x, "ctx", ctx_size, 1) for x in columns]
+        early, early_xors = [beside, *columns], (1, 4, 2, 6)
+    else:
+        early, early_xors = [], ()
     q = jnp.transpose(query_heads, (1, 0, 2)).reshape(rows, head_dim)
 
     m, l, acc = pl.pallas_call(
-        functools.partial(own_block_kernel, (1,) * len(early)),
+        functools.partial(own_block_kernel, early_xors),
         out_shape=(
             jax.ShapeDtypeStruct((1, rows), jnp.float32),
             jax.ShapeDtypeStruct((1, rows), jnp.float32),
@@ -193,16 +196,9 @@
         cost_estimate=pl.CostEstimate(flops=130_000_000, bytes_accessed=1_000_000, transcendentals=260_000),
     )(reached, q, kv, *early)
 
-    if ctx_size == DIRECT_SIZE:
-        columns[0], m = lax.optimization_barrier((columns[0], m))
     state = (m, l, acc)
     state_shapes = tuple(jax.ShapeDtypeStruct(x.shape, x.dtype) for x in state)
     if ctx_size == DIRECT_SIZE:
-        late, m = lax.optimization_barrier((kv, m))
-        state = (m, l, acc)
-        beside = swap(late, "ctx", ctx_size, 1)
-        pairs = [swap(x, "ctx", ctx_size, 1) for x in columns]
-
         def absorbed(state, xors, arrived):
             return pl.pallas_call(
                 functools.partial(others_kernel, xors),
@@ -214,7 +210,6 @@
                 cost_estimate=pl.CostEstimate(flops=270_000_000, bytes_accessed=1_000_000, transcendentals=500_000),
             )(reached, q, *state, *arrived)
 
-        state = absorbed(state, (4, 2, 6), columns)
         state = absorbed(state, (3, 7), pairs[1:])
         xors, pieces, tree, tree_spec = (5,), pairs[:1], reached, vmem
     else:

time: 28.8 us -> 28.2 us (0.979)
  waiting for transfers between devices: 9.49 us -> 9.17 us
    ppermute x12, waiting for transfers between devices: 9.49 us -> 9.17 us  [swap(): return lax.ppermute(x, axis, [(i, i ^ other) for i in range(size)])]
  transfers between devices with their start and end apart: 12 -> 12, of which waited for: 6 -> 7; matrix products, arithmetic and copies ran while one was open for 0% -> 0% of each run, Pallas kernels for 7% -> 7%
where the time goes in v7:
time: 28.2 us; the launch traced here: 28.1 us
  starting transfers between devices  14.3 us (51%)
  waiting for transfers between devices  9.17 us (33%)
  Pallas kernels  3.59 us (13%)
  other arithmetic  0.87 us (3%)
    ppermute x12, starting transfers between devices, swap(): return lax.ppermute(x, axis, [(i, i ^ other) for i in range(size)])  14.3 us
    ppermute x12, waiting for transfers between devices, swap(): return lax.ppermute(x, axis, [(i, i ^ other) for i in range(size)])  9.17 us
    pallas_call x2, Pallas kernels, projected(): pl.pallas_call(functools.partial(project_pair, flip, part), out_shape=sha...  1.18 us
    pallas_call x1, Pallas kernels, shards(): pl.pallas_call(functools.partial(pack_kernel, ctx_size == DIRECT_SIZE), o...  0.95 us
    convert_element_type x1, other arithmetic, shards(): (keep_near + near_in.astype(jnp.float32) + from_far).astype(jnp.bfloat16)  0.8 us
    pallas_call x1, Pallas kernels, shards(): pl.pallas_call(functools.partial(last_kernel, xors), out_shape=(jax.Shape...  0.71 us
  transfers between devices with their start and end apart: 12, of which 7 were waited for; matrix products, arithmetic and copies ran while one was open for 0% of the time, Pallas kernels for 7%

profile of v7, /device:TPU:0, one launch (start us, length us, event | category | flops | bytes accessed | tf_op | source)
XLA Modules:
  0.0 28.1 jit_solution(2744769018079926767)
XLA Ops:
  0.0 0.0 copy-start.1
  0.0 0.0 copy-start
  0.0 0.9 %shard_map.55 = (bf16[256,128]{1,0:T(8,128)(2,1)S(1)}, s32[8,128]{1,0:T(8,128)S(1)}) custom-call(bf16[128,128]{1,0:T(8,128)(2,1)} %bitcast.8, bf16[128,128]{1,0:T(8,128)(2,1)} %bitcast.9, s32[8]{0:T(128)} %parents_hbm.1), custom_call_target="tpu_custom_call" | custom-call | flops 8000000000 | bytes 130000 | tf_op jit(solution)/shard_map/pallas_call | solution.py:165
  1.0 5.1 %collective-permute-start.3 = (bf16[256,128]{1,0:T(8,128)(2,1)S(1)}, bf16[256,128]{1,0:T(8,128)(2,1)S(1)}, u32[]{:S(2)}, u32[]{:S(2)}) collective-permute-start(bf16[256,128]{1,0:T(8,128)(2,1)S(1)} %get-tuple-element.22.kv_ref), channel_id=1, source_target_pairs={{0,24},{4,28},{8,16},{12,20},{16,8},{20,12},{24,0},{28,4},{1,25},{... | collective-permute-start | bytes 196616 | tf_op jit(solution)/shard_map/ppermute | solution.py:163
  6.1 0.0 collective-permute-start.2
  6.1 0.6 %collective-permute-start.1 = (bf16[256,128]{1,0:T(8,128)(2,1)S(1)}, bf16[256,128]{1,0:T(8,128)(2,1)S(1)}, u32[]{:S(2)}, u32[]{:S(2)}) collective-permute-start(bf16[256,128]{1,0:T(8,128)(2,1)S(1)} %get-tuple-element.22.kv_ref), channel_id=1, source_target_pairs={{0,16},{4,20},{8,24},{12,28},{16,0},{20,4},{24,8},{28,12},{1,17},{... | collective-permute-start | bytes 196616 | tf_op jit(solution)/shard_map/ppermute | solution.py:163
  6.7 1.7 %collective-permute-start = (bf16[256,128]{1,0:T(8,128)(2,1)S(1)}, bf16[256,128]{1,0:T(8,128)(2,1)S(1)}, u32[]{:S(2)}, u32[]{:S(2)}) collective-permute-start(bf16[256,128]{1,0:T(8,128)(2,1)S(1)} %get-tuple-element.22.kv_ref), channel_id=1, source_target_pairs={{0,4},{4,0},{8,12},{12,8},{16,20},{20,16},{24,28},{28,24},{1,5},{5... | collective-permute-start | bytes 196616 | tf_op jit(solution)/shard_map/ppermute | solution.py:163
  8.4 0.6 %collective-permute-done.3.refs_3_ = bf16[256,128]{1,0:T(8,128)(2,1)S(1)} collective-permute-done((bf16[256,128]{1,0:T(8,128)(2,1)S(1)}, bf16[256,128]{1,0:T(8,128)(2,1)S(1)}, u32[]{:S(2)}, u32[]{:S(2)}) %collective-permute-start.3) | collective-permute-done | bytes 65568 | tf_op jit(solution)/shard_map/ppermute | solution.py:163
  9.0 1.5 %collective-permute-start.5 = (bf16[256,128]{1,0:T(8,128)(2,1)S(1)}, bf16[256,128]{1,0:T(8,128)(2,1)S(1)}, u32[]{:S(2)}, u32[]{:S(2)}) collective-permute-start(bf16[256,128]{1,0:T(8,128)(2,1)S(1)} %collective-permute-done.3.refs_3_), channel_id=1, source_target_pairs={{0,4},{4,0},{8,12},{12,8},{16,20},{20,16},{24,28},{28,24},{1,5},{5... | collective-permute-start | bytes 196616 | tf_op jit(solution)/shard_map/ppermute | solution.py:163
  10.5 0.2 collective-permute-done.2.refs_2_
  10.7 1.7 %collective-permute-start.4 = (bf16[256,128]{1,0:T(8,128)(2,1)S(1)}, bf16[256,128]{1,0:T(8,128)(2,1)S(1)}, u32[]{:S(2)}, u32[]{:S(2)}) collective-permute-start(bf16[256,128]{1,0:T(8,128)(2,1)S(1)} %collective-permute-done.2.refs_2_), channel_id=1, source_target_pairs={{0,4},{4,0},{8,12},{12,8},{16,20},{20,16},{24,28},{28,24},{1,5},{5... | collective-permute-start | bytes 196616 | tf_op jit(solution)/shard_map/ppermute | solution.py:163
  12.4 0.0 collective-permute-done.1.refs_1_
  12.4 0.8 %collective-permute-start.6 = (bf16[256,128]{1,0:T(8,128)(2,1)S(1)}, bf16[256,128]{1,0:T(8,128)(2,1)S(1)}, u32[]{:S(2)}, u32[]{:S(2)}) collective-permute-start(bf16[256,128]{1,0:T(8,128)(2,1)S(1)} %collective-permute-done.1.refs_1_), channel_id=1, source_target_pairs={{0,4},{4,0},{8,12},{12,8},{16,20},{20,16},{24,28},{28,24},{1,5},{5... | collective-permute-start | bytes 196616 | tf_op jit(solution)/shard_map/ppermute | solution.py:163
  13.2 0.0 copy-done.1
  13.3 0.0 collective-permute-done.refs_0_
  13.3 0.5 %shard_map.56 = (f32[1,1024]{1,0:T(1,128)S(1)}, f32[1,1024]{1,0:T(1,128)S(1)}, f32[128,1024]{1,0:T(8,128)S(1)}) custom-call(s32[8,128]{1,0:T(8,128)S(1)} %get-tuple-element.21.reached_ref.tree_ref, bf16[1024,128]{1,0:T(8,128)(2,1)S(1)} %bitcast.4, bf16[256,128]{1,0:T(8,128)(2,1)S(1)} %get-tuple-element.22.kv_ref, ...), custom_call_target="tpu_custom_call" | custom-call | flops 130000000 | bytes 1000000 | tf_op jit(solution)/shard_map/pallas_call | solution.py:186
  13.8 0.0 collective-permute-done.5.refs_1_
  13.8 1.9 %collective-permute-done.4.refs_0_ = bf16[256,128]{1,0:T(8,128)(2,1)S(1)} collective-permute-done((bf16[256,128]{1,0:T(8,128)(2,1)S(1)}, bf16[256,128]{1,0:T(8,128)(2,1)S(1)}, u32[]{:S(2)}, u32[]{:S(2)}) %collective-permute-start.4) | collective-permute-done | bytes 65568 | tf_op jit(solution)/shard_map/ppermute | solution.py:163
  15.7 0.2 shard_map.57
  15.9 0.7 %collective-permute-done.6.refs_0_ = bf16[256,128]{1,0:T(8,128)(2,1)S(1)} collective-permute-done((bf16[256,128]{1,0:T(8,128)(2,1)S(1)}, bf16[256,128]{1,0:T(8,128)(2,1)S(1)}, u32[]{:S(2)}, u32[]{:S(2)}) %collective-permute-start.6) | collective-permute-done | bytes 65568 | tf_op jit(solution)/shard_map/ppermute | solution.py:163
  16.7 0.0 copy-done
  16.7 0.7 %shard_map.58 = (bf16[128,1024]{1,0:T(8,128)(2,1)S(1)}, bf16[128,512]{1,0:T(8,128)(2,1)S(1)}, f32[128,512]{1,0:T(8,128)S(1)}, f32[1,1024]{1,0:T(1,128)S(1)}, f32...) custom-call(s32[8,128]{1,0:T(8,128)S(1)} %get-tuple-element.21.reached_ref, ...), custom_call_target="tpu_custom_call", output_to_operand_aliasing={{3}: (2, {}), {4}: (3, {}), {5}: (4, {})} | custom-call | flops 1000000000 | bytes 10000000 | tf_op jit(solution)/shard_map/pallas_call | solution.py:223
  17.4 0.1 collective-permute-start.7
  17.5 0.5 %shard_map.60 = (bf16[128,512]{1,0:T(8,128)(2,1)S(1)}, f32[128,512]{1,0:T(8,128)S(1)}) custom-call(bf16[128,1024]{1,0:T(8,128)(2,1)S(1)} %get-tuple-element.32.att_ref, bf16[1024,4096]{1,0:T(8,128)(2,1)S(1)} %copy-done), custom_call_target="tpu_custom_call" | custom-call | flops 540000000 | bytes 4000000 | tf_op jit(solution)/shard_map/pallas_call | solution.py:234
  17.9 0.6 %collective-permute-start.10 = (bf16[128,512]{1,0:T(8,128)(2,1)S(1)}, bf16[128,512]{1,0:T(8,128)(2,1)S(1)}, u32[]{:S(2)}, u32[]{:S(2)}) collective-permute-start(bf16[128,512]{1,0:T(8,128)(2,1)S(1)} %get-tuple-element.36), channel_id=1, source_target_pairs={{0,1},{1,0},{2,3},{3,2},{4,5},{5,4},{6,7},{7,6},{8,9},{9,8},{10,11... | collective-permute-start | bytes 393224 | tf_op jit(solution)/shard_map/ppermute | solution.py:163
  18.5 0.3 %collective-permute-done.7 = bf16[128,512]{1,0:T(8,128)(2,1)S(1)} collective-permute-done((bf16[128,512]{1,0:T(8,128)(2,1)S(1)}, bf16[128,512]{1,0:T(8,128)(2,1)S(1)}, u32[]{:S(2)}, u32[]{:S(2)}) %collective-permute-start.7) | collective-permute-done | bytes 131104 | tf_op jit(solution)/shard_map/ppermute | solution.py:163
  18.8 1.6 %collective-permute-start.9 = (bf16[128,512]{1,0:T(8,128)(2,1)S(1)}, bf16[128,512]{1,0:T(8,128)(2,1)S(1)}, u32[]{:S(2)}, u32[]{:S(2)}) collective-permute-start(bf16[128,512]{1,0:T(8,128)(2,1)S(1)} %add_convert_fusion.2), channel_id=1, source_target_pairs={{0,2},{1,3},{2,0},{3,1},{4,6},{5,7},{6,4},{7,5},{8,10},{9,11},{10,... | collective-permute-start | bytes 393224 | tf_op jit(solution)/shard_map/ppermute | solution.py:163
  20.4 0.7 %shard_map.59 = (bf16[128,1024]{1,0:T(8,128)(2,1)S(1)}, f32[128,1024]{1,0:T(8,128)S(1)}) custom-call(bf16[128,1024]{1,0:T(8,128)(2,1)S(1)} %get-tuple-element.32.att_ref, bf16[1024,4096]{1,0:T(8,128)(2,1)S(1)} %copy-done), custom_call_target="tpu_custom_call" | custom-call | flops 540000000 | bytes 4000000 | tf_op jit(solution)/shard_map/pallas_call | solution.py:234
  21.1 0.1 collective-permute-start.8
  21.2 0.0 collective-permute-done.10
  21.2 0.6 %collective-permute-start.11 = (bf16[128,512]{1,0:T(8,128)(2,1)S(1)}, bf16[128,512]{1,0:T(8,128)(2,1)S(1)}, u32[]{:S(2)}, u32[]{:S(2)}) collective-permute-start(bf16[128,512]{1,0:T(8,128)(2,1)S(1)} %add_convert_fusion.1), channel_id=1, source_target_pairs={{0,2},{1,3},{2,0},{3,1},{4,6},{5,7},{6,4},{7,5},{8,10},{9,11},{10,... | collective-permute-start | bytes 393224 | tf_op jit(solution)/shard_map/ppermute | solution.py:163
  21.8 2.6 %collective-permute-done.9 = bf16[128,512]{1,0:T(8,128)(2,1)S(1)} collective-permute-done((bf16[128,512]{1,0:T(8,128)(2,1)S(1)}, bf16[128,512]{1,0:T(8,128)(2,1)S(1)}, u32[]{:S(2)}, u32[]{:S(2)}) %collective-permute-start.9) | collective-permute-done | bytes 131104 | tf_op jit(solution)/shard_map/ppermute | solution.py:163
  24.4 2.8 %collective-permute-done.11 = bf16[128,512]{1,0:T(8,128)(2,1)S(1)} collective-permute-done((bf16[128,512]{1,0:T(8,128)(2,1)S(1)}, bf16[128,512]{1,0:T(8,128)(2,1)S(1)}, u32[]{:S(2)}, u32[]{:S(2)}) %collective-permute-start.11) | collective-permute-done | bytes 131104 | tf_op jit(solution)/shard_map/ppermute | solution.py:163
  27.3 0.0 collective-permute-done.8
  27.3 0.8 %add_convert_fusion = bf16[128,1024]{1,0:T(8,128)(2,1)} fusion(f32[128,1024]{1,0:T(8,128)S(1)} %get-tuple-element.33, bf16[128,1024]{1,0:T(8,128)(2,1)S(1)} %collective-permute-done.8, bf16[128,512]{1,0:T(8,128)(2,1)S(1)} %collective-permute-done.11, bf16[128,512]{1,0:T(8,128)(2,1)S(1)} %collective-permute-done.9), kind=kLoop, calls=%fused_computation | loop fusion | flops 1048576 | bytes 1310720 | tf_op jit(solution)/shard_map/convert_element_type | solution.py:262
  (3 shorter events, 0.1 us)
Async XLA Ops:
  0.0 13.2 %copy-start.1 = (bf16[128,8,128]{2,1,0:T(8,128)(2,1)S(1)}, bf16[128,8,128]{2,1,0:T(8,128)(2,1)}, u32[]{:S(2)}) copy-start(bf16[128,8,128]{2,1,0:T(8,128)(2,1)} %param.5) | copy-start | bytes 786436
  0.0 16.7 %copy-start = (bf16[1024,4096]{1,0:T(8,128)(2,1)S(1)}, bf16[1024,4096]{1,0:T(8,128)(2,1)}, u32[]{:S(2)}) copy-start(bf16[1024,4096]{1,0:T(8,128)(2,1)} %w_ref.3) | copy-start | bytes 25165828
  1.0 8.0 %collective-permute-start.3 = (bf16[256,128]{1,0:T(8,128)(2,1)S(1)}, bf16[256,128]{1,0:T(8,128)(2,1)S(1)}, u32[]{:S(2)}, u32[]{:S(2)}) collective-permute-start(bf16[256,128]{1,0:T(8,128)(2,1)S(1)} %get-tuple-element.22.kv_ref), channel_id=1, source_target_pairs={{0,24},{4,28},{8,16},{12,20},{16,8},{20,12},{24,0},{28,4},{1,25},{... | collective-permute-start | bytes 196616 | tf_op jit(solution)/shard_map/ppermute | solution.py:163
  6.1 4.7 %collective-permute-start.2 = (bf16[256,128]{1,0:T(8,128)(2,1)S(1)}, bf16[256,128]{1,0:T(8,128)(2,1)S(1)}, u32[]{:S(2)}, u32[]{:S(2)}) collective-permute-start(bf16[256,128]{1,0:T(8,128)(2,1)S(1)} %get-tuple-element.22.kv_ref), channel_id=1, source_target_pairs={{0,8},{4,12},{8,0},{12,4},{16,24},{20,28},{24,16},{28,20},{1,9},{5... | collective-permute-start | bytes 196616 | tf_op jit(solution)/shard_map/ppermute | solution.py:163
  6.1 6.3 %collective-permute-start.1 = (bf16[256,128]{1,0:T(8,128)(2,1)S(1)}, bf16[256,128]{1,0:T(8,128)(2,1)S(1)}, u32[]{:S(2)}, u32[]{:S(2)}) collective-permute-start(bf16[256,128]{1,0:T(8,128)(2,1)S(1)} %get-tuple-element.22.kv_ref), channel_id=1, source_target_pairs={{0,16},{4,20},{8,24},{12,28},{16,0},{20,4},{24,8},{28,12},{1,17},{... | collective-permute-start | bytes 196616 | tf_op jit(solution)/shard_map/ppermute | solution.py:163
  6.7 6.6 %collective-permute-start = (bf16[256,128]{1,0:T(8,128)(2,1)S(1)}, bf16[256,128]{1,0:T(8,128)(2,1)S(1)}, u32[]{:S(2)}, u32[]{:S(2)}) collective-permute-start(bf16[256,128]{1,0:T(8,128)(2,1)S(1)} %get-tuple-element.22.kv_ref), channel_id=1, source_target_pairs={{0,4},{4,0},{8,12},{12,8},{16,20},{20,16},{24,28},{28,24},{1,5},{5... | collective-permute-start | bytes 196616 | tf_op jit(solution)/shard_map/ppermute | solution.py:163
  9.0 4.9 %collective-permute-start.5 = (bf16[256,128]{1,0:T(8,128)(2,1)S(1)}, bf16[256,128]{1,0:T(8,128)(2,1)S(1)}, u32[]{:S(2)}, u32[]{:S(2)}) collective-permute-start(bf16[256,128]{1,0:T(8,128)(2,1)S(1)} %collective-permute-done.3.refs_3_), channel_id=1, source_target_pairs={{0,4},{4,0},{8,12},{12,8},{16,20},{20,16},{24,28},{28,24},{1,5},{5... | collective-permute-start | bytes 196616 | tf_op jit(solution)/shard_map/ppermute | solution.py:163
  10.7 5.0 %collective-permute-start.4 = (bf16[256,128]{1,0:T(8,128)(2,1)S(1)}, bf16[256,128]{1,0:T(8,128)(2,1)S(1)}, u32[]{:S(2)}, u32[]{:S(2)}) collective-permute-start(bf16[256,128]{1,0:T(8,128)(2,1)S(1)} %collective-permute-done.2.refs_2_), channel_id=1, source_target_pairs={{0,4},{4,0},{8,12},{12,8},{16,20},{20,16},{24,28},{28,24},{1,5},{5... | collective-permute-start | bytes 196616 | tf_op jit(solution)/shard_map/ppermute | solution.py:163
  12.4 4.3 %collective-permute-start.6 = (bf16[256,128]{1,0:T(8,128)(2,1)S(1)}, bf16[256,128]{1,0:T(8,128)(2,1)S(1)}, u32[]{:S(2)}, u32[]{:S(2)}) collective-permute-start(bf16[256,128]{1,0:T(8,128)(2,1)S(1)} %collective-permute-done.1.refs_1_), channel_id=1, source_target_pairs={{0,4},{4,0},{8,12},{12,8},{16,20},{20,16},{24,28},{28,24},{1,5},{5... | collective-permute-start | bytes 196616 | tf_op jit(solution)/shard_map/ppermute | solution.py:163
  17.4 1.4 %collective-permute-start.7 = (bf16[128,512]{1,0:T(8,128)(2,1)S(1)}, bf16[128,512]{1,0:T(8,128)(2,1)S(1)}, u32[]{:S(2)}, u32[]{:S(2)}) collective-permute-start(bf16[128,512]{1,0:T(8,128)(2,1)S(1)} %get-tuple-element.31), channel_id=1, source_target_pairs={{0,1},{1,0},{2,3},{3,2},{4,5},{5,4},{6,7},{7,6},{8,9},{9,8},{10,11... | collective-permute-start | bytes 393224 | tf_op jit(solution)/shard_map/ppermute | solution.py:163
  17.9 3.3 %collective-permute-start.10 = (bf16[128,512]{1,0:T(8,128)(2,1)S(1)}, bf16[128,512]{1,0:T(8,128)(2,1)S(1)}, u32[]{:S(2)}, u32[]{:S(2)}) collective-permute-start(bf16[128,512]{1,0:T(8,128)(2,1)S(1)} %get-tuple-element.36), channel_id=1, source_target_pairs={{0,1},{1,0},{2,3},{3,2},{4,5},{5,4},{6,7},{7,6},{8,9},{9,8},{10,11... | collective-permute-start | bytes 393224 | tf_op jit(solution)/shard_map/ppermute | solution.py:163
  18.8 5.6 %collective-permute-start.9 = (bf16[128,512]{1,0:T(8,128)(2,1)S(1)}, bf16[128,512]{1,0:T(8,128)(2,1)S(1)}, u32[]{:S(2)}, u32[]{:S(2)}) collective-permute-start(bf16[128,512]{1,0:T(8,128)(2,1)S(1)} %add_convert_fusion.2), channel_id=1, source_target_pairs={{0,2},{1,3},{2,0},{3,1},{4,6},{5,7},{6,4},{7,5},{8,10},{9,11},{10,... | collective-permute-start | bytes 393224 | tf_op jit(solution)/shard_map/ppermute | solution.py:163
  21.1 6.1 %collective-permute-start.8 = (bf16[128,1024]{1,0:T(8,128)(2,1)S(1)}, bf16[128,1024]{1,0:T(8,128)(2,1)S(1)}, u32[]{:S(2)}, u32[]{:S(2)}) collective-permute-start(bf16[128,1024]{1,0:T(8,128)(2,1)S(1)} %get-tuple-element.34), channel_id=1, source_target_pairs={{0,1},{1,0},{2,3},{3,2},{4,5},{5,4},{6,7},{7,6},{8,9},{9,8},{10,11... | collective-permute-start | bytes 786440 | tf_op jit(solution)/shard_map/ppermute | solution.py:163
  21.2 6.0 %collective-permute-start.11 = (bf16[128,512]{1,0:T(8,128)(2,1)S(1)}, bf16[128,512]{1,0:T(8,128)(2,1)S(1)}, u32[]{:S(2)}, u32[]{:S(2)}) collective-permute-start(bf16[128,512]{1,0:T(8,128)(2,1)S(1)} %add_convert_fusion.1), channel_id=1, source_target_pairs={{0,2},{1,3},{2,0},{3,1},{4,6},{5,7},{6,4},{7,5},{8,10},{9,11},{10,... | collective-permute-start | bytes 393224 | tf_op jit(solution)/shard_map/ppermute | solution.py:163

commit v8 on v7

--- a/solution.py
+++ b/solution.py
@@ -73,10 +73,14 @@
     scale = exponent_scale(q_ref.shape[1])
     me = lax.axis_index("ctx")
     reached = jnp.max(reached_ref[...])
-    for other, kv_ref in zip(xors, kv_refs):
-        @pl.when((lax.shift_right_logical(reached, me ^ other) & 1) == 1)
-        def _():
-            absorb(scale, q_ref, kv_ref[0:BLOCK, :], kv_ref[BLOCK:, :], *state)
+    for others, kv_ref in zip(xors, kv_refs):
+        for at, other in enumerate(others):
+            keys = slice(2 * at * BLOCK, (2 * at + 1) * BLOCK)
+            values = slice((2 * at + 1) * BLOCK, (2 * at + 2) * BLOCK)
+
+            @pl.when((lax.shift_right_logical(reached, me ^ other) & 1) == 1)
+            def _():
+                absorb(scale, q_ref, kv_ref[keys, :], kv_ref[values, :], *state)
 
 
 def absorb_walk(parents_ref, q_ref, piece, state):
@@ -175,10 +179,14 @@
         cost_estimate=pl.CostEstimate(flops=8_000_000_000, bytes_accessed=130_000, transcendentals=0),
     )(in_hbm(key_heads[:, 0, :]), in_hbm(value_heads[:, 0, :]), in_hbm(parents))
     if ctx_size == DIRECT_SIZE:
-        columns = [swap(kv, "ctx", ctx_size, other) for other in (4, 2, 6)]
-        beside = swap(kv, "ctx", ctx_size, 1)
-        pairs = [swap(x, "ctx", ctx_size, 1) for x in columns]
-        early, early_xors = [beside, *columns], (1, 4, 2, 6)
+        by_4 = swap(kv, "ctx", ctx_size, 4)
+        by_1 = swap(kv, "ctx", ctx_size, 1)
+        by_6 = swap(kv, "ctx", ctx_size, 6)
+        held, _ = lax.optimization_barrier((by_1, by_6))
+        by_23 = swap(jnp.concatenate([kv, held], axis=0), "ctx", ctx_size, 2)
+        by_7 = swap(by_6, "ctx", ctx_size, 1)
+        by_5 = swap(by_4, "ctx", ctx_size, 1)
+        early, early_xors = [by_1, by_6, by_4], ((1,), (6,), (4,))
     else:
         early, early_xors = [], ()
     q = jnp.transpose(query_heads, (1, 0, 2)).reshape(rows, head_dim)
@@ -199,19 +207,17 @@
     state = (m, l, acc)
     state_shapes = tuple(jax.ShapeDtypeStruct(x.shape, x.dtype) for x in state)
     if ctx_size == DIRECT_SIZE:
-        def absorbed(state, xors, arrived):
-            return pl.pallas_call(
-                functools.partial(others_kernel, xors),
-                out_shape=state_shapes,
-                in_specs=[vmem] * (5 + len(xors)),
-                out_specs=(vmem,) * 3,
-                input_output_aliases={2: 0, 3: 1, 4: 2},
-                compiler_params=params,
-                cost_estimate=pl.CostEstimate(flops=270_000_000, bytes_accessed=1_000_000, transcendentals=500_000),
-            )(reached, q, *state, *arrived)
-
-        state = absorbed(state, (3, 7), pairs[1:])
-        xors, pieces, tree, tree_spec = (5,), pairs[:1], reached, vmem
+        xors = ((7,),)
+        state = pl.pallas_call(
+            functools.partial(others_kernel, xors),
+            out_shape=state_shapes,
+            in_specs=[vmem] * (5 + len(xors)),
+            out_specs=(vmem,) * 3,
+            input_output_aliases={2: 0, 3: 1, 4: 2},
+            compiler_params=params,
+            cost_estimate=pl.CostEstimate(flops=270_000_000, bytes_accessed=1_000_000, transcendentals=500_000),
+        )(reached, q, *state, by_7)
+        xors, pieces, tree, tree_spec = ((2, 3), (5,)), [by_23, by_5], reached, vmem
     else:
         xors, pieces, tree, tree_spec = (), [lax.all_gather(kv, "ctx", axis=0, tiled=True)], parents, smem
 

time: 28.2 us -> 28.7 us (1.018)
  waiting for transfers between devices: 9.17 us -> 12.4 us
  starting transfers between devices: 14.3 us -> 11.5 us
    ppermute x12 -> x11, waiting for transfers between devices: 9.17 us -> 12.4 us  [swap(): return lax.ppermute(x, axis, [(i, i ^ other) for i in range(size)])]
    ppermute x12 -> x11, starting transfers between devices: 14.3 us -> 11.5 us  [swap(): return lax.ppermute(x, axis, [(i, i ^ other) for i in range(size)])]
  transfers between devices with their start and end apart: 12 -> 11, of which waited for: 7 -> 8; matrix products, arithmetic and copies ran while one was open for 0% -> 0% of each run, Pallas kernels for 7% -> 7%
where the time goes in v8:
time: 28.7 us; the launch traced here: 28.6 us
  waiting for transfers between devices  12.4 us (43%)
  starting transfers between devices  11.5 us (40%)
  Pallas kernels  3.6 us (13%)
  other arithmetic  0.88 us (3%)
    ppermute x11, waiting for transfers between devices, swap(): return lax.ppermute(x, axis, [(i, i ^ other) for i in range(size)])  12.4 us
    ppermute x11, starting transfers between devices, swap(): return lax.ppermute(x, axis, [(i, i ^ other) for i in range(size)])  11.5 us
    pallas_call x2, Pallas kernels, projected(): pl.pallas_call(functools.partial(project_pair, flip, part), out_shape=sha...  1.19 us
    pallas_call x1, Pallas kernels, shards(): pl.pallas_call(functools.partial(pack_kernel, ctx_size == DIRECT_SIZE), o...  0.95 us
    convert_element_type x1, other arithmetic, shards(): (keep_near + near_in.astype(jnp.float32) + from_far).astype(jnp.bfloat16)  0.8 us
    pallas_call x1, Pallas kernels, shards(): pl.pallas_call(functools.partial(last_kernel, xors), out_shape=(jax.Shape...  0.72 us
  transfers between devices with their start and end apart: 11, of which 8 were waited for; matrix products, arithmetic and copies ran while one was open for 0% of the time, Pallas kernels for 7%

profile of v8, /device:TPU:0, one launch (start us, length us, event | category | flops | bytes accessed | tf_op | source)
XLA Modules:
  0.0 28.6 jit_solution(12823464219718957074)
XLA Ops:
  0.0 0.0 copy-start.1
  0.0 0.0 copy-start
  0.0 0.9 %shard_map.55 = (bf16[256,128]{1,0:T(8,128)(2,1)S(1)}, s32[8,128]{1,0:T(8,128)S(1)}) custom-call(bf16[128,128]{1,0:T(8,128)(2,1)} %bitcast.8, bf16[128,128]{1,0:T(8,128)(2,1)} %bitcast.9, s32[8]{0:T(128)} %parents_hbm.1), custom_call_target="tpu_custom_call" | custom-call | flops 8000000000 | bytes 130000 | tf_op jit(solution)/shard_map/pallas_call | solution.py:169
  1.0 5.1 %collective-permute-start.1 = (bf16[256,128]{1,0:T(8,128)(2,1)S(1)}, bf16[256,128]{1,0:T(8,128)(2,1)S(1)}, u32[]{:S(2)}, u32[]{:S(2)}) collective-permute-start(bf16[256,128]{1,0:T(8,128)(2,1)S(1)} %get-tuple-element.23.kv_ref), channel_id=1, source_target_pairs={{0,24},{4,28},{8,16},{12,20},{16,8},{20,12},{24,0},{28,4},{1,25},{... | collective-permute-start | bytes 196616 | tf_op jit(solution)/shard_map/ppermute | solution.py:167
  6.1 1.5 %collective-permute-start = (bf16[256,128]{1,0:T(8,128)(2,1)S(1)}, bf16[256,128]{1,0:T(8,128)(2,1)S(1)}, u32[]{:S(2)}, u32[]{:S(2)}) collective-permute-start(bf16[256,128]{1,0:T(8,128)(2,1)S(1)} %get-tuple-element.23.kv_ref), channel_id=1, source_target_pairs={{0,4},{4,0},{8,12},{12,8},{16,20},{20,16},{24,28},{28,24},{1,5},{5... | collective-permute-start | bytes 196616 | tf_op jit(solution)/shard_map/ppermute | solution.py:167
  7.6 0.0 collective-permute-start.2
  7.6 0.9 %collective-permute-done.1.refs_1_ = bf16[256,128]{1,0:T(8,128)(2,1)S(1)} collective-permute-done((bf16[256,128]{1,0:T(8,128)(2,1)S(1)}, bf16[256,128]{1,0:T(8,128)(2,1)S(1)}, u32[]{:S(2)}, u32[]{:S(2)}) %collective-permute-start.1) | collective-permute-done | bytes 65568 | tf_op jit(solution)/shard_map/ppermute | solution.py:167
  8.5 1.9 %collective-permute-done.refs_0_ = bf16[256,128]{1,0:T(8,128)(2,1)S(1)} collective-permute-done((bf16[256,128]{1,0:T(8,128)(2,1)S(1)}, bf16[256,128]{1,0:T(8,128)(2,1)S(1)}, u32[]{:S(2)}, u32[]{:S(2)}) %collective-permute-start) | collective-permute-done | bytes 65568 | tf_op jit(solution)/shard_map/ppermute | solution.py:167
  10.4 0.1 collective-permute-start.4
  10.4 1.6 %collective-permute-start.3 = (bf16[256,128]{1,0:T(8,128)(2,1)S(1)}, bf16[256,128]{1,0:T(8,128)(2,1)S(1)}, u32[]{:S(2)}, u32[]{:S(2)}) collective-permute-start(bf16[256,128]{1,0:T(8,128)(2,1)S(1)} %collective-permute-done.1.refs_1_), channel_id=1, source_target_pairs={{0,4},{4,0},{8,12},{12,8},{16,20},{20,16},{24,28},{28,24},{1,5},{5... | collective-permute-start | bytes 196616 | tf_op jit(solution)/shard_map/ppermute | solution.py:167
  12.0 0.8 %collective-permute-done.2.refs_2_ = bf16[256,128]{1,0:T(8,128)(2,1)S(1)} collective-permute-done((bf16[256,128]{1,0:T(8,128)(2,1)S(1)}, bf16[256,128]{1,0:T(8,128)(2,1)S(1)}, u32[]{:S(2)}, u32[]{:S(2)}) %collective-permute-start.2) | collective-permute-done | bytes 65568 | tf_op jit(solution)/shard_map/ppermute | solution.py:167
  12.9 0.4 %collective-permute-start.5 = (bf16[256,128]{1,0:T(8,128)(2,1)S(1)}, bf16[256,128]{1,0:T(8,128)(2,1)S(1)}, u32[]{:S(2)}, u32[]{:S(2)}) collective-permute-start(bf16[256,128]{1,0:T(8,128)(2,1)S(1)} %collective-permute-done.2.refs_2_), channel_id=1, source_target_pairs={{0,4},{4,0},{8,12},{12,8},{16,20},{20,16},{24,28},{28,24},{1,5},{5... | collective-permute-start | bytes 196616 | tf_op jit(solution)/shard_map/ppermute | solution.py:167
  13.3 0.0 copy-done.1
  13.3 0.5 %shard_map.56 = (f32[1,1024]{1,0:T(1,128)S(1)}, f32[1,1024]{1,0:T(1,128)S(1)}, f32[128,1024]{1,0:T(8,128)S(1)}) custom-call(s32[8,128]{1,0:T(8,128)S(1)} %get-tuple-element.22.reached_ref.tree_ref, bf16[1024,128]{1,0:T(8,128)(2,1)S(1)} %bitcast.4, bf16[256,128]{1,0:T(8,128)(2,1)S(1)} %get-tuple-element.23.kv_ref, ...), custom_call_target="tpu_custom_call" | custom-call | flops 130000000 | bytes 1000000 | tf_op jit(solution)/shard_map/pallas_call | solution.py:194
  13.9 1.1 %collective-permute-done.3.refs_0_ = bf16[256,128]{1,0:T(8,128)(2,1)S(1)} collective-permute-done((bf16[256,128]{1,0:T(8,128)(2,1)S(1)}, bf16[256,128]{1,0:T(8,128)(2,1)S(1)}, u32[]{:S(2)}, u32[]{:S(2)}) %collective-permute-start.3) | collective-permute-done | bytes 65568 | tf_op jit(solution)/shard_map/ppermute | solution.py:167
  14.9 0.2 shard_map.57
  15.1 2.0 %collective-permute-done.5.refs_1_ = bf16[256,128]{1,0:T(8,128)(2,1)S(1)} collective-permute-done((bf16[256,128]{1,0:T(8,128)(2,1)S(1)}, bf16[256,128]{1,0:T(8,128)(2,1)S(1)}, u32[]{:S(2)}, u32[]{:S(2)}) %collective-permute-start.5) | collective-permute-done | bytes 65568 | tf_op jit(solution)/shard_map/ppermute | solution.py:167
  17.1 0.0 collective-permute-done.4.refs_0_
  17.1 0.0 copy-done
  17.1 0.7 %shard_map.58 = (bf16[128,1024]{1,0:T(8,128)(2,1)S(1)}, bf16[128,512]{1,0:T(8,128)(2,1)S(1)}, f32[128,512]{1,0:T(8,128)S(1)}, f32[1,1024]{1,0:T(1,128)S(1)}, f32...) custom-call(s32[8,128]{1,0:T(8,128)S(1)} %get-tuple-element.22.reached_ref, ...), custom_call_target="tpu_custom_call", output_to_operand_aliasing={{3}: (2, {}), {4}: (3, {}), {5}: (4, {})} | custom-call | flops 1000000000 | bytes 10000000 | tf_op jit(solution)/shard_map/pallas_call | solution.py:229
  17.9 0.1 collective-permute-start.6
  17.9 0.5 %shard_map.60 = (bf16[128,512]{1,0:T(8,128)(2,1)S(1)}, f32[128,512]{1,0:T(8,128)S(1)}) custom-call(bf16[128,1024]{1,0:T(8,128)(2,1)S(1)} %get-tuple-element.34.att_ref, bf16[1024,4096]{1,0:T(8,128)(2,1)S(1)} %copy-done), custom_call_target="tpu_custom_call" | custom-call | flops 540000000 | bytes 4000000 | tf_op jit(solution)/shard_map/pallas_call | solution.py:240
  18.4 0.6 %collective-permute-start.9 = (bf16[128,512]{1,0:T(8,128)(2,1)S(1)}, bf16[128,512]{1,0:T(8,128)(2,1)S(1)}, u32[]{:S(2)}, u32[]{:S(2)}) collective-permute-start(bf16[128,512]{1,0:T(8,128)(2,1)S(1)} %get-tuple-element.38), channel_id=1, source_target_pairs={{0,1},{1,0},{2,3},{3,2},{4,5},{5,4},{6,7},{7,6},{8,9},{9,8},{10,11... | collective-permute-start | bytes 393224 | tf_op jit(solution)/shard_map/ppermute | solution.py:167
  19.0 0.3 %collective-permute-done.6 = bf16[128,512]{1,0:T(8,128)(2,1)S(1)} collective-permute-done((bf16[128,512]{1,0:T(8,128)(2,1)S(1)}, bf16[128,512]{1,0:T(8,128)(2,1)S(1)}, u32[]{:S(2)}, u32[]{:S(2)}) %collective-permute-start.6) | collective-permute-done | bytes 131104 | tf_op jit(solution)/shard_map/ppermute | solution.py:167
  19.3 1.6 %collective-permute-start.8 = (bf16[128,512]{1,0:T(8,128)(2,1)S(1)}, bf16[128,512]{1,0:T(8,128)(2,1)S(1)}, u32[]{:S(2)}, u32[]{:S(2)}) collective-permute-start(bf16[128,512]{1,0:T(8,128)(2,1)S(1)} %add_convert_fusion.2), channel_id=1, source_target_pairs={{0,2},{1,3},{2,0},{3,1},{4,6},{5,7},{6,4},{7,5},{8,10},{9,11},{10,... | collective-permute-start | bytes 393224 | tf_op jit(solution)/shard_map/ppermute | solution.py:167
  20.9 0.7 %shard_map.59 = (bf16[128,1024]{1,0:T(8,128)(2,1)S(1)}, f32[128,1024]{1,0:T(8,128)S(1)}) custom-call(bf16[128,1024]{1,0:T(8,128)(2,1)S(1)} %get-tuple-element.34.att_ref, bf16[1024,4096]{1,0:T(8,128)(2,1)S(1)} %copy-done), custom_call_target="tpu_custom_call" | custom-call | flops 540000000 | bytes 4000000 | tf_op jit(solution)/shard_map/pallas_call | solution.py:240
  21.6 0.1 collective-permute-start.7
  21.7 0.0 collective-permute-done.9
  21.8 0.6 %collective-permute-start.10 = (bf16[128,512]{1,0:T(8,128)(2,1)S(1)}, bf16[128,512]{1,0:T(8,128)(2,1)S(1)}, u32[]{:S(2)}, u32[]{:S(2)}) collective-permute-start(bf16[128,512]{1,0:T(8,128)(2,1)S(1)} %add_convert_fusion.1), channel_id=1, source_target_pairs={{0,2},{1,3},{2,0},{3,1},{4,6},{5,7},{6,4},{7,5},{8,10},{9,11},{10,... | collective-permute-start | bytes 393224 | tf_op jit(solution)/shard_map/ppermute | solution.py:167
  22.3 2.6 %collective-permute-done.8 = bf16[128,512]{1,0:T(8,128)(2,1)S(1)} collective-permute-done((bf16[128,512]{1,0:T(8,128)(2,1)S(1)}, bf16[128,512]{1,0:T(8,128)(2,1)S(1)}, u32[]{:S(2)}, u32[]{:S(2)}) %collective-permute-start.8) | collective-permute-done | bytes 131104 | tf_op jit(solution)/shard_map/ppermute | solution.py:167
  24.9 2.8 %collective-permute-done.10 = bf16[128,512]{1,0:T(8,128)(2,1)S(1)} collective-permute-done((bf16[128,512]{1,0:T(8,128)(2,1)S(1)}, bf16[128,512]{1,0:T(8,128)(2,1)S(1)}, u32[]{:S(2)}, u32[]{:S(2)}) %collective-permute-start.10) | collective-permute-done | bytes 131104 | tf_op jit(solution)/shard_map/ppermute | solution.py:167
  27.7 0.0 collective-permute-done.7
  27.8 0.8 %add_convert_fusion = bf16[128,1024]{1,0:T(8,128)(2,1)} fusion(f32[128,1024]{1,0:T(8,128)S(1)} %get-tuple-element.35, bf16[128,1024]{1,0:T(8,128)(2,1)S(1)} %collective-permute-done.7, bf16[128,512]{1,0:T(8,128)(2,1)S(1)} %collective-permute-done.10, bf16[128,512]{1,0:T(8,128)(2,1)S(1)} %collective-permute-done.8), kind=kLoop, calls=%fused_computation | loop fusion | flops 1048576 | bytes 1310720 | tf_op jit(solution)/shard_map/convert_element_type | solution.py:268
  (4 shorter events, 0.1 us)
Async XLA Ops:
  0.0 13.3 %copy-start.1 = (bf16[128,8,128]{2,1,0:T(8,128)(2,1)S(1)}, bf16[128,8,128]{2,1,0:T(8,128)(2,1)}, u32[]{:S(2)}) copy-start(bf16[128,8,128]{2,1,0:T(8,128)(2,1)} %param.5) | copy-start | bytes 786436
  0.0 17.1 %copy-start = (bf16[1024,4096]{1,0:T(8,128)(2,1)S(1)}, bf16[1024,4096]{1,0:T(8,128)(2,1)}, u32[]{:S(2)}) copy-start(bf16[1024,4096]{1,0:T(8,128)(2,1)} %w_ref.3) | copy-start | bytes 25165828
  1.0 7.5 %collective-permute-start.1 = (bf16[256,128]{1,0:T(8,128)(2,1)S(1)}, bf16[256,128]{1,0:T(8,128)(2,1)S(1)}, u32[]{:S(2)}, u32[]{:S(2)}) collective-permute-start(bf16[256,128]{1,0:T(8,128)(2,1)S(1)} %get-tuple-element.23.kv_ref), channel_id=1, source_target_pairs={{0,24},{4,28},{8,16},{12,20},{16,8},{20,12},{24,0},{28,4},{1,25},{... | collective-permute-start | bytes 196616 | tf_op jit(solution)/shard_map/ppermute | solution.py:167
  6.1 4.3 %collective-permute-start = (bf16[256,128]{1,0:T(8,128)(2,1)S(1)}, bf16[256,128]{1,0:T(8,128)(2,1)S(1)}, u32[]{:S(2)}, u32[]{:S(2)}) collective-permute-start(bf16[256,128]{1,0:T(8,128)(2,1)S(1)} %get-tuple-element.23.kv_ref), channel_id=1, source_target_pairs={{0,4},{4,0},{8,12},{12,8},{16,20},{20,16},{24,28},{28,24},{1,5},{5... | collective-permute-start | bytes 196616 | tf_op jit(solution)/shard_map/ppermute | solution.py:167
  7.6 5.3 %collective-permute-start.2 = (bf16[256,128]{1,0:T(8,128)(2,1)S(1)}, bf16[256,128]{1,0:T(8,128)(2,1)S(1)}, u32[]{:S(2)}, u32[]{:S(2)}) collective-permute-start(bf16[256,128]{1,0:T(8,128)(2,1)S(1)} %get-tuple-element.23.kv_ref), channel_id=1, source_target_pairs={{0,16},{4,20},{8,24},{12,28},{16,0},{20,4},{24,8},{28,12},{1,17},{... | collective-permute-start | bytes 196616 | tf_op jit(solution)/shard_map/ppermute | solution.py:167
  10.4 6.8 %collective-permute-start.4 = (bf16[512,128]{1,0:T(8,128)(2,1)S(1)}, bf16[512,128]{1,0:T(8,128)(2,1)S(1)}, u32[]{:S(2)}, u32[]{:S(2)}) collective-permute-start(bf16[512,128]{1,0:T(8,128)(2,1)S(1)} %pad_maximum_fusion), channel_id=1, source_target_pairs={{0,8},{4,12},{8,0},{12,4},{16,24},{20,28},{24,16},{28,20},{1,9},{5... | collective-permute-start | bytes 393224 | tf_op jit(solution)/shard_map/ppermute | solution.py:167
  10.4 4.5 %collective-permute-start.3 = (bf16[256,128]{1,0:T(8,128)(2,1)S(1)}, bf16[256,128]{1,0:T(8,128)(2,1)S(1)}, u32[]{:S(2)}, u32[]{:S(2)}) collective-permute-start(bf16[256,128]{1,0:T(8,128)(2,1)S(1)} %collective-permute-done.1.refs_1_), channel_id=1, source_target_pairs={{0,4},{4,0},{8,12},{12,8},{16,20},{20,16},{24,28},{28,24},{1,5},{5... | collective-permute-start | bytes 196616 | tf_op jit(solution)/shard_map/ppermute | solution.py:167
  12.9 4.3 %collective-permute-start.5 = (bf16[256,128]{1,0:T(8,128)(2,1)S(1)}, bf16[256,128]{1,0:T(8,128)(2,1)S(1)}, u32[]{:S(2)}, u32[]{:S(2)}) collective-permute-start(bf16[256,128]{1,0:T(8,128)(2,1)S(1)} %collective-permute-done.2.refs_2_), channel_id=1, source_target_pairs={{0,4},{4,0},{8,12},{12,8},{16,20},{20,16},{24,28},{28,24},{1,5},{5... | collective-permute-start | bytes 196616 | tf_op jit(solution)/shard_map/ppermute | solution.py:167
  17.9 1.4 %collective-permute-start.6 = (bf16[128,512]{1,0:T(8,128)(2,1)S(1)}, bf16[128,512]{1,0:T(8,128)(2,1)S(1)}, u32[]{:S(2)}, u32[]{:S(2)}) collective-permute-start(bf16[128,512]{1,0:T(8,128)(2,1)S(1)} %get-tuple-element.33), channel_id=1, source_target_pairs={{0,1},{1,0},{2,3},{3,2},{4,5},{5,4},{6,7},{7,6},{8,9},{9,8},{10,11... | collective-permute-start | bytes 393224 | tf_op jit(solution)/shard_map/ppermute | solution.py:167
  18.4 3.3 %collective-permute-start.9 = (bf16[128,512]{1,0:T(8,128)(2,1)S(1)}, bf16[128,512]{1,0:T(8,128)(2,1)S(1)}, u32[]{:S(2)}, u32[]{:S(2)}) collective-permute-start(bf16[128,512]{1,0:T(8,128)(2,1)S(1)} %get-tuple-element.38), channel_id=1, source_target_pairs={{0,1},{1,0},{2,3},{3,2},{4,5},{5,4},{6,7},{7,6},{8,9},{9,8},{10,11... | collective-permute-start | bytes 393224 | tf_op jit(solution)/shard_map/ppermute | solution.py:167
  19.3 5.6 %collective-permute-start.8 = (bf16[128,512]{1,0:T(8,128)(2,1)S(1)}, bf16[128,512]{1,0:T(8,128)(2,1)S(1)}, u32[]{:S(2)}, u32[]{:S(2)}) collective-permute-start(bf16[128,512]{1,0:T(8,128)(2,1)S(1)} %add_convert_fusion.2), channel_id=1, source_target_pairs={{0,2},{1,3},{2,0},{3,1},{4,6},{5,7},{6,4},{7,5},{8,10},{9,11},{10,... | collective-permute-start | bytes 393224 | tf_op jit(solution)/shard_map/ppermute | solution.py:167
  21.6 6.1 %collective-permute-start.7 = (bf16[128,1024]{1,0:T(8,128)(2,1)S(1)}, bf16[128,1024]{1,0:T(8,128)(2,1)S(1)}, u32[]{:S(2)}, u32[]{:S(2)}) collective-permute-start(bf16[128,1024]{1,0:T(8,128)(2,1)S(1)} %get-tuple-element.36), channel_id=1, source_target_pairs={{0,1},{1,0},{2,3},{3,2},{4,5},{5,4},{6,7},{7,6},{8,9},{9,8},{10,11... | collective-permute-start | bytes 786440 | tf_op jit(solution)/shard_map/ppermute | solution.py:167
  21.8 6.0 %collective-permute-start.10 = (bf16[128,512]{1,0:T(8,128)(2,1)S(1)}, bf16[128,512]{1,0:T(8,128)(2,1)S(1)}, u32[]{:S(2)}, u32[]{:S(2)}) collective-permute-start(bf16[128,512]{1,0:T(8,128)(2,1)S(1)} %add_convert_fusion.1), channel_id=1, source_target_pairs={{0,2},{1,3},{2,0},{3,1},{4,6},{5,7},{6,4},{7,5},{8,10},{9,11},{10,... | collective-permute-start | bytes 393224 | tf_op jit(solution)/shard_map/ppermute | solution.py:167

commit v9 on v7

--- a/solution.py
+++ b/solution.py
@@ -161,6 +161,10 @@
 
     def swap(x, axis, size, other):
         return lax.ppermute(x, axis, [(i, i ^ other) for i in range(size)])
+
+    def forward(x, other):
+        route = [(i, i ^ 1 if i ^ other < i else i) for i in range(ctx_size)]
+        return lax.ppermute(x, "ctx", route)
 
     kv, reached = pl.pallas_call(
         functools.partial(pack_kernel, ctx_size == DIRECT_SIZE),
@@ -177,7 +181,7 @@
     if ctx_size == DIRECT_SIZE:
         columns = [swap(kv, "ctx", ctx_size, other) for other in (4, 2, 6)]
         beside = swap(kv, "ctx", ctx_size, 1)
-        pairs = [swap(x, "ctx", ctx_size, 1) for x in columns]
+        pairs = [forward(x, other) for x, other in zip(columns, (4, 2, 6))]
         early, early_xors = [beside, *columns], (1, 4, 2, 6)
     else:
         early, early_xors = [], ()

time: 28.2 us -> 32 us (1.13)
  the two profiles are of different devices: /device:TPU:0 before, /device:TPU:28 now
where the time goes in v9:
time: 32 us; the launch traced here: 31.7 us
  starting transfers between devices  16.1 us (50%)
  waiting for transfers between devices  8.01 us (25%)
  Pallas kernels  6.6 us (21%)
  other arithmetic  0.87 us (3%)
    ppermute x3, starting transfers between devices, forward(): return lax.ppermute(x, 'ctx', route)  8.24 us
    ppermute x9, starting transfers between devices, swap(): return lax.ppermute(x, axis, [(i, i ^ other) for i in range(size)])  7.81 us
    ppermute x9, waiting for transfers between devices, swap(): return lax.ppermute(x, axis, [(i, i ^ other) for i in range(size)])  7.62 us
    pallas_call x1, Pallas kernels, shards(): pl.pallas_call(functools.partial(own_block_kernel, early_xors), out_shape...  2.55 us
    pallas_call x1, Pallas kernels, shards(): pl.pallas_call(functools.partial(last_kernel, xors), out_shape=(jax.Shape...  1.21 us
    pallas_call x2, Pallas kernels, projected(): pl.pallas_call(functools.partial(project_pair, flip, part), out_shape=sha...  1.18 us
    pallas_call x1, Pallas kernels, shards(): pl.pallas_call(functools.partial(pack_kernel, ctx_size == DIRECT_SIZE), o...  0.95 us
    convert_element_type x1, other arithmetic, shards(): (keep_near + near_in.astype(jnp.float32) + from_far).astype(jnp.bfloat16)  0.8 us
  transfers between devices with their start and end apart: 12, of which 5 were waited for; matrix products, arithmetic and copies ran while one was open for 0% of the time, Pallas kernels for 14%

profile of v9, /device:TPU:28, one launch (start us, length us, event | category | flops | bytes accessed | tf_op | source)
XLA Modules:
  0.0 31.7 jit_solution(4145216447996385210)
XLA Ops:
  0.0 0.0 copy-start.1
  0.0 0.0 copy-start
  0.0 0.9 %shard_map.55 = (bf16[256,128]{1,0:T(8,128)(2,1)S(1)}, s32[8,128]{1,0:T(8,128)S(1)}) custom-call(bf16[128,128]{1,0:T(8,128)(2,1)} %bitcast.8, bf16[128,128]{1,0:T(8,128)(2,1)} %bitcast.9, s32[8]{0:T(128)} %parents_hbm.1), custom_call_target="tpu_custom_call" | custom-call | flops 8000000000 | bytes 130000 | tf_op jit(solution)/shard_map/pallas_call | solution.py:169
  1.0 0.3 collective-permute-start.3
  1.2 0.7 %collective-permute-start.2 = (bf16[256,128]{1,0:T(8,128)(2,1)S(1)}, bf16[256,128]{1,0:T(8,128)(2,1)S(1)}, u32[]{:S(2)}, u32[]{:S(2)}) collective-permute-start(bf16[256,128]{1,0:T(8,128)(2,1)S(1)} %get-tuple-element.22.kv_ref), channel_id=1, source_target_pairs={{0,8},{4,12},{8,0},{12,4},{16,24},{20,28},{24,16},{28,20},{1,9},{5... | collective-permute-start | bytes 196616 | tf_op jit(solution)/shard_map/ppermute | solution.py:163
  1.9 3.5 %collective-permute-start.1 = (bf16[256,128]{1,0:T(8,128)(2,1)S(1)}, bf16[256,128]{1,0:T(8,128)(2,1)S(1)}, u32[]{:S(2)}, u32[]{:S(2)}) collective-permute-start(bf16[256,128]{1,0:T(8,128)(2,1)S(1)} %get-tuple-element.22.kv_ref), channel_id=1, source_target_pairs={{0,16},{4,20},{8,24},{12,28},{16,0},{20,4},{24,8},{28,12},{1,17},{... | collective-permute-start | bytes 196616 | tf_op jit(solution)/shard_map/ppermute | solution.py:163
  5.4 0.5 %collective-permute-start = (bf16[256,128]{1,0:T(8,128)(2,1)S(1)}, bf16[256,128]{1,0:T(8,128)(2,1)S(1)}, u32[]{:S(2)}, u32[]{:S(2)}) collective-permute-start(bf16[256,128]{1,0:T(8,128)(2,1)S(1)} %get-tuple-element.22.kv_ref), channel_id=1, source_target_pairs={{0,4},{4,0},{8,12},{12,8},{16,20},{20,16},{24,28},{28,24},{1,5},{5... | collective-permute-start | bytes 196616 | tf_op jit(solution)/shard_map/ppermute | solution.py:163
  5.9 1.9 %collective-permute-done.3.refs_3_ = bf16[256,128]{1,0:T(8,128)(2,1)S(1)} collective-permute-done((bf16[256,128]{1,0:T(8,128)(2,1)S(1)}, bf16[256,128]{1,0:T(8,128)(2,1)S(1)}, u32[]{:S(2)}, u32[]{:S(2)}) %collective-permute-start.3) | collective-permute-done | bytes 65568 | tf_op jit(solution)/shard_map/ppermute | solution.py:163
  7.8 2.4 %collective-permute-start.5 = (bf16[256,128]{1,0:T(8,128)(2,1)S(1)}, bf16[256,128]{1,0:T(8,128)(2,1)S(1)}, u32[]{:S(2)}, u32[]{:S(2)}) collective-permute-start(bf16[256,128]{1,0:T(8,128)(2,1)S(1)} %collective-permute-done.3.refs_3_), channel_id=1, source_target_pairs={{0,0},{4,4},{8,8},{12,12},{16,20},{20,16},{24,28},{28,24},{1,1},{5... | collective-permute-start | bytes 196616 | tf_op jit(solution)/shard_map/ppermute | solution.py:167
  10.2 0.0 collective-permute-done.2.refs_2_
  10.2 3.4 %collective-permute-start.4 = (bf16[256,128]{1,0:T(8,128)(2,1)S(1)}, bf16[256,128]{1,0:T(8,128)(2,1)S(1)}, u32[]{:S(2)}, u32[]{:S(2)}) collective-permute-start(bf16[256,128]{1,0:T(8,128)(2,1)S(1)} %collective-permute-done.2.refs_2_), channel_id=1, source_target_pairs={{0,0},{4,4},{8,12},{12,8},{16,16},{20,20},{24,28},{28,24},{1,1},{5... | collective-permute-start | bytes 196616 | tf_op jit(solution)/shard_map/ppermute | solution.py:167
  13.7 0.0 collective-permute-done.1.refs_1_
  13.7 2.4 %collective-permute-start.6 = (bf16[256,128]{1,0:T(8,128)(2,1)S(1)}, bf16[256,128]{1,0:T(8,128)(2,1)S(1)}, u32[]{:S(2)}, u32[]{:S(2)}) collective-permute-start(bf16[256,128]{1,0:T(8,128)(2,1)S(1)} %collective-permute-done.1.refs_1_), channel_id=1, source_target_pairs={{0,0},{4,4},{8,8},{12,12},{16,20},{20,16},{24,28},{28,24},{1,1},{5... | collective-permute-start | bytes 196616 | tf_op jit(solution)/shard_map/ppermute | solution.py:167
  16.1 0.0 copy-done.1
  16.2 0.0 collective-permute-done.refs_0_
  16.2 2.5 %shard_map.56 = (f32[1,1024]{1,0:T(1,128)S(1)}, f32[1,1024]{1,0:T(1,128)S(1)}, f32[128,1024]{1,0:T(8,128)S(1)}) custom-call(s32[8,128]{1,0:T(8,128)S(1)} %get-tuple-element.21.reached_ref.tree_ref, bf16[1024,128]{1,0:T(8,128)(2,1)S(1)} %bitcast.4, bf16[256,128]{1,0:T(8,128)(2,1)S(1)} %get-tuple-element.22.kv_ref, ...), custom_call_target="tpu_custom_call" | custom-call | flops 130000000 | bytes 1000000 | tf_op jit(solution)/shard_map/pallas_call | solution.py:190
  18.7 0.0 collective-permute-done.5.refs_1_
  18.7 0.0 collective-permute-done.4.refs_0_
  18.7 0.7 %shard_map.57 = (f32[1,1024]{1,0:T(1,128)S(1)}, f32[1,1024]{1,0:T(1,128)S(1)}, f32[128,1024]{1,0:T(8,128)S(1)}) custom-call(s32[8,128]{1,0:T(8,128)S(1)} %get-tuple-element.21.reached_ref.tree_ref, bf16[1024,128]{1,0:T(8,128)(2,1)S(1)} %bitcast.5, f32[1,1024]{1,0:T(1,128)S(1)} %get-tuple-element.23.m_in, ...), custom_call_target="tpu_custom_call", output_to_operand_aliasing={{0}: (2, {}), {1}: (3, {}), {2}: (4, {})} | custom-call | flops 270000000 | bytes 1000000 | tf_op jit(solution)/shard_map/pallas_call | solution.py:207
  19.5 0.4 %collective-permute-done.6.refs_0_ = bf16[256,128]{1,0:T(8,128)(2,1)S(1)} collective-permute-done((bf16[256,128]{1,0:T(8,128)(2,1)S(1)}, bf16[256,128]{1,0:T(8,128)(2,1)S(1)}, u32[]{:S(2)}, u32[]{:S(2)}) %collective-permute-start.6) | collective-permute-done | bytes 65568 | tf_op jit(solution)/shard_map/ppermute | solution.py:167
  19.8 0.0 copy-done
  19.8 1.2 %shard_map.58 = (bf16[128,1024]{1,0:T(8,128)(2,1)S(1)}, bf16[128,512]{1,0:T(8,128)(2,1)S(1)}, f32[128,512]{1,0:T(8,128)S(1)}, f32[1,1024]{1,0:T(1,128)S(1)}, f32...) custom-call(s32[8,128]{1,0:T(8,128)S(1)} %get-tuple-element.21.reached_ref, ...), custom_call_target="tpu_custom_call", output_to_operand_aliasing={{3}: (2, {}), {4}: (3, {}), {5}: (4, {})} | custom-call | flops 1000000000 | bytes 10000000 | tf_op jit(solution)/shard_map/pallas_call | solution.py:227
  21.1 0.1 collective-permute-start.7
  21.1 0.5 %shard_map.60 = (bf16[128,512]{1,0:T(8,128)(2,1)S(1)}, f32[128,512]{1,0:T(8,128)S(1)}) custom-call(bf16[128,1024]{1,0:T(8,128)(2,1)S(1)} %get-tuple-element.32.att_ref, bf16[1024,4096]{1,0:T(8,128)(2,1)S(1)} %copy-done), custom_call_target="tpu_custom_call" | custom-call | flops 540000000 | bytes 4000000 | tf_op jit(solution)/shard_map/pallas_call | solution.py:238
  21.6 0.6 %collective-permute-start.10 = (bf16[128,512]{1,0:T(8,128)(2,1)S(1)}, bf16[128,512]{1,0:T(8,128)(2,1)S(1)}, u32[]{:S(2)}, u32[]{:S(2)}) collective-permute-start(bf16[128,512]{1,0:T(8,128)(2,1)S(1)} %get-tuple-element.36), channel_id=1, source_target_pairs={{0,1},{1,0},{2,3},{3,2},{4,5},{5,4},{6,7},{7,6},{8,9},{9,8},{10,11... | collective-permute-start | bytes 393224 | tf_op jit(solution)/shard_map/ppermute | solution.py:163
  22.2 0.3 %collective-permute-done.7 = bf16[128,512]{1,0:T(8,128)(2,1)S(1)} collective-permute-done((bf16[128,512]{1,0:T(8,128)(2,1)S(1)}, bf16[128,512]{1,0:T(8,128)(2,1)S(1)}, u32[]{:S(2)}, u32[]{:S(2)}) %collective-permute-start.7) | collective-permute-done | bytes 131104 | tf_op jit(solution)/shard_map/ppermute | solution.py:163
  22.5 1.6 %collective-permute-start.9 = (bf16[128,512]{1,0:T(8,128)(2,1)S(1)}, bf16[128,512]{1,0:T(8,128)(2,1)S(1)}, u32[]{:S(2)}, u32[]{:S(2)}) collective-permute-start(bf16[128,512]{1,0:T(8,128)(2,1)S(1)} %add_convert_fusion.2), channel_id=1, source_target_pairs={{0,2},{1,3},{2,0},{3,1},{4,6},{5,7},{6,4},{7,5},{8,10},{9,11},{10,... | collective-permute-start | bytes 393224 | tf_op jit(solution)/shard_map/ppermute | solution.py:163
  24.1 0.7 %shard_map.59 = (bf16[128,1024]{1,0:T(8,128)(2,1)S(1)}, f32[128,1024]{1,0:T(8,128)S(1)}) custom-call(bf16[128,1024]{1,0:T(8,128)(2,1)S(1)} %get-tuple-element.32.att_ref, bf16[1024,4096]{1,0:T(8,128)(2,1)S(1)} %copy-done), custom_call_target="tpu_custom_call" | custom-call | flops 540000000 | bytes 4000000 | tf_op jit(solution)/shard_map/pallas_call | solution.py:238
  24.8 0.1 collective-permute-start.8
  24.9 0.0 collective-permute-done.10
  24.9 0.6 %collective-permute-start.11 = (bf16[128,512]{1,0:T(8,128)(2,1)S(1)}, bf16[128,512]{1,0:T(8,128)(2,1)S(1)}, u32[]{:S(2)}, u32[]{:S(2)}) collective-permute-start(bf16[128,512]{1,0:T(8,128)(2,1)S(1)} %add_convert_fusion.1), channel_id=1, source_target_pairs={{0,2},{1,3},{2,0},{3,1},{4,6},{5,7},{6,4},{7,5},{8,10},{9,11},{10,... | collective-permute-start | bytes 393224 | tf_op jit(solution)/shard_map/ppermute | solution.py:163
  25.5 2.6 %collective-permute-done.9 = bf16[128,512]{1,0:T(8,128)(2,1)S(1)} collective-permute-done((bf16[128,512]{1,0:T(8,128)(2,1)S(1)}, bf16[128,512]{1,0:T(8,128)(2,1)S(1)}, u32[]{:S(2)}, u32[]{:S(2)}) %collective-permute-start.9) | collective-permute-done | bytes 131104 | tf_op jit(solution)/shard_map/ppermute | solution.py:163
  28.1 2.8 %collective-permute-done.11 = bf16[128,512]{1,0:T(8,128)(2,1)S(1)} collective-permute-done((bf16[128,512]{1,0:T(8,128)(2,1)S(1)}, bf16[128,512]{1,0:T(8,128)(2,1)S(1)}, u32[]{:S(2)}, u32[]{:S(2)}) %collective-permute-start.11) | collective-permute-done | bytes 131104 | tf_op jit(solution)/shard_map/ppermute | solution.py:163
  30.9 0.0 collective-permute-done.8
  30.9 0.8 %add_convert_fusion = bf16[128,1024]{1,0:T(8,128)(2,1)} fusion(f32[128,1024]{1,0:T(8,128)S(1)} %get-tuple-element.33, bf16[128,1024]{1,0:T(8,128)(2,1)S(1)} %collective-permute-done.8, bf16[128,512]{1,0:T(8,128)(2,1)S(1)} %collective-permute-done.11, bf16[128,512]{1,0:T(8,128)(2,1)S(1)} %collective-permute-done.9), kind=kLoop, calls=%fused_computation | loop fusion | flops 1048576 | bytes 1310720 | tf_op jit(solution)/shard_map/convert_element_type | solution.py:266
  (3 shorter events, 0.1 us)
Async XLA Ops:
  0.0 16.1 %copy-start.1 = (bf16[128,8,128]{2,1,0:T(8,128)(2,1)S(1)}, bf16[128,8,128]{2,1,0:T(8,128)(2,1)}, u32[]{:S(2)}) copy-start(bf16[128,8,128]{2,1,0:T(8,128)(2,1)} %param.5) | copy-start | bytes 786436
  0.0 19.8 %copy-start = (bf16[1024,4096]{1,0:T(8,128)(2,1)S(1)}, bf16[1024,4096]{1,0:T(8,128)(2,1)}, u32[]{:S(2)}) copy-start(bf16[1024,4096]{1,0:T(8,128)(2,1)} %w_ref.3) | copy-start | bytes 25165828
  1.0 6.8 %collective-permute-start.3 = (bf16[256,128]{1,0:T(8,128)(2,1)S(1)}, bf16[256,128]{1,0:T(8,128)(2,1)S(1)}, u32[]{:S(2)}, u32[]{:S(2)}) collective-permute-start(bf16[256,128]{1,0:T(8,128)(2,1)S(1)} %get-tuple-element.22.kv_ref), channel_id=1, source_target_pairs={{0,24},{4,28},{8,16},{12,20},{16,8},{20,12},{24,0},{28,4},{1,25},{... | collective-permute-start | bytes 196616 | tf_op jit(solution)/shard_map/ppermute | solution.py:163
  1.2 9.0 %collective-permute-start.2 = (bf16[256,128]{1,0:T(8,128)(2,1)S(1)}, bf16[256,128]{1,0:T(8,128)(2,1)S(1)}, u32[]{:S(2)}, u32[]{:S(2)}) collective-permute-start(bf16[256,128]{1,0:T(8,128)(2,1)S(1)} %get-tuple-element.22.kv_ref), channel_id=1, source_target_pairs={{0,8},{4,12},{8,0},{12,4},{16,24},{20,28},{24,16},{28,20},{1,9},{5... | collective-permute-start | bytes 196616 | tf_op jit(solution)/shard_map/ppermute | solution.py:163
  1.9 11.7 %collective-permute-start.1 = (bf16[256,128]{1,0:T(8,128)(2,1)S(1)}, bf16[256,128]{1,0:T(8,128)(2,1)S(1)}, u32[]{:S(2)}, u32[]{:S(2)}) collective-permute-start(bf16[256,128]{1,0:T(8,128)(2,1)S(1)} %get-tuple-element.22.kv_ref), channel_id=1, source_target_pairs={{0,16},{4,20},{8,24},{12,28},{16,0},{20,4},{24,8},{28,12},{1,17},{... | collective-permute-start | bytes 196616 | tf_op jit(solution)/shard_map/ppermute | solution.py:163
  5.4 10.7 %collective-permute-start = (bf16[256,128]{1,0:T(8,128)(2,1)S(1)}, bf16[256,128]{1,0:T(8,128)(2,1)S(1)}, u32[]{:S(2)}, u32[]{:S(2)}) collective-permute-start(bf16[256,128]{1,0:T(8,128)(2,1)S(1)} %get-tuple-element.22.kv_ref), channel_id=1, source_target_pairs={{0,4},{4,0},{8,12},{12,8},{16,20},{20,16},{24,28},{28,24},{1,5},{5... | collective-permute-start | bytes 196616 | tf_op jit(solution)/shard_map/ppermute | solution.py:163
  7.8 10.9 %collective-permute-start.5 = (bf16[256,128]{1,0:T(8,128)(2,1)S(1)}, bf16[256,128]{1,0:T(8,128)(2,1)S(1)}, u32[]{:S(2)}, u32[]{:S(2)}) collective-permute-start(bf16[256,128]{1,0:T(8,128)(2,1)S(1)} %collective-permute-done.3.refs_3_), channel_id=1, source_target_pairs={{0,0},{4,4},{8,8},{12,12},{16,20},{20,16},{24,28},{28,24},{1,1},{5... | collective-permute-start | bytes 196616 | tf_op jit(solution)/shard_map/ppermute | solution.py:167
  10.2 8.5 %collective-permute-start.4 = (bf16[256,128]{1,0:T(8,128)(2,1)S(1)}, bf16[256,128]{1,0:T(8,128)(2,1)S(1)}, u32[]{:S(2)}, u32[]{:S(2)}) collective-permute-start(bf16[256,128]{1,0:T(8,128)(2,1)S(1)} %collective-permute-done.2.refs_2_), channel_id=1, source_target_pairs={{0,0},{4,4},{8,12},{12,8},{16,16},{20,20},{24,28},{28,24},{1,1},{5... | collective-permute-start | bytes 196616 | tf_op jit(solution)/shard_map/ppermute | solution.py:167
  13.7 6.2 %collective-permute-start.6 = (bf16[256,128]{1,0:T(8,128)(2,1)S(1)}, bf16[256,128]{1,0:T(8,128)(2,1)S(1)}, u32[]{:S(2)}, u32[]{:S(2)}) collective-permute-start(bf16[256,128]{1,0:T(8,128)(2,1)S(1)} %collective-permute-done.1.refs_1_), channel_id=1, source_target_pairs={{0,0},{4,4},{8,8},{12,12},{16,20},{20,16},{24,28},{28,24},{1,1},{5... | collective-permute-start | bytes 196616 | tf_op jit(solution)/shard_map/ppermute | solution.py:167
  21.1 1.4 %collective-permute-start.7 = (bf16[128,512]{1,0:T(8,128)(2,1)S(1)}, bf16[128,512]{1,0:T(8,128)(2,1)S(1)}, u32[]{:S(2)}, u32[]{:S(2)}) collective-permute-start(bf16[128,512]{1,0:T(8,128)(2,1)S(1)} %get-tuple-element.31), channel_id=1, source_target_pairs={{0,1},{1,0},{2,3},{3,2},{4,5},{5,4},{6,7},{7,6},{8,9},{9,8},{10,11... | collective-permute-start | bytes 393224 | tf_op jit(solution)/shard_map/ppermute | solution.py:163
  21.6 3.3 %collective-permute-start.10 = (bf16[128,512]{1,0:T(8,128)(2,1)S(1)}, bf16[128,512]{1,0:T(8,128)(2,1)S(1)}, u32[]{:S(2)}, u32[]{:S(2)}) collective-permute-start(bf16[128,512]{1,0:T(8,128)(2,1)S(1)} %get-tuple-element.36), channel_id=1, source_target_pairs={{0,1},{1,0},{2,3},{3,2},{4,5},{5,4},{6,7},{7,6},{8,9},{9,8},{10,11... | collective-permute-start | bytes 393224 | tf_op jit(solution)/shard_map/ppermute | solution.py:163
  22.5 5.6 %collective-permute-start.9 = (bf16[128,512]{1,0:T(8,128)(2,1)S(1)}, bf16[128,512]{1,0:T(8,128)(2,1)S(1)}, u32[]{:S(2)}, u32[]{:S(2)}) collective-permute-start(bf16[128,512]{1,0:T(8,128)(2,1)S(1)} %add_convert_fusion.2), channel_id=1, source_target_pairs={{0,2},{1,3},{2,0},{3,1},{4,6},{5,7},{6,4},{7,5},{8,10},{9,11},{10,... | collective-permute-start | bytes 393224 | tf_op jit(solution)/shard_map/ppermute | solution.py:163
  24.8 6.1 %collective-permute-start.8 = (bf16[128,1024]{1,0:T(8,128)(2,1)S(1)}, bf16[128,1024]{1,0:T(8,128)(2,1)S(1)}, u32[]{:S(2)}, u32[]{:S(2)}) collective-permute-start(bf16[128,1024]{1,0:T(8,128)(2,1)S(1)} %get-tuple-element.34), channel_id=1, source_target_pairs={{0,1},{1,0},{2,3},{3,2},{4,5},{5,4},{6,7},{7,6},{8,9},{9,8},{10,11... | collective-permute-start | bytes 786440 | tf_op jit(solution)/shard_map/ppermute | solution.py:163
  24.9 6.0 %collective-permute-start.11 = (bf16[128,512]{1,0:T(8,128)(2,1)S(1)}, bf16[128,512]{1,0:T(8,128)(2,1)S(1)}, u32[]{:S(2)}, u32[]{:S(2)}) collective-permute-start(bf16[128,512]{1,0:T(8,128)(2,1)S(1)} %add_convert_fusion.1), channel_id=1, source_target_pairs={{0,2},{1,3},{2,0},{3,1},{4,6},{5,7},{6,4},{7,5},{8,10},{9,11},{10,... | collective-permute-start | bytes 393224 | tf_op jit(solution)/shard_map/ppermute | solution.py:163

commit v10 on v8

--- a/solution.py
+++ b/solution.py
@@ -180,13 +180,14 @@
     )(in_hbm(key_heads[:, 0, :]), in_hbm(value_heads[:, 0, :]), in_hbm(parents))
     if ctx_size == DIRECT_SIZE:
         by_4 = swap(kv, "ctx", ctx_size, 4)
+        by_2 = swap(kv, "ctx", ctx_size, 2)
         by_1 = swap(kv, "ctx", ctx_size, 1)
-        by_6 = swap(kv, "ctx", ctx_size, 6)
-        held, _ = lax.optimization_barrier((by_1, by_6))
-        by_23 = swap(jnp.concatenate([kv, held], axis=0), "ctx", ctx_size, 2)
+        held, _ = lax.optimization_barrier((by_4, by_1))
+        by_6 = swap(held, "ctx", ctx_size, 2)
+        by_5 = swap(by_4, "ctx", ctx_size, 1)
+        by_3 = swap(by_2, "ctx", ctx_size, 1)
         by_7 = swap(by_6, "ctx", ctx_size, 1)
-        by_5 = swap(by_4, "ctx", ctx_size, 1)
-        early, early_xors = [by_1, by_6, by_4], ((1,), (6,), (4,))
+        early, early_xors = [by_1, by_2, by_4, by_6], ((1,), (2,), (4,), (6,))
     else:
         early, early_xors = [], ()
     q = jnp.transpose(query_heads, (1, 0, 2)).reshape(rows, head_dim)
@@ -207,7 +208,7 @@
     state = (m, l, acc)
     state_shapes = tuple(jax.ShapeDtypeStruct(x.shape, x.dtype) for x in state)
     if ctx_size == DIRECT_SIZE:
-        xors = ((7,),)
+        xors = ((5,), (3,))
         state = pl.pallas_call(
             functools.partial(others_kernel, xors),
             out_shape=state_shapes,
@@ -216,8 +217,8 @@
             input_output_aliases={2: 0, 3: 1, 4: 2},
             compiler_params=params,
             cost_estimate=pl.CostEstimate(flops=270_000_000, bytes_accessed=1_000_000, transcendentals=500_000),
-        )(reached, q, *state, by_7)
-        xors, pieces, tree, tree_spec = ((2, 3), (5,)), [by_23, by_5], reached, vmem
+        )(reached, q, *state, by_5, by_3)
+        xors, pieces, tree, tree_spec = ((7,),), [by_7], reached, vmem
     else:
         xors, pieces, tree, tree_spec = (), [lax.all_gather(kv, "ctx", axis=0, tiled=True)], parents, smem
 

time: 28.7 us -> 29.4 us (1.024)
  starting transfers between devices: 11.5 us -> 15.2 us
  waiting for transfers between devices: 12.4 us -> 9.49 us
    ppermute x11 -> x12, starting transfers between devices: 11.5 us -> 15.2 us  [swap(): return lax.ppermute(x, axis, [(i, i ^ other) for i in range(size)])]
    ppermute x11 -> x12, waiting for transfers between devices: 12.4 us -> 9.49 us  [swap(): return lax.ppermute(x, axis, [(i, i ^ other) for i in range(size)])]
  transfers between devices with their start and end apart: 11 -> 12, of which waited for: 8 -> 8; matrix products, arithmetic and copies ran while one was open for 0% -> 0% of each run, Pallas kernels for 7% -> 7%
where the time goes in v10:
time: 29.4 us; the launch traced here: 29.3 us
  starting transfers between devices  15.2 us (52%)
  waiting for transfers between devices  9.49 us (32%)
  Pallas kernels  3.59 us (12%)
  other arithmetic  0.87 us (3%)
    ppermute x12, starting transfers between devices, swap(): return lax.ppermute(x, axis, [(i, i ^ other) for i in range(size)])  15.2 us
    ppermute x12, waiting for transfers between devices, swap(): return lax.ppermute(x, axis, [(i, i ^ other) for i in range(size)])  9.49 us
    pallas_call x2, Pallas kernels, projected(): pl.pallas_call(functools.partial(project_pair, flip, part), out_shape=sha...  1.18 us
    pallas_call x1, Pallas kernels, shards(): pl.pallas_call(functools.partial(pack_kernel, ctx_size == DIRECT_SIZE), o...  0.95 us
    convert_element_type x1, other arithmetic, shards(): (keep_near + near_in.astype(jnp.float32) + from_far).astype(jnp.bfloat16)  0.8 us
    pallas_call x1, Pallas kernels, shards(): pl.pallas_call(functools.partial(last_kernel, xors), out_shape=(jax.Shape...  0.71 us
  transfers between devices with their start and end apart: 12, of which 8 were waited for; matrix products, arithmetic and copies ran while one was open for 0% of the time, Pallas kernels for 7%

profile of v10, /device:TPU:0, one launch (start us, length us, event | category | flops | bytes accessed | tf_op | source)
XLA Modules:
  0.0 29.3 jit_solution(5621819421263265824)
XLA Ops:
  0.0 0.0 copy-start.1
  0.0 0.0 copy-start
  0.0 0.9 %shard_map.55 = (bf16[256,128]{1,0:T(8,128)(2,1)S(1)}, s32[8,128]{1,0:T(8,128)S(1)}) custom-call(bf16[128,128]{1,0:T(8,128)(2,1)} %bitcast.8, bf16[128,128]{1,0:T(8,128)(2,1)} %bitcast.9, s32[8]{0:T(128)} %parents_hbm.1), custom_call_target="tpu_custom_call" | custom-call | flops 8000000000 | bytes 130000 | tf_op jit(solution)/shard_map/pallas_call | solution.py:169
  1.0 4.1 %collective-permute-start.2 = (bf16[256,128]{1,0:T(8,128)(2,1)S(1)}, bf16[256,128]{1,0:T(8,128)(2,1)S(1)}, u32[]{:S(2)}, u32[]{:S(2)}) collective-permute-start(bf16[256,128]{1,0:T(8,128)(2,1)S(1)} %get-tuple-element.23.kv_ref), channel_id=1, source_target_pairs={{0,16},{4,20},{8,24},{12,28},{16,0},{20,4},{24,8},{28,12},{1,17},{... | collective-permute-start | bytes 196616 | tf_op jit(solution)/shard_map/ppermute | solution.py:167
  5.1 1.5 %collective-permute-start = (bf16[256,128]{1,0:T(8,128)(2,1)S(1)}, bf16[256,128]{1,0:T(8,128)(2,1)S(1)}, u32[]{:S(2)}, u32[]{:S(2)}) collective-permute-start(bf16[256,128]{1,0:T(8,128)(2,1)S(1)} %get-tuple-element.23.kv_ref), channel_id=1, source_target_pairs={{0,4},{4,0},{8,12},{12,8},{16,20},{20,16},{24,28},{28,24},{1,5},{5... | collective-permute-start | bytes 196616 | tf_op jit(solution)/shard_map/ppermute | solution.py:167
  6.6 1.6 %collective-permute-start.1 = (bf16[256,128]{1,0:T(8,128)(2,1)S(1)}, bf16[256,128]{1,0:T(8,128)(2,1)S(1)}, u32[]{:S(2)}, u32[]{:S(2)}) collective-permute-start(bf16[256,128]{1,0:T(8,128)(2,1)S(1)} %get-tuple-element.23.kv_ref), channel_id=1, source_target_pairs={{0,8},{4,12},{8,0},{12,4},{16,24},{20,28},{24,16},{28,20},{1,9},{5... | collective-permute-start | bytes 196616 | tf_op jit(solution)/shard_map/ppermute | solution.py:167
  8.2 0.2 collective-permute-done.2.refs_2_
  8.4 1.0 %collective-permute-done.refs_0_ = bf16[256,128]{1,0:T(8,128)(2,1)S(1)} collective-permute-done((bf16[256,128]{1,0:T(8,128)(2,1)S(1)}, bf16[256,128]{1,0:T(8,128)(2,1)S(1)}, u32[]{:S(2)}, u32[]{:S(2)}) %collective-permute-start) | collective-permute-done | bytes 65568 | tf_op jit(solution)/shard_map/ppermute | solution.py:167
  9.3 1.6 %collective-permute-start.3 = (bf16[256,128]{1,0:T(8,128)(2,1)S(1)}, bf16[256,128]{1,0:T(8,128)(2,1)S(1)}, u32[]{:S(2)}, u32[]{:S(2)}) collective-permute-start(bf16[256,128]{1,0:T(8,128)(2,1)S(1)} %collective-permute-done.2.refs_2_), channel_id=1, source_target_pairs={{0,8},{4,12},{8,0},{12,4},{16,24},{20,28},{24,16},{28,20},{1,9},{5... | collective-permute-start | bytes 196616 | tf_op jit(solution)/shard_map/ppermute | solution.py:167
  10.9 1.5 %collective-permute-start.4 = (bf16[256,128]{1,0:T(8,128)(2,1)S(1)}, bf16[256,128]{1,0:T(8,128)(2,1)S(1)}, u32[]{:S(2)}, u32[]{:S(2)}) collective-permute-start(bf16[256,128]{1,0:T(8,128)(2,1)S(1)} %collective-permute-done.2.refs_2_), channel_id=1, source_target_pairs={{0,4},{4,0},{8,12},{12,8},{16,20},{20,16},{24,28},{28,24},{1,5},{5... | collective-permute-start | bytes 196616 | tf_op jit(solution)/shard_map/ppermute | solution.py:167
  12.4 0.0 collective-permute-done.1.refs_1_
  12.4 0.5 %collective-permute-start.5 = (bf16[256,128]{1,0:T(8,128)(2,1)S(1)}, bf16[256,128]{1,0:T(8,128)(2,1)S(1)}, u32[]{:S(2)}, u32[]{:S(2)}) collective-permute-start(bf16[256,128]{1,0:T(8,128)(2,1)S(1)} %collective-permute-done.1.refs_1_), channel_id=1, source_target_pairs={{0,4},{4,0},{8,12},{12,8},{16,20},{20,16},{24,28},{28,24},{1,5},{5... | collective-permute-start | bytes 196616 | tf_op jit(solution)/shard_map/ppermute | solution.py:167
  12.9 0.7 %collective-permute-done.3.refs_3_ = bf16[256,128]{1,0:T(8,128)(2,1)S(1)} collective-permute-done((bf16[256,128]{1,0:T(8,128)(2,1)S(1)}, bf16[256,128]{1,0:T(8,128)(2,1)S(1)}, u32[]{:S(2)}, u32[]{:S(2)}) %collective-permute-start.3) | collective-permute-done | bytes 65568 | tf_op jit(solution)/shard_map/ppermute | solution.py:167
  13.6 1.5 %collective-permute-start.6 = (bf16[256,128]{1,0:T(8,128)(2,1)S(1)}, bf16[256,128]{1,0:T(8,128)(2,1)S(1)}, u32[]{:S(2)}, u32[]{:S(2)}) collective-permute-start(bf16[256,128]{1,0:T(8,128)(2,1)S(1)} %collective-permute-done.3.refs_3_), channel_id=1, source_target_pairs={{0,4},{4,0},{8,12},{12,8},{16,20},{20,16},{24,28},{28,24},{1,5},{5... | collective-permute-start | bytes 196616 | tf_op jit(solution)/shard_map/ppermute | solution.py:167
  15.1 0.0 copy-done.1
  15.2 0.5 %shard_map.56 = (f32[1,1024]{1,0:T(1,128)S(1)}, f32[1,1024]{1,0:T(1,128)S(1)}, f32[128,1024]{1,0:T(8,128)S(1)}) custom-call(s32[8,128]{1,0:T(8,128)S(1)} %get-tuple-element.22.reached_ref.tree_ref, bf16[1024,128]{1,0:T(8,128)(2,1)S(1)} %bitcast.4, bf16[256,128]{1,0:T(8,128)(2,1)S(1)} %get-tuple-element.23.kv_ref, ...), custom_call_target="tpu_custom_call" | custom-call | flops 130000000 | bytes 1000000 | tf_op jit(solution)/shard_map/pallas_call | solution.py:195
  15.7 0.0 collective-permute-done.4.refs_0_
  15.7 1.0 %collective-permute-done.5.refs_1_ = bf16[256,128]{1,0:T(8,128)(2,1)S(1)} collective-permute-done((bf16[256,128]{1,0:T(8,128)(2,1)S(1)}, bf16[256,128]{1,0:T(8,128)(2,1)S(1)}, u32[]{:S(2)}, u32[]{:S(2)}) %collective-permute-start.5) | collective-permute-done | bytes 65568 | tf_op jit(solution)/shard_map/ppermute | solution.py:167
  16.7 0.2 shard_map.57
  16.9 0.9 %collective-permute-done.6.refs_0_ = bf16[256,128]{1,0:T(8,128)(2,1)S(1)} collective-permute-done((bf16[256,128]{1,0:T(8,128)(2,1)S(1)}, bf16[256,128]{1,0:T(8,128)(2,1)S(1)}, u32[]{:S(2)}, u32[]{:S(2)}) %collective-permute-start.6) | collective-permute-done | bytes 65568 | tf_op jit(solution)/shard_map/ppermute | solution.py:167
  17.9 0.0 copy-done
  17.9 0.7 %shard_map.58 = (bf16[128,1024]{1,0:T(8,128)(2,1)S(1)}, bf16[128,512]{1,0:T(8,128)(2,1)S(1)}, f32[128,512]{1,0:T(8,128)S(1)}, f32[1,1024]{1,0:T(1,128)S(1)}, f32...) custom-call(s32[8,128]{1,0:T(8,128)S(1)} %get-tuple-element.22.reached_ref, ...), custom_call_target="tpu_custom_call", output_to_operand_aliasing={{3}: (2, {}), {4}: (3, {}), {5}: (4, {})} | custom-call | flops 1000000000 | bytes 10000000 | tf_op jit(solution)/shard_map/pallas_call | solution.py:230
  18.6 0.1 collective-permute-start.7
  18.7 0.5 %shard_map.60 = (bf16[128,512]{1,0:T(8,128)(2,1)S(1)}, f32[128,512]{1,0:T(8,128)S(1)}) custom-call(bf16[128,1024]{1,0:T(8,128)(2,1)S(1)} %get-tuple-element.34.att_ref, bf16[1024,4096]{1,0:T(8,128)(2,1)S(1)} %copy-done), custom_call_target="tpu_custom_call" | custom-call | flops 540000000 | bytes 4000000 | tf_op jit(solution)/shard_map/pallas_call | solution.py:241
  19.1 0.6 %collective-permute-start.10 = (bf16[128,512]{1,0:T(8,128)(2,1)S(1)}, bf16[128,512]{1,0:T(8,128)(2,1)S(1)}, u32[]{:S(2)}, u32[]{:S(2)}) collective-permute-start(bf16[128,512]{1,0:T(8,128)(2,1)S(1)} %get-tuple-element.38), channel_id=1, source_target_pairs={{0,1},{1,0},{2,3},{3,2},{4,5},{5,4},{6,7},{7,6},{8,9},{9,8},{10,11... | collective-permute-start | bytes 393224 | tf_op jit(solution)/shard_map/ppermute | solution.py:167
  19.7 0.3 %collective-permute-done.7 = bf16[128,512]{1,0:T(8,128)(2,1)S(1)} collective-permute-done((bf16[128,512]{1,0:T(8,128)(2,1)S(1)}, bf16[128,512]{1,0:T(8,128)(2,1)S(1)}, u32[]{:S(2)}, u32[]{:S(2)}) %collective-permute-start.7) | collective-permute-done | bytes 131104 | tf_op jit(solution)/shard_map/ppermute | solution.py:167
  20.0 1.6 %collective-permute-start.9 = (bf16[128,512]{1,0:T(8,128)(2,1)S(1)}, bf16[128,512]{1,0:T(8,128)(2,1)S(1)}, u32[]{:S(2)}, u32[]{:S(2)}) collective-permute-start(bf16[128,512]{1,0:T(8,128)(2,1)S(1)} %add_convert_fusion.2), channel_id=1, source_target_pairs={{0,2},{1,3},{2,0},{3,1},{4,6},{5,7},{6,4},{7,5},{8,10},{9,11},{10,... | collective-permute-start | bytes 393224 | tf_op jit(solution)/shard_map/ppermute | solution.py:167
  21.6 0.7 %shard_map.59 = (bf16[128,1024]{1,0:T(8,128)(2,1)S(1)}, f32[128,1024]{1,0:T(8,128)S(1)}) custom-call(bf16[128,1024]{1,0:T(8,128)(2,1)S(1)} %get-tuple-element.34.att_ref, bf16[1024,4096]{1,0:T(8,128)(2,1)S(1)} %copy-done), custom_call_target="tpu_custom_call" | custom-call | flops 540000000 | bytes 4000000 | tf_op jit(solution)/shard_map/pallas_call | solution.py:241
  22.3 0.1 collective-permute-start.8
  22.4 0.0 collective-permute-done.10
  22.5 0.6 %collective-permute-start.11 = (bf16[128,512]{1,0:T(8,128)(2,1)S(1)}, bf16[128,512]{1,0:T(8,128)(2,1)S(1)}, u32[]{:S(2)}, u32[]{:S(2)}) collective-permute-start(bf16[128,512]{1,0:T(8,128)(2,1)S(1)} %add_convert_fusion.1), channel_id=1, source_target_pairs={{0,2},{1,3},{2,0},{3,1},{4,6},{5,7},{6,4},{7,5},{8,10},{9,11},{10,... | collective-permute-start | bytes 393224 | tf_op jit(solution)/shard_map/ppermute | solution.py:167
  23.1 2.6 %collective-permute-done.9 = bf16[128,512]{1,0:T(8,128)(2,1)S(1)} collective-permute-done((bf16[128,512]{1,0:T(8,128)(2,1)S(1)}, bf16[128,512]{1,0:T(8,128)(2,1)S(1)}, u32[]{:S(2)}, u32[]{:S(2)}) %collective-permute-start.9) | collective-permute-done | bytes 131104 | tf_op jit(solution)/shard_map/ppermute | solution.py:167
  25.7 2.8 %collective-permute-done.11 = bf16[128,512]{1,0:T(8,128)(2,1)S(1)} collective-permute-done((bf16[128,512]{1,0:T(8,128)(2,1)S(1)}, bf16[128,512]{1,0:T(8,128)(2,1)S(1)}, u32[]{:S(2)}, u32[]{:S(2)}) %collective-permute-start.11) | collective-permute-done | bytes 131104 | tf_op jit(solution)/shard_map/ppermute | solution.py:167
  28.5 0.0 collective-permute-done.8
  28.5 0.8 %add_convert_fusion = bf16[128,1024]{1,0:T(8,128)(2,1)} fusion(f32[128,1024]{1,0:T(8,128)S(1)} %get-tuple-element.35, bf16[128,1024]{1,0:T(8,128)(2,1)S(1)} %collective-permute-done.8, bf16[128,512]{1,0:T(8,128)(2,1)S(1)} %collective-permute-done.11, bf16[128,512]{1,0:T(8,128)(2,1)S(1)} %collective-permute-done.9), kind=kLoop, calls=%fused_computation | loop fusion | flops 1048576 | bytes 1310720 | tf_op jit(solution)/shard_map/convert_element_type | solution.py:269
  (3 shorter events, 0.1 us)
Async XLA Ops:
  0.0 15.1 %copy-start.1 = (bf16[128,8,128]{2,1,0:T(8,128)(2,1)S(1)}, bf16[128,8,128]{2,1,0:T(8,128)(2,1)}, u32[]{:S(2)}) copy-start(bf16[128,8,128]{2,1,0:T(8,128)(2,1)} %param.5) | copy-start | bytes 786436
  0.0 17.9 %copy-start = (bf16[1024,4096]{1,0:T(8,128)(2,1)S(1)}, bf16[1024,4096]{1,0:T(8,128)(2,1)}, u32[]{:S(2)}) copy-start(bf16[1024,4096]{1,0:T(8,128)(2,1)} %w_ref.3) | copy-start | bytes 25165828
  1.0 7.4 %collective-permute-start.2 = (bf16[256,128]{1,0:T(8,128)(2,1)S(1)}, bf16[256,128]{1,0:T(8,128)(2,1)S(1)}, u32[]{:S(2)}, u32[]{:S(2)}) collective-permute-start(bf16[256,128]{1,0:T(8,128)(2,1)S(1)} %get-tuple-element.23.kv_ref), channel_id=1, source_target_pairs={{0,16},{4,20},{8,24},{12,28},{16,0},{20,4},{24,8},{28,12},{1,17},{... | collective-permute-start | bytes 196616 | tf_op jit(solution)/shard_map/ppermute | solution.py:167
  5.1 4.3 %collective-permute-start = (bf16[256,128]{1,0:T(8,128)(2,1)S(1)}, bf16[256,128]{1,0:T(8,128)(2,1)S(1)}, u32[]{:S(2)}, u32[]{:S(2)}) collective-permute-start(bf16[256,128]{1,0:T(8,128)(2,1)S(1)} %get-tuple-element.23.kv_ref), channel_id=1, source_target_pairs={{0,4},{4,0},{8,12},{12,8},{16,20},{20,16},{24,28},{28,24},{1,5},{5... | collective-permute-start | bytes 196616 | tf_op jit(solution)/shard_map/ppermute | solution.py:167
  6.6 5.8 %collective-permute-start.1 = (bf16[256,128]{1,0:T(8,128)(2,1)S(1)}, bf16[256,128]{1,0:T(8,128)(2,1)S(1)}, u32[]{:S(2)}, u32[]{:S(2)}) collective-permute-start(bf16[256,128]{1,0:T(8,128)(2,1)S(1)} %get-tuple-element.23.kv_ref), channel_id=1, source_target_pairs={{0,8},{4,12},{8,0},{12,4},{16,24},{20,28},{24,16},{28,20},{1,9},{5... | collective-permute-start | bytes 196616 | tf_op jit(solution)/shard_map/ppermute | solution.py:167
  9.3 4.3 %collective-permute-start.3 = (bf16[256,128]{1,0:T(8,128)(2,1)S(1)}, bf16[256,128]{1,0:T(8,128)(2,1)S(1)}, u32[]{:S(2)}, u32[]{:S(2)}) collective-permute-start(bf16[256,128]{1,0:T(8,128)(2,1)S(1)} %collective-permute-done.2.refs_2_), channel_id=1, source_target_pairs={{0,8},{4,12},{8,0},{12,4},{16,24},{20,28},{24,16},{28,20},{1,9},{5... | collective-permute-start | bytes 196616 | tf_op jit(solution)/shard_map/ppermute | solution.py:167
  10.9 4.8 %collective-permute-start.4 = (bf16[256,128]{1,0:T(8,128)(2,1)S(1)}, bf16[256,128]{1,0:T(8,128)(2,1)S(1)}, u32[]{:S(2)}, u32[]{:S(2)}) collective-permute-start(bf16[256,128]{1,0:T(8,128)(2,1)S(1)} %collective-permute-done.2.refs_2_), channel_id=1, source_target_pairs={{0,4},{4,0},{8,12},{12,8},{16,20},{20,16},{24,28},{28,24},{1,5},{5... | collective-permute-start | bytes 196616 | tf_op jit(solution)/shard_map/ppermute | solution.py:167
  12.4 4.3 %collective-permute-start.5 = (bf16[256,128]{1,0:T(8,128)(2,1)S(1)}, bf16[256,128]{1,0:T(8,128)(2,1)S(1)}, u32[]{:S(2)}, u32[]{:S(2)}) collective-permute-start(bf16[256,128]{1,0:T(8,128)(2,1)S(1)} %collective-permute-done.1.refs_1_), channel_id=1, source_target_pairs={{0,4},{4,0},{8,12},{12,8},{16,20},{20,16},{24,28},{28,24},{1,5},{5... | collective-permute-start | bytes 196616 | tf_op jit(solution)/shard_map/ppermute | solution.py:167
  13.6 4.3 %collective-permute-start.6 = (bf16[256,128]{1,0:T(8,128)(2,1)S(1)}, bf16[256,128]{1,0:T(8,128)(2,1)S(1)}, u32[]{:S(2)}, u32[]{:S(2)}) collective-permute-start(bf16[256,128]{1,0:T(8,128)(2,1)S(1)} %collective-permute-done.3.refs_3_), channel_id=1, source_target_pairs={{0,4},{4,0},{8,12},{12,8},{16,20},{20,16},{24,28},{28,24},{1,5},{5... | collective-permute-start | bytes 196616 | tf_op jit(solution)/shard_map/ppermute | solution.py:167
  18.6 1.4 %collective-permute-start.7 = (bf16[128,512]{1,0:T(8,128)(2,1)S(1)}, bf16[128,512]{1,0:T(8,128)(2,1)S(1)}, u32[]{:S(2)}, u32[]{:S(2)}) collective-permute-start(bf16[128,512]{1,0:T(8,128)(2,1)S(1)} %get-tuple-element.33), channel_id=1, source_target_pairs={{0,1},{1,0},{2,3},{3,2},{4,5},{5,4},{6,7},{7,6},{8,9},{9,8},{10,11... | collective-permute-start | bytes 393224 | tf_op jit(solution)/shard_map/ppermute | solution.py:167
  19.1 3.3 %collective-permute-start.10 = (bf16[128,512]{1,0:T(8,128)(2,1)S(1)}, bf16[128,512]{1,0:T(8,128)(2,1)S(1)}, u32[]{:S(2)}, u32[]{:S(2)}) collective-permute-start(bf16[128,512]{1,0:T(8,128)(2,1)S(1)} %get-tuple-element.38), channel_id=1, source_target_pairs={{0,1},{1,0},{2,3},{3,2},{4,5},{5,4},{6,7},{7,6},{8,9},{9,8},{10,11... | collective-permute-start | bytes 393224 | tf_op jit(solution)/shard_map/ppermute | solution.py:167
  20.0 5.6 %collective-permute-start.9 = (bf16[128,512]{1,0:T(8,128)(2,1)S(1)}, bf16[128,512]{1,0:T(8,128)(2,1)S(1)}, u32[]{:S(2)}, u32[]{:S(2)}) collective-permute-start(bf16[128,512]{1,0:T(8,128)(2,1)S(1)} %add_convert_fusion.2), channel_id=1, source_target_pairs={{0,2},{1,3},{2,0},{3,1},{4,6},{5,7},{6,4},{7,5},{8,10},{9,11},{10,... | collective-permute-start | bytes 393224 | tf_op jit(solution)/shard_map/ppermute | solution.py:167
  22.3 6.1 %collective-permute-start.8 = (bf16[128,1024]{1,0:T(8,128)(2,1)S(1)}, bf16[128,1024]{1,0:T(8,128)(2,1)S(1)}, u32[]{:S(2)}, u32[]{:S(2)}) collective-permute-start(bf16[128,1024]{1,0:T(8,128)(2,1)S(1)} %get-tuple-element.36), channel_id=1, source_target_pairs={{0,1},{1,0},{2,3},{3,2},{4,5},{5,4},{6,7},{7,6},{8,9},{9,8},{10,11... | collective-permute-start | bytes 786440 | tf_op jit(solution)/shard_map/ppermute | solution.py:167
  22.5 6.0 %collective-permute-start.11 = (bf16[128,512]{1,0:T(8,128)(2,1)S(1)}, bf16[128,512]{1,0:T(8,128)(2,1)S(1)}, u32[]{:S(2)}, u32[]{:S(2)}) collective-permute-start(bf16[128,512]{1,0:T(8,128)(2,1)S(1)} %add_convert_fusion.1), channel_id=1, source_target_pairs={{0,2},{1,3},{2,0},{3,1},{4,6},{5,7},{6,4},{7,5},{8,10},{9,11},{10,... | collective-permute-start | bytes 393224 | tf_op jit(solution)/shard_map/ppermute | solution.py:167

commit v11 on v7

--- a/solution.py
+++ b/solution.py
@@ -177,7 +177,10 @@
     if ctx_size == DIRECT_SIZE:
         columns = [swap(kv, "ctx", ctx_size, other) for other in (4, 2, 6)]
         beside = swap(kv, "ctx", ctx_size, 1)
-        pairs = [swap(x, "ctx", ctx_size, 1) for x in columns]
+        by_3 = swap(beside, "ctx", ctx_size, 2)
+        by_7 = swap(columns[2], "ctx", ctx_size, 1)
+        by_5 = swap(columns[0], "ctx", ctx_size, 1)
+        pairs = [by_5, by_3, by_7]
         early, early_xors = [beside, *columns], (1, 4, 2, 6)
     else:
         early, early_xors = [], ()
@@ -210,8 +213,8 @@
                 cost_estimate=pl.CostEstimate(flops=270_000_000, bytes_accessed=1_000_000, transcendentals=500_000),
             )(reached, q, *state, *arrived)
 
-        state = absorbed(state, (3, 7), pairs[1:])
-        xors, pieces, tree, tree_spec = (5,), pairs[:1], reached, vmem
+        state = absorbed(state, (7,), [by_7])
+        xors, pieces, tree, tree_spec = (3, 5), [by_3, by_5], reached, vmem
     else:
         xors, pieces, tree, tree_spec = (), [lax.all_gather(kv, "ctx", axis=0, tiled=True)], parents, smem
 

time: 28.2 us -> 29.1 us (1.032)
  waiting for transfers between devices: 9.17 us -> 10.6 us
  starting transfers between devices: 14.3 us -> 13.7 us
    ppermute x12, waiting for transfers between devices: 9.17 us -> 10.6 us  [swap(): return lax.ppermute(x, axis, [(i, i ^ other) for i in range(size)])]
    ppermute x12, starting transfers between devices: 14.3 us -> 13.7 us  [swap(): return lax.ppermute(x, axis, [(i, i ^ other) for i in range(size)])]
where the time goes in v11:
time: 29.1 us; the launch traced here: 29 us
  starting transfers between devices  13.7 us (47%)
  waiting for transfers between devices  10.6 us (36%)
  Pallas kernels  3.59 us (12%)
  other arithmetic  0.87 us (3%)
    ppermute x12, starting transfers between devices, swap(): return lax.ppermute(x, axis, [(i, i ^ other) for i in range(size)])  13.7 us
    ppermute x12, waiting for transfers between devices, swap(): return lax.ppermute(x, axis, [(i, i ^ other) for i in range(size)])  10.6 us
    pallas_call x2, Pallas kernels, projected(): pl.pallas_call(functools.partial(project_pair, flip, part), out_shape=sha...  1.18 us
    pallas_call x1, Pallas kernels, shards(): pl.pallas_call(functools.partial(pack_kernel, ctx_size == DIRECT_SIZE), o...  0.95 us
    convert_element_type x1, other arithmetic, shards(): (keep_near + near_in.astype(jnp.float32) + from_far).astype(jnp.bfloat16)  0.8 us
    pallas_call x1, Pallas kernels, shards(): pl.pallas_call(functools.partial(last_kernel, xors), out_shape=(jax.Shape...  0.71 us
  transfers between devices with their start and end apart: 12, of which 7 were waited for; matrix products, arithmetic and copies ran while one was open for 0% of the time, Pallas kernels for 7%

profile of v11, /device:TPU:0, one launch (start us, length us, event | category | flops | bytes accessed | tf_op | source)
XLA Modules:
  0.0 29.0 jit_solution(8715818961313227217)
XLA Ops:
  0.0 0.0 copy-start.1
  0.0 0.0 copy-start
  0.0 0.9 %shard_map.55 = (bf16[256,128]{1,0:T(8,128)(2,1)S(1)}, s32[8,128]{1,0:T(8,128)S(1)}) custom-call(bf16[128,128]{1,0:T(8,128)(2,1)} %bitcast.8, bf16[128,128]{1,0:T(8,128)(2,1)} %bitcast.9, s32[8]{0:T(128)} %parents_hbm.1), custom_call_target="tpu_custom_call" | custom-call | flops 8000000000 | bytes 130000 | tf_op jit(solution)/shard_map/pallas_call | solution.py:165
  1.0 5.1 %collective-permute-start.3 = (bf16[256,128]{1,0:T(8,128)(2,1)S(1)}, bf16[256,128]{1,0:T(8,128)(2,1)S(1)}, u32[]{:S(2)}, u32[]{:S(2)}) collective-permute-start(bf16[256,128]{1,0:T(8,128)(2,1)S(1)} %get-tuple-element.22.kv_ref), channel_id=1, source_target_pairs={{0,24},{4,28},{8,16},{12,20},{16,8},{20,12},{24,0},{28,4},{1,25},{... | collective-permute-start | bytes 196616 | tf_op jit(solution)/shard_map/ppermute | solution.py:163
  6.1 0.0 collective-permute-start.1
  6.1 1.5 %collective-permute-start = (bf16[256,128]{1,0:T(8,128)(2,1)S(1)}, bf16[256,128]{1,0:T(8,128)(2,1)S(1)}, u32[]{:S(2)}, u32[]{:S(2)}) collective-permute-start(bf16[256,128]{1,0:T(8,128)(2,1)S(1)} %get-tuple-element.22.kv_ref), channel_id=1, source_target_pairs={{0,4},{4,0},{8,12},{12,8},{16,20},{20,16},{24,28},{28,24},{1,5},{5... | collective-permute-start | bytes 196616 | tf_op jit(solution)/shard_map/ppermute | solution.py:163
  7.6 0.8 %collective-permute-start.2 = (bf16[256,128]{1,0:T(8,128)(2,1)S(1)}, bf16[256,128]{1,0:T(8,128)(2,1)S(1)}, u32[]{:S(2)}, u32[]{:S(2)}) collective-permute-start(bf16[256,128]{1,0:T(8,128)(2,1)S(1)} %get-tuple-element.22.kv_ref), channel_id=1, source_target_pairs={{0,8},{4,12},{8,0},{12,4},{16,24},{20,28},{24,16},{28,20},{1,9},{5... | collective-permute-start | bytes 196616 | tf_op jit(solution)/shard_map/ppermute | solution.py:163
  8.4 0.3 collective-permute-done.3.refs_3_
  8.7 1.9 %collective-permute-start.4 = (bf16[256,128]{1,0:T(8,128)(2,1)S(1)}, bf16[256,128]{1,0:T(8,128)(2,1)S(1)}, u32[]{:S(2)}, u32[]{:S(2)}) collective-permute-start(bf16[256,128]{1,0:T(8,128)(2,1)S(1)} %collective-permute-done.3.refs_3_), channel_id=1, source_target_pairs={{0,4},{4,0},{8,12},{12,8},{16,20},{20,16},{24,28},{28,24},{1,5},{5... | collective-permute-start | bytes 196616 | tf_op jit(solution)/shard_map/ppermute | solution.py:163
  10.5 1.2 %collective-permute-done.1.refs_1_ = bf16[256,128]{1,0:T(8,128)(2,1)S(1)} collective-permute-done((bf16[256,128]{1,0:T(8,128)(2,1)S(1)}, bf16[256,128]{1,0:T(8,128)(2,1)S(1)}, u32[]{:S(2)}, u32[]{:S(2)}) %collective-permute-start.1) | collective-permute-done | bytes 65568 | tf_op jit(solution)/shard_map/ppermute | solution.py:163
  11.7 1.6 %collective-permute-start.6 = (bf16[256,128]{1,0:T(8,128)(2,1)S(1)}, bf16[256,128]{1,0:T(8,128)(2,1)S(1)}, u32[]{:S(2)}, u32[]{:S(2)}) collective-permute-start(bf16[256,128]{1,0:T(8,128)(2,1)S(1)} %collective-permute-done.1.refs_1_), channel_id=1, source_target_pairs={{0,4},{4,0},{8,12},{12,8},{16,20},{20,16},{24,28},{28,24},{1,5},{5... | collective-permute-start | bytes 196616 | tf_op jit(solution)/shard_map/ppermute | solution.py:163
  13.3 0.0 collective-permute-done.refs_0_
  13.3 0.0 collective-permute-start.5
  13.3 0.0 copy-done.1
  13.4 0.0 collective-permute-done.2.refs_2_
  13.4 0.5 %shard_map.56 = (f32[1,1024]{1,0:T(1,128)S(1)}, f32[1,1024]{1,0:T(1,128)S(1)}, f32[128,1024]{1,0:T(8,128)S(1)}) custom-call(s32[8,128]{1,0:T(8,128)S(1)} %get-tuple-element.21.reached_ref.tree_ref, bf16[1024,128]{1,0:T(8,128)(2,1)S(1)} %bitcast.4, bf16[256,128]{1,0:T(8,128)(2,1)S(1)} %get-tuple-element.22.kv_ref, ...), custom_call_target="tpu_custom_call" | custom-call | flops 130000000 | bytes 1000000 | tf_op jit(solution)/shard_map/pallas_call | solution.py:189
  13.9 0.0 collective-permute-done.4.refs_0_
  13.9 0.2 shard_map.57
  14.1 1.9 %collective-permute-done.6.refs_1_ = bf16[256,128]{1,0:T(8,128)(2,1)S(1)} collective-permute-done((bf16[256,128]{1,0:T(8,128)(2,1)S(1)}, bf16[256,128]{1,0:T(8,128)(2,1)S(1)}, u32[]{:S(2)}, u32[]{:S(2)}) %collective-permute-start.6) | collective-permute-done | bytes 65568 | tf_op jit(solution)/shard_map/ppermute | solution.py:163
  16.0 1.6 %collective-permute-done.5.refs_0_ = bf16[256,128]{1,0:T(8,128)(2,1)S(1)} collective-permute-done((bf16[256,128]{1,0:T(8,128)(2,1)S(1)}, bf16[256,128]{1,0:T(8,128)(2,1)S(1)}, u32[]{:S(2)}, u32[]{:S(2)}) %collective-permute-start.5) | collective-permute-done | bytes 65568 | tf_op jit(solution)/shard_map/ppermute | solution.py:163
  17.6 0.0 copy-done
  17.6 0.7 %shard_map.58 = (bf16[128,1024]{1,0:T(8,128)(2,1)S(1)}, bf16[128,512]{1,0:T(8,128)(2,1)S(1)}, f32[128,512]{1,0:T(8,128)S(1)}, f32[1,1024]{1,0:T(1,128)S(1)}, f32...) custom-call(s32[8,128]{1,0:T(8,128)S(1)} %get-tuple-element.21.reached_ref, ...), custom_call_target="tpu_custom_call", output_to_operand_aliasing={{3}: (2, {}), {4}: (3, {}), {5}: (4, {})} | custom-call | flops 1000000000 | bytes 10000000 | tf_op jit(solution)/shard_map/pallas_call | solution.py:226
  18.3 0.1 collective-permute-start.7
  18.4 0.5 %shard_map.60 = (bf16[128,512]{1,0:T(8,128)(2,1)S(1)}, f32[128,512]{1,0:T(8,128)S(1)}) custom-call(bf16[128,1024]{1,0:T(8,128)(2,1)S(1)} %get-tuple-element.32.att_ref, bf16[1024,4096]{1,0:T(8,128)(2,1)S(1)} %copy-done), custom_call_target="tpu_custom_call" | custom-call | flops 540000000 | bytes 4000000 | tf_op jit(solution)/shard_map/pallas_call | solution.py:237
  18.8 0.6 %collective-permute-start.10 = (bf16[128,512]{1,0:T(8,128)(2,1)S(1)}, bf16[128,512]{1,0:T(8,128)(2,1)S(1)}, u32[]{:S(2)}, u32[]{:S(2)}) collective-permute-start(bf16[128,512]{1,0:T(8,128)(2,1)S(1)} %get-tuple-element.36), channel_id=1, source_target_pairs={{0,1},{1,0},{2,3},{3,2},{4,5},{5,4},{6,7},{7,6},{8,9},{9,8},{10,11... | collective-permute-start | bytes 393224 | tf_op jit(solution)/shard_map/ppermute | solution.py:163
  19.4 0.3 %collective-permute-done.7 = bf16[128,512]{1,0:T(8,128)(2,1)S(1)} collective-permute-done((bf16[128,512]{1,0:T(8,128)(2,1)S(1)}, bf16[128,512]{1,0:T(8,128)(2,1)S(1)}, u32[]{:S(2)}, u32[]{:S(2)}) %collective-permute-start.7) | collective-permute-done | bytes 131104 | tf_op jit(solution)/shard_map/ppermute | solution.py:163
  19.8 1.6 %collective-permute-start.9 = (bf16[128,512]{1,0:T(8,128)(2,1)S(1)}, bf16[128,512]{1,0:T(8,128)(2,1)S(1)}, u32[]{:S(2)}, u32[]{:S(2)}) collective-permute-start(bf16[128,512]{1,0:T(8,128)(2,1)S(1)} %add_convert_fusion.2), channel_id=1, source_target_pairs={{0,2},{1,3},{2,0},{3,1},{4,6},{5,7},{6,4},{7,5},{8,10},{9,11},{10,... | collective-permute-start | bytes 393224 | tf_op jit(solution)/shard_map/ppermute | solution.py:163
  21.3 0.7 %shard_map.59 = (bf16[128,1024]{1,0:T(8,128)(2,1)S(1)}, f32[128,1024]{1,0:T(8,128)S(1)}) custom-call(bf16[128,1024]{1,0:T(8,128)(2,1)S(1)} %get-tuple-element.32.att_ref, bf16[1024,4096]{1,0:T(8,128)(2,1)S(1)} %copy-done), custom_call_target="tpu_custom_call" | custom-call | flops 540000000 | bytes 4000000 | tf_op jit(solution)/shard_map/pallas_call | solution.py:237
  22.0 0.1 collective-permute-start.8
  22.1 0.0 collective-permute-done.10
  22.2 0.6 %collective-permute-start.11 = (bf16[128,512]{1,0:T(8,128)(2,1)S(1)}, bf16[128,512]{1,0:T(8,128)(2,1)S(1)}, u32[]{:S(2)}, u32[]{:S(2)}) collective-permute-start(bf16[128,512]{1,0:T(8,128)(2,1)S(1)} %add_convert_fusion.1), channel_id=1, source_target_pairs={{0,2},{1,3},{2,0},{3,1},{4,6},{5,7},{6,4},{7,5},{8,10},{9,11},{10,... | collective-permute-start | bytes 393224 | tf_op jit(solution)/shard_map/ppermute | solution.py:163
  22.8 2.6 %collective-permute-done.9 = bf16[128,512]{1,0:T(8,128)(2,1)S(1)} collective-permute-done((bf16[128,512]{1,0:T(8,128)(2,1)S(1)}, bf16[128,512]{1,0:T(8,128)(2,1)S(1)}, u32[]{:S(2)}, u32[]{:S(2)}) %collective-permute-start.9) | collective-permute-done | bytes 131104 | tf_op jit(solution)/shard_map/ppermute | solution.py:163
  25.4 2.8 %collective-permute-done.11 = bf16[128,512]{1,0:T(8,128)(2,1)S(1)} collective-permute-done((bf16[128,512]{1,0:T(8,128)(2,1)S(1)}, bf16[128,512]{1,0:T(8,128)(2,1)S(1)}, u32[]{:S(2)}, u32[]{:S(2)}) %collective-permute-start.11) | collective-permute-done | bytes 131104 | tf_op jit(solution)/shard_map/ppermute | solution.py:163
  28.2 0.0 collective-permute-done.8
  28.2 0.8 %add_convert_fusion = bf16[128,1024]{1,0:T(8,128)(2,1)} fusion(f32[128,1024]{1,0:T(8,128)S(1)} %get-tuple-element.33, bf16[128,1024]{1,0:T(8,128)(2,1)S(1)} %collective-permute-done.8, bf16[128,512]{1,0:T(8,128)(2,1)S(1)} %collective-permute-done.11, bf16[128,512]{1,0:T(8,128)(2,1)S(1)} %collective-permute-done.9), kind=kLoop, calls=%fused_computation | loop fusion | flops 1048576 | bytes 1310720 | tf_op jit(solution)/shard_map/convert_element_type | solution.py:265
  (3 shorter events, 0.1 us)
Async XLA Ops:
  0.0 13.3 %copy-start.1 = (bf16[128,8,128]{2,1,0:T(8,128)(2,1)S(1)}, bf16[128,8,128]{2,1,0:T(8,128)(2,1)}, u32[]{:S(2)}) copy-start(bf16[128,8,128]{2,1,0:T(8,128)(2,1)} %param.5) | copy-start | bytes 786436
  0.0 17.6 %copy-start = (bf16[1024,4096]{1,0:T(8,128)(2,1)S(1)}, bf16[1024,4096]{1,0:T(8,128)(2,1)}, u32[]{:S(2)}) copy-start(bf16[1024,4096]{1,0:T(8,128)(2,1)} %w_ref.3) | copy-start | bytes 25165828
  1.0 7.7 %collective-permute-start.3 = (bf16[256,128]{1,0:T(8,128)(2,1)S(1)}, bf16[256,128]{1,0:T(8,128)(2,1)S(1)}, u32[]{:S(2)}, u32[]{:S(2)}) collective-permute-start(bf16[256,128]{1,0:T(8,128)(2,1)S(1)} %get-tuple-element.22.kv_ref), channel_id=1, source_target_pairs={{0,24},{4,28},{8,16},{12,20},{16,8},{20,12},{24,0},{28,4},{1,25},{... | collective-permute-start | bytes 196616 | tf_op jit(solution)/shard_map/ppermute | solution.py:163
  6.1 5.7 %collective-permute-start.1 = (bf16[256,128]{1,0:T(8,128)(2,1)S(1)}, bf16[256,128]{1,0:T(8,128)(2,1)S(1)}, u32[]{:S(2)}, u32[]{:S(2)}) collective-permute-start(bf16[256,128]{1,0:T(8,128)(2,1)S(1)} %get-tuple-element.22.kv_ref), channel_id=1, source_target_pairs={{0,16},{4,20},{8,24},{12,28},{16,0},{20,4},{24,8},{28,12},{1,17},{... | collective-permute-start | bytes 196616 | tf_op jit(solution)/shard_map/ppermute | solution.py:163
  6.1 7.2 %collective-permute-start = (bf16[256,128]{1,0:T(8,128)(2,1)S(1)}, bf16[256,128]{1,0:T(8,128)(2,1)S(1)}, u32[]{:S(2)}, u32[]{:S(2)}) collective-permute-start(bf16[256,128]{1,0:T(8,128)(2,1)S(1)} %get-tuple-element.22.kv_ref), channel_id=1, source_target_pairs={{0,4},{4,0},{8,12},{12,8},{16,20},{20,16},{24,28},{28,24},{1,5},{5... | collective-permute-start | bytes 196616 | tf_op jit(solution)/shard_map/ppermute | solution.py:163
  7.6 5.8 %collective-permute-start.2 = (bf16[256,128]{1,0:T(8,128)(2,1)S(1)}, bf16[256,128]{1,0:T(8,128)(2,1)S(1)}, u32[]{:S(2)}, u32[]{:S(2)}) collective-permute-start(bf16[256,128]{1,0:T(8,128)(2,1)S(1)} %get-tuple-element.22.kv_ref), channel_id=1, source_target_pairs={{0,8},{4,12},{8,0},{12,4},{16,24},{20,28},{24,16},{28,20},{1,9},{5... | collective-permute-start | bytes 196616 | tf_op jit(solution)/shard_map/ppermute | solution.py:163
  8.7 5.3 %collective-permute-start.4 = (bf16[256,128]{1,0:T(8,128)(2,1)S(1)}, bf16[256,128]{1,0:T(8,128)(2,1)S(1)}, u32[]{:S(2)}, u32[]{:S(2)}) collective-permute-start(bf16[256,128]{1,0:T(8,128)(2,1)S(1)} %collective-permute-done.3.refs_3_), channel_id=1, source_target_pairs={{0,4},{4,0},{8,12},{12,8},{16,20},{20,16},{24,28},{28,24},{1,5},{5... | collective-permute-start | bytes 196616 | tf_op jit(solution)/shard_map/ppermute | solution.py:163
  11.7 4.3 %collective-permute-start.6 = (bf16[256,128]{1,0:T(8,128)(2,1)S(1)}, bf16[256,128]{1,0:T(8,128)(2,1)S(1)}, u32[]{:S(2)}, u32[]{:S(2)}) collective-permute-start(bf16[256,128]{1,0:T(8,128)(2,1)S(1)} %collective-permute-done.1.refs_1_), channel_id=1, source_target_pairs={{0,4},{4,0},{8,12},{12,8},{16,20},{20,16},{24,28},{28,24},{1,5},{5... | collective-permute-start | bytes 196616 | tf_op jit(solution)/shard_map/ppermute | solution.py:163
  13.3 4.3 %collective-permute-start.5 = (bf16[256,128]{1,0:T(8,128)(2,1)S(1)}, bf16[256,128]{1,0:T(8,128)(2,1)S(1)}, u32[]{:S(2)}, u32[]{:S(2)}) collective-permute-start(bf16[256,128]{1,0:T(8,128)(2,1)S(1)} %collective-permute-done.refs_0_), channel_id=1, source_target_pairs={{0,8},{4,12},{8,0},{12,4},{16,24},{20,28},{24,16},{28,20},{1,9},{5... | collective-permute-start | bytes 196616 | tf_op jit(solution)/shard_map/ppermute | solution.py:163
  18.3 1.4 %collective-permute-start.7 = (bf16[128,512]{1,0:T(8,128)(2,1)S(1)}, bf16[128,512]{1,0:T(8,128)(2,1)S(1)}, u32[]{:S(2)}, u32[]{:S(2)}) collective-permute-start(bf16[128,512]{1,0:T(8,128)(2,1)S(1)} %get-tuple-element.31), channel_id=1, source_target_pairs={{0,1},{1,0},{2,3},{3,2},{4,5},{5,4},{6,7},{7,6},{8,9},{9,8},{10,11... | collective-permute-start | bytes 393224 | tf_op jit(solution)/shard_map/ppermute | solution.py:163
  18.8 3.3 %collective-permute-start.10 = (bf16[128,512]{1,0:T(8,128)(2,1)S(1)}, bf16[128,512]{1,0:T(8,128)(2,1)S(1)}, u32[]{:S(2)}, u32[]{:S(2)}) collective-permute-start(bf16[128,512]{1,0:T(8,128)(2,1)S(1)} %get-tuple-element.36), channel_id=1, source_target_pairs={{0,1},{1,0},{2,3},{3,2},{4,5},{5,4},{6,7},{7,6},{8,9},{9,8},{10,11... | collective-permute-start | bytes 393224 | tf_op jit(solution)/shard_map/ppermute | solution.py:163
  19.8 5.6 %collective-permute-start.9 = (bf16[128,512]{1,0:T(8,128)(2,1)S(1)}, bf16[128,512]{1,0:T(8,128)(2,1)S(1)}, u32[]{:S(2)}, u32[]{:S(2)}) collective-permute-start(bf16[128,512]{1,0:T(8,128)(2,1)S(1)} %add_convert_fusion.2), channel_id=1, source_target_pairs={{0,2},{1,3},{2,0},{3,1},{4,6},{5,7},{6,4},{7,5},{8,10},{9,11},{10,... | collective-permute-start | bytes 393224 | tf_op jit(solution)/shard_map/ppermute | solution.py:163
  22.0 6.1 %collective-permute-start.8 = (bf16[128,1024]{1,0:T(8,128)(2,1)S(1)}, bf16[128,1024]{1,0:T(8,128)(2,1)S(1)}, u32[]{:S(2)}, u32[]{:S(2)}) collective-permute-start(bf16[128,1024]{1,0:T(8,128)(2,1)S(1)} %get-tuple-element.34), channel_id=1, source_target_pairs={{0,1},{1,0},{2,3},{3,2},{4,5},{5,4},{6,7},{7,6},{8,9},{9,8},{10,11... | collective-permute-start | bytes 786440 | tf_op jit(solution)/shard_map/ppermute | solution.py:163
  22.2 6.0 %collective-permute-start.11 = (bf16[128,512]{1,0:T(8,128)(2,1)S(1)}, bf16[128,512]{1,0:T(8,128)(2,1)S(1)}, u32[]{:S(2)}, u32[]{:S(2)}) collective-permute-start(bf16[128,512]{1,0:T(8,128)(2,1)S(1)} %add_convert_fusion.1), channel_id=1, source_target_pairs={{0,2},{1,3},{2,0},{3,1},{4,6},{5,7},{6,4},{7,5},{8,10},{9,11},{10,... | collective-permute-start | bytes 393224 | tf_op jit(solution)/shard_map/ppermute | solution.py:163

commit v12 on v9

--- a/solution.py
+++ b/solution.py
@@ -163,8 +163,12 @@
         return lax.ppermute(x, axis, [(i, i ^ other) for i in range(size)])
 
     def forward(x, other):
-        route = [(i, i ^ 1 if i ^ other < i else i) for i in range(ctx_size)]
-        return lax.ppermute(x, "ctx", route)
+        route = []
+        for i in range(ctx_size):
+            for j in range(tp_size):
+                target = (i ^ 1, j) if i ^ other < i else (i, j ^ 1)
+                route.append((i * tp_size + j, target[0] * tp_size + target[1]))
+        return lax.ppermute(x, ("ctx", "tp"), route)
 
     kv, reached = pl.pallas_call(
         functools.partial(pack_kernel, ctx_size == DIRECT_SIZE),

time: 32 us -> 26.6 us (0.83)
  the two profiles are of different devices: /device:TPU:28 before, /device:TPU:24 now
where the time goes in v12:
time: 26.6 us; the launch traced here: 26.7 us
  starting transfers between devices  12.4 us (47%)
  waiting for transfers between devices  7.26 us (27%)
  Pallas kernels  6.07 us (23%)
  other arithmetic  0.87 us (3%)
    ppermute x9, starting transfers between devices, swap(): return lax.ppermute(x, axis, [(i, i ^ other) for i in range(size)])  8.82 us
    ppermute x9, waiting for transfers between devices, swap(): return lax.ppermute(x, axis, [(i, i ^ other) for i in range(size)])  6.61 us
    ppermute x3, starting transfers between devices, forward(): return lax.ppermute(x, ('ctx', 'tp'), route)  3.55 us
    pallas_call x1, Pallas kernels, shards(): pl.pallas_call(functools.partial(own_block_kernel, early_xors), out_shape...  1.52 us
    pallas_call x1, Pallas kernels, shards(): pl.pallas_call(functools.partial(last_kernel, xors), out_shape=(jax.Shape...  1.21 us
    pallas_call x1, Pallas kernels, absorbed(): pl.pallas_call(functools.partial(others_kernel, xors), out_shape=state_sh...  1.2 us
    pallas_call x2, Pallas kernels, projected(): pl.pallas_call(functools.partial(project_pair, flip, part), out_shape=sha...  1.18 us
    pallas_call x1, Pallas kernels, shards(): pl.pallas_call(functools.partial(pack_kernel, ctx_size == DIRECT_SIZE), o...  0.95 us
  transfers between devices with their start and end apart: 12, of which 5 were waited for; matrix products, arithmetic and copies ran while one was open for 0% of the time, Pallas kernels for 15%

profile of v12, /device:TPU:24, one launch (start us, length us, event | category | flops | bytes accessed | tf_op | source)
XLA Modules:
  0.0 26.7 jit_solution(9538591252768453231)
XLA Ops:
  0.0 0.0 copy-start.1
  0.0 0.0 copy-start
  0.0 0.9 %shard_map.55 = (bf16[256,128]{1,0:T(8,128)(2,1)S(1)}, s32[8,128]{1,0:T(8,128)S(1)}) custom-call(bf16[128,128]{1,0:T(8,128)(2,1)} %bitcast.8, bf16[128,128]{1,0:T(8,128)(2,1)} %bitcast.9, s32[8]{0:T(128)} %parents_hbm.1), custom_call_target="tpu_custom_call" | custom-call | flops 8000000000 | bytes 130000 | tf_op jit(solution)/shard_map/pallas_call | solution.py:173
  1.0 0.1 collective-permute-start.3
  1.0 0.9 %collective-permute-start.2 = (bf16[256,128]{1,0:T(8,128)(2,1)S(1)}, bf16[256,128]{1,0:T(8,128)(2,1)S(1)}, u32[]{:S(2)}, u32[]{:S(2)}) collective-permute-start(bf16[256,128]{1,0:T(8,128)(2,1)S(1)} %get-tuple-element.22.kv_ref), channel_id=1, source_target_pairs={{0,8},{4,12},{8,0},{12,4},{16,24},{20,28},{24,16},{28,20},{1,9},{5... | collective-permute-start | bytes 196616 | tf_op jit(solution)/shard_map/ppermute | solution.py:163
  1.9 3.5 %collective-permute-start.1 = (bf16[256,128]{1,0:T(8,128)(2,1)S(1)}, bf16[256,128]{1,0:T(8,128)(2,1)S(1)}, u32[]{:S(2)}, u32[]{:S(2)}) collective-permute-start(bf16[256,128]{1,0:T(8,128)(2,1)S(1)} %get-tuple-element.22.kv_ref), channel_id=1, source_target_pairs={{0,16},{4,20},{8,24},{12,28},{16,0},{20,4},{24,8},{28,12},{1,17},{... | collective-permute-start | bytes 196616 | tf_op jit(solution)/shard_map/ppermute | solution.py:163
  5.4 1.5 %collective-permute-start = (bf16[256,128]{1,0:T(8,128)(2,1)S(1)}, bf16[256,128]{1,0:T(8,128)(2,1)S(1)}, u32[]{:S(2)}, u32[]{:S(2)}) collective-permute-start(bf16[256,128]{1,0:T(8,128)(2,1)S(1)} %get-tuple-element.22.kv_ref), channel_id=1, source_target_pairs={{0,4},{4,0},{8,12},{12,8},{16,20},{20,16},{24,28},{28,24},{1,5},{5... | collective-permute-start | bytes 196616 | tf_op jit(solution)/shard_map/ppermute | solution.py:163
  6.9 0.9 %collective-permute-done.3.refs_3_ = bf16[256,128]{1,0:T(8,128)(2,1)S(1)} collective-permute-done((bf16[256,128]{1,0:T(8,128)(2,1)S(1)}, bf16[256,128]{1,0:T(8,128)(2,1)S(1)}, u32[]{:S(2)}, u32[]{:S(2)}) %collective-permute-start.3) | collective-permute-done | bytes 65568 | tf_op jit(solution)/shard_map/ppermute | solution.py:163
  7.8 1.5 %collective-permute-start.5 = (bf16[256,128]{1,0:T(8,128)(2,1)S(1)}, bf16[256,128]{1,0:T(8,128)(2,1)S(1)}, u32[]{:S(2)}, u32[]{:S(2)}) collective-permute-start(bf16[256,128]{1,0:T(8,128)(2,1)S(1)} %collective-permute-done.3.refs_3_), channel_id=1, source_target_pairs={{0,1},{1,0},{2,3},{3,2},{4,5},{5,4},{6,7},{7,6},{8,9},{9,8},{10,11... | collective-permute-start | bytes 196616 | tf_op jit(solution)/shard_map/ppermute | solution.py:171
  9.3 0.0 collective-permute-done.2.refs_2_
  9.3 0.5 %collective-permute-start.4 = (bf16[256,128]{1,0:T(8,128)(2,1)S(1)}, bf16[256,128]{1,0:T(8,128)(2,1)S(1)}, u32[]{:S(2)}, u32[]{:S(2)}) collective-permute-start(bf16[256,128]{1,0:T(8,128)(2,1)S(1)} %collective-permute-done.2.refs_2_), channel_id=1, source_target_pairs={{0,1},{1,0},{2,3},{3,2},{4,5},{5,4},{6,7},{7,6},{8,12},{9,13},{10,... | collective-permute-start | bytes 196616 | tf_op jit(solution)/shard_map/ppermute | solution.py:171
  9.8 0.0 collective-permute-done.1.refs_1_
  9.8 1.5 %collective-permute-start.6 = (bf16[256,128]{1,0:T(8,128)(2,1)S(1)}, bf16[256,128]{1,0:T(8,128)(2,1)S(1)}, u32[]{:S(2)}, u32[]{:S(2)}) collective-permute-start(bf16[256,128]{1,0:T(8,128)(2,1)S(1)} %collective-permute-done.1.refs_1_), channel_id=1, source_target_pairs={{0,1},{1,0},{2,3},{3,2},{4,5},{5,4},{6,7},{7,6},{8,9},{9,8},{10,11... | collective-permute-start | bytes 196616 | tf_op jit(solution)/shard_map/ppermute | solution.py:171
  11.4 0.0 copy-done.1
  11.4 0.0 collective-permute-done.refs_0_
  11.4 1.5 %shard_map.56 = (f32[1,1024]{1,0:T(1,128)S(1)}, f32[1,1024]{1,0:T(1,128)S(1)}, f32[128,1024]{1,0:T(8,128)S(1)}) custom-call(s32[8,128]{1,0:T(8,128)S(1)} %get-tuple-element.21.reached_ref.tree_ref, bf16[1024,128]{1,0:T(8,128)(2,1)S(1)} %bitcast.4, bf16[256,128]{1,0:T(8,128)(2,1)S(1)} %get-tuple-element.22.kv_ref, ...), custom_call_target="tpu_custom_call" | custom-call | flops 130000000 | bytes 1000000 | tf_op jit(solution)/shard_map/pallas_call | solution.py:194
  12.9 0.0 collective-permute-done.5.refs_1_
  13.0 0.6 %collective-permute-done.4.refs_0_ = bf16[256,128]{1,0:T(8,128)(2,1)S(1)} collective-permute-done((bf16[256,128]{1,0:T(8,128)(2,1)S(1)}, bf16[256,128]{1,0:T(8,128)(2,1)S(1)}, u32[]{:S(2)}, u32[]{:S(2)}) %collective-permute-start.4) | collective-permute-done | bytes 65568 | tf_op jit(solution)/shard_map/ppermute | solution.py:171
  13.6 1.2 %shard_map.57 = (f32[1,1024]{1,0:T(1,128)S(1)}, f32[1,1024]{1,0:T(1,128)S(1)}, f32[128,1024]{1,0:T(8,128)S(1)}) custom-call(s32[8,128]{1,0:T(8,128)S(1)} %get-tuple-element.21.reached_ref.tree_ref, bf16[1024,128]{1,0:T(8,128)(2,1)S(1)} %bitcast.5, f32[1,1024]{1,0:T(1,128)S(1)} %get-tuple-element.23.m_in, ...), custom_call_target="tpu_custom_call", output_to_operand_aliasing={{0}: (2, {}), {1}: (3, {}), {2}: (4, {})} | custom-call | flops 270000000 | bytes 1000000 | tf_op jit(solution)/shard_map/pallas_call | solution.py:211
  14.8 0.0 collective-permute-done.6.refs_0_
  14.8 0.0 copy-done
  14.8 1.2 %shard_map.58 = (bf16[128,1024]{1,0:T(8,128)(2,1)S(1)}, bf16[128,512]{1,0:T(8,128)(2,1)S(1)}, f32[128,512]{1,0:T(8,128)S(1)}, f32[1,1024]{1,0:T(1,128)S(1)}, f32...) custom-call(s32[8,128]{1,0:T(8,128)S(1)} %get-tuple-element.21.reached_ref, ...), custom_call_target="tpu_custom_call", output_to_operand_aliasing={{3}: (2, {}), {4}: (3, {}), {5}: (4, {})} | custom-call | flops 1000000000 | bytes 10000000 | tf_op jit(solution)/shard_map/pallas_call | solution.py:231
  16.0 0.1 collective-permute-start.7
  16.1 0.5 %shard_map.60 = (bf16[128,512]{1,0:T(8,128)(2,1)S(1)}, f32[128,512]{1,0:T(8,128)S(1)}) custom-call(bf16[128,1024]{1,0:T(8,128)(2,1)S(1)} %get-tuple-element.32.att_ref, bf16[1024,4096]{1,0:T(8,128)(2,1)S(1)} %copy-done), custom_call_target="tpu_custom_call" | custom-call | flops 540000000 | bytes 4000000 | tf_op jit(solution)/shard_map/pallas_call | solution.py:242
  16.6 0.6 %collective-permute-start.10 = (bf16[128,512]{1,0:T(8,128)(2,1)S(1)}, bf16[128,512]{1,0:T(8,128)(2,1)S(1)}, u32[]{:S(2)}, u32[]{:S(2)}) collective-permute-start(bf16[128,512]{1,0:T(8,128)(2,1)S(1)} %get-tuple-element.36), channel_id=1, source_target_pairs={{0,1},{1,0},{2,3},{3,2},{4,5},{5,4},{6,7},{7,6},{8,9},{9,8},{10,11... | collective-permute-start | bytes 393224 | tf_op jit(solution)/shard_map/ppermute | solution.py:163
  17.1 0.3 %collective-permute-done.7 = bf16[128,512]{1,0:T(8,128)(2,1)S(1)} collective-permute-done((bf16[128,512]{1,0:T(8,128)(2,1)S(1)}, bf16[128,512]{1,0:T(8,128)(2,1)S(1)}, u32[]{:S(2)}, u32[]{:S(2)}) %collective-permute-start.7) | collective-permute-done | bytes 131104 | tf_op jit(solution)/shard_map/ppermute | solution.py:163
  17.5 1.6 %collective-permute-start.9 = (bf16[128,512]{1,0:T(8,128)(2,1)S(1)}, bf16[128,512]{1,0:T(8,128)(2,1)S(1)}, u32[]{:S(2)}, u32[]{:S(2)}) collective-permute-start(bf16[128,512]{1,0:T(8,128)(2,1)S(1)} %add_convert_fusion.2), channel_id=1, source_target_pairs={{0,2},{1,3},{2,0},{3,1},{4,6},{5,7},{6,4},{7,5},{8,10},{9,11},{10,... | collective-permute-start | bytes 393224 | tf_op jit(solution)/shard_map/ppermute | solution.py:163
  19.1 0.7 %shard_map.59 = (bf16[128,1024]{1,0:T(8,128)(2,1)S(1)}, f32[128,1024]{1,0:T(8,128)S(1)}) custom-call(bf16[128,1024]{1,0:T(8,128)(2,1)S(1)} %get-tuple-element.32.att_ref, bf16[1024,4096]{1,0:T(8,128)(2,1)S(1)} %copy-done), custom_call_target="tpu_custom_call" | custom-call | flops 540000000 | bytes 4000000 | tf_op jit(solution)/shard_map/pallas_call | solution.py:242
  19.8 0.1 collective-permute-start.8
  19.9 0.0 collective-permute-done.10
  19.9 0.6 %collective-permute-start.11 = (bf16[128,512]{1,0:T(8,128)(2,1)S(1)}, bf16[128,512]{1,0:T(8,128)(2,1)S(1)}, u32[]{:S(2)}, u32[]{:S(2)}) collective-permute-start(bf16[128,512]{1,0:T(8,128)(2,1)S(1)} %add_convert_fusion.1), channel_id=1, source_target_pairs={{0,2},{1,3},{2,0},{3,1},{4,6},{5,7},{6,4},{7,5},{8,10},{9,11},{10,... | collective-permute-start | bytes 393224 | tf_op jit(solution)/shard_map/ppermute | solution.py:163
  20.5 2.6 %collective-permute-done.9 = bf16[128,512]{1,0:T(8,128)(2,1)S(1)} collective-permute-done((bf16[128,512]{1,0:T(8,128)(2,1)S(1)}, bf16[128,512]{1,0:T(8,128)(2,1)S(1)}, u32[]{:S(2)}, u32[]{:S(2)}) %collective-permute-start.9) | collective-permute-done | bytes 131104 | tf_op jit(solution)/shard_map/ppermute | solution.py:163
  23.1 2.8 %collective-permute-done.11 = bf16[128,512]{1,0:T(8,128)(2,1)S(1)} collective-permute-done((bf16[128,512]{1,0:T(8,128)(2,1)S(1)}, bf16[128,512]{1,0:T(8,128)(2,1)S(1)}, u32[]{:S(2)}, u32[]{:S(2)}) %collective-permute-start.11) | collective-permute-done | bytes 131104 | tf_op jit(solution)/shard_map/ppermute | solution.py:163
  25.9 0.0 collective-permute-done.8
  25.9 0.8 %add_convert_fusion = bf16[128,1024]{1,0:T(8,128)(2,1)} fusion(f32[128,1024]{1,0:T(8,128)S(1)} %get-tuple-element.33, bf16[128,1024]{1,0:T(8,128)(2,1)S(1)} %collective-permute-done.8, bf16[128,512]{1,0:T(8,128)(2,1)S(1)} %collective-permute-done.11, bf16[128,512]{1,0:T(8,128)(2,1)S(1)} %collective-permute-done.9), kind=kLoop, calls=%fused_computation | loop fusion | flops 1048576 | bytes 1310720 | tf_op jit(solution)/shard_map/convert_element_type | solution.py:270
  (3 shorter events, 0.1 us)
Async XLA Ops:
  0.0 11.4 %copy-start.1 = (bf16[128,8,128]{2,1,0:T(8,128)(2,1)S(1)}, bf16[128,8,128]{2,1,0:T(8,128)(2,1)}, u32[]{:S(2)}) copy-start(bf16[128,8,128]{2,1,0:T(8,128)(2,1)} %param.5) | copy-start | bytes 786436
  0.0 14.8 %copy-start = (bf16[1024,4096]{1,0:T(8,128)(2,1)S(1)}, bf16[1024,4096]{1,0:T(8,128)(2,1)}, u32[]{:S(2)}) copy-start(bf16[1024,4096]{1,0:T(8,128)(2,1)} %w_ref.3) | copy-start | bytes 25165828
  1.0 6.8 %collective-permute-start.3 = (bf16[256,128]{1,0:T(8,128)(2,1)S(1)}, bf16[256,128]{1,0:T(8,128)(2,1)S(1)}, u32[]{:S(2)}, u32[]{:S(2)}) collective-permute-start(bf16[256,128]{1,0:T(8,128)(2,1)S(1)} %get-tuple-element.22.kv_ref), channel_id=1, source_target_pairs={{0,24},{4,28},{8,16},{12,20},{16,8},{20,12},{24,0},{28,4},{1,25},{... | collective-permute-start | bytes 196616 | tf_op jit(solution)/shard_map/ppermute | solution.py:163
  1.0 8.3 %collective-permute-start.2 = (bf16[256,128]{1,0:T(8,128)(2,1)S(1)}, bf16[256,128]{1,0:T(8,128)(2,1)S(1)}, u32[]{:S(2)}, u32[]{:S(2)}) collective-permute-start(bf16[256,128]{1,0:T(8,128)(2,1)S(1)} %get-tuple-element.22.kv_ref), channel_id=1, source_target_pairs={{0,8},{4,12},{8,0},{12,4},{16,24},{20,28},{24,16},{28,20},{1,9},{5... | collective-permute-start | bytes 196616 | tf_op jit(solution)/shard_map/ppermute | solution.py:163
  1.9 7.9 %collective-permute-start.1 = (bf16[256,128]{1,0:T(8,128)(2,1)S(1)}, bf16[256,128]{1,0:T(8,128)(2,1)S(1)}, u32[]{:S(2)}, u32[]{:S(2)}) collective-permute-start(bf16[256,128]{1,0:T(8,128)(2,1)S(1)} %get-tuple-element.22.kv_ref), channel_id=1, source_target_pairs={{0,16},{4,20},{8,24},{12,28},{16,0},{20,4},{24,8},{28,12},{1,17},{... | collective-permute-start | bytes 196616 | tf_op jit(solution)/shard_map/ppermute | solution.py:163
  5.4 6.0 %collective-permute-start = (bf16[256,128]{1,0:T(8,128)(2,1)S(1)}, bf16[256,128]{1,0:T(8,128)(2,1)S(1)}, u32[]{:S(2)}, u32[]{:S(2)}) collective-permute-start(bf16[256,128]{1,0:T(8,128)(2,1)S(1)} %get-tuple-element.22.kv_ref), channel_id=1, source_target_pairs={{0,4},{4,0},{8,12},{12,8},{16,20},{20,16},{24,28},{28,24},{1,5},{5... | collective-permute-start | bytes 196616 | tf_op jit(solution)/shard_map/ppermute | solution.py:163
  7.8 5.1 %collective-permute-start.5 = (bf16[256,128]{1,0:T(8,128)(2,1)S(1)}, bf16[256,128]{1,0:T(8,128)(2,1)S(1)}, u32[]{:S(2)}, u32[]{:S(2)}) collective-permute-start(bf16[256,128]{1,0:T(8,128)(2,1)S(1)} %collective-permute-done.3.refs_3_), channel_id=1, source_target_pairs={{0,1},{1,0},{2,3},{3,2},{4,5},{5,4},{6,7},{7,6},{8,9},{9,8},{10,11... | collective-permute-start | bytes 196616 | tf_op jit(solution)/shard_map/ppermute | solution.py:171
  9.3 4.3 %collective-permute-start.4 = (bf16[256,128]{1,0:T(8,128)(2,1)S(1)}, bf16[256,128]{1,0:T(8,128)(2,1)S(1)}, u32[]{:S(2)}, u32[]{:S(2)}) collective-permute-start(bf16[256,128]{1,0:T(8,128)(2,1)S(1)} %collective-permute-done.2.refs_2_), channel_id=1, source_target_pairs={{0,1},{1,0},{2,3},{3,2},{4,5},{5,4},{6,7},{7,6},{8,12},{9,13},{10,... | collective-permute-start | bytes 196616 | tf_op jit(solution)/shard_map/ppermute | solution.py:171
  9.8 5.0 %collective-permute-start.6 = (bf16[256,128]{1,0:T(8,128)(2,1)S(1)}, bf16[256,128]{1,0:T(8,128)(2,1)S(1)}, u32[]{:S(2)}, u32[]{:S(2)}) collective-permute-start(bf16[256,128]{1,0:T(8,128)(2,1)S(1)} %collective-permute-done.1.refs_1_), channel_id=1, source_target_pairs={{0,1},{1,0},{2,3},{3,2},{4,5},{5,4},{6,7},{7,6},{8,9},{9,8},{10,11... | collective-permute-start | bytes 196616 | tf_op jit(solution)/shard_map/ppermute | solution.py:171
  16.0 1.4 %collective-permute-start.7 = (bf16[128,512]{1,0:T(8,128)(2,1)S(1)}, bf16[128,512]{1,0:T(8,128)(2,1)S(1)}, u32[]{:S(2)}, u32[]{:S(2)}) collective-permute-start(bf16[128,512]{1,0:T(8,128)(2,1)S(1)} %get-tuple-element.31), channel_id=1, source_target_pairs={{0,1},{1,0},{2,3},{3,2},{4,5},{5,4},{6,7},{7,6},{8,9},{9,8},{10,11... | collective-permute-start | bytes 393224 | tf_op jit(solution)/shard_map/ppermute | solution.py:163
  16.6 3.3 %collective-permute-start.10 = (bf16[128,512]{1,0:T(8,128)(2,1)S(1)}, bf16[128,512]{1,0:T(8,128)(2,1)S(1)}, u32[]{:S(2)}, u32[]{:S(2)}) collective-permute-start(bf16[128,512]{1,0:T(8,128)(2,1)S(1)} %get-tuple-element.36), channel_id=1, source_target_pairs={{0,1},{1,0},{2,3},{3,2},{4,5},{5,4},{6,7},{7,6},{8,9},{9,8},{10,11... | collective-permute-start | bytes 393224 | tf_op jit(solution)/shard_map/ppermute | solution.py:163
  17.5 5.6 %collective-permute-start.9 = (bf16[128,512]{1,0:T(8,128)(2,1)S(1)}, bf16[128,512]{1,0:T(8,128)(2,1)S(1)}, u32[]{:S(2)}, u32[]{:S(2)}) collective-permute-start(bf16[128,512]{1,0:T(8,128)(2,1)S(1)} %add_convert_fusion.2), channel_id=1, source_target_pairs={{0,2},{1,3},{2,0},{3,1},{4,6},{5,7},{6,4},{7,5},{8,10},{9,11},{10,... | collective-permute-start | bytes 393224 | tf_op jit(solution)/shard_map/ppermute | solution.py:163
  19.8 6.1 %collective-permute-start.8 = (bf16[128,1024]{1,0:T(8,128)(2,1)S(1)}, bf16[128,1024]{1,0:T(8,128)(2,1)S(1)}, u32[]{:S(2)}, u32[]{:S(2)}) collective-permute-start(bf16[128,1024]{1,0:T(8,128)(2,1)S(1)} %get-tuple-element.34), channel_id=1, source_target_pairs={{0,1},{1,0},{2,3},{3,2},{4,5},{5,4},{6,7},{7,6},{8,9},{9,8},{10,11... | collective-permute-start | bytes 786440 | tf_op jit(solution)/shard_map/ppermute | solution.py:163
  19.9 6.0 %collective-permute-start.11 = (bf16[128,512]{1,0:T(8,128)(2,1)S(1)}, bf16[128,512]{1,0:T(8,128)(2,1)S(1)}, u32[]{:S(2)}, u32[]{:S(2)}) collective-permute-start(bf16[128,512]{1,0:T(8,128)(2,1)S(1)} %add_convert_fusion.1), channel_id=1, source_target_pairs={{0,2},{1,3},{2,0},{3,1},{4,6},{5,7},{6,4},{7,5},{8,10},{9,11},{10,... | collective-permute-start | bytes 393224 | tf_op jit(solution)/shard_map/ppermute | solution.py:163

commit v13 on v12

--- a/solution.py
+++ b/solution.py
@@ -13,12 +13,15 @@
 VMEM_LIMIT = 32 * 1024 * 1024
 
 
+CHUNK = 256
+
+
 def scores_of(k, q):
     return lax.dot_general(k, q, (((1,), (1,)), ((), ())), preferred_element_type=jnp.float32)
 
 
-def weighted(v, p):
-    return lax.dot_general(v, p.astype(jnp.bfloat16), (((0,), (0,)), ((), ())), preferred_element_type=jnp.float32)
+def weighted(v_turned, p):
+    return jnp.dot(v_turned, p.astype(jnp.bfloat16), preferred_element_type=jnp.float32)
 
 
 def exponent_scale(head_dim):
@@ -59,14 +62,17 @@
 
 
 def absorb(scale, q_ref, k, v, m_ref, l_ref, acc_ref):
-    s = scores_of(k, q_ref[...])
-    m_old = m_ref[...]
-    m_new = jnp.maximum(m_old, jnp.max(s, axis=0, keepdims=True))
-    p = jnp.exp2((s - m_new) * scale)
-    factor = jnp.exp2((m_old - m_new) * scale)
-    m_ref[...] = m_new
-    l_ref[...] = l_ref[...] * factor + jnp.sum(p, axis=0, keepdims=True)
-    acc_ref[...] = acc_ref[...] * factor + weighted(v, p)
+    v_turned = v.T
+    for start in range(0, q_ref.shape[0], CHUNK):
+        at = slice(start, start + CHUNK)
+        s = scores_of(k, q_ref[at, :])
+        m_old = m_ref[:, at]
+        m_new = jnp.maximum(m_old, jnp.max(s, axis=0, keepdims=True))
+        p = jnp.exp2((s - m_new) * scale)
+        factor = jnp.exp2((m_old - m_new) * scale)
+        m_ref[:, at] = m_new
+        l_ref[:, at] = l_ref[:, at] * factor + jnp.sum(p, axis=0, keepdims=True)
+        acc_ref[:, at] = acc_ref[:, at] * factor + weighted(v_turned, p)
 
 
 def absorb_reached(xors, reached_ref, q_ref, kv_refs, state):
@@ -102,15 +108,19 @@
     state = refs[len(xors):]
     m_ref, l_ref, acc_ref = state
     scale = exponent_scale(q_ref.shape[1])
-    s = scores_of(kv_ref[0:BLOCK, :], q_ref[...])
-    key_at = lax.broadcasted_iota(jnp.int32, s.shape, 0)
-    query_at = lax.broadcasted_iota(jnp.int32, s.shape, 1) & (BLOCK - 1)
-    s = jnp.where(key_at <= query_at, s, -1e30)
-    m = jnp.max(s, axis=0, keepdims=True)
-    p = jnp.exp2((s - m) * scale)
-    m_ref[...] = m
-    l_ref[...] = jnp.sum(p, axis=0, keepdims=True)
-    acc_ref[...] = weighted(kv_ref[BLOCK:, :], p)
+    k = kv_ref[0:BLOCK, :]
+    v_turned = kv_ref[BLOCK:, :].T
+    for start in range(0, q_ref.shape[0], CHUNK):
+        at = slice(start, start + CHUNK)
+        s = scores_of(k, q_ref[at, :])
+        key_at = lax.broadcasted_iota(jnp.int32, s.shape, 0)
+        query_at = lax.broadcasted_iota(jnp.int32, s.shape, 1) & (BLOCK - 1)
+        s = jnp.where(key_at <= query_at, s, -1e30)
+        m = jnp.max(s, axis=0, keepdims=True)
+        p = jnp.exp2((s - m) * scale)
+        m_ref[:, at] = m
+        l_ref[:, at] = jnp.sum(p, axis=0, keepdims=True)
+        acc_ref[:, at] = weighted(v_turned, p)
     absorb_reached(xors, reached_ref, q_ref, refs[:len(xors)], state)
 
 

time: 26.6 us -> 26.4 us (level)
  the two profiles are of different devices: /device:TPU:24 before, /device:TPU:26 now
where the time goes in v13:
time: 26.4 us; the launch traced here: 26.6 us
  starting transfers between devices  12.4 us (47%)
  waiting for transfers between devices  7.42 us (28%)
  Pallas kernels  5.75 us (22%)
  other arithmetic  0.87 us (3%)
    ppermute x9, starting transfers between devices, swap(): return lax.ppermute(x, axis, [(i, i ^ other) for i in range(size)])  8.83 us
    ppermute x9, waiting for transfers between devices, swap(): return lax.ppermute(x, axis, [(i, i ^ other) for i in range(size)])  6.6 us
    ppermute x3, starting transfers between devices, forward(): return lax.ppermute(x, ('ctx', 'tp'), route)  3.55 us
    pallas_call x1, Pallas kernels, shards(): pl.pallas_call(functools.partial(last_kernel, xors), out_shape=(jax.Shape...  1.39 us
    pallas_call x1, Pallas kernels, shards(): pl.pallas_call(functools.partial(own_block_kernel, early_xors), out_shape...  1.36 us
    pallas_call x2, Pallas kernels, projected(): pl.pallas_call(functools.partial(project_pair, flip, part), out_shape=sha...  1.18 us
    pallas_call x1, Pallas kernels, shards(): pl.pallas_call(functools.partial(pack_kernel, ctx_size == DIRECT_SIZE), o...  0.95 us
    pallas_call x1, Pallas kernels, absorbed(): pl.pallas_call(functools.partial(others_kernel, xors), out_shape=state_sh...  0.88 us
  transfers between devices with their start and end apart: 12, of which 5 were waited for; matrix products, arithmetic and copies ran while one was open for 0% of the time, Pallas kernels for 13%

profile of v13, /device:TPU:26, one launch (start us, length us, event | category | flops | bytes accessed | tf_op | source)
XLA Modules:
  0.0 26.6 jit_solution(14053783959662867092)
XLA Ops:
  0.0 0.0 copy-start.1
  0.0 0.0 copy-start
  0.0 0.9 %shard_map.55 = (bf16[256,128]{1,0:T(8,128)(2,1)S(1)}, s32[8,128]{1,0:T(8,128)S(1)}) custom-call(bf16[128,128]{1,0:T(8,128)(2,1)} %bitcast.8, bf16[128,128]{1,0:T(8,128)(2,1)} %bitcast.9, s32[8]{0:T(128)} %parents_hbm.1), custom_call_target="tpu_custom_call" | custom-call | flops 8000000000 | bytes 130000 | tf_op jit(solution)/shard_map/pallas_call | solution.py:183
  1.0 0.3 %collective-permute-start.3 = (bf16[256,128]{1,0:T(8,128)(2,1)S(1)}, bf16[256,128]{1,0:T(8,128)(2,1)S(1)}, u32[]{:S(2)}, u32[]{:S(2)}) collective-permute-start(bf16[256,128]{1,0:T(8,128)(2,1)S(1)} %get-tuple-element.22.kv_ref), channel_id=1, source_target_pairs={{0,24},{4,28},{8,16},{12,20},{16,8},{20,12},{24,0},{28,4},{1,25},{... | collective-permute-start | bytes 196616 | tf_op jit(solution)/shard_map/ppermute | solution.py:173
  1.2 0.7 %collective-permute-start.2 = (bf16[256,128]{1,0:T(8,128)(2,1)S(1)}, bf16[256,128]{1,0:T(8,128)(2,1)S(1)}, u32[]{:S(2)}, u32[]{:S(2)}) collective-permute-start(bf16[256,128]{1,0:T(8,128)(2,1)S(1)} %get-tuple-element.22.kv_ref), channel_id=1, source_target_pairs={{0,8},{4,12},{8,0},{12,4},{16,24},{20,28},{24,16},{28,20},{1,9},{5... | collective-permute-start | bytes 196616 | tf_op jit(solution)/shard_map/ppermute | solution.py:173
  1.9 3.5 %collective-permute-start.1 = (bf16[256,128]{1,0:T(8,128)(2,1)S(1)}, bf16[256,128]{1,0:T(8,128)(2,1)S(1)}, u32[]{:S(2)}, u32[]{:S(2)}) collective-permute-start(bf16[256,128]{1,0:T(8,128)(2,1)S(1)} %get-tuple-element.22.kv_ref), channel_id=1, source_target_pairs={{0,16},{4,20},{8,24},{12,28},{16,0},{20,4},{24,8},{28,12},{1,17},{... | collective-permute-start | bytes 196616 | tf_op jit(solution)/shard_map/ppermute | solution.py:173
  5.4 1.5 %collective-permute-start = (bf16[256,128]{1,0:T(8,128)(2,1)S(1)}, bf16[256,128]{1,0:T(8,128)(2,1)S(1)}, u32[]{:S(2)}, u32[]{:S(2)}) collective-permute-start(bf16[256,128]{1,0:T(8,128)(2,1)S(1)} %get-tuple-element.22.kv_ref), channel_id=1, source_target_pairs={{0,4},{4,0},{8,12},{12,8},{16,20},{20,16},{24,28},{28,24},{1,5},{5... | collective-permute-start | bytes 196616 | tf_op jit(solution)/shard_map/ppermute | solution.py:173
  6.9 0.9 %collective-permute-done.3.refs_3_ = bf16[256,128]{1,0:T(8,128)(2,1)S(1)} collective-permute-done((bf16[256,128]{1,0:T(8,128)(2,1)S(1)}, bf16[256,128]{1,0:T(8,128)(2,1)S(1)}, u32[]{:S(2)}, u32[]{:S(2)}) %collective-permute-start.3) | collective-permute-done | bytes 65568 | tf_op jit(solution)/shard_map/ppermute | solution.py:173
  7.8 1.5 %collective-permute-start.5 = (bf16[256,128]{1,0:T(8,128)(2,1)S(1)}, bf16[256,128]{1,0:T(8,128)(2,1)S(1)}, u32[]{:S(2)}, u32[]{:S(2)}) collective-permute-start(bf16[256,128]{1,0:T(8,128)(2,1)S(1)} %collective-permute-done.3.refs_3_), channel_id=1, source_target_pairs={{0,1},{1,0},{2,3},{3,2},{4,5},{5,4},{6,7},{7,6},{8,9},{9,8},{10,11... | collective-permute-start | bytes 196616 | tf_op jit(solution)/shard_map/ppermute | solution.py:181
  9.3 0.0 collective-permute-done.2.refs_2_
  9.3 0.5 %collective-permute-start.4 = (bf16[256,128]{1,0:T(8,128)(2,1)S(1)}, bf16[256,128]{1,0:T(8,128)(2,1)S(1)}, u32[]{:S(2)}, u32[]{:S(2)}) collective-permute-start(bf16[256,128]{1,0:T(8,128)(2,1)S(1)} %collective-permute-done.2.refs_2_), channel_id=1, source_target_pairs={{0,1},{1,0},{2,3},{3,2},{4,5},{5,4},{6,7},{7,6},{8,12},{9,13},{10,... | collective-permute-start | bytes 196616 | tf_op jit(solution)/shard_map/ppermute | solution.py:181
  9.8 0.0 collective-permute-done.1.refs_1_
  9.8 1.5 %collective-permute-start.6 = (bf16[256,128]{1,0:T(8,128)(2,1)S(1)}, bf16[256,128]{1,0:T(8,128)(2,1)S(1)}, u32[]{:S(2)}, u32[]{:S(2)}) collective-permute-start(bf16[256,128]{1,0:T(8,128)(2,1)S(1)} %collective-permute-done.1.refs_1_), channel_id=1, source_target_pairs={{0,1},{1,0},{2,3},{3,2},{4,5},{5,4},{6,7},{7,6},{8,9},{9,8},{10,11... | collective-permute-start | bytes 196616 | tf_op jit(solution)/shard_map/ppermute | solution.py:181
  11.4 0.0 copy-done.1
  11.4 0.0 collective-permute-done.refs_0_
  11.4 1.4 %shard_map.56 = (f32[1,1024]{1,0:T(1,128)S(1)}, f32[1,1024]{1,0:T(1,128)S(1)}, f32[128,1024]{1,0:T(8,128)S(1)}) custom-call(s32[8,128]{1,0:T(8,128)S(1)} %get-tuple-element.21.reached_ref.tree_ref, bf16[1024,128]{1,0:T(8,128)(2,1)S(1)} %bitcast.4, bf16[256,128]{1,0:T(8,128)(2,1)S(1)} %get-tuple-element.22.kv_ref, ...), custom_call_target="tpu_custom_call" | custom-call | flops 130000000 | bytes 1000000 | tf_op jit(solution)/shard_map/pallas_call | solution.py:204
  12.8 0.0 collective-permute-done.5.refs_1_
  12.8 0.8 %collective-permute-done.4.refs_0_ = bf16[256,128]{1,0:T(8,128)(2,1)S(1)} collective-permute-done((bf16[256,128]{1,0:T(8,128)(2,1)S(1)}, bf16[256,128]{1,0:T(8,128)(2,1)S(1)}, u32[]{:S(2)}, u32[]{:S(2)}) %collective-permute-start.4) | collective-permute-done | bytes 65568 | tf_op jit(solution)/shard_map/ppermute | solution.py:181
  13.6 0.9 %shard_map.57 = (f32[1,1024]{1,0:T(1,128)S(1)}, f32[1,1024]{1,0:T(1,128)S(1)}, f32[128,1024]{1,0:T(8,128)S(1)}) custom-call(s32[8,128]{1,0:T(8,128)S(1)} %get-tuple-element.21.reached_ref.tree_ref, bf16[1024,128]{1,0:T(8,128)(2,1)S(1)} %bitcast.5, f32[1,1024]{1,0:T(1,128)S(1)} %get-tuple-element.23.m_in, ...), custom_call_target="tpu_custom_call", output_to_operand_aliasing={{0}: (2, {}), {1}: (3, {}), {2}: (4, {})} | custom-call | flops 270000000 | bytes 1000000 | tf_op jit(solution)/shard_map/pallas_call | solution.py:221
  14.5 0.0 collective-permute-done.6.refs_0_
  14.5 0.0 copy-done
  14.5 1.4 %shard_map.58 = (bf16[128,1024]{1,0:T(8,128)(2,1)S(1)}, bf16[128,512]{1,0:T(8,128)(2,1)S(1)}, f32[128,512]{1,0:T(8,128)S(1)}, f32[1,1024]{1,0:T(1,128)S(1)}, f32...) custom-call(s32[8,128]{1,0:T(8,128)S(1)} %get-tuple-element.21.reached_ref, ...), custom_call_target="tpu_custom_call", output_to_operand_aliasing={{3}: (2, {}), {4}: (3, {}), {5}: (4, {})} | custom-call | flops 1000000000 | bytes 10000000 | tf_op jit(solution)/shard_map/pallas_call | solution.py:241
  15.9 0.1 collective-permute-start.7
  16.0 0.5 %shard_map.60 = (bf16[128,512]{1,0:T(8,128)(2,1)S(1)}, f32[128,512]{1,0:T(8,128)S(1)}) custom-call(bf16[128,1024]{1,0:T(8,128)(2,1)S(1)} %get-tuple-element.32.att_ref, bf16[1024,4096]{1,0:T(8,128)(2,1)S(1)} %copy-done), custom_call_target="tpu_custom_call" | custom-call | flops 540000000 | bytes 4000000 | tf_op jit(solution)/shard_map/pallas_call | solution.py:252
  16.4 0.6 %collective-permute-start.10 = (bf16[128,512]{1,0:T(8,128)(2,1)S(1)}, bf16[128,512]{1,0:T(8,128)(2,1)S(1)}, u32[]{:S(2)}, u32[]{:S(2)}) collective-permute-start(bf16[128,512]{1,0:T(8,128)(2,1)S(1)} %get-tuple-element.36), channel_id=1, source_target_pairs={{0,1},{1,0},{2,3},{3,2},{4,5},{5,4},{6,7},{7,6},{8,9},{9,8},{10,11... | collective-permute-start | bytes 393224 | tf_op jit(solution)/shard_map/ppermute | solution.py:173
  17.0 0.3 %collective-permute-done.7 = bf16[128,512]{1,0:T(8,128)(2,1)S(1)} collective-permute-done((bf16[128,512]{1,0:T(8,128)(2,1)S(1)}, bf16[128,512]{1,0:T(8,128)(2,1)S(1)}, u32[]{:S(2)}, u32[]{:S(2)}) %collective-permute-start.7) | collective-permute-done | bytes 131104 | tf_op jit(solution)/shard_map/ppermute | solution.py:173
  17.3 0.6 %collective-permute-start.9 = (bf16[128,512]{1,0:T(8,128)(2,1)S(1)}, bf16[128,512]{1,0:T(8,128)(2,1)S(1)}, u32[]{:S(2)}, u32[]{:S(2)}) collective-permute-start(bf16[128,512]{1,0:T(8,128)(2,1)S(1)} %add_convert_fusion.2), channel_id=1, source_target_pairs={{0,2},{1,3},{2,0},{3,1},{4,6},{5,7},{6,4},{7,5},{8,10},{9,11},{10,... | collective-permute-start | bytes 393224 | tf_op jit(solution)/shard_map/ppermute | solution.py:173
  17.9 0.7 %shard_map.59 = (bf16[128,1024]{1,0:T(8,128)(2,1)S(1)}, f32[128,1024]{1,0:T(8,128)S(1)}) custom-call(bf16[128,1024]{1,0:T(8,128)(2,1)S(1)} %get-tuple-element.32.att_ref, bf16[1024,4096]{1,0:T(8,128)(2,1)S(1)} %copy-done), custom_call_target="tpu_custom_call" | custom-call | flops 540000000 | bytes 4000000 | tf_op jit(solution)/shard_map/pallas_call | solution.py:252
  18.7 0.1 collective-permute-start.8
  18.8 0.0 collective-permute-done.10
  18.8 1.6 %collective-permute-start.11 = (bf16[128,512]{1,0:T(8,128)(2,1)S(1)}, bf16[128,512]{1,0:T(8,128)(2,1)S(1)}, u32[]{:S(2)}, u32[]{:S(2)}) collective-permute-start(bf16[128,512]{1,0:T(8,128)(2,1)S(1)} %add_convert_fusion.1), channel_id=1, source_target_pairs={{0,2},{1,3},{2,0},{3,1},{4,6},{5,7},{6,4},{7,5},{8,10},{9,11},{10,... | collective-permute-start | bytes 393224 | tf_op jit(solution)/shard_map/ppermute | solution.py:173
  20.4 3.4 %collective-permute-done.9 = bf16[128,512]{1,0:T(8,128)(2,1)S(1)} collective-permute-done((bf16[128,512]{1,0:T(8,128)(2,1)S(1)}, bf16[128,512]{1,0:T(8,128)(2,1)S(1)}, u32[]{:S(2)}, u32[]{:S(2)}) %collective-permute-start.9) | collective-permute-done | bytes 131104 | tf_op jit(solution)/shard_map/ppermute | solution.py:173
  23.8 2.0 %collective-permute-done.11 = bf16[128,512]{1,0:T(8,128)(2,1)S(1)} collective-permute-done((bf16[128,512]{1,0:T(8,128)(2,1)S(1)}, bf16[128,512]{1,0:T(8,128)(2,1)S(1)}, u32[]{:S(2)}, u32[]{:S(2)}) %collective-permute-start.11) | collective-permute-done | bytes 131104 | tf_op jit(solution)/shard_map/ppermute | solution.py:173
  25.8 0.0 collective-permute-done.8
  25.8 0.8 %add_convert_fusion = bf16[128,1024]{1,0:T(8,128)(2,1)} fusion(f32[128,1024]{1,0:T(8,128)S(1)} %get-tuple-element.33, bf16[128,1024]{1,0:T(8,128)(2,1)S(1)} %collective-permute-done.8, bf16[128,512]{1,0:T(8,128)(2,1)S(1)} %collective-permute-done.11, bf16[128,512]{1,0:T(8,128)(2,1)S(1)} %collective-permute-done.9), kind=kLoop, calls=%fused_computation | loop fusion | flops 1048576 | bytes 1310720 | tf_op jit(solution)/shard_map/convert_element_type | solution.py:280
  (3 shorter events, 0.1 us)
Async XLA Ops:
  0.0 11.4 %copy-start.1 = (bf16[128,8,128]{2,1,0:T(8,128)(2,1)S(1)}, bf16[128,8,128]{2,1,0:T(8,128)(2,1)}, u32[]{:S(2)}) copy-start(bf16[128,8,128]{2,1,0:T(8,128)(2,1)} %param.5) | copy-start | bytes 786436
  0.0 14.5 %copy-start = (bf16[1024,4096]{1,0:T(8,128)(2,1)S(1)}, bf16[1024,4096]{1,0:T(8,128)(2,1)}, u32[]{:S(2)}) copy-start(bf16[1024,4096]{1,0:T(8,128)(2,1)} %w_ref.3) | copy-start | bytes 25165828
  1.0 6.8 %collective-permute-start.3 = (bf16[256,128]{1,0:T(8,128)(2,1)S(1)}, bf16[256,128]{1,0:T(8,128)(2,1)S(1)}, u32[]{:S(2)}, u32[]{:S(2)}) collective-permute-start(bf16[256,128]{1,0:T(8,128)(2,1)S(1)} %get-tuple-element.22.kv_ref), channel_id=1, source_target_pairs={{0,24},{4,28},{8,16},{12,20},{16,8},{20,12},{24,0},{28,4},{1,25},{... | collective-permute-start | bytes 196616 | tf_op jit(solution)/shard_map/ppermute | solution.py:173
  1.2 8.1 %collective-permute-start.2 = (bf16[256,128]{1,0:T(8,128)(2,1)S(1)}, bf16[256,128]{1,0:T(8,128)(2,1)S(1)}, u32[]{:S(2)}, u32[]{:S(2)}) collective-permute-start(bf16[256,128]{1,0:T(8,128)(2,1)S(1)} %get-tuple-element.22.kv_ref), channel_id=1, source_target_pairs={{0,8},{4,12},{8,0},{12,4},{16,24},{20,28},{24,16},{28,20},{1,9},{5... | collective-permute-start | bytes 196616 | tf_op jit(solution)/shard_map/ppermute | solution.py:173
  1.9 7.9 %collective-permute-start.1 = (bf16[256,128]{1,0:T(8,128)(2,1)S(1)}, bf16[256,128]{1,0:T(8,128)(2,1)S(1)}, u32[]{:S(2)}, u32[]{:S(2)}) collective-permute-start(bf16[256,128]{1,0:T(8,128)(2,1)S(1)} %get-tuple-element.22.kv_ref), channel_id=1, source_target_pairs={{0,16},{4,20},{8,24},{12,28},{16,0},{20,4},{24,8},{28,12},{1,17},{... | collective-permute-start | bytes 196616 | tf_op jit(solution)/shard_map/ppermute | solution.py:173
  5.4 6.0 %collective-permute-start = (bf16[256,128]{1,0:T(8,128)(2,1)S(1)}, bf16[256,128]{1,0:T(8,128)(2,1)S(1)}, u32[]{:S(2)}, u32[]{:S(2)}) collective-permute-start(bf16[256,128]{1,0:T(8,128)(2,1)S(1)} %get-tuple-element.22.kv_ref), channel_id=1, source_target_pairs={{0,4},{4,0},{8,12},{12,8},{16,20},{20,16},{24,28},{28,24},{1,5},{5... | collective-permute-start | bytes 196616 | tf_op jit(solution)/shard_map/ppermute | solution.py:173
  7.8 5.0 %collective-permute-start.5 = (bf16[256,128]{1,0:T(8,128)(2,1)S(1)}, bf16[256,128]{1,0:T(8,128)(2,1)S(1)}, u32[]{:S(2)}, u32[]{:S(2)}) collective-permute-start(bf16[256,128]{1,0:T(8,128)(2,1)S(1)} %collective-permute-done.3.refs_3_), channel_id=1, source_target_pairs={{0,1},{1,0},{2,3},{3,2},{4,5},{5,4},{6,7},{7,6},{8,9},{9,8},{10,11... | collective-permute-start | bytes 196616 | tf_op jit(solution)/shard_map/ppermute | solution.py:181
  9.3 4.3 %collective-permute-start.4 = (bf16[256,128]{1,0:T(8,128)(2,1)S(1)}, bf16[256,128]{1,0:T(8,128)(2,1)S(1)}, u32[]{:S(2)}, u32[]{:S(2)}) collective-permute-start(bf16[256,128]{1,0:T(8,128)(2,1)S(1)} %collective-permute-done.2.refs_2_), channel_id=1, source_target_pairs={{0,1},{1,0},{2,3},{3,2},{4,5},{5,4},{6,7},{7,6},{8,12},{9,13},{10,... | collective-permute-start | bytes 196616 | tf_op jit(solution)/shard_map/ppermute | solution.py:181
  9.8 4.6 %collective-permute-start.6 = (bf16[256,128]{1,0:T(8,128)(2,1)S(1)}, bf16[256,128]{1,0:T(8,128)(2,1)S(1)}, u32[]{:S(2)}, u32[]{:S(2)}) collective-permute-start(bf16[256,128]{1,0:T(8,128)(2,1)S(1)} %collective-permute-done.1.refs_1_), channel_id=1, source_target_pairs={{0,1},{1,0},{2,3},{3,2},{4,5},{5,4},{6,7},{7,6},{8,9},{9,8},{10,11... | collective-permute-start | bytes 196616 | tf_op jit(solution)/shard_map/ppermute | solution.py:181
  15.9 1.4 %collective-permute-start.7 = (bf16[128,512]{1,0:T(8,128)(2,1)S(1)}, bf16[128,512]{1,0:T(8,128)(2,1)S(1)}, u32[]{:S(2)}, u32[]{:S(2)}) collective-permute-start(bf16[128,512]{1,0:T(8,128)(2,1)S(1)} %get-tuple-element.31), channel_id=1, source_target_pairs={{0,1},{1,0},{2,3},{3,2},{4,5},{5,4},{6,7},{7,6},{8,9},{9,8},{10,11... | collective-permute-start | bytes 393224 | tf_op jit(solution)/shard_map/ppermute | solution.py:173
  16.4 2.3 %collective-permute-start.10 = (bf16[128,512]{1,0:T(8,128)(2,1)S(1)}, bf16[128,512]{1,0:T(8,128)(2,1)S(1)}, u32[]{:S(2)}, u32[]{:S(2)}) collective-permute-start(bf16[128,512]{1,0:T(8,128)(2,1)S(1)} %get-tuple-element.36), channel_id=1, source_target_pairs={{0,1},{1,0},{2,3},{3,2},{4,5},{5,4},{6,7},{7,6},{8,9},{9,8},{10,11... | collective-permute-start | bytes 393224 | tf_op jit(solution)/shard_map/ppermute | solution.py:173
  17.3 6.4 %collective-permute-start.9 = (bf16[128,512]{1,0:T(8,128)(2,1)S(1)}, bf16[128,512]{1,0:T(8,128)(2,1)S(1)}, u32[]{:S(2)}, u32[]{:S(2)}) collective-permute-start(bf16[128,512]{1,0:T(8,128)(2,1)S(1)} %add_convert_fusion.2), channel_id=1, source_target_pairs={{0,2},{1,3},{2,0},{3,1},{4,6},{5,7},{6,4},{7,5},{8,10},{9,11},{10,... | collective-permute-start | bytes 393224 | tf_op jit(solution)/shard_map/ppermute | solution.py:173
  18.7 7.1 %collective-permute-start.8 = (bf16[128,1024]{1,0:T(8,128)(2,1)S(1)}, bf16[128,1024]{1,0:T(8,128)(2,1)S(1)}, u32[]{:S(2)}, u32[]{:S(2)}) collective-permute-start(bf16[128,1024]{1,0:T(8,128)(2,1)S(1)} %get-tuple-element.34), channel_id=1, source_target_pairs={{0,1},{1,0},{2,3},{3,2},{4,5},{5,4},{6,7},{7,6},{8,9},{9,8},{10,11... | collective-permute-start | bytes 786440 | tf_op jit(solution)/shard_map/ppermute | solution.py:173
  18.8 7.0 %collective-permute-start.11 = (bf16[128,512]{1,0:T(8,128)(2,1)S(1)}, bf16[128,512]{1,0:T(8,128)(2,1)S(1)}, u32[]{:S(2)}, u32[]{:S(2)}) collective-permute-start(bf16[128,512]{1,0:T(8,128)(2,1)S(1)} %add_convert_fusion.1), channel_id=1, source_target_pairs={{0,2},{1,3},{2,0},{3,1},{4,6},{5,7},{6,4},{7,5},{8,10},{9,11},{10,... | collective-permute-start | bytes 393224 | tf_op jit(solution)/shard_map/ppermute | solution.py:173

commit v14 on v12

--- a/solution.py
+++ b/solution.py
@@ -183,10 +183,8 @@
         cost_estimate=pl.CostEstimate(flops=8_000_000_000, bytes_accessed=130_000, transcendentals=0),
     )(in_hbm(key_heads[:, 0, :]), in_hbm(value_heads[:, 0, :]), in_hbm(parents))
     if ctx_size == DIRECT_SIZE:
-        columns = [swap(kv, "ctx", ctx_size, other) for other in (4, 2, 6)]
-        beside = swap(kv, "ctx", ctx_size, 1)
-        pairs = [forward(x, other) for x, other in zip(columns, (4, 2, 6))]
-        early, early_xors = [beside, *columns], (1, 4, 2, 6)
+        by_6, by_1, by_4, by_2 = [swap(kv, "ctx", ctx_size, other) for other in (6, 1, 4, 2)]
+        early, early_xors = [by_1], (1,)
     else:
         early, early_xors = [], ()
     q = jnp.transpose(query_heads, (1, 0, 2)).reshape(rows, head_dim)
@@ -218,8 +216,12 @@
                 cost_estimate=pl.CostEstimate(flops=270_000_000, bytes_accessed=1_000_000, transcendentals=500_000),
             )(reached, q, *state, *arrived)
 
-        state = absorbed(state, (3, 7), pairs[1:])
-        xors, pieces, tree, tree_spec = (5,), pairs[:1], reached, vmem
+        by_7 = forward(by_6, 6)
+        by_3 = swap(by_1, "ctx", ctx_size, 2)
+        by_5 = forward(by_4, 4)
+        state = absorbed(state, (2, 4, 6), [by_2, by_4, by_6])
+        state = absorbed(state, (3, 7), [by_3, by_7])
+        xors, pieces, tree, tree_spec = (5,), [by_5], reached, vmem
     else:
         xors, pieces, tree, tree_spec = (), [lax.all_gather(kv, "ctx", axis=0, tiled=True)], parents, smem
 

time: 26.6 us -> 27 us (1.015)
  the two profiles are of different devices: /device:TPU:24 before, /device:TPU:18 now
where the time goes in v14:
time: 27 us; the launch traced here: 27.1 us
  starting transfers between devices  13.2 us (49%)
  waiting for transfers between devices  8.1 us (30%)
  Pallas kernels  4.79 us (18%)
  other arithmetic  0.86 us (3%)
    ppermute x10, starting transfers between devices, swap(): return lax.ppermute(x, axis, [(i, i ^ other) for i in range(size)])  9.86 us
    ppermute x10, waiting for transfers between devices, swap(): return lax.ppermute(x, axis, [(i, i ^ other) for i in range(size)])  6.83 us
    ppermute x2, starting transfers between devices, forward(): return lax.ppermute(x, ('ctx', 'tp'), route)  3.32 us
    ppermute x2, waiting for transfers between devices, forward(): return lax.ppermute(x, ('ctx', 'tp'), route)  1.27 us
    pallas_call x1, Pallas kernels, shards(): pl.pallas_call(functools.partial(last_kernel, xors), out_shape=(jax.Shape...  1.21 us
    pallas_call x2, Pallas kernels, projected(): pl.pallas_call(functools.partial(project_pair, flip, part), out_shape=sha...  1.19 us
    pallas_call x1, Pallas kernels, shards(): pl.pallas_call(functools.partial(pack_kernel, ctx_size == DIRECT_SIZE), o...  0.96 us
    pallas_call x2, Pallas kernels, absorbed(): pl.pallas_call(functools.partial(others_kernel, xors), out_shape=state_sh...  0.91 us
  transfers between devices with their start and end apart: 12, of which 5 were waited for; matrix products, arithmetic and copies ran while one was open for 0% of the time, Pallas kernels for 10%

profile of v14, /device:TPU:18, one launch (start us, length us, event | category | flops | bytes accessed | tf_op | source)
XLA Modules:
  0.0 27.1 jit_solution(11750065869310366824)
XLA Ops:
  0.0 0.0 slice-start
  0.0 0.0 copy-start
  0.0 0.0 slice-start.1
  0.0 1.0 %shard_map.55 = (bf16[256,128]{1,0:T(8,128)(2,1)S(1)}, s32[8,128]{1,0:T(8,128)S(1)}) custom-call(bf16[128,128]{1,0:T(8,128)(2,1)} %bitcast.11, bf16[128,128]{1,0:T(8,128)(2,1)} %bitcast.12, s32[8]{0:T(128)} %parents_hbm.1), custom_call_target="tpu_custom_call" | custom-call | flops 8000000000 | bytes 130000 | tf_op jit(solution)/shard_map/pallas_call | solution.py:173
  1.0 0.5 %collective-permute-start.3 = (bf16[256,128]{1,0:T(8,128)(2,1)S(1)}, bf16[256,128]{1,0:T(8,128)(2,1)S(1)}, u32[]{:S(2)}, u32[]{:S(2)}) collective-permute-start(bf16[256,128]{1,0:T(8,128)(2,1)S(1)} %get-tuple-element.25.kv_ref), channel_id=1, source_target_pairs={{0,24},{4,28},{8,16},{12,20},{16,8},{20,12},{24,0},{28,4},{1,25},{... | collective-permute-start | bytes 196616 | tf_op jit(solution)/shard_map/ppermute | solution.py:163
  1.5 1.5 %collective-permute-start = (bf16[256,128]{1,0:T(8,128)(2,1)S(1)}, bf16[256,128]{1,0:T(8,128)(2,1)S(1)}, u32[]{:S(2)}, u32[]{:S(2)}) collective-permute-start(bf16[256,128]{1,0:T(8,128)(2,1)S(1)} %get-tuple-element.25.kv_ref), channel_id=1, source_target_pairs={{0,4},{4,0},{8,12},{12,8},{16,20},{20,16},{24,28},{28,24},{1,5},{5... | collective-permute-start | bytes 196616 | tf_op jit(solution)/shard_map/ppermute | solution.py:163
  3.0 3.5 %collective-permute-start.2 = (bf16[256,128]{1,0:T(8,128)(2,1)S(1)}, bf16[256,128]{1,0:T(8,128)(2,1)S(1)}, u32[]{:S(2)}, u32[]{:S(2)}) collective-permute-start(bf16[256,128]{1,0:T(8,128)(2,1)S(1)} %get-tuple-element.25.kv_ref), channel_id=1, source_target_pairs={{0,16},{4,20},{8,24},{12,28},{16,0},{20,4},{24,8},{28,12},{1,17},{... | collective-permute-start | bytes 196616 | tf_op jit(solution)/shard_map/ppermute | solution.py:163
  6.5 0.0 collective-permute-start.1
  6.5 0.0 collective-permute-done.3.refs_2_
  6.5 2.9 %collective-permute-start.5 = (bf16[256,128]{1,0:T(8,128)(2,1)S(1)}, bf16[256,128]{1,0:T(8,128)(2,1)S(1)}, u32[]{:S(2)}, u32[]{:S(2)}) collective-permute-start(bf16[256,128]{1,0:T(8,128)(2,1)S(1)} %collective-permute-done.3.refs_2_), channel_id=1, source_target_pairs={{0,1},{1,0},{2,3},{3,2},{4,5},{5,4},{6,7},{7,6},{8,9},{9,8},{10,11... | collective-permute-start | bytes 196616 | tf_op jit(solution)/shard_map/ppermute | solution.py:171
  9.4 0.0 collective-permute-done.refs_0_
  9.4 1.5 %collective-permute-start.4 = (bf16[256,128]{1,0:T(8,128)(2,1)S(1)}, bf16[256,128]{1,0:T(8,128)(2,1)S(1)}, u32[]{:S(2)}, u32[]{:S(2)}) collective-permute-start(bf16[256,128]{1,0:T(8,128)(2,1)S(1)} %collective-permute-done.refs_0_), channel_id=1, source_target_pairs={{0,8},{4,12},{8,0},{12,4},{16,24},{20,28},{24,16},{28,20},{1,9},{5... | collective-permute-start | bytes 196616 | tf_op jit(solution)/shard_map/ppermute | solution.py:163
  10.9 0.0 collective-permute-done.2.refs_1_
  10.9 0.4 %collective-permute-start.6 = (bf16[256,128]{1,0:T(8,128)(2,1)S(1)}, bf16[256,128]{1,0:T(8,128)(2,1)S(1)}, u32[]{:S(2)}, u32[]{:S(2)}) collective-permute-start(bf16[256,128]{1,0:T(8,128)(2,1)S(1)} %collective-permute-done.2.refs_1_), channel_id=1, source_target_pairs={{0,1},{1,0},{2,3},{3,2},{4,5},{5,4},{6,7},{7,6},{8,9},{9,8},{10,11... | collective-permute-start | bytes 196616 | tf_op jit(solution)/shard_map/ppermute | solution.py:171
  11.3 0.0 copy-done
  11.4 0.5 %shard_map.56 = (f32[1,1024]{1,0:T(1,128)S(1)}, f32[1,1024]{1,0:T(1,128)S(1)}, f32[128,1024]{1,0:T(8,128)S(1)}) custom-call(s32[8,128]{1,0:T(8,128)S(1)} %get-tuple-element.24.reached_ref.tree_ref, bf16[1024,128]{1,0:T(8,128)(2,1)S(1)} %bitcast.6, bf16[256,128]{1,0:T(8,128)(2,1)S(1)} %get-tuple-element.25.kv_ref, ...), custom_call_target="tpu_custom_call" | custom-call | flops 130000000 | bytes 1000000 | tf_op jit(solution)/shard_map/pallas_call | solution.py:192
  11.9 0.0 collective-permute-done.1.refs_0_
  11.9 0.7 %shard_map.57 = (f32[1,1024]{1,0:T(1,128)S(1)}, f32[1,1024]{1,0:T(1,128)S(1)}, f32[128,1024]{1,0:T(8,128)S(1)}) custom-call(s32[8,128]{1,0:T(8,128)S(1)} %get-tuple-element.24.reached_ref.tree_ref, bf16[1024,128]{1,0:T(8,128)(2,1)S(1)} %bitcast.7, f32[1,1024]{1,0:T(1,128)S(1)} %get-tuple-element.26.m_in, ...), custom_call_target="tpu_custom_call", output_to_operand_aliasing={{0}: (2, {}), {1}: (3, {}), {2}: (4, {})} | custom-call | flops 270000000 | bytes 1000000 | tf_op jit(solution)/shard_map/pallas_call | solution.py:209
  12.6 0.0 collective-permute-done.5.refs_1_
  12.6 1.1 %collective-permute-done.4.refs_0_ = bf16[256,128]{1,0:T(8,128)(2,1)S(1)} collective-permute-done((bf16[256,128]{1,0:T(8,128)(2,1)S(1)}, bf16[256,128]{1,0:T(8,128)(2,1)S(1)}, u32[]{:S(2)}, u32[]{:S(2)}) %collective-permute-start.4) | collective-permute-done | bytes 65568 | tf_op jit(solution)/shard_map/ppermute | solution.py:163
  13.7 0.2 shard_map.58
  13.9 1.3 %collective-permute-done.6.refs_0_ = bf16[256,128]{1,0:T(8,128)(2,1)S(1)} collective-permute-done((bf16[256,128]{1,0:T(8,128)(2,1)S(1)}, bf16[256,128]{1,0:T(8,128)(2,1)S(1)}, u32[]{:S(2)}, u32[]{:S(2)}) %collective-permute-start.6) | collective-permute-done | bytes 65568 | tf_op jit(solution)/shard_map/ppermute | solution.py:171
  15.2 0.0 slice-done
  15.2 0.0 slice-done.1
  15.2 1.2 %shard_map.59 = (bf16[128,1024]{1,0:T(8,128)(2,1)S(1)}, bf16[128,512]{1,0:T(8,128)(2,1)S(1)}, f32[128,512]{1,0:T(8,128)S(1)}, f32[1,1024]{1,0:T(1,128)S(1)}, f32...) custom-call(s32[8,128]{1,0:T(8,128)S(1)} %get-tuple-element.24.reached_ref, ...), custom_call_target="tpu_custom_call", output_to_operand_aliasing={{3}: (2, {}), {4}: (3, {}), {5}: (4, {})} | custom-call | flops 1000000000 | bytes 10000000 | tf_op jit(solution)/shard_map/pallas_call | solution.py:233
  16.4 0.1 collective-permute-start.7
  16.5 0.5 %shard_map.61 = (bf16[128,512]{1,0:T(8,128)(2,1)S(1)}, f32[128,512]{1,0:T(8,128)S(1)}) custom-call(bf16[128,1024]{1,0:T(8,128)(2,1)S(1)} %get-tuple-element.38.att_ref, bf16[1024,4096]{1,0:T(8,128)(2,1)S(1)} %bitcast.5), custom_call_target="tpu_custom_call" | custom-call | flops 540000000 | bytes 4000000 | tf_op jit(solution)/shard_map/pallas_call | solution.py:244
  17.0 0.6 %collective-permute-start.10 = (bf16[128,512]{1,0:T(8,128)(2,1)S(1)}, bf16[128,512]{1,0:T(8,128)(2,1)S(1)}, u32[]{:S(2)}, u32[]{:S(2)}) collective-permute-start(bf16[128,512]{1,0:T(8,128)(2,1)S(1)} %get-tuple-element.42), channel_id=1, source_target_pairs={{0,1},{1,0},{2,3},{3,2},{4,5},{5,4},{6,7},{7,6},{8,9},{9,8},{10,11... | collective-permute-start | bytes 393224 | tf_op jit(solution)/shard_map/ppermute | solution.py:163
  17.5 0.3 %collective-permute-done.7 = bf16[128,512]{1,0:T(8,128)(2,1)S(1)} collective-permute-done((bf16[128,512]{1,0:T(8,128)(2,1)S(1)}, bf16[128,512]{1,0:T(8,128)(2,1)S(1)}, u32[]{:S(2)}, u32[]{:S(2)}) %collective-permute-start.7) | collective-permute-done | bytes 131104 | tf_op jit(solution)/shard_map/ppermute | solution.py:163
  17.9 0.6 %collective-permute-start.9 = (bf16[128,512]{1,0:T(8,128)(2,1)S(1)}, bf16[128,512]{1,0:T(8,128)(2,1)S(1)}, u32[]{:S(2)}, u32[]{:S(2)}) collective-permute-start(bf16[128,512]{1,0:T(8,128)(2,1)S(1)} %add_convert_fusion.2), channel_id=1, source_target_pairs={{0,2},{1,3},{2,0},{3,1},{4,6},{5,7},{6,4},{7,5},{8,10},{9,11},{10,... | collective-permute-start | bytes 393224 | tf_op jit(solution)/shard_map/ppermute | solution.py:163
  18.5 0.7 %shard_map.60 = (bf16[128,1024]{1,0:T(8,128)(2,1)S(1)}, f32[128,1024]{1,0:T(8,128)S(1)}) custom-call(bf16[128,1024]{1,0:T(8,128)(2,1)S(1)} %get-tuple-element.38.att_ref, bf16[1024,4096]{1,0:T(8,128)(2,1)S(1)} %bitcast.5), custom_call_target="tpu_custom_call" | custom-call | flops 540000000 | bytes 4000000 | tf_op jit(solution)/shard_map/pallas_call | solution.py:244
  19.2 0.1 collective-permute-start.8
  19.3 0.0 collective-permute-done.10
  19.3 1.6 %collective-permute-start.11 = (bf16[128,512]{1,0:T(8,128)(2,1)S(1)}, bf16[128,512]{1,0:T(8,128)(2,1)S(1)}, u32[]{:S(2)}, u32[]{:S(2)}) collective-permute-start(bf16[128,512]{1,0:T(8,128)(2,1)S(1)} %add_convert_fusion.1), channel_id=1, source_target_pairs={{0,2},{1,3},{2,0},{3,1},{4,6},{5,7},{6,4},{7,5},{8,10},{9,11},{10,... | collective-permute-start | bytes 393224 | tf_op jit(solution)/shard_map/ppermute | solution.py:163
  20.9 3.4 %collective-permute-done.9 = bf16[128,512]{1,0:T(8,128)(2,1)S(1)} collective-permute-done((bf16[128,512]{1,0:T(8,128)(2,1)S(1)}, bf16[128,512]{1,0:T(8,128)(2,1)S(1)}, u32[]{:S(2)}, u32[]{:S(2)}) %collective-permute-start.9) | collective-permute-done | bytes 131104 | tf_op jit(solution)/shard_map/ppermute | solution.py:163
  24.3 2.0 %collective-permute-done.11 = bf16[128,512]{1,0:T(8,128)(2,1)S(1)} collective-permute-done((bf16[128,512]{1,0:T(8,128)(2,1)S(1)}, bf16[128,512]{1,0:T(8,128)(2,1)S(1)}, u32[]{:S(2)}, u32[]{:S(2)}) %collective-permute-start.11) | collective-permute-done | bytes 131104 | tf_op jit(solution)/shard_map/ppermute | solution.py:163
  26.3 0.0 collective-permute-done.8
  26.3 0.8 %add_convert_fusion = bf16[128,1024]{1,0:T(8,128)(2,1)} fusion(f32[128,1024]{1,0:T(8,128)S(1)} %get-tuple-element.39, bf16[128,1024]{1,0:T(8,128)(2,1)S(1)} %collective-permute-done.8, bf16[128,512]{1,0:T(8,128)(2,1)S(1)} %collective-permute-done.11, bf16[128,512]{1,0:T(8,128)(2,1)S(1)} %collective-permute-done.9), kind=kLoop, calls=%fused_computation | loop fusion | flops 1048576 | bytes 1310720 | tf_op jit(solution)/shard_map/convert_element_type | solution.py:272
  (4 shorter events, 0.1 us)
Async XLA Ops:
  0.0 15.2 %slice-start = ((s8[8388608]{0:T(1024)(128)(4,1)}), s8[4194304]{0:T(1024)(128)(4,1)S(1)}, s32[]{:S(2)}) async-start(s8[8388608]{0:T(1024)(128)(4,1)} %bitcast.4), calls=%async_computation | async-start | bytes 8388608
  0.0 11.3 %copy-start = (bf16[128,8,128]{2,1,0:T(8,128)(2,1)S(1)}, bf16[128,8,128]{2,1,0:T(8,128)(2,1)}, u32[]{:S(2)}) copy-start(bf16[128,8,128]{2,1,0:T(8,128)(2,1)} %param.5) | copy-start | bytes 786436
  0.0 15.2 %slice-start.1 = ((s8[8388608]{0:T(1024)(128)(4,1)}), s8[4194304]{0:T(1024)(128)(4,1)S(1)}, s32[]{:S(2)}) async-start(s8[8388608]{0:T(1024)(128)(4,1)} %bitcast.4), calls=%async_computation.1 | async-start | bytes 8388608
  1.0 5.5 %collective-permute-start.3 = (bf16[256,128]{1,0:T(8,128)(2,1)S(1)}, bf16[256,128]{1,0:T(8,128)(2,1)S(1)}, u32[]{:S(2)}, u32[]{:S(2)}) collective-permute-start(bf16[256,128]{1,0:T(8,128)(2,1)S(1)} %get-tuple-element.25.kv_ref), channel_id=1, source_target_pairs={{0,24},{4,28},{8,16},{12,20},{16,8},{20,12},{24,0},{28,4},{1,25},{... | collective-permute-start | bytes 196616 | tf_op jit(solution)/shard_map/ppermute | solution.py:163
  1.5 8.0 %collective-permute-start = (bf16[256,128]{1,0:T(8,128)(2,1)S(1)}, bf16[256,128]{1,0:T(8,128)(2,1)S(1)}, u32[]{:S(2)}, u32[]{:S(2)}) collective-permute-start(bf16[256,128]{1,0:T(8,128)(2,1)S(1)} %get-tuple-element.25.kv_ref), channel_id=1, source_target_pairs={{0,4},{4,0},{8,12},{12,8},{16,20},{20,16},{24,28},{28,24},{1,5},{5... | collective-permute-start | bytes 196616 | tf_op jit(solution)/shard_map/ppermute | solution.py:163
  3.0 7.9 %collective-permute-start.2 = (bf16[256,128]{1,0:T(8,128)(2,1)S(1)}, bf16[256,128]{1,0:T(8,128)(2,1)S(1)}, u32[]{:S(2)}, u32[]{:S(2)}) collective-permute-start(bf16[256,128]{1,0:T(8,128)(2,1)S(1)} %get-tuple-element.25.kv_ref), channel_id=1, source_target_pairs={{0,16},{4,20},{8,24},{12,28},{16,0},{20,4},{24,8},{28,12},{1,17},{... | collective-permute-start | bytes 196616 | tf_op jit(solution)/shard_map/ppermute | solution.py:163
  6.5 5.4 %collective-permute-start.1 = (bf16[256,128]{1,0:T(8,128)(2,1)S(1)}, bf16[256,128]{1,0:T(8,128)(2,1)S(1)}, u32[]{:S(2)}, u32[]{:S(2)}) collective-permute-start(bf16[256,128]{1,0:T(8,128)(2,1)S(1)} %get-tuple-element.25.kv_ref), channel_id=1, source_target_pairs={{0,8},{4,12},{8,0},{12,4},{16,24},{20,28},{24,16},{28,20},{1,9},{5... | collective-permute-start | bytes 196616 | tf_op jit(solution)/shard_map/ppermute | solution.py:163
  6.5 6.1 %collective-permute-start.5 = (bf16[256,128]{1,0:T(8,128)(2,1)S(1)}, bf16[256,128]{1,0:T(8,128)(2,1)S(1)}, u32[]{:S(2)}, u32[]{:S(2)}) collective-permute-start(bf16[256,128]{1,0:T(8,128)(2,1)S(1)} %collective-permute-done.3.refs_2_), channel_id=1, source_target_pairs={{0,1},{1,0},{2,3},{3,2},{4,5},{5,4},{6,7},{7,6},{8,9},{9,8},{10,11... | collective-permute-start | bytes 196616 | tf_op jit(solution)/shard_map/ppermute | solution.py:171
  9.4 4.3 %collective-permute-start.4 = (bf16[256,128]{1,0:T(8,128)(2,1)S(1)}, bf16[256,128]{1,0:T(8,128)(2,1)S(1)}, u32[]{:S(2)}, u32[]{:S(2)}) collective-permute-start(bf16[256,128]{1,0:T(8,128)(2,1)S(1)} %collective-permute-done.refs_0_), channel_id=1, source_target_pairs={{0,8},{4,12},{8,0},{12,4},{16,24},{20,28},{24,16},{28,20},{1,9},{5... | collective-permute-start | bytes 196616 | tf_op jit(solution)/shard_map/ppermute | solution.py:163
  10.9 4.3 %collective-permute-start.6 = (bf16[256,128]{1,0:T(8,128)(2,1)S(1)}, bf16[256,128]{1,0:T(8,128)(2,1)S(1)}, u32[]{:S(2)}, u32[]{:S(2)}) collective-permute-start(bf16[256,128]{1,0:T(8,128)(2,1)S(1)} %collective-permute-done.2.refs_1_), channel_id=1, source_target_pairs={{0,1},{1,0},{2,3},{3,2},{4,5},{5,4},{6,7},{7,6},{8,9},{9,8},{10,11... | collective-permute-start | bytes 196616 | tf_op jit(solution)/shard_map/ppermute | solution.py:171
  16.4 1.4 %collective-permute-start.7 = (bf16[128,512]{1,0:T(8,128)(2,1)S(1)}, bf16[128,512]{1,0:T(8,128)(2,1)S(1)}, u32[]{:S(2)}, u32[]{:S(2)}) collective-permute-start(bf16[128,512]{1,0:T(8,128)(2,1)S(1)} %get-tuple-element.37), channel_id=1, source_target_pairs={{0,1},{1,0},{2,3},{3,2},{4,5},{5,4},{6,7},{7,6},{8,9},{9,8},{10,11... | collective-permute-start | bytes 393224 | tf_op jit(solution)/shard_map/ppermute | solution.py:163
  17.0 2.3 %collective-permute-start.10 = (bf16[128,512]{1,0:T(8,128)(2,1)S(1)}, bf16[128,512]{1,0:T(8,128)(2,1)S(1)}, u32[]{:S(2)}, u32[]{:S(2)}) collective-permute-start(bf16[128,512]{1,0:T(8,128)(2,1)S(1)} %get-tuple-element.42), channel_id=1, source_target_pairs={{0,1},{1,0},{2,3},{3,2},{4,5},{5,4},{6,7},{7,6},{8,9},{9,8},{10,11... | collective-permute-start | bytes 393224 | tf_op jit(solution)/shard_map/ppermute | solution.py:163
  17.9 6.4 %collective-permute-start.9 = (bf16[128,512]{1,0:T(8,128)(2,1)S(1)}, bf16[128,512]{1,0:T(8,128)(2,1)S(1)}, u32[]{:S(2)}, u32[]{:S(2)}) collective-permute-start(bf16[128,512]{1,0:T(8,128)(2,1)S(1)} %add_convert_fusion.2), channel_id=1, source_target_pairs={{0,2},{1,3},{2,0},{3,1},{4,6},{5,7},{6,4},{7,5},{8,10},{9,11},{10,... | collective-permute-start | bytes 393224 | tf_op jit(solution)/shard_map/ppermute | solution.py:163
  19.2 7.1 %collective-permute-start.8 = (bf16[128,1024]{1,0:T(8,128)(2,1)S(1)}, bf16[128,1024]{1,0:T(8,128)(2,1)S(1)}, u32[]{:S(2)}, u32[]{:S(2)}) collective-permute-start(bf16[128,1024]{1,0:T(8,128)(2,1)S(1)} %get-tuple-element.40), channel_id=1, source_target_pairs={{0,1},{1,0},{2,3},{3,2},{4,5},{5,4},{6,7},{7,6},{8,9},{9,8},{10,11... | collective-permute-start | bytes 786440 | tf_op jit(solution)/shard_map/ppermute | solution.py:163
  19.3 7.0 %collective-permute-start.11 = (bf16[128,512]{1,0:T(8,128)(2,1)S(1)}, bf16[128,512]{1,0:T(8,128)(2,1)S(1)}, u32[]{:S(2)}, u32[]{:S(2)}) collective-permute-start(bf16[128,512]{1,0:T(8,128)(2,1)S(1)} %add_convert_fusion.1), channel_id=1, source_target_pairs={{0,2},{1,3},{2,0},{3,1},{4,6},{5,7},{6,4},{7,5},{8,10},{9,11},{10,... | collective-permute-start | bytes 393224 | tf_op jit(solution)/shard_map/ppermute | solution.py:163

commit v15 on v12

--- a/solution.py
+++ b/solution.py
@@ -13,12 +13,14 @@
 VMEM_LIMIT = 32 * 1024 * 1024
 
 
-def scores_of(k, q):
-    return lax.dot_general(k, q, (((1,), (1,)), ((), ())), preferred_element_type=jnp.float32)
-
-
-def weighted(v, p):
-    return lax.dot_general(v, p.astype(jnp.bfloat16), (((0,), (0,)), ((), ())), preferred_element_type=jnp.float32)
+def scores_of(q, k):
+    return lax.dot_general(q, k, (((1,), (1,)), ((), ())), preferred_element_type=jnp.float32)
+
+
+def weighted_and_sums(p, v):
+    beside = jnp.concatenate([v, jnp.ones_like(v)], axis=1)
+    both = jnp.dot(p.astype(jnp.bfloat16), beside, preferred_element_type=jnp.float32)
+    return both[:, :v.shape[1]], both[:, v.shape[1]:]
 
 
 def exponent_scale(head_dim):
@@ -59,14 +61,15 @@
 
 
 def absorb(scale, q_ref, k, v, m_ref, l_ref, acc_ref):
-    s = scores_of(k, q_ref[...])
+    s = scores_of(q_ref[...], k)
     m_old = m_ref[...]
-    m_new = jnp.maximum(m_old, jnp.max(s, axis=0, keepdims=True))
+    m_new = jnp.maximum(m_old, jnp.max(s, axis=1, keepdims=True))
     p = jnp.exp2((s - m_new) * scale)
     factor = jnp.exp2((m_old - m_new) * scale)
+    part, sums = weighted_and_sums(p, v)
     m_ref[...] = m_new
-    l_ref[...] = l_ref[...] * factor + jnp.sum(p, axis=0, keepdims=True)
-    acc_ref[...] = acc_ref[...] * factor + weighted(v, p)
+    l_ref[...] = l_ref[...] * factor + sums
+    acc_ref[...] = acc_ref[...] * factor + part
 
 
 def absorb_reached(xors, reached_ref, q_ref, kv_refs, state):
@@ -102,15 +105,16 @@
     state = refs[len(xors):]
     m_ref, l_ref, acc_ref = state
     scale = exponent_scale(q_ref.shape[1])
-    s = scores_of(kv_ref[0:BLOCK, :], q_ref[...])
-    key_at = lax.broadcasted_iota(jnp.int32, s.shape, 0)
-    query_at = lax.broadcasted_iota(jnp.int32, s.shape, 1) & (BLOCK - 1)
+    s = scores_of(q_ref[...], kv_ref[0:BLOCK, :])
+    query_at = lax.broadcasted_iota(jnp.int32, s.shape, 0) & (BLOCK - 1)
+    key_at = lax.broadcasted_iota(jnp.int32, s.shape, 1)
     s = jnp.where(key_at <= query_at, s, -1e30)
-    m = jnp.max(s, axis=0, keepdims=True)
+    m = jnp.broadcast_to(jnp.max(s, axis=1, keepdims=True), s.shape)
     p = jnp.exp2((s - m) * scale)
+    part, sums = weighted_and_sums(p, kv_ref[BLOCK:, :])
     m_ref[...] = m
-    l_ref[...] = jnp.sum(p, axis=0, keepdims=True)
-    acc_ref[...] = weighted(kv_ref[BLOCK:, :], p)
+    l_ref[...] = sums
+    acc_ref[...] = part
     absorb_reached(xors, reached_ref, q_ref, refs[:len(xors)], state)
 
 
@@ -131,8 +135,7 @@
 
     for head in range(rows // BLOCK):
         at = slice(head * BLOCK, (head + 1) * BLOCK)
-        part = acc_ref[:, at] / l_ref[:, at]
-        att_ref[:, head * head_dim:(head + 1) * head_dim] = part.T.astype(jnp.bfloat16)
+        att_ref[:, head * head_dim:(head + 1) * head_dim] = (acc_ref[at, :] / l_ref[at, :]).astype(jnp.bfloat16)
 
     project_pair(2, 0, att_ref, w_ref, send_ref, keep_ref)
 
@@ -194,9 +197,9 @@
     m, l, acc = pl.pallas_call(
         functools.partial(own_block_kernel, early_xors),
         out_shape=(
-            jax.ShapeDtypeStruct((1, rows), jnp.float32),
-            jax.ShapeDtypeStruct((1, rows), jnp.float32),
-            jax.ShapeDtypeStruct((head_dim, rows), jnp.float32),
+            jax.ShapeDtypeStruct((rows, BLOCK), jnp.float32),
+            jax.ShapeDtypeStruct((rows, head_dim), jnp.float32),
+            jax.ShapeDtypeStruct((rows, head_dim), jnp.float32),
         ),
         in_specs=[vmem] * (3 + len(early)),
         out_specs=(vmem,) * 3,

time: 26.6 us -> 26 us (0.977)
  the two profiles are of different devices: /device:TPU:24 before, /device:TPU:22 now
where the time goes in v15:
time: 26 us; the launch traced here: 25.9 us
  waiting for transfers between devices  11.2 us (43%)
  starting transfers between devices  9.39 us (36%)
  Pallas kernels  4.24 us (16%)
  other arithmetic  0.85 us (3%)
    ppermute x9, waiting for transfers between devices, swap(): return lax.ppermute(x, axis, [(i, i ^ other) for i in range(size)])  8.36 us
    ppermute x9, starting transfers between devices, swap(): return lax.ppermute(x, axis, [(i, i ^ other) for i in range(size)])  7.37 us
    ppermute x3, waiting for transfers between devices, forward(): return lax.ppermute(x, ('ctx', 'tp'), route)  2.85 us
    ppermute x3, starting transfers between devices, forward(): return lax.ppermute(x, ('ctx', 'tp'), route)  2.03 us
    pallas_call x1, Pallas kernels, shards(): pl.pallas_call(functools.partial(last_kernel, xors), out_shape=(jax.Shape...  1.28 us
    pallas_call x2, Pallas kernels, projected(): pl.pallas_call(functools.partial(project_pair, flip, part), out_shape=sha...  1.18 us
    pallas_call x1, Pallas kernels, shards(): pl.pallas_call(functools.partial(pack_kernel, ctx_size == DIRECT_SIZE), o...  0.96 us
    convert_element_type x1, other arithmetic, shards(): (keep_near + near_in.astype(jnp.float32) + from_far).astype(jnp.bfloat16)  0.79 us
  transfers between devices with their start and end apart: 12, of which 5 were waited for; matrix products, arithmetic and copies ran while one was open for 0% of the time, Pallas kernels for 8%

profile of v15, /device:TPU:22, one launch (start us, length us, event | category | flops | bytes accessed | tf_op | source)
XLA Modules:
  0.0 25.9 jit_solution(9524307531801786983)
XLA Ops:
  0.0 0.0 slice-start
  0.0 0.0 copy-start
  0.0 0.0 slice-start.1
  0.0 1.0 %shard_map.55 = (bf16[256,128]{1,0:T(8,128)(2,1)S(1)}, s32[8,128]{1,0:T(8,128)S(1)}) custom-call(bf16[128,128]{1,0:T(8,128)(2,1)} %bitcast.10, bf16[128,128]{1,0:T(8,128)(2,1)} %bitcast.11, s32[8]{0:T(128)} %parents_hbm.1), custom_call_target="tpu_custom_call" | custom-call | flops 8000000000 | bytes 130000 | tf_op jit(solution)/shard_map/pallas_call | solution.py:176
  1.0 0.5 %collective-permute-start.3 = (bf16[256,128]{1,0:T(8,128)(2,1)S(1)}, bf16[256,128]{1,0:T(8,128)(2,1)S(1)}, u32[]{:S(2)}, u32[]{:S(2)}) collective-permute-start(bf16[256,128]{1,0:T(8,128)(2,1)S(1)} %get-tuple-element.22.kv_ref), channel_id=1, source_target_pairs={{0,24},{4,28},{8,16},{12,20},{16,8},{20,12},{24,0},{28,4},{1,25},{... | collective-permute-start | bytes 196616 | tf_op jit(solution)/shard_map/ppermute | solution.py:166
  1.5 1.3 %collective-permute-start.2 = (bf16[256,128]{1,0:T(8,128)(2,1)S(1)}, bf16[256,128]{1,0:T(8,128)(2,1)S(1)}, u32[]{:S(2)}, u32[]{:S(2)}) collective-permute-start(bf16[256,128]{1,0:T(8,128)(2,1)S(1)} %get-tuple-element.22.kv_ref), channel_id=1, source_target_pairs={{0,8},{4,12},{8,0},{12,4},{16,24},{20,28},{24,16},{28,20},{1,9},{5... | collective-permute-start | bytes 196616 | tf_op jit(solution)/shard_map/ppermute | solution.py:166
  2.8 2.1 %collective-permute-start.1 = (bf16[256,128]{1,0:T(8,128)(2,1)S(1)}, bf16[256,128]{1,0:T(8,128)(2,1)S(1)}, u32[]{:S(2)}, u32[]{:S(2)}) collective-permute-start(bf16[256,128]{1,0:T(8,128)(2,1)S(1)} %get-tuple-element.22.kv_ref), channel_id=1, source_target_pairs={{0,16},{4,20},{8,24},{12,28},{16,0},{20,4},{24,8},{28,12},{1,17},{... | collective-permute-start | bytes 196616 | tf_op jit(solution)/shard_map/ppermute | solution.py:166
  5.0 0.5 %collective-permute-start = (bf16[256,128]{1,0:T(8,128)(2,1)S(1)}, bf16[256,128]{1,0:T(8,128)(2,1)S(1)}, u32[]{:S(2)}, u32[]{:S(2)}) collective-permute-start(bf16[256,128]{1,0:T(8,128)(2,1)S(1)} %get-tuple-element.22.kv_ref), channel_id=1, source_target_pairs={{0,4},{4,0},{8,12},{12,8},{16,20},{20,16},{24,28},{28,24},{1,5},{5... | collective-permute-start | bytes 196616 | tf_op jit(solution)/shard_map/ppermute | solution.py:166
  5.5 0.0 collective-permute-done.3.refs_3_
  5.5 1.5 %collective-permute-start.5 = (bf16[256,128]{1,0:T(8,128)(2,1)S(1)}, bf16[256,128]{1,0:T(8,128)(2,1)S(1)}, u32[]{:S(2)}, u32[]{:S(2)}) collective-permute-start(bf16[256,128]{1,0:T(8,128)(2,1)S(1)} %collective-permute-done.3.refs_3_), channel_id=1, source_target_pairs={{0,1},{1,0},{2,3},{3,2},{4,5},{5,4},{6,7},{7,6},{8,9},{9,8},{10,11... | collective-permute-start | bytes 196616 | tf_op jit(solution)/shard_map/ppermute | solution.py:174
  7.0 0.0 collective-permute-done.2.refs_2_
  7.0 0.0 collective-permute-start.4
  7.0 2.6 %collective-permute-done.1.refs_1_ = bf16[256,128]{1,0:T(8,128)(2,1)S(1)} collective-permute-done((bf16[256,128]{1,0:T(8,128)(2,1)S(1)}, bf16[256,128]{1,0:T(8,128)(2,1)S(1)}, u32[]{:S(2)}, u32[]{:S(2)}) %collective-permute-start.1) | collective-permute-done | bytes 65568 | tf_op jit(solution)/shard_map/ppermute | solution.py:166
  9.6 0.5 %collective-permute-start.6 = (bf16[256,128]{1,0:T(8,128)(2,1)S(1)}, bf16[256,128]{1,0:T(8,128)(2,1)S(1)}, u32[]{:S(2)}, u32[]{:S(2)}) collective-permute-start(bf16[256,128]{1,0:T(8,128)(2,1)S(1)} %collective-permute-done.1.refs_1_), channel_id=1, source_target_pairs={{0,1},{1,0},{2,3},{3,2},{4,5},{5,4},{6,7},{7,6},{8,9},{9,8},{10,11... | collective-permute-start | bytes 196616 | tf_op jit(solution)/shard_map/ppermute | solution.py:174
  10.2 0.0 copy-done
  10.2 0.0 collective-permute-done.refs_0_
  10.2 0.6 %shard_map.56 = (f32[1024,128]{1,0:T(8,128)S(1)}, f32[1024,128]{1,0:T(8,128)S(1)}, f32[1024,128]{1,0:T(8,128)S(1)}) custom-call(s32[8,128]{1,0:T(8,128)S(1)} %get-tuple-element.21.reached_ref.tree_ref, bf16[1024,128]{1,0:T(8,128)(2,1)S(1)} %bitcast.6, bf16[256,128]{1,0:T(8,128)(2,1)S(1)} %get-tuple-element.22.kv_ref, ...), custom_call_target="tpu_custom_call" | custom-call | flops 130000000 | bytes 1000000 | tf_op jit(solution)/shard_map/pallas_call | solution.py:197
  10.8 0.0 collective-permute-done.5.refs_1_
  10.8 0.0 collective-permute-done.4.refs_0_
  10.8 0.2 shard_map.57
  11.1 2.8 %collective-permute-done.6.refs_0_ = bf16[256,128]{1,0:T(8,128)(2,1)S(1)} collective-permute-done((bf16[256,128]{1,0:T(8,128)(2,1)S(1)}, bf16[256,128]{1,0:T(8,128)(2,1)S(1)}, u32[]{:S(2)}, u32[]{:S(2)}) %collective-permute-start.6) | collective-permute-done | bytes 65568 | tf_op jit(solution)/shard_map/ppermute | solution.py:174
  13.9 0.0 slice-done
  13.9 0.0 slice-done.1
  13.9 1.3 %shard_map.58 = (bf16[128,1024]{1,0:T(8,128)(2,1)S(1)}, bf16[128,512]{1,0:T(8,128)(2,1)S(1)}, f32[128,512]{1,0:T(8,128)S(1)}, f32[1024,128]{1,0:T(8,128)S(1)}, f...) custom-call(s32[8,128]{1,0:T(8,128)S(1)} %get-tuple-element.21.reached, ...), custom_call_target="tpu_custom_call", output_to_operand_aliasing={{3}: (2, {}), {4}: (3, {}), {5}: (4, {})} | custom-call | flops 1000000000 | bytes 10000000 | tf_op jit(solution)/shard_map/pallas_call | solution.py:234
  15.2 0.1 collective-permute-start.7
  15.3 0.5 %shard_map.60 = (bf16[128,512]{1,0:T(8,128)(2,1)S(1)}, f32[128,512]{1,0:T(8,128)S(1)}) custom-call(bf16[128,1024]{1,0:T(8,128)(2,1)S(1)} %get-tuple-element.32.att_ref, bf16[1024,4096]{1,0:T(8,128)(2,1)S(1)} %bitcast.5), custom_call_target="tpu_custom_call" | custom-call | flops 540000000 | bytes 4000000 | tf_op jit(solution)/shard_map/pallas_call | solution.py:245
  15.8 0.6 %collective-permute-start.10 = (bf16[128,512]{1,0:T(8,128)(2,1)S(1)}, bf16[128,512]{1,0:T(8,128)(2,1)S(1)}, u32[]{:S(2)}, u32[]{:S(2)}) collective-permute-start(bf16[128,512]{1,0:T(8,128)(2,1)S(1)} %get-tuple-element.36), channel_id=1, source_target_pairs={{0,1},{1,0},{2,3},{3,2},{4,5},{5,4},{6,7},{7,6},{8,9},{9,8},{10,11... | collective-permute-start | bytes 393224 | tf_op jit(solution)/shard_map/ppermute | solution.py:166
  16.3 0.3 %collective-permute-done.7 = bf16[128,512]{1,0:T(8,128)(2,1)S(1)} collective-permute-done((bf16[128,512]{1,0:T(8,128)(2,1)S(1)}, bf16[128,512]{1,0:T(8,128)(2,1)S(1)}, u32[]{:S(2)}, u32[]{:S(2)}) %collective-permute-start.7) | collective-permute-done | bytes 131104 | tf_op jit(solution)/shard_map/ppermute | solution.py:166
  16.7 0.6 %collective-permute-start.9 = (bf16[128,512]{1,0:T(8,128)(2,1)S(1)}, bf16[128,512]{1,0:T(8,128)(2,1)S(1)}, u32[]{:S(2)}, u32[]{:S(2)}) collective-permute-start(bf16[128,512]{1,0:T(8,128)(2,1)S(1)} %add_convert_fusion.2), channel_id=1, source_target_pairs={{0,2},{1,3},{2,0},{3,1},{4,6},{5,7},{6,4},{7,5},{8,10},{9,11},{10,... | collective-permute-start | bytes 393224 | tf_op jit(solution)/shard_map/ppermute | solution.py:166
  17.2 0.7 %shard_map.59 = (bf16[128,1024]{1,0:T(8,128)(2,1)S(1)}, f32[128,1024]{1,0:T(8,128)S(1)}) custom-call(bf16[128,1024]{1,0:T(8,128)(2,1)S(1)} %get-tuple-element.32.att_ref, bf16[1024,4096]{1,0:T(8,128)(2,1)S(1)} %bitcast.5), custom_call_target="tpu_custom_call" | custom-call | flops 540000000 | bytes 4000000 | tf_op jit(solution)/shard_map/pallas_call | solution.py:245
  18.0 0.1 collective-permute-start.8
  18.1 0.0 collective-permute-done.10
  18.1 1.6 %collective-permute-start.11 = (bf16[128,512]{1,0:T(8,128)(2,1)S(1)}, bf16[128,512]{1,0:T(8,128)(2,1)S(1)}, u32[]{:S(2)}, u32[]{:S(2)}) collective-permute-start(bf16[128,512]{1,0:T(8,128)(2,1)S(1)} %add_convert_fusion.1), channel_id=1, source_target_pairs={{0,2},{1,3},{2,0},{3,1},{4,6},{5,7},{6,4},{7,5},{8,10},{9,11},{10,... | collective-permute-start | bytes 393224 | tf_op jit(solution)/shard_map/ppermute | solution.py:166
  19.7 3.4 %collective-permute-done.9 = bf16[128,512]{1,0:T(8,128)(2,1)S(1)} collective-permute-done((bf16[128,512]{1,0:T(8,128)(2,1)S(1)}, bf16[128,512]{1,0:T(8,128)(2,1)S(1)}, u32[]{:S(2)}, u32[]{:S(2)}) %collective-permute-start.9) | collective-permute-done | bytes 131104 | tf_op jit(solution)/shard_map/ppermute | solution.py:166
  23.1 2.0 %collective-permute-done.11 = bf16[128,512]{1,0:T(8,128)(2,1)S(1)} collective-permute-done((bf16[128,512]{1,0:T(8,128)(2,1)S(1)}, bf16[128,512]{1,0:T(8,128)(2,1)S(1)}, u32[]{:S(2)}, u32[]{:S(2)}) %collective-permute-start.11) | collective-permute-done | bytes 131104 | tf_op jit(solution)/shard_map/ppermute | solution.py:166
  25.1 0.0 collective-permute-done.8
  25.1 0.8 %add_convert_fusion = bf16[128,1024]{1,0:T(8,128)(2,1)} fusion(f32[128,1024]{1,0:T(8,128)S(1)} %get-tuple-element.33, bf16[128,1024]{1,0:T(8,128)(2,1)S(1)} %collective-permute-done.8, bf16[128,512]{1,0:T(8,128)(2,1)S(1)} %collective-permute-done.11, bf16[128,512]{1,0:T(8,128)(2,1)S(1)} %collective-permute-done.9), kind=kLoop, calls=%fused_computation | loop fusion | flops 1048576 | bytes 1310720 | tf_op jit(solution)/shard_map/convert_element_type | solution.py:273
  (4 shorter events, 0.1 us)
Async XLA Ops:
  0.0 13.9 %slice-start = ((s8[8388608]{0:T(1024)(128)(4,1)}), s8[4194304]{0:T(1024)(128)(4,1)S(1)}, s32[]{:S(2)}) async-start(s8[8388608]{0:T(1024)(128)(4,1)} %bitcast.4), calls=%async_computation | async-start | bytes 8388608
  0.0 10.2 %copy-start = (bf16[128,8,128]{2,1,0:T(8,128)(2,1)S(1)}, bf16[128,8,128]{2,1,0:T(8,128)(2,1)}, u32[]{:S(2)}) copy-start(bf16[128,8,128]{2,1,0:T(8,128)(2,1)} %param.5) | copy-start | bytes 786436
  0.0 13.9 %slice-start.1 = ((s8[8388608]{0:T(1024)(128)(4,1)}), s8[4194304]{0:T(1024)(128)(4,1)S(1)}, s32[]{:S(2)}) async-start(s8[8388608]{0:T(1024)(128)(4,1)} %bitcast.4), calls=%async_computation.1 | async-start | bytes 8388608
  1.0 4.5 %collective-permute-start.3 = (bf16[256,128]{1,0:T(8,128)(2,1)S(1)}, bf16[256,128]{1,0:T(8,128)(2,1)S(1)}, u32[]{:S(2)}, u32[]{:S(2)}) collective-permute-start(bf16[256,128]{1,0:T(8,128)(2,1)S(1)} %get-tuple-element.22.kv_ref), channel_id=1, source_target_pairs={{0,24},{4,28},{8,16},{12,20},{16,8},{20,12},{24,0},{28,4},{1,25},{... | collective-permute-start | bytes 196616 | tf_op jit(solution)/shard_map/ppermute | solution.py:166
  1.5 5.5 %collective-permute-start.2 = (bf16[256,128]{1,0:T(8,128)(2,1)S(1)}, bf16[256,128]{1,0:T(8,128)(2,1)S(1)}, u32[]{:S(2)}, u32[]{:S(2)}) collective-permute-start(bf16[256,128]{1,0:T(8,128)(2,1)S(1)} %get-tuple-element.22.kv_ref), channel_id=1, source_target_pairs={{0,8},{4,12},{8,0},{12,4},{16,24},{20,28},{24,16},{28,20},{1,9},{5... | collective-permute-start | bytes 196616 | tf_op jit(solution)/shard_map/ppermute | solution.py:166
  2.8 6.8 %collective-permute-start.1 = (bf16[256,128]{1,0:T(8,128)(2,1)S(1)}, bf16[256,128]{1,0:T(8,128)(2,1)S(1)}, u32[]{:S(2)}, u32[]{:S(2)}) collective-permute-start(bf16[256,128]{1,0:T(8,128)(2,1)S(1)} %get-tuple-element.22.kv_ref), channel_id=1, source_target_pairs={{0,16},{4,20},{8,24},{12,28},{16,0},{20,4},{24,8},{28,12},{1,17},{... | collective-permute-start | bytes 196616 | tf_op jit(solution)/shard_map/ppermute | solution.py:166
  5.0 5.2 %collective-permute-start = (bf16[256,128]{1,0:T(8,128)(2,1)S(1)}, bf16[256,128]{1,0:T(8,128)(2,1)S(1)}, u32[]{:S(2)}, u32[]{:S(2)}) collective-permute-start(bf16[256,128]{1,0:T(8,128)(2,1)S(1)} %get-tuple-element.22.kv_ref), channel_id=1, source_target_pairs={{0,4},{4,0},{8,12},{12,8},{16,20},{20,16},{24,28},{28,24},{1,5},{5... | collective-permute-start | bytes 196616 | tf_op jit(solution)/shard_map/ppermute | solution.py:166
  5.5 5.3 %collective-permute-start.5 = (bf16[256,128]{1,0:T(8,128)(2,1)S(1)}, bf16[256,128]{1,0:T(8,128)(2,1)S(1)}, u32[]{:S(2)}, u32[]{:S(2)}) collective-permute-start(bf16[256,128]{1,0:T(8,128)(2,1)S(1)} %collective-permute-done.3.refs_3_), channel_id=1, source_target_pairs={{0,1},{1,0},{2,3},{3,2},{4,5},{5,4},{6,7},{7,6},{8,9},{9,8},{10,11... | collective-permute-start | bytes 196616 | tf_op jit(solution)/shard_map/ppermute | solution.py:174
  7.0 3.8 %collective-permute-start.4 = (bf16[256,128]{1,0:T(8,128)(2,1)S(1)}, bf16[256,128]{1,0:T(8,128)(2,1)S(1)}, u32[]{:S(2)}, u32[]{:S(2)}) collective-permute-start(bf16[256,128]{1,0:T(8,128)(2,1)S(1)} %collective-permute-done.2.refs_2_), channel_id=1, source_target_pairs={{0,1},{1,0},{2,3},{3,2},{4,5},{5,4},{6,7},{7,6},{8,12},{9,13},{10,... | collective-permute-start | bytes 196616 | tf_op jit(solution)/shard_map/ppermute | solution.py:174
  9.6 4.3 %collective-permute-start.6 = (bf16[256,128]{1,0:T(8,128)(2,1)S(1)}, bf16[256,128]{1,0:T(8,128)(2,1)S(1)}, u32[]{:S(2)}, u32[]{:S(2)}) collective-permute-start(bf16[256,128]{1,0:T(8,128)(2,1)S(1)} %collective-permute-done.1.refs_1_), channel_id=1, source_target_pairs={{0,1},{1,0},{2,3},{3,2},{4,5},{5,4},{6,7},{7,6},{8,9},{9,8},{10,11... | collective-permute-start | bytes 196616 | tf_op jit(solution)/shard_map/ppermute | solution.py:174
  15.2 1.4 %collective-permute-start.7 = (bf16[128,512]{1,0:T(8,128)(2,1)S(1)}, bf16[128,512]{1,0:T(8,128)(2,1)S(1)}, u32[]{:S(2)}, u32[]{:S(2)}) collective-permute-start(bf16[128,512]{1,0:T(8,128)(2,1)S(1)} %get-tuple-element.31), channel_id=1, source_target_pairs={{0,1},{1,0},{2,3},{3,2},{4,5},{5,4},{6,7},{7,6},{8,9},{9,8},{10,11... | collective-permute-start | bytes 393224 | tf_op jit(solution)/shard_map/ppermute | solution.py:166
  15.8 2.3 %collective-permute-start.10 = (bf16[128,512]{1,0:T(8,128)(2,1)S(1)}, bf16[128,512]{1,0:T(8,128)(2,1)S(1)}, u32[]{:S(2)}, u32[]{:S(2)}) collective-permute-start(bf16[128,512]{1,0:T(8,128)(2,1)S(1)} %get-tuple-element.36), channel_id=1, source_target_pairs={{0,1},{1,0},{2,3},{3,2},{4,5},{5,4},{6,7},{7,6},{8,9},{9,8},{10,11... | collective-permute-start | bytes 393224 | tf_op jit(solution)/shard_map/ppermute | solution.py:166
  16.7 6.4 %collective-permute-start.9 = (bf16[128,512]{1,0:T(8,128)(2,1)S(1)}, bf16[128,512]{1,0:T(8,128)(2,1)S(1)}, u32[]{:S(2)}, u32[]{:S(2)}) collective-permute-start(bf16[128,512]{1,0:T(8,128)(2,1)S(1)} %add_convert_fusion.2), channel_id=1, source_target_pairs={{0,2},{1,3},{2,0},{3,1},{4,6},{5,7},{6,4},{7,5},{8,10},{9,11},{10,... | collective-permute-start | bytes 393224 | tf_op jit(solution)/shard_map/ppermute | solution.py:166
  18.0 7.1 %collective-permute-start.8 = (bf16[128,1024]{1,0:T(8,128)(2,1)S(1)}, bf16[128,1024]{1,0:T(8,128)(2,1)S(1)}, u32[]{:S(2)}, u32[]{:S(2)}) collective-permute-start(bf16[128,1024]{1,0:T(8,128)(2,1)S(1)} %get-tuple-element.34), channel_id=1, source_target_pairs={{0,1},{1,0},{2,3},{3,2},{4,5},{5,4},{6,7},{7,6},{8,9},{9,8},{10,11... | collective-permute-start | bytes 786440 | tf_op jit(solution)/shard_map/ppermute | solution.py:166
  18.1 7.0 %collective-permute-start.11 = (bf16[128,512]{1,0:T(8,128)(2,1)S(1)}, bf16[128,512]{1,0:T(8,128)(2,1)S(1)}, u32[]{:S(2)}, u32[]{:S(2)}) collective-permute-start(bf16[128,512]{1,0:T(8,128)(2,1)S(1)} %add_convert_fusion.1), channel_id=1, source_target_pairs={{0,2},{1,3},{2,0},{3,1},{4,6},{5,7},{6,4},{7,5},{8,10},{9,11},{10,... | collective-permute-start | bytes 393224 | tf_op jit(solution)/shard_map/ppermute | solution.py:166

commit v16 on v12

--- a/solution.py
+++ b/solution.py
@@ -182,13 +182,10 @@
         compiler_params=params,
         cost_estimate=pl.CostEstimate(flops=8_000_000_000, bytes_accessed=130_000, transcendentals=0),
     )(in_hbm(key_heads[:, 0, :]), in_hbm(value_heads[:, 0, :]), in_hbm(parents))
+    early, early_xors = [], ()
     if ctx_size == DIRECT_SIZE:
-        columns = [swap(kv, "ctx", ctx_size, other) for other in (4, 2, 6)]
+        columns = [swap(kv, "ctx", ctx_size, other) for other in (2, 4, 6)]
         beside = swap(kv, "ctx", ctx_size, 1)
-        pairs = [forward(x, other) for x, other in zip(columns, (4, 2, 6))]
-        early, early_xors = [beside, *columns], (1, 4, 2, 6)
-    else:
-        early, early_xors = [], ()
     q = jnp.transpose(query_heads, (1, 0, 2)).reshape(rows, head_dim)
 
     m, l, acc = pl.pallas_call(
@@ -204,6 +201,9 @@
         cost_estimate=pl.CostEstimate(flops=130_000_000, bytes_accessed=1_000_000, transcendentals=260_000),
     )(reached, q, kv, *early)
 
+    if ctx_size == DIRECT_SIZE:
+        columns[2], m = lax.optimization_barrier((columns[2], m))
+        pairs = [forward(x, other) for x, other in zip(columns, (2, 4, 6))]
     state = (m, l, acc)
     state_shapes = tuple(jax.ShapeDtypeStruct(x.shape, x.dtype) for x in state)
     if ctx_size == DIRECT_SIZE:
@@ -218,8 +218,9 @@
                 cost_estimate=pl.CostEstimate(flops=270_000_000, bytes_accessed=1_000_000, transcendentals=500_000),
             )(reached, q, *state, *arrived)
 
-        state = absorbed(state, (3, 7), pairs[1:])
-        xors, pieces, tree, tree_spec = (5,), pairs[:1], reached, vmem
+        state = absorbed(state, (1, 2, 4, 6), [beside, *columns])
+        state = absorbed(state, (5, 7), pairs[1:])
+        xors, pieces, tree, tree_spec = (3,), pairs[:1], reached, vmem
     else:
         xors, pieces, tree, tree_spec = (), [lax.all_gather(kv, "ctx", axis=0, tiled=True)], parents, smem
 

time: 26.6 us -> 27.8 us (1.045)
  the two profiles are of different devices: /device:TPU:24 before, /device:TPU:28 now
where the time goes in v16:
time: 27.8 us; the launch traced here: 27.6 us
  starting transfers between devices  10.3 us (37%)
  waiting for transfers between devices  9.91 us (36%)
  Pallas kernels  6.3 us (23%)
  other arithmetic  0.88 us (3%)
    ppermute x9, waiting for transfers between devices, swap(): return lax.ppermute(x, axis, [(i, i ^ other) for i in range(size)])  8.59 us
    ppermute x9, starting transfers between devices, swap(): return lax.ppermute(x, axis, [(i, i ^ other) for i in range(size)])  7.81 us
    ppermute x3, starting transfers between devices, forward(): return lax.ppermute(x, ('ctx', 'tp'), route)  2.53 us
    pallas_call x2, Pallas kernels, absorbed(): pl.pallas_call(functools.partial(others_kernel, xors), out_shape=state_sh...  2.42 us
    ppermute x3, waiting for transfers between devices, forward(): return lax.ppermute(x, ('ctx', 'tp'), route)  1.32 us
    pallas_call x1, Pallas kernels, shards(): pl.pallas_call(functools.partial(last_kernel, xors), out_shape=(jax.Shape...  1.21 us
    pallas_call x2, Pallas kernels, projected(): pl.pallas_call(functools.partial(project_pair, flip, part), out_shape=sha...  1.18 us
    pallas_call x1, Pallas kernels, shards(): pl.pallas_call(functools.partial(pack_kernel, ctx_size == DIRECT_SIZE), o...  0.96 us
  transfers between devices with their start and end apart: 12, of which 8 were waited for; matrix products, arithmetic and copies ran while one was open for 0% of the time, Pallas kernels for 15%

profile of v16, /device:TPU:28, one launch (start us, length us, event | category | flops | bytes accessed | tf_op | source)
XLA Modules:
  0.0 27.6 jit_solution(12039372269170667491)
XLA Ops:
  0.0 0.0 slice-start
  0.0 0.0 copy-start
  0.0 0.0 slice-start.1
  0.0 1.0 %shard_map.55 = (bf16[256,128]{1,0:T(8,128)(2,1)S(1)}, s32[8,128]{1,0:T(8,128)S(1)}) custom-call(bf16[128,128]{1,0:T(8,128)(2,1)} %bitcast.11, bf16[128,128]{1,0:T(8,128)(2,1)} %bitcast.12, s32[8]{0:T(128)} %parents_hbm.1), custom_call_target="tpu_custom_call" | custom-call | flops 8000000000 | bytes 130000 | tf_op jit(solution)/shard_map/pallas_call | solution.py:173
  1.0 0.3 %collective-permute-start = (bf16[256,128]{1,0:T(8,128)(2,1)S(1)}, bf16[256,128]{1,0:T(8,128)(2,1)S(1)}, u32[]{:S(2)}, u32[]{:S(2)}) collective-permute-start(bf16[256,128]{1,0:T(8,128)(2,1)S(1)} %get-tuple-element.27.kv_ref), channel_id=1, source_target_pairs={{0,24},{4,28},{8,16},{12,20},{16,8},{20,12},{24,0},{28,4},{1,25},{... | collective-permute-start | bytes 196616 | tf_op jit(solution)/shard_map/ppermute | solution.py:163
  1.3 1.7 %collective-permute-start.3 = (bf16[256,128]{1,0:T(8,128)(2,1)S(1)}, bf16[256,128]{1,0:T(8,128)(2,1)S(1)}, u32[]{:S(2)}, u32[]{:S(2)}) collective-permute-start(bf16[256,128]{1,0:T(8,128)(2,1)S(1)} %get-tuple-element.27.kv_ref), channel_id=1, source_target_pairs={{0,16},{4,20},{8,24},{12,28},{16,0},{20,4},{24,8},{28,12},{1,17},{... | collective-permute-start | bytes 196616 | tf_op jit(solution)/shard_map/ppermute | solution.py:163
  3.0 2.5 %collective-permute-start.2 = (bf16[256,128]{1,0:T(8,128)(2,1)S(1)}, bf16[256,128]{1,0:T(8,128)(2,1)S(1)}, u32[]{:S(2)}, u32[]{:S(2)}) collective-permute-start(bf16[256,128]{1,0:T(8,128)(2,1)S(1)} %get-tuple-element.27.kv_ref), channel_id=1, source_target_pairs={{0,8},{4,12},{8,0},{12,4},{16,24},{20,28},{24,16},{28,20},{1,9},{5... | collective-permute-start | bytes 196616 | tf_op jit(solution)/shard_map/ppermute | solution.py:163
  5.4 0.5 %collective-permute-start.1 = (bf16[256,128]{1,0:T(8,128)(2,1)S(1)}, bf16[256,128]{1,0:T(8,128)(2,1)S(1)}, u32[]{:S(2)}, u32[]{:S(2)}) collective-permute-start(bf16[256,128]{1,0:T(8,128)(2,1)S(1)} %get-tuple-element.27.kv_ref), channel_id=1, source_target_pairs={{0,4},{4,0},{8,12},{12,8},{16,20},{20,16},{24,28},{28,24},{1,5},{5... | collective-permute-start | bytes 196616 | tf_op jit(solution)/shard_map/ppermute | solution.py:163
  5.9 0.0 copy-done
  6.0 0.5 %shard_map.56 = (f32[1,1024]{1,0:T(1,128)S(1)}, f32[1,1024]{1,0:T(1,128)S(1)}, f32[128,1024]{1,0:T(8,128)S(1)}) custom-call(s32[8,128]{1,0:T(8,128)S(1)} %get-tuple-element.26.reached_ref.tree_ref, bf16[1024,128]{1,0:T(8,128)(2,1)S(1)} %bitcast.6, bf16[256,128]{1,0:T(8,128)(2,1)S(1)} %get-tuple-element.27.kv_ref), custom_call_target="tpu_custom_call" | custom-call | flops 130000000 | bytes 1000000 | tf_op jit(solution)/shard_map/pallas_call | solution.py:191
  6.5 1.3 %collective-permute-done.refs_3_ = bf16[256,128]{1,0:T(8,128)(2,1)S(1)} collective-permute-done((bf16[256,128]{1,0:T(8,128)(2,1)S(1)}, bf16[256,128]{1,0:T(8,128)(2,1)S(1)}, u32[]{:S(2)}, u32[]{:S(2)}) %collective-permute-start) | collective-permute-done | bytes 65568 | tf_op jit(solution)/shard_map/ppermute | solution.py:163
  7.8 1.5 %collective-permute-done.3.refs_2_ = bf16[256,128]{1,0:T(8,128)(2,1)S(1)} collective-permute-done((bf16[256,128]{1,0:T(8,128)(2,1)S(1)}, bf16[256,128]{1,0:T(8,128)(2,1)S(1)}, u32[]{:S(2)}, u32[]{:S(2)}) %collective-permute-start.3) | collective-permute-done | bytes 65568 | tf_op jit(solution)/shard_map/ppermute | solution.py:163
  9.4 0.5 %collective-permute-start.4 = (bf16[256,128]{1,0:T(8,128)(2,1)S(1)}, bf16[256,128]{1,0:T(8,128)(2,1)S(1)}, u32[]{:S(2)}, u32[]{:S(2)}) collective-permute-start(bf16[256,128]{1,0:T(8,128)(2,1)S(1)} %collective-permute-done.3.refs_2_), channel_id=1, source_target_pairs={{0,1},{1,0},{2,3},{3,2},{4,5},{5,4},{6,7},{7,6},{8,9},{9,8},{10,11... | collective-permute-start | bytes 196616 | tf_op jit(solution)/shard_map/ppermute | solution.py:171
  9.9 1.5 %collective-permute-start.5 = (bf16[256,128]{1,0:T(8,128)(2,1)S(1)}, bf16[256,128]{1,0:T(8,128)(2,1)S(1)}, u32[]{:S(2)}, u32[]{:S(2)}) collective-permute-start(bf16[256,128]{1,0:T(8,128)(2,1)S(1)} %collective-permute-done.refs_3_), channel_id=1, source_target_pairs={{0,1},{1,0},{2,3},{3,2},{4,5},{5,4},{6,7},{7,6},{8,9},{9,8},{10,11... | collective-permute-start | bytes 196616 | tf_op jit(solution)/shard_map/ppermute | solution.py:171
  11.4 0.0 collective-permute-done.2.refs_1_
  11.4 0.5 %collective-permute-start.6 = (bf16[256,128]{1,0:T(8,128)(2,1)S(1)}, bf16[256,128]{1,0:T(8,128)(2,1)S(1)}, u32[]{:S(2)}, u32[]{:S(2)}) collective-permute-start(bf16[256,128]{1,0:T(8,128)(2,1)S(1)} %collective-permute-done.2.refs_1_), channel_id=1, source_target_pairs={{0,1},{1,0},{2,3},{3,2},{4,5},{5,4},{6,7},{7,6},{8,12},{9,13},{10,... | collective-permute-start | bytes 196616 | tf_op jit(solution)/shard_map/ppermute | solution.py:171
  11.9 0.0 collective-permute-done.1.refs_0_
  11.9 1.2 %shard_map.57 = (f32[1,1024]{1,0:T(1,128)S(1)}, f32[1,1024]{1,0:T(1,128)S(1)}, f32[128,1024]{1,0:T(8,128)S(1)}) custom-call(s32[8,128]{1,0:T(8,128)S(1)} %get-tuple-element.26.reached_ref.tree_ref, bf16[1024,128]{1,0:T(8,128)(2,1)S(1)} %bitcast.7, f32[1,1024]{1,0:T(1,128)S(1)} %get-tuple-element.29.m_in, ...), custom_call_target="tpu_custom_call", output_to_operand_aliasing={{0}: (2, {}), {1}: (3, {}), {2}: (4, {})} | custom-call | flops 270000000 | bytes 1000000 | tf_op jit(solution)/shard_map/pallas_call | solution.py:211
  13.1 0.5 %collective-permute-done.4.refs_0_ = bf16[256,128]{1,0:T(8,128)(2,1)S(1)} collective-permute-done((bf16[256,128]{1,0:T(8,128)(2,1)S(1)}, bf16[256,128]{1,0:T(8,128)(2,1)S(1)}, u32[]{:S(2)}, u32[]{:S(2)}) %collective-permute-start.4) | collective-permute-done | bytes 65568 | tf_op jit(solution)/shard_map/ppermute | solution.py:171
  13.6 0.7 %collective-permute-done.5.refs_1_ = bf16[256,128]{1,0:T(8,128)(2,1)S(1)} collective-permute-done((bf16[256,128]{1,0:T(8,128)(2,1)S(1)}, bf16[256,128]{1,0:T(8,128)(2,1)S(1)}, u32[]{:S(2)}, u32[]{:S(2)}) %collective-permute-start.5) | collective-permute-done | bytes 65568 | tf_op jit(solution)/shard_map/ppermute | solution.py:171
  14.3 1.2 %shard_map.58 = (f32[1,1024]{1,0:T(1,128)S(1)}, f32[1,1024]{1,0:T(1,128)S(1)}, f32[128,1024]{1,0:T(8,128)S(1)}) custom-call(s32[8,128]{1,0:T(8,128)S(1)} %get-tuple-element.26.reached_ref.tree_ref, bf16[1024,128]{1,0:T(8,128)(2,1)S(1)} %bitcast.8, f32[1,1024]{1,0:T(1,128)S(1)} %get-tuple-element.33.m_in, ...), custom_call_target="tpu_custom_call", output_to_operand_aliasing={{0}: (2, {}), {1}: (3, {}), {2}: (4, {})} | custom-call | flops 270000000 | bytes 1000000 | tf_op jit(solution)/shard_map/pallas_call | solution.py:211
  15.5 0.1 collective-permute-done.6.refs_0_
  15.7 0.0 slice-done
  15.7 0.0 slice-done.1
  15.7 1.2 %shard_map.59 = (bf16[128,1024]{1,0:T(8,128)(2,1)S(1)}, bf16[128,512]{1,0:T(8,128)(2,1)S(1)}, f32[128,512]{1,0:T(8,128)S(1)}, f32[1,1024]{1,0:T(1,128)S(1)}, f32...) custom-call(s32[8,128]{1,0:T(8,128)S(1)} %get-tuple-element.26.reached_ref, ...), custom_call_target="tpu_custom_call", output_to_operand_aliasing={{3}: (2, {}), {4}: (3, {}), {5}: (4, {})} | custom-call | flops 1000000000 | bytes 10000000 | tf_op jit(solution)/shard_map/pallas_call | solution.py:232
  16.9 0.1 collective-permute-start.7
  17.0 0.5 %shard_map.61 = (bf16[128,512]{1,0:T(8,128)(2,1)S(1)}, f32[128,512]{1,0:T(8,128)S(1)}) custom-call(bf16[128,1024]{1,0:T(8,128)(2,1)S(1)} %get-tuple-element.42.att_ref, bf16[1024,4096]{1,0:T(8,128)(2,1)S(1)} %bitcast.5), custom_call_target="tpu_custom_call" | custom-call | flops 540000000 | bytes 4000000 | tf_op jit(solution)/shard_map/pallas_call | solution.py:243
  17.4 0.6 %collective-permute-start.10 = (bf16[128,512]{1,0:T(8,128)(2,1)S(1)}, bf16[128,512]{1,0:T(8,128)(2,1)S(1)}, u32[]{:S(2)}, u32[]{:S(2)}) collective-permute-start(bf16[128,512]{1,0:T(8,128)(2,1)S(1)} %get-tuple-element.46), channel_id=1, source_target_pairs={{0,1},{1,0},{2,3},{3,2},{4,5},{5,4},{6,7},{7,6},{8,9},{9,8},{10,11... | collective-permute-start | bytes 393224 | tf_op jit(solution)/shard_map/ppermute | solution.py:163
  18.0 0.3 %collective-permute-done.7 = bf16[128,512]{1,0:T(8,128)(2,1)S(1)} collective-permute-done((bf16[128,512]{1,0:T(8,128)(2,1)S(1)}, bf16[128,512]{1,0:T(8,128)(2,1)S(1)}, u32[]{:S(2)}, u32[]{:S(2)}) %collective-permute-start.7) | collective-permute-done | bytes 131104 | tf_op jit(solution)/shard_map/ppermute | solution.py:163
  18.3 1.6 %collective-permute-start.9 = (bf16[128,512]{1,0:T(8,128)(2,1)S(1)}, bf16[128,512]{1,0:T(8,128)(2,1)S(1)}, u32[]{:S(2)}, u32[]{:S(2)}) collective-permute-start(bf16[128,512]{1,0:T(8,128)(2,1)S(1)} %add_convert_fusion.2), channel_id=1, source_target_pairs={{0,2},{1,3},{2,0},{3,1},{4,6},{5,7},{6,4},{7,5},{8,10},{9,11},{10,... | collective-permute-start | bytes 393224 | tf_op jit(solution)/shard_map/ppermute | solution.py:163
  19.9 0.7 %shard_map.60 = (bf16[128,1024]{1,0:T(8,128)(2,1)S(1)}, f32[128,1024]{1,0:T(8,128)S(1)}) custom-call(bf16[128,1024]{1,0:T(8,128)(2,1)S(1)} %get-tuple-element.42.att_ref, bf16[1024,4096]{1,0:T(8,128)(2,1)S(1)} %bitcast.5), custom_call_target="tpu_custom_call" | custom-call | flops 540000000 | bytes 4000000 | tf_op jit(solution)/shard_map/pallas_call | solution.py:243
  20.6 0.1 collective-permute-start.8
  20.7 0.0 collective-permute-done.10
  20.8 0.6 %collective-permute-start.11 = (bf16[128,512]{1,0:T(8,128)(2,1)S(1)}, bf16[128,512]{1,0:T(8,128)(2,1)S(1)}, u32[]{:S(2)}, u32[]{:S(2)}) collective-permute-start(bf16[128,512]{1,0:T(8,128)(2,1)S(1)} %add_convert_fusion.1), channel_id=1, source_target_pairs={{0,2},{1,3},{2,0},{3,1},{4,6},{5,7},{6,4},{7,5},{8,10},{9,11},{10,... | collective-permute-start | bytes 393224 | tf_op jit(solution)/shard_map/ppermute | solution.py:163
  21.4 2.6 %collective-permute-done.9 = bf16[128,512]{1,0:T(8,128)(2,1)S(1)} collective-permute-done((bf16[128,512]{1,0:T(8,128)(2,1)S(1)}, bf16[128,512]{1,0:T(8,128)(2,1)S(1)}, u32[]{:S(2)}, u32[]{:S(2)}) %collective-permute-start.9) | collective-permute-done | bytes 131104 | tf_op jit(solution)/shard_map/ppermute | solution.py:163
  24.0 2.8 %collective-permute-done.11 = bf16[128,512]{1,0:T(8,128)(2,1)S(1)} collective-permute-done((bf16[128,512]{1,0:T(8,128)(2,1)S(1)}, bf16[128,512]{1,0:T(8,128)(2,1)S(1)}, u32[]{:S(2)}, u32[]{:S(2)}) %collective-permute-start.11) | collective-permute-done | bytes 131104 | tf_op jit(solution)/shard_map/ppermute | solution.py:163
  26.8 0.0 collective-permute-done.8
  26.8 0.8 %add_convert_fusion = bf16[128,1024]{1,0:T(8,128)(2,1)} fusion(f32[128,1024]{1,0:T(8,128)S(1)} %get-tuple-element.43, bf16[128,1024]{1,0:T(8,128)(2,1)S(1)} %collective-permute-done.8, bf16[128,512]{1,0:T(8,128)(2,1)S(1)} %collective-permute-done.11, bf16[128,512]{1,0:T(8,128)(2,1)S(1)} %collective-permute-done.9), kind=kLoop, calls=%fused_computation | loop fusion | flops 1048576 | bytes 1310720 | tf_op jit(solution)/shard_map/convert_element_type | solution.py:271
  (4 shorter events, 0.1 us)
Async XLA Ops:
  0.0 15.7 %slice-start = ((s8[8388608]{0:T(1024)(128)(4,1)}), s8[4194304]{0:T(1024)(128)(4,1)S(1)}, s32[]{:S(2)}) async-start(s8[8388608]{0:T(1024)(128)(4,1)} %bitcast.4), calls=%async_computation | async-start | bytes 8388608
  0.0 5.9 %copy-start = (bf16[128,8,128]{2,1,0:T(8,128)(2,1)S(1)}, bf16[128,8,128]{2,1,0:T(8,128)(2,1)}, u32[]{:S(2)}) copy-start(bf16[128,8,128]{2,1,0:T(8,128)(2,1)} %param.5) | copy-start | bytes 786436
  0.0 15.7 %slice-start.1 = ((s8[8388608]{0:T(1024)(128)(4,1)}), s8[4194304]{0:T(1024)(128)(4,1)S(1)}, s32[]{:S(2)}) async-start(s8[8388608]{0:T(1024)(128)(4,1)} %bitcast.4), calls=%async_computation.1 | async-start | bytes 8388608
  1.0 6.8 %collective-permute-start = (bf16[256,128]{1,0:T(8,128)(2,1)S(1)}, bf16[256,128]{1,0:T(8,128)(2,1)S(1)}, u32[]{:S(2)}, u32[]{:S(2)}) collective-permute-start(bf16[256,128]{1,0:T(8,128)(2,1)S(1)} %get-tuple-element.27.kv_ref), channel_id=1, source_target_pairs={{0,24},{4,28},{8,16},{12,20},{16,8},{20,12},{24,0},{28,4},{1,25},{... | collective-permute-start | bytes 196616 | tf_op jit(solution)/shard_map/ppermute | solution.py:163
  1.3 8.1 %collective-permute-start.3 = (bf16[256,128]{1,0:T(8,128)(2,1)S(1)}, bf16[256,128]{1,0:T(8,128)(2,1)S(1)}, u32[]{:S(2)}, u32[]{:S(2)}) collective-permute-start(bf16[256,128]{1,0:T(8,128)(2,1)S(1)} %get-tuple-element.27.kv_ref), channel_id=1, source_target_pairs={{0,16},{4,20},{8,24},{12,28},{16,0},{20,4},{24,8},{28,12},{1,17},{... | collective-permute-start | bytes 196616 | tf_op jit(solution)/shard_map/ppermute | solution.py:163
  3.0 8.4 %collective-permute-start.2 = (bf16[256,128]{1,0:T(8,128)(2,1)S(1)}, bf16[256,128]{1,0:T(8,128)(2,1)S(1)}, u32[]{:S(2)}, u32[]{:S(2)}) collective-permute-start(bf16[256,128]{1,0:T(8,128)(2,1)S(1)} %get-tuple-element.27.kv_ref), channel_id=1, source_target_pairs={{0,8},{4,12},{8,0},{12,4},{16,24},{20,28},{24,16},{28,20},{1,9},{5... | collective-permute-start | bytes 196616 | tf_op jit(solution)/shard_map/ppermute | solution.py:163
  5.4 6.5 %collective-permute-start.1 = (bf16[256,128]{1,0:T(8,128)(2,1)S(1)}, bf16[256,128]{1,0:T(8,128)(2,1)S(1)}, u32[]{:S(2)}, u32[]{:S(2)}) collective-permute-start(bf16[256,128]{1,0:T(8,128)(2,1)S(1)} %get-tuple-element.27.kv_ref), channel_id=1, source_target_pairs={{0,4},{4,0},{8,12},{12,8},{16,20},{20,16},{24,28},{28,24},{1,5},{5... | collective-permute-start | bytes 196616 | tf_op jit(solution)/shard_map/ppermute | solution.py:163
  9.4 4.3 %collective-permute-start.4 = (bf16[256,128]{1,0:T(8,128)(2,1)S(1)}, bf16[256,128]{1,0:T(8,128)(2,1)S(1)}, u32[]{:S(2)}, u32[]{:S(2)}) collective-permute-start(bf16[256,128]{1,0:T(8,128)(2,1)S(1)} %collective-permute-done.3.refs_2_), channel_id=1, source_target_pairs={{0,1},{1,0},{2,3},{3,2},{4,5},{5,4},{6,7},{7,6},{8,9},{9,8},{10,11... | collective-permute-start | bytes 196616 | tf_op jit(solution)/shard_map/ppermute | solution.py:171
  9.9 4.5 %collective-permute-start.5 = (bf16[256,128]{1,0:T(8,128)(2,1)S(1)}, bf16[256,128]{1,0:T(8,128)(2,1)S(1)}, u32[]{:S(2)}, u32[]{:S(2)}) collective-permute-start(bf16[256,128]{1,0:T(8,128)(2,1)S(1)} %collective-permute-done.refs_3_), channel_id=1, source_target_pairs={{0,1},{1,0},{2,3},{3,2},{4,5},{5,4},{6,7},{7,6},{8,9},{9,8},{10,11... | collective-permute-start | bytes 196616 | tf_op jit(solution)/shard_map/ppermute | solution.py:171
  11.4 4.3 %collective-permute-start.6 = (bf16[256,128]{1,0:T(8,128)(2,1)S(1)}, bf16[256,128]{1,0:T(8,128)(2,1)S(1)}, u32[]{:S(2)}, u32[]{:S(2)}) collective-permute-start(bf16[256,128]{1,0:T(8,128)(2,1)S(1)} %collective-permute-done.2.refs_1_), channel_id=1, source_target_pairs={{0,1},{1,0},{2,3},{3,2},{4,5},{5,4},{6,7},{7,6},{8,12},{9,13},{10,... | collective-permute-start | bytes 196616 | tf_op jit(solution)/shard_map/ppermute | solution.py:171
  16.9 1.4 %collective-permute-start.7 = (bf16[128,512]{1,0:T(8,128)(2,1)S(1)}, bf16[128,512]{1,0:T(8,128)(2,1)S(1)}, u32[]{:S(2)}, u32[]{:S(2)}) collective-permute-start(bf16[128,512]{1,0:T(8,128)(2,1)S(1)} %get-tuple-element.41), channel_id=1, source_target_pairs={{0,1},{1,0},{2,3},{3,2},{4,5},{5,4},{6,7},{7,6},{8,9},{9,8},{10,11... | collective-permute-start | bytes 393224 | tf_op jit(solution)/shard_map/ppermute | solution.py:163
  17.4 3.3 %collective-permute-start.10 = (bf16[128,512]{1,0:T(8,128)(2,1)S(1)}, bf16[128,512]{1,0:T(8,128)(2,1)S(1)}, u32[]{:S(2)}, u32[]{:S(2)}) collective-permute-start(bf16[128,512]{1,0:T(8,128)(2,1)S(1)} %get-tuple-element.46), channel_id=1, source_target_pairs={{0,1},{1,0},{2,3},{3,2},{4,5},{5,4},{6,7},{7,6},{8,9},{9,8},{10,11... | collective-permute-start | bytes 393224 | tf_op jit(solution)/shard_map/ppermute | solution.py:163
  18.3 5.6 %collective-permute-start.9 = (bf16[128,512]{1,0:T(8,128)(2,1)S(1)}, bf16[128,512]{1,0:T(8,128)(2,1)S(1)}, u32[]{:S(2)}, u32[]{:S(2)}) collective-permute-start(bf16[128,512]{1,0:T(8,128)(2,1)S(1)} %add_convert_fusion.2), channel_id=1, source_target_pairs={{0,2},{1,3},{2,0},{3,1},{4,6},{5,7},{6,4},{7,5},{8,10},{9,11},{10,... | collective-permute-start | bytes 393224 | tf_op jit(solution)/shard_map/ppermute | solution.py:163
  20.6 6.1 %collective-permute-start.8 = (bf16[128,1024]{1,0:T(8,128)(2,1)S(1)}, bf16[128,1024]{1,0:T(8,128)(2,1)S(1)}, u32[]{:S(2)}, u32[]{:S(2)}) collective-permute-start(bf16[128,1024]{1,0:T(8,128)(2,1)S(1)} %get-tuple-element.44), channel_id=1, source_target_pairs={{0,1},{1,0},{2,3},{3,2},{4,5},{5,4},{6,7},{7,6},{8,9},{9,8},{10,11... | collective-permute-start | bytes 786440 | tf_op jit(solution)/shard_map/ppermute | solution.py:163
  20.8 6.0 %collective-permute-start.11 = (bf16[128,512]{1,0:T(8,128)(2,1)S(1)}, bf16[128,512]{1,0:T(8,128)(2,1)S(1)}, u32[]{:S(2)}, u32[]{:S(2)}) collective-permute-start(bf16[128,512]{1,0:T(8,128)(2,1)S(1)} %add_convert_fusion.1), channel_id=1, source_target_pairs={{0,2},{1,3},{2,0},{3,1},{4,6},{5,7},{6,4},{7,5},{8,10},{9,11},{10,... | collective-permute-start | bytes 393224 | tf_op jit(solution)/shard_map/ppermute | solution.py:163

commit v17 on v12

--- a/solution.py
+++ b/solution.py
@@ -131,8 +131,8 @@
 
     for head in range(rows // BLOCK):
         at = slice(head * BLOCK, (head + 1) * BLOCK)
-        part = acc_ref[:, at] / l_ref[:, at]
-        att_ref[:, head * head_dim:(head + 1) * head_dim] = part.T.astype(jnp.bfloat16)
+        part = (acc_ref[:, at] / l_ref[:, at]).astype(jnp.bfloat16)
+        att_ref[:, head * head_dim:(head + 1) * head_dim] = part.T
 
     project_pair(2, 0, att_ref, w_ref, send_ref, keep_ref)
 
@@ -182,13 +182,10 @@
         compiler_params=params,
         cost_estimate=pl.CostEstimate(flops=8_000_000_000, bytes_accessed=130_000, transcendentals=0),
     )(in_hbm(key_heads[:, 0, :]), in_hbm(value_heads[:, 0, :]), in_hbm(parents))
+    early, early_xors = [], ()
     if ctx_size == DIRECT_SIZE:
         columns = [swap(kv, "ctx", ctx_size, other) for other in (4, 2, 6)]
         beside = swap(kv, "ctx", ctx_size, 1)
-        pairs = [forward(x, other) for x, other in zip(columns, (4, 2, 6))]
-        early, early_xors = [beside, *columns], (1, 4, 2, 6)
-    else:
-        early, early_xors = [], ()
     q = jnp.transpose(query_heads, (1, 0, 2)).reshape(rows, head_dim)
 
     m, l, acc = pl.pallas_call(
@@ -204,6 +201,9 @@
         cost_estimate=pl.CostEstimate(flops=130_000_000, bytes_accessed=1_000_000, transcendentals=260_000),
     )(reached, q, kv, *early)
 
+    if ctx_size == DIRECT_SIZE:
+        columns[2], m = lax.optimization_barrier((columns[2], m))
+        pairs = [forward(x, other) for x, other in zip(columns, (4, 2, 6))]
     state = (m, l, acc)
     state_shapes = tuple(jax.ShapeDtypeStruct(x.shape, x.dtype) for x in state)
     if ctx_size == DIRECT_SIZE:
@@ -218,6 +218,7 @@
                 cost_estimate=pl.CostEstimate(flops=270_000_000, bytes_accessed=1_000_000, transcendentals=500_000),
             )(reached, q, *state, *arrived)
 
+        state = absorbed(state, (1, 4, 2, 6), [beside, *columns])
         state = absorbed(state, (3, 7), pairs[1:])
         xors, pieces, tree, tree_spec = (5,), pairs[:1], reached, vmem
     else:

time: 26.6 us -> 26.3 us (0.989)
  the two profiles are of different devices: /device:TPU:24 before, /device:TPU:30 now
where the time goes in v17:
time: 26.3 us; the launch traced here: 26 us
  starting transfers between devices  10.3 us (39%)
  waiting for transfers between devices  7.86 us (30%)
  Pallas kernels  6.78 us (26%)
  other arithmetic  0.88 us (3%)
    ppermute x9, starting transfers between devices, swap(): return lax.ppermute(x, axis, [(i, i ^ other) for i in range(size)])  7.81 us
    ppermute x9, waiting for transfers between devices, swap(): return lax.ppermute(x, axis, [(i, i ^ other) for i in range(size)])  7.05 us
    pallas_call x2, Pallas kernels, absorbed(): pl.pallas_call(functools.partial(others_kernel, xors), out_shape=state_sh...  2.92 us
    ppermute x3, starting transfers between devices, forward(): return lax.ppermute(x, ('ctx', 'tp'), route)  2.53 us
    pallas_call x1, Pallas kernels, shards(): pl.pallas_call(functools.partial(last_kernel, xors), out_shape=(jax.Shape...  1.19 us
    pallas_call x2, Pallas kernels, projected(): pl.pallas_call(functools.partial(project_pair, flip, part), out_shape=sha...  1.18 us
    pallas_call x1, Pallas kernels, shards(): pl.pallas_call(functools.partial(pack_kernel, ctx_size == DIRECT_SIZE), o...  0.96 us
    ppermute x3, waiting for transfers between devices, forward(): return lax.ppermute(x, ('ctx', 'tp'), route)  0.81 us
  transfers between devices with their start and end apart: 12, of which 6 were waited for; matrix products, arithmetic and copies ran while one was open for 0% of the time, Pallas kernels for 18%

profile of v17, /device:TPU:30, one launch (start us, length us, event | category | flops | bytes accessed | tf_op | source)
XLA Modules:
  0.0 26.0 jit_solution(12159407188835806850)
XLA Ops:
  0.0 0.0 slice-start
  0.0 0.0 copy-start
  0.0 0.0 slice-start.1
  0.0 1.0 %shard_map.55 = (bf16[256,128]{1,0:T(8,128)(2,1)S(1)}, s32[8,128]{1,0:T(8,128)S(1)}) custom-call(bf16[128,128]{1,0:T(8,128)(2,1)} %bitcast.11, bf16[128,128]{1,0:T(8,128)(2,1)} %bitcast.12, s32[8]{0:T(128)} %parents_hbm.1), custom_call_target="tpu_custom_call" | custom-call | flops 8000000000 | bytes 130000 | tf_op jit(solution)/shard_map/pallas_call | solution.py:173
  1.0 0.3 %collective-permute-start = (bf16[256,128]{1,0:T(8,128)(2,1)S(1)}, bf16[256,128]{1,0:T(8,128)(2,1)S(1)}, u32[]{:S(2)}, u32[]{:S(2)}) collective-permute-start(bf16[256,128]{1,0:T(8,128)(2,1)S(1)} %get-tuple-element.27.kv_ref), channel_id=1, source_target_pairs={{0,24},{4,28},{8,16},{12,20},{16,8},{20,12},{24,0},{28,4},{1,25},{... | collective-permute-start | bytes 196616 | tf_op jit(solution)/shard_map/ppermute | solution.py:163
  1.3 0.7 %collective-permute-start.3 = (bf16[256,128]{1,0:T(8,128)(2,1)S(1)}, bf16[256,128]{1,0:T(8,128)(2,1)S(1)}, u32[]{:S(2)}, u32[]{:S(2)}) collective-permute-start(bf16[256,128]{1,0:T(8,128)(2,1)S(1)} %get-tuple-element.27.kv_ref), channel_id=1, source_target_pairs={{0,8},{4,12},{8,0},{12,4},{16,24},{20,28},{24,16},{28,20},{1,9},{5... | collective-permute-start | bytes 196616 | tf_op jit(solution)/shard_map/ppermute | solution.py:163
  1.9 3.5 %collective-permute-start.2 = (bf16[256,128]{1,0:T(8,128)(2,1)S(1)}, bf16[256,128]{1,0:T(8,128)(2,1)S(1)}, u32[]{:S(2)}, u32[]{:S(2)}) collective-permute-start(bf16[256,128]{1,0:T(8,128)(2,1)S(1)} %get-tuple-element.27.kv_ref), channel_id=1, source_target_pairs={{0,16},{4,20},{8,24},{12,28},{16,0},{20,4},{24,8},{28,12},{1,17},{... | collective-permute-start | bytes 196616 | tf_op jit(solution)/shard_map/ppermute | solution.py:163
  5.4 0.5 %collective-permute-start.1 = (bf16[256,128]{1,0:T(8,128)(2,1)S(1)}, bf16[256,128]{1,0:T(8,128)(2,1)S(1)}, u32[]{:S(2)}, u32[]{:S(2)}) collective-permute-start(bf16[256,128]{1,0:T(8,128)(2,1)S(1)} %get-tuple-element.27.kv_ref), channel_id=1, source_target_pairs={{0,4},{4,0},{8,12},{12,8},{16,20},{20,16},{24,28},{28,24},{1,5},{5... | collective-permute-start | bytes 196616 | tf_op jit(solution)/shard_map/ppermute | solution.py:163
  5.9 0.0 copy-done
  6.0 0.5 %shard_map.56 = (f32[1,1024]{1,0:T(1,128)S(1)}, f32[1,1024]{1,0:T(1,128)S(1)}, f32[128,1024]{1,0:T(8,128)S(1)}) custom-call(s32[8,128]{1,0:T(8,128)S(1)} %get-tuple-element.26.reached_ref.tree_ref, bf16[1024,128]{1,0:T(8,128)(2,1)S(1)} %bitcast.6, bf16[256,128]{1,0:T(8,128)(2,1)S(1)} %get-tuple-element.27.kv_ref), custom_call_target="tpu_custom_call" | custom-call | flops 130000000 | bytes 1000000 | tf_op jit(solution)/shard_map/pallas_call | solution.py:191
  6.5 1.3 %collective-permute-done.refs_3_ = bf16[256,128]{1,0:T(8,128)(2,1)S(1)} collective-permute-done((bf16[256,128]{1,0:T(8,128)(2,1)S(1)}, bf16[256,128]{1,0:T(8,128)(2,1)S(1)}, u32[]{:S(2)}, u32[]{:S(2)}) %collective-permute-start) | collective-permute-done | bytes 65568 | tf_op jit(solution)/shard_map/ppermute | solution.py:163
  7.8 0.0 collective-permute-done.3.refs_2_
  7.8 0.5 %collective-permute-start.4 = (bf16[256,128]{1,0:T(8,128)(2,1)S(1)}, bf16[256,128]{1,0:T(8,128)(2,1)S(1)}, u32[]{:S(2)}, u32[]{:S(2)}) collective-permute-start(bf16[256,128]{1,0:T(8,128)(2,1)S(1)} %collective-permute-done.3.refs_2_), channel_id=1, source_target_pairs={{0,1},{1,0},{2,3},{3,2},{4,5},{5,4},{6,7},{7,6},{8,12},{9,13},{10,... | collective-permute-start | bytes 196616 | tf_op jit(solution)/shard_map/ppermute | solution.py:171
  8.3 1.5 %collective-permute-start.5 = (bf16[256,128]{1,0:T(8,128)(2,1)S(1)}, bf16[256,128]{1,0:T(8,128)(2,1)S(1)}, u32[]{:S(2)}, u32[]{:S(2)}) collective-permute-start(bf16[256,128]{1,0:T(8,128)(2,1)S(1)} %collective-permute-done.refs_3_), channel_id=1, source_target_pairs={{0,1},{1,0},{2,3},{3,2},{4,5},{5,4},{6,7},{7,6},{8,9},{9,8},{10,11... | collective-permute-start | bytes 196616 | tf_op jit(solution)/shard_map/ppermute | solution.py:171
  9.9 0.0 collective-permute-done.2.refs_1_
  9.9 0.5 %collective-permute-start.6 = (bf16[256,128]{1,0:T(8,128)(2,1)S(1)}, bf16[256,128]{1,0:T(8,128)(2,1)S(1)}, u32[]{:S(2)}, u32[]{:S(2)}) collective-permute-start(bf16[256,128]{1,0:T(8,128)(2,1)S(1)} %collective-permute-done.2.refs_1_), channel_id=1, source_target_pairs={{0,1},{1,0},{2,3},{3,2},{4,5},{5,4},{6,7},{7,6},{8,9},{9,8},{10,11... | collective-permute-start | bytes 196616 | tf_op jit(solution)/shard_map/ppermute | solution.py:171
  10.4 0.0 collective-permute-done.1.refs_0_
  10.4 1.7 %shard_map.57 = (f32[1,1024]{1,0:T(1,128)S(1)}, f32[1,1024]{1,0:T(1,128)S(1)}, f32[128,1024]{1,0:T(8,128)S(1)}) custom-call(s32[8,128]{1,0:T(8,128)S(1)} %get-tuple-element.26.reached_ref.tree_ref, bf16[1024,128]{1,0:T(8,128)(2,1)S(1)} %bitcast.7, f32[1,1024]{1,0:T(1,128)S(1)} %get-tuple-element.29.m_in, ...), custom_call_target="tpu_custom_call", output_to_operand_aliasing={{0}: (2, {}), {1}: (3, {}), {2}: (4, {})} | custom-call | flops 270000000 | bytes 1000000 | tf_op jit(solution)/shard_map/pallas_call | solution.py:211
  12.1 0.0 collective-permute-done.4.refs_0_
  12.1 0.7 %collective-permute-done.5.refs_1_ = bf16[256,128]{1,0:T(8,128)(2,1)S(1)} collective-permute-done((bf16[256,128]{1,0:T(8,128)(2,1)S(1)}, bf16[256,128]{1,0:T(8,128)(2,1)S(1)}, u32[]{:S(2)}, u32[]{:S(2)}) %collective-permute-start.5) | collective-permute-done | bytes 65568 | tf_op jit(solution)/shard_map/ppermute | solution.py:171
  12.8 1.2 %shard_map.58 = (f32[1,1024]{1,0:T(1,128)S(1)}, f32[1,1024]{1,0:T(1,128)S(1)}, f32[128,1024]{1,0:T(8,128)S(1)}) custom-call(s32[8,128]{1,0:T(8,128)S(1)} %get-tuple-element.26.reached_ref.tree_ref, bf16[1024,128]{1,0:T(8,128)(2,1)S(1)} %bitcast.8, f32[1,1024]{1,0:T(1,128)S(1)} %get-tuple-element.33.m_in, ...), custom_call_target="tpu_custom_call", output_to_operand_aliasing={{0}: (2, {}), {1}: (3, {}), {2}: (4, {})} | custom-call | flops 270000000 | bytes 1000000 | tf_op jit(solution)/shard_map/pallas_call | solution.py:211
  14.0 0.1 collective-permute-done.6.refs_0_
  14.1 0.0 slice-done
  14.1 0.0 slice-done.1
  14.1 1.2 %shard_map.59 = (bf16[128,1024]{1,0:T(8,128)(2,1)S(1)}, bf16[128,512]{1,0:T(8,128)(2,1)S(1)}, f32[128,512]{1,0:T(8,128)S(1)}, f32[1,1024]{1,0:T(1,128)S(1)}, f32...) custom-call(s32[8,128]{1,0:T(8,128)S(1)} %get-tuple-element.26.reached_ref, ...), custom_call_target="tpu_custom_call", output_to_operand_aliasing={{3}: (2, {}), {4}: (3, {}), {5}: (4, {})} | custom-call | flops 1000000000 | bytes 10000000 | tf_op jit(solution)/shard_map/pallas_call | solution.py:232
  15.3 0.1 collective-permute-start.7
  15.4 0.5 %shard_map.61 = (bf16[128,512]{1,0:T(8,128)(2,1)S(1)}, f32[128,512]{1,0:T(8,128)S(1)}) custom-call(bf16[128,1024]{1,0:T(8,128)(2,1)S(1)} %get-tuple-element.42.att_ref, bf16[1024,4096]{1,0:T(8,128)(2,1)S(1)} %bitcast.5), custom_call_target="tpu_custom_call" | custom-call | flops 540000000 | bytes 4000000 | tf_op jit(solution)/shard_map/pallas_call | solution.py:243
  15.9 0.6 %collective-permute-start.10 = (bf16[128,512]{1,0:T(8,128)(2,1)S(1)}, bf16[128,512]{1,0:T(8,128)(2,1)S(1)}, u32[]{:S(2)}, u32[]{:S(2)}) collective-permute-start(bf16[128,512]{1,0:T(8,128)(2,1)S(1)} %get-tuple-element.46), channel_id=1, source_target_pairs={{0,1},{1,0},{2,3},{3,2},{4,5},{5,4},{6,7},{7,6},{8,9},{9,8},{10,11... | collective-permute-start | bytes 393224 | tf_op jit(solution)/shard_map/ppermute | solution.py:163
  16.4 0.3 %collective-permute-done.7 = bf16[128,512]{1,0:T(8,128)(2,1)S(1)} collective-permute-done((bf16[128,512]{1,0:T(8,128)(2,1)S(1)}, bf16[128,512]{1,0:T(8,128)(2,1)S(1)}, u32[]{:S(2)}, u32[]{:S(2)}) %collective-permute-start.7) | collective-permute-done | bytes 131104 | tf_op jit(solution)/shard_map/ppermute | solution.py:163
  16.8 0.6 %collective-permute-start.9 = (bf16[128,512]{1,0:T(8,128)(2,1)S(1)}, bf16[128,512]{1,0:T(8,128)(2,1)S(1)}, u32[]{:S(2)}, u32[]{:S(2)}) collective-permute-start(bf16[128,512]{1,0:T(8,128)(2,1)S(1)} %add_convert_fusion.2), channel_id=1, source_target_pairs={{0,2},{1,3},{2,0},{3,1},{4,6},{5,7},{6,4},{7,5},{8,10},{9,11},{10,... | collective-permute-start | bytes 393224 | tf_op jit(solution)/shard_map/ppermute | solution.py:163
  17.4 0.7 %shard_map.60 = (bf16[128,1024]{1,0:T(8,128)(2,1)S(1)}, f32[128,1024]{1,0:T(8,128)S(1)}) custom-call(bf16[128,1024]{1,0:T(8,128)(2,1)S(1)} %get-tuple-element.42.att_ref, bf16[1024,4096]{1,0:T(8,128)(2,1)S(1)} %bitcast.5), custom_call_target="tpu_custom_call" | custom-call | flops 540000000 | bytes 4000000 | tf_op jit(solution)/shard_map/pallas_call | solution.py:243
  18.1 0.1 collective-permute-start.8
  18.2 0.0 collective-permute-done.10
  18.2 1.6 %collective-permute-start.11 = (bf16[128,512]{1,0:T(8,128)(2,1)S(1)}, bf16[128,512]{1,0:T(8,128)(2,1)S(1)}, u32[]{:S(2)}, u32[]{:S(2)}) collective-permute-start(bf16[128,512]{1,0:T(8,128)(2,1)S(1)} %add_convert_fusion.1), channel_id=1, source_target_pairs={{0,2},{1,3},{2,0},{3,1},{4,6},{5,7},{6,4},{7,5},{8,10},{9,11},{10,... | collective-permute-start | bytes 393224 | tf_op jit(solution)/shard_map/ppermute | solution.py:163
  19.8 3.4 %collective-permute-done.9 = bf16[128,512]{1,0:T(8,128)(2,1)S(1)} collective-permute-done((bf16[128,512]{1,0:T(8,128)(2,1)S(1)}, bf16[128,512]{1,0:T(8,128)(2,1)S(1)}, u32[]{:S(2)}, u32[]{:S(2)}) %collective-permute-start.9) | collective-permute-done | bytes 131104 | tf_op jit(solution)/shard_map/ppermute | solution.py:163
  23.2 2.0 %collective-permute-done.11 = bf16[128,512]{1,0:T(8,128)(2,1)S(1)} collective-permute-done((bf16[128,512]{1,0:T(8,128)(2,1)S(1)}, bf16[128,512]{1,0:T(8,128)(2,1)S(1)}, u32[]{:S(2)}, u32[]{:S(2)}) %collective-permute-start.11) | collective-permute-done | bytes 131104 | tf_op jit(solution)/shard_map/ppermute | solution.py:163
  25.2 0.0 collective-permute-done.8
  25.2 0.8 %add_convert_fusion = bf16[128,1024]{1,0:T(8,128)(2,1)} fusion(f32[128,1024]{1,0:T(8,128)S(1)} %get-tuple-element.43, bf16[128,1024]{1,0:T(8,128)(2,1)S(1)} %collective-permute-done.8, bf16[128,512]{1,0:T(8,128)(2,1)S(1)} %collective-permute-done.11, bf16[128,512]{1,0:T(8,128)(2,1)S(1)} %collective-permute-done.9), kind=kLoop, calls=%fused_computation | loop fusion | flops 1048576 | bytes 1310720 | tf_op jit(solution)/shard_map/convert_element_type | solution.py:271
  (4 shorter events, 0.1 us)
Async XLA Ops:
  0.0 14.1 %slice-start = ((s8[8388608]{0:T(1024)(128)(4,1)}), s8[4194304]{0:T(1024)(128)(4,1)S(1)}, s32[]{:S(2)}) async-start(s8[8388608]{0:T(1024)(128)(4,1)} %bitcast.4), calls=%async_computation | async-start | bytes 8388608
  0.0 5.9 %copy-start = (bf16[128,8,128]{2,1,0:T(8,128)(2,1)S(1)}, bf16[128,8,128]{2,1,0:T(8,128)(2,1)}, u32[]{:S(2)}) copy-start(bf16[128,8,128]{2,1,0:T(8,128)(2,1)} %param.5) | copy-start | bytes 786436
  0.0 14.1 %slice-start.1 = ((s8[8388608]{0:T(1024)(128)(4,1)}), s8[4194304]{0:T(1024)(128)(4,1)S(1)}, s32[]{:S(2)}) async-start(s8[8388608]{0:T(1024)(128)(4,1)} %bitcast.4), calls=%async_computation.1 | async-start | bytes 8388608
  1.0 6.8 %collective-permute-start = (bf16[256,128]{1,0:T(8,128)(2,1)S(1)}, bf16[256,128]{1,0:T(8,128)(2,1)S(1)}, u32[]{:S(2)}, u32[]{:S(2)}) collective-permute-start(bf16[256,128]{1,0:T(8,128)(2,1)S(1)} %get-tuple-element.27.kv_ref), channel_id=1, source_target_pairs={{0,24},{4,28},{8,16},{12,20},{16,8},{20,12},{24,0},{28,4},{1,25},{... | collective-permute-start | bytes 196616 | tf_op jit(solution)/shard_map/ppermute | solution.py:163
  1.3 6.6 %collective-permute-start.3 = (bf16[256,128]{1,0:T(8,128)(2,1)S(1)}, bf16[256,128]{1,0:T(8,128)(2,1)S(1)}, u32[]{:S(2)}, u32[]{:S(2)}) collective-permute-start(bf16[256,128]{1,0:T(8,128)(2,1)S(1)} %get-tuple-element.27.kv_ref), channel_id=1, source_target_pairs={{0,8},{4,12},{8,0},{12,4},{16,24},{20,28},{24,16},{28,20},{1,9},{5... | collective-permute-start | bytes 196616 | tf_op jit(solution)/shard_map/ppermute | solution.py:163
  1.9 7.9 %collective-permute-start.2 = (bf16[256,128]{1,0:T(8,128)(2,1)S(1)}, bf16[256,128]{1,0:T(8,128)(2,1)S(1)}, u32[]{:S(2)}, u32[]{:S(2)}) collective-permute-start(bf16[256,128]{1,0:T(8,128)(2,1)S(1)} %get-tuple-element.27.kv_ref), channel_id=1, source_target_pairs={{0,16},{4,20},{8,24},{12,28},{16,0},{20,4},{24,8},{28,12},{1,17},{... | collective-permute-start | bytes 196616 | tf_op jit(solution)/shard_map/ppermute | solution.py:163
  5.4 4.9 %collective-permute-start.1 = (bf16[256,128]{1,0:T(8,128)(2,1)S(1)}, bf16[256,128]{1,0:T(8,128)(2,1)S(1)}, u32[]{:S(2)}, u32[]{:S(2)}) collective-permute-start(bf16[256,128]{1,0:T(8,128)(2,1)S(1)} %get-tuple-element.27.kv_ref), channel_id=1, source_target_pairs={{0,4},{4,0},{8,12},{12,8},{16,20},{20,16},{24,28},{28,24},{1,5},{5... | collective-permute-start | bytes 196616 | tf_op jit(solution)/shard_map/ppermute | solution.py:163
  7.8 4.3 %collective-permute-start.4 = (bf16[256,128]{1,0:T(8,128)(2,1)S(1)}, bf16[256,128]{1,0:T(8,128)(2,1)S(1)}, u32[]{:S(2)}, u32[]{:S(2)}) collective-permute-start(bf16[256,128]{1,0:T(8,128)(2,1)S(1)} %collective-permute-done.3.refs_2_), channel_id=1, source_target_pairs={{0,1},{1,0},{2,3},{3,2},{4,5},{5,4},{6,7},{7,6},{8,12},{9,13},{10,... | collective-permute-start | bytes 196616 | tf_op jit(solution)/shard_map/ppermute | solution.py:171
  8.3 4.5 %collective-permute-start.5 = (bf16[256,128]{1,0:T(8,128)(2,1)S(1)}, bf16[256,128]{1,0:T(8,128)(2,1)S(1)}, u32[]{:S(2)}, u32[]{:S(2)}) collective-permute-start(bf16[256,128]{1,0:T(8,128)(2,1)S(1)} %collective-permute-done.refs_3_), channel_id=1, source_target_pairs={{0,1},{1,0},{2,3},{3,2},{4,5},{5,4},{6,7},{7,6},{8,9},{9,8},{10,11... | collective-permute-start | bytes 196616 | tf_op jit(solution)/shard_map/ppermute | solution.py:171
  9.9 4.3 %collective-permute-start.6 = (bf16[256,128]{1,0:T(8,128)(2,1)S(1)}, bf16[256,128]{1,0:T(8,128)(2,1)S(1)}, u32[]{:S(2)}, u32[]{:S(2)}) collective-permute-start(bf16[256,128]{1,0:T(8,128)(2,1)S(1)} %collective-permute-done.2.refs_1_), channel_id=1, source_target_pairs={{0,1},{1,0},{2,3},{3,2},{4,5},{5,4},{6,7},{7,6},{8,9},{9,8},{10,11... | collective-permute-start | bytes 196616 | tf_op jit(solution)/shard_map/ppermute | solution.py:171
  15.3 1.4 %collective-permute-start.7 = (bf16[128,512]{1,0:T(8,128)(2,1)S(1)}, bf16[128,512]{1,0:T(8,128)(2,1)S(1)}, u32[]{:S(2)}, u32[]{:S(2)}) collective-permute-start(bf16[128,512]{1,0:T(8,128)(2,1)S(1)} %get-tuple-element.41), channel_id=1, source_target_pairs={{0,1},{1,0},{2,3},{3,2},{4,5},{5,4},{6,7},{7,6},{8,9},{9,8},{10,11... | collective-permute-start | bytes 393224 | tf_op jit(solution)/shard_map/ppermute | solution.py:163
  15.9 2.3 %collective-permute-start.10 = (bf16[128,512]{1,0:T(8,128)(2,1)S(1)}, bf16[128,512]{1,0:T(8,128)(2,1)S(1)}, u32[]{:S(2)}, u32[]{:S(2)}) collective-permute-start(bf16[128,512]{1,0:T(8,128)(2,1)S(1)} %get-tuple-element.46), channel_id=1, source_target_pairs={{0,1},{1,0},{2,3},{3,2},{4,5},{5,4},{6,7},{7,6},{8,9},{9,8},{10,11... | collective-permute-start | bytes 393224 | tf_op jit(solution)/shard_map/ppermute | solution.py:163
  16.8 6.4 %collective-permute-start.9 = (bf16[128,512]{1,0:T(8,128)(2,1)S(1)}, bf16[128,512]{1,0:T(8,128)(2,1)S(1)}, u32[]{:S(2)}, u32[]{:S(2)}) collective-permute-start(bf16[128,512]{1,0:T(8,128)(2,1)S(1)} %add_convert_fusion.2), channel_id=1, source_target_pairs={{0,2},{1,3},{2,0},{3,1},{4,6},{5,7},{6,4},{7,5},{8,10},{9,11},{10,... | collective-permute-start | bytes 393224 | tf_op jit(solution)/shard_map/ppermute | solution.py:163
  18.1 7.1 %collective-permute-start.8 = (bf16[128,1024]{1,0:T(8,128)(2,1)S(1)}, bf16[128,1024]{1,0:T(8,128)(2,1)S(1)}, u32[]{:S(2)}, u32[]{:S(2)}) collective-permute-start(bf16[128,1024]{1,0:T(8,128)(2,1)S(1)} %get-tuple-element.44), channel_id=1, source_target_pairs={{0,1},{1,0},{2,3},{3,2},{4,5},{5,4},{6,7},{7,6},{8,9},{9,8},{10,11... | collective-permute-start | bytes 786440 | tf_op jit(solution)/shard_map/ppermute | solution.py:163
  18.2 7.0 %collective-permute-start.11 = (bf16[128,512]{1,0:T(8,128)(2,1)S(1)}, bf16[128,512]{1,0:T(8,128)(2,1)S(1)}, u32[]{:S(2)}, u32[]{:S(2)}) collective-permute-start(bf16[128,512]{1,0:T(8,128)(2,1)S(1)} %add_convert_fusion.1), channel_id=1, source_target_pairs={{0,2},{1,3},{2,0},{3,1},{4,6},{5,7},{6,4},{7,5},{8,10},{9,11},{10,... | collective-permute-start | bytes 393224 | tf_op jit(solution)/shard_map/ppermute | solution.py:163

commit v18 on v12

--- a/solution.py
+++ b/solution.py
@@ -73,10 +73,14 @@
     scale = exponent_scale(q_ref.shape[1])
     me = lax.axis_index("ctx")
     reached = jnp.max(reached_ref[...])
-    for other, kv_ref in zip(xors, kv_refs):
-        @pl.when((lax.shift_right_logical(reached, me ^ other) & 1) == 1)
-        def _():
-            absorb(scale, q_ref, kv_ref[0:BLOCK, :], kv_ref[BLOCK:, :], *state)
+    for others, kv_ref in zip(xors, kv_refs):
+        for at, other in enumerate(others):
+            keys = slice(2 * at * BLOCK, (2 * at + 1) * BLOCK)
+            values = slice((2 * at + 1) * BLOCK, (2 * at + 2) * BLOCK)
+
+            @pl.when((lax.shift_right_logical(reached, me ^ other) & 1) == 1)
+            def _():
+                absorb(scale, q_ref, kv_ref[keys, :], kv_ref[values, :], *state)
 
 
 def absorb_walk(parents_ref, q_ref, piece, state):
@@ -183,10 +187,15 @@
         cost_estimate=pl.CostEstimate(flops=8_000_000_000, bytes_accessed=130_000, transcendentals=0),
     )(in_hbm(key_heads[:, 0, :]), in_hbm(value_heads[:, 0, :]), in_hbm(parents))
     if ctx_size == DIRECT_SIZE:
-        columns = [swap(kv, "ctx", ctx_size, other) for other in (4, 2, 6)]
-        beside = swap(kv, "ctx", ctx_size, 1)
-        pairs = [forward(x, other) for x, other in zip(columns, (4, 2, 6))]
-        early, early_xors = [beside, *columns], (1, 4, 2, 6)
+        by_6 = swap(kv, "ctx", ctx_size, 6)
+        by_1 = swap(kv, "ctx", ctx_size, 1)
+        by_4 = swap(kv, "ctx", ctx_size, 4)
+        pair = jnp.concatenate([kv, by_1], axis=0)
+        by_23 = swap(pair, "ctx", ctx_size, 2)
+        held, _ = lax.optimization_barrier((by_6, pair))
+        by_7 = forward(held, 6)
+        by_5 = forward(by_4, 4)
+        early, early_xors = [by_1, by_6, by_4], ((1,), (6,), (4,))
     else:
         early, early_xors = [], ()
     q = jnp.transpose(query_heads, (1, 0, 2)).reshape(rows, head_dim)
@@ -207,7 +216,7 @@
     state = (m, l, acc)
     state_shapes = tuple(jax.ShapeDtypeStruct(x.shape, x.dtype) for x in state)
     if ctx_size == DIRECT_SIZE:
-        def absorbed(state, xors, arrived):
+        def absorbed(state, xors, flops, *arrived):
             return pl.pallas_call(
                 functools.partial(others_kernel, xors),
                 out_shape=state_shapes,
@@ -215,11 +224,11 @@
                 out_specs=(vmem,) * 3,
                 input_output_aliases={2: 0, 3: 1, 4: 2},
                 compiler_params=params,
-                cost_estimate=pl.CostEstimate(flops=270_000_000, bytes_accessed=1_000_000, transcendentals=500_000),
+                cost_estimate=pl.CostEstimate(flops=flops, bytes_accessed=1_000_000, transcendentals=500_000),
             )(reached, q, *state, *arrived)
 
-        state = absorbed(state, (3, 7), pairs[1:])
-        xors, pieces, tree, tree_spec = (5,), pairs[:1], reached, vmem
+        state = absorbed(state, ((7,),), 270_000_000, by_7)
+        xors, pieces, tree, tree_spec = ((2, 3), (5,)), [by_23, by_5], reached, vmem
     else:
         xors, pieces, tree, tree_spec = (), [lax.all_gather(kv, "ctx", axis=0, tiled=True)], parents, smem
 

time: 26.6 us -> 27.6 us (1.038)
  the two profiles are of different devices: /device:TPU:24 before, /device:TPU:0 now
where the time goes in v18:
time: 27.6 us; the launch traced here: 27.1 us
  waiting for transfers between devices  11.9 us (43%)
  starting transfers between devices  10.6 us (38%)
  Pallas kernels  3.58 us (13%)
  other arithmetic  0.87 us (3%)
    ppermute x9, waiting for transfers between devices, swap(): return lax.ppermute(x, axis, [(i, i ^ other) for i in range(size)])  11.7 us
    ppermute x9, starting transfers between devices, swap(): return lax.ppermute(x, axis, [(i, i ^ other) for i in range(size)])  10.1 us
    pallas_call x2, Pallas kernels, projected(): pl.pallas_call(functools.partial(project_pair, flip, part), out_shape=sha...  1.18 us
    pallas_call x1, Pallas kernels, shards(): pl.pallas_call(functools.partial(pack_kernel, ctx_size == DIRECT_SIZE), o...  0.95 us
    convert_element_type x1, other arithmetic, shards(): (keep_near + near_in.astype(jnp.float32) + from_far).astype(jnp.bfloat16)  0.8 us
    pallas_call x1, Pallas kernels, shards(): pl.pallas_call(functools.partial(last_kernel, xors), out_shape=(jax.Shape...  0.72 us
  transfers between devices with their start and end apart: 11, of which 7 were waited for; matrix products, arithmetic and copies ran while one was open for 0% of the time, Pallas kernels for 7%

profile of v18, /device:TPU:0, one launch (start us, length us, event | category | flops | bytes accessed | tf_op | source)
XLA Modules:
  0.0 27.1 jit_solution(9403572523127460082)
XLA Ops:
  0.0 0.0 copy-start.1
  0.0 0.0 copy-start
  0.0 0.9 %shard_map.55 = (bf16[256,128]{1,0:T(8,128)(2,1)S(1)}, s32[8,128]{1,0:T(8,128)S(1)}) custom-call(bf16[128,128]{1,0:T(8,128)(2,1)} %bitcast.8, bf16[128,128]{1,0:T(8,128)(2,1)} %bitcast.9, s32[8]{0:T(128)} %parents_hbm.1), custom_call_target="tpu_custom_call" | custom-call | flops 8000000000 | bytes 130000 | tf_op jit(solution)/shard_map/pallas_call | solution.py:177
  1.0 4.1 %collective-permute-start.2 = (bf16[256,128]{1,0:T(8,128)(2,1)S(1)}, bf16[256,128]{1,0:T(8,128)(2,1)S(1)}, u32[]{:S(2)}, u32[]{:S(2)}) collective-permute-start(bf16[256,128]{1,0:T(8,128)(2,1)S(1)} %get-tuple-element.23.kv_ref), channel_id=1, source_target_pairs={{0,16},{4,20},{8,24},{12,28},{16,0},{20,4},{24,8},{28,12},{1,17},{... | collective-permute-start | bytes 196616 | tf_op jit(solution)/shard_map/ppermute | solution.py:167
  5.1 1.3 %collective-permute-start.1 = (bf16[256,128]{1,0:T(8,128)(2,1)S(1)}, bf16[256,128]{1,0:T(8,128)(2,1)S(1)}, u32[]{:S(2)}, u32[]{:S(2)}) collective-permute-start(bf16[256,128]{1,0:T(8,128)(2,1)S(1)} %get-tuple-element.23.kv_ref), channel_id=1, source_target_pairs={{0,24},{4,28},{8,16},{12,20},{16,8},{20,12},{24,0},{28,4},{1,25},{... | collective-permute-start | bytes 196616 | tf_op jit(solution)/shard_map/ppermute | solution.py:167
  6.4 1.5 %collective-permute-start = (bf16[256,128]{1,0:T(8,128)(2,1)S(1)}, bf16[256,128]{1,0:T(8,128)(2,1)S(1)}, u32[]{:S(2)}, u32[]{:S(2)}) collective-permute-start(bf16[256,128]{1,0:T(8,128)(2,1)S(1)} %get-tuple-element.23.kv_ref), channel_id=1, source_target_pairs={{0,4},{4,0},{8,12},{12,8},{16,20},{20,16},{24,28},{28,24},{1,5},{5... | collective-permute-start | bytes 196616 | tf_op jit(solution)/shard_map/ppermute | solution.py:167
  7.9 2.7 %collective-permute-done.refs_0_ = bf16[256,128]{1,0:T(8,128)(2,1)S(1)} collective-permute-done((bf16[256,128]{1,0:T(8,128)(2,1)S(1)}, bf16[256,128]{1,0:T(8,128)(2,1)S(1)}, u32[]{:S(2)}, u32[]{:S(2)}) %collective-permute-start) | collective-permute-done | bytes 65568 | tf_op jit(solution)/shard_map/ppermute | solution.py:167
  10.7 0.3 %collective-permute-start.4 = (bf16[512,128]{1,0:T(8,128)(2,1)S(1)}, bf16[512,128]{1,0:T(8,128)(2,1)S(1)}, u32[]{:S(2)}, u32[]{:S(2)}) collective-permute-start(bf16[512,128]{1,0:T(8,128)(2,1)S(1)} %constant_dynamic-update-slice_fusion), channel_id=1, source_target_pairs={{0,8},{4,12},{8,0},{12,4},{16,24},{20,28},{24,16},{28,20},{1,9},{5... | collective-permute-start | bytes 393224 | tf_op jit(solution)/shard_map/ppermute | solution.py:167
  11.0 0.2 collective-permute-done.1.refs_1_
  11.2 0.0 collective-permute-start.3
  11.2 0.0 collective-permute-done.2.refs_2_
  11.2 0.5 %collective-permute-start.5 = (bf16[256,128]{1,0:T(8,128)(2,1)S(1)}, bf16[256,128]{1,0:T(8,128)(2,1)S(1)}, u32[]{:S(2)}, u32[]{:S(2)}) collective-permute-start(bf16[256,128]{1,0:T(8,128)(2,1)S(1)} %collective-permute-done.2.refs_2_), channel_id=1, source_target_pairs={{0,1},{1,0},{2,3},{3,2},{4,5},{5,4},{6,7},{7,6},{8,9},{9,8},{10,11... | collective-permute-start | bytes 196616 | tf_op jit(solution)/shard_map/ppermute | solution.py:175
  11.8 0.0 copy-done.1
  11.8 0.5 %shard_map.56 = (f32[1,1024]{1,0:T(1,128)S(1)}, f32[1,1024]{1,0:T(1,128)S(1)}, f32[128,1024]{1,0:T(8,128)S(1)}) custom-call(s32[8,128]{1,0:T(8,128)S(1)} %get-tuple-element.22.reached_ref.tree_ref, bf16[1024,128]{1,0:T(8,128)(2,1)S(1)} %bitcast.4, bf16[256,128]{1,0:T(8,128)(2,1)S(1)} %get-tuple-element.23.kv_ref, ...), custom_call_target="tpu_custom_call" | custom-call | flops 130000000 | bytes 1000000 | tf_op jit(solution)/shard_map/pallas_call | solution.py:203
  12.3 0.2 collective-permute-done.3.refs_0_
  12.5 0.2 shard_map.57
  12.7 0.0 collective-permute-done.5.refs_1_
  12.7 3.0 %collective-permute-done.4.refs_0_ = bf16[512,128]{1,0:T(8,128)(2,1)S(1)} collective-permute-done((bf16[512,128]{1,0:T(8,128)(2,1)S(1)}, bf16[512,128]{1,0:T(8,128)(2,1)S(1)}, u32[]{:S(2)}, u32[]{:S(2)}) %collective-permute-start.4) | collective-permute-done | bytes 131104 | tf_op jit(solution)/shard_map/ppermute | solution.py:167
  15.7 0.0 copy-done
  15.7 0.7 %shard_map.58 = (bf16[128,1024]{1,0:T(8,128)(2,1)S(1)}, bf16[128,512]{1,0:T(8,128)(2,1)S(1)}, f32[128,512]{1,0:T(8,128)S(1)}, f32[1,1024]{1,0:T(1,128)S(1)}, f32...) custom-call(s32[8,128]{1,0:T(8,128)S(1)} %get-tuple-element.22.reached_ref, ...), custom_call_target="tpu_custom_call", output_to_operand_aliasing={{3}: (2, {}), {4}: (3, {}), {5}: (4, {})} | custom-call | flops 1000000000 | bytes 10000000 | tf_op jit(solution)/shard_map/pallas_call | solution.py:240
  16.5 0.1 collective-permute-start.6
  16.5 0.5 %shard_map.60 = (bf16[128,512]{1,0:T(8,128)(2,1)S(1)}, f32[128,512]{1,0:T(8,128)S(1)}) custom-call(bf16[128,1024]{1,0:T(8,128)(2,1)S(1)} %get-tuple-element.34.att_ref, bf16[1024,4096]{1,0:T(8,128)(2,1)S(1)} %copy-done), custom_call_target="tpu_custom_call" | custom-call | flops 540000000 | bytes 4000000 | tf_op jit(solution)/shard_map/pallas_call | solution.py:251
  17.0 0.6 %collective-permute-start.9 = (bf16[128,512]{1,0:T(8,128)(2,1)S(1)}, bf16[128,512]{1,0:T(8,128)(2,1)S(1)}, u32[]{:S(2)}, u32[]{:S(2)}) collective-permute-start(bf16[128,512]{1,0:T(8,128)(2,1)S(1)} %get-tuple-element.38), channel_id=1, source_target_pairs={{0,1},{1,0},{2,3},{3,2},{4,5},{5,4},{6,7},{7,6},{8,9},{9,8},{10,11... | collective-permute-start | bytes 393224 | tf_op jit(solution)/shard_map/ppermute | solution.py:167
  17.6 0.3 %collective-permute-done.6 = bf16[128,512]{1,0:T(8,128)(2,1)S(1)} collective-permute-done((bf16[128,512]{1,0:T(8,128)(2,1)S(1)}, bf16[128,512]{1,0:T(8,128)(2,1)S(1)}, u32[]{:S(2)}, u32[]{:S(2)}) %collective-permute-start.6) | collective-permute-done | bytes 131104 | tf_op jit(solution)/shard_map/ppermute | solution.py:167
  17.9 1.6 %collective-permute-start.8 = (bf16[128,512]{1,0:T(8,128)(2,1)S(1)}, bf16[128,512]{1,0:T(8,128)(2,1)S(1)}, u32[]{:S(2)}, u32[]{:S(2)}) collective-permute-start(bf16[128,512]{1,0:T(8,128)(2,1)S(1)} %add_convert_fusion.2), channel_id=1, source_target_pairs={{0,2},{1,3},{2,0},{3,1},{4,6},{5,7},{6,4},{7,5},{8,10},{9,11},{10,... | collective-permute-start | bytes 393224 | tf_op jit(solution)/shard_map/ppermute | solution.py:167
  19.5 0.7 %shard_map.59 = (bf16[128,1024]{1,0:T(8,128)(2,1)S(1)}, f32[128,1024]{1,0:T(8,128)S(1)}) custom-call(bf16[128,1024]{1,0:T(8,128)(2,1)S(1)} %get-tuple-element.34.att_ref, bf16[1024,4096]{1,0:T(8,128)(2,1)S(1)} %copy-done), custom_call_target="tpu_custom_call" | custom-call | flops 540000000 | bytes 4000000 | tf_op jit(solution)/shard_map/pallas_call | solution.py:251
  20.2 0.1 collective-permute-start.7
  20.3 0.0 collective-permute-done.9
  20.3 0.6 %collective-permute-start.10 = (bf16[128,512]{1,0:T(8,128)(2,1)S(1)}, bf16[128,512]{1,0:T(8,128)(2,1)S(1)}, u32[]{:S(2)}, u32[]{:S(2)}) collective-permute-start(bf16[128,512]{1,0:T(8,128)(2,1)S(1)} %add_convert_fusion.1), channel_id=1, source_target_pairs={{0,2},{1,3},{2,0},{3,1},{4,6},{5,7},{6,4},{7,5},{8,10},{9,11},{10,... | collective-permute-start | bytes 393224 | tf_op jit(solution)/shard_map/ppermute | solution.py:167
  20.9 2.6 %collective-permute-done.8 = bf16[128,512]{1,0:T(8,128)(2,1)S(1)} collective-permute-done((bf16[128,512]{1,0:T(8,128)(2,1)S(1)}, bf16[128,512]{1,0:T(8,128)(2,1)S(1)}, u32[]{:S(2)}, u32[]{:S(2)}) %collective-permute-start.8) | collective-permute-done | bytes 131104 | tf_op jit(solution)/shard_map/ppermute | solution.py:167
  23.5 2.8 %collective-permute-done.10 = bf16[128,512]{1,0:T(8,128)(2,1)S(1)} collective-permute-done((bf16[128,512]{1,0:T(8,128)(2,1)S(1)}, bf16[128,512]{1,0:T(8,128)(2,1)S(1)}, u32[]{:S(2)}, u32[]{:S(2)}) %collective-permute-start.10) | collective-permute-done | bytes 131104 | tf_op jit(solution)/shard_map/ppermute | solution.py:167
  26.3 0.0 collective-permute-done.7
  26.3 0.8 %add_convert_fusion = bf16[128,1024]{1,0:T(8,128)(2,1)} fusion(f32[128,1024]{1,0:T(8,128)S(1)} %get-tuple-element.35, bf16[128,1024]{1,0:T(8,128)(2,1)S(1)} %collective-permute-done.7, bf16[128,512]{1,0:T(8,128)(2,1)S(1)} %collective-permute-done.10, bf16[128,512]{1,0:T(8,128)(2,1)S(1)} %collective-permute-done.8), kind=kLoop, calls=%fused_computation | loop fusion | flops 1048576 | bytes 1310720 | tf_op jit(solution)/shard_map/convert_element_type | solution.py:279
  (5 shorter events, 0.1 us)
Async XLA Ops:
  0.0 11.8 %copy-start.1 = (bf16[128,8,128]{2,1,0:T(8,128)(2,1)S(1)}, bf16[128,8,128]{2,1,0:T(8,128)(2,1)}, u32[]{:S(2)}) copy-start(bf16[128,8,128]{2,1,0:T(8,128)(2,1)} %param.5) | copy-start | bytes 786436
  0.0 15.7 %copy-start = (bf16[1024,4096]{1,0:T(8,128)(2,1)S(1)}, bf16[1024,4096]{1,0:T(8,128)(2,1)}, u32[]{:S(2)}) copy-start(bf16[1024,4096]{1,0:T(8,128)(2,1)} %w_ref.3) | copy-start | bytes 25165828
  1.0 10.3 %collective-permute-start.2 = (bf16[256,128]{1,0:T(8,128)(2,1)S(1)}, bf16[256,128]{1,0:T(8,128)(2,1)S(1)}, u32[]{:S(2)}, u32[]{:S(2)}) collective-permute-start(bf16[256,128]{1,0:T(8,128)(2,1)S(1)} %get-tuple-element.23.kv_ref), channel_id=1, source_target_pairs={{0,16},{4,20},{8,24},{12,28},{16,0},{20,4},{24,8},{28,12},{1,17},{... | collective-permute-start | bytes 196616 | tf_op jit(solution)/shard_map/ppermute | solution.py:167
  5.1 6.2 %collective-permute-start.1 = (bf16[256,128]{1,0:T(8,128)(2,1)S(1)}, bf16[256,128]{1,0:T(8,128)(2,1)S(1)}, u32[]{:S(2)}, u32[]{:S(2)}) collective-permute-start(bf16[256,128]{1,0:T(8,128)(2,1)S(1)} %get-tuple-element.23.kv_ref), channel_id=1, source_target_pairs={{0,24},{4,28},{8,16},{12,20},{16,8},{20,12},{24,0},{28,4},{1,25},{... | collective-permute-start | bytes 196616 | tf_op jit(solution)/shard_map/ppermute | solution.py:167
  6.4 4.3 %collective-permute-start = (bf16[256,128]{1,0:T(8,128)(2,1)S(1)}, bf16[256,128]{1,0:T(8,128)(2,1)S(1)}, u32[]{:S(2)}, u32[]{:S(2)}) collective-permute-start(bf16[256,128]{1,0:T(8,128)(2,1)S(1)} %get-tuple-element.23.kv_ref), channel_id=1, source_target_pairs={{0,4},{4,0},{8,12},{12,8},{16,20},{20,16},{24,28},{28,24},{1,5},{5... | collective-permute-start | bytes 196616 | tf_op jit(solution)/shard_map/ppermute | solution.py:167
  10.7 5.0 %collective-permute-start.4 = (bf16[512,128]{1,0:T(8,128)(2,1)S(1)}, bf16[512,128]{1,0:T(8,128)(2,1)S(1)}, u32[]{:S(2)}, u32[]{:S(2)}) collective-permute-start(bf16[512,128]{1,0:T(8,128)(2,1)S(1)} %constant_dynamic-update-slice_fusion), channel_id=1, source_target_pairs={{0,8},{4,12},{8,0},{12,4},{16,24},{20,28},{24,16},{28,20},{1,9},{5... | collective-permute-start | bytes 393224 | tf_op jit(solution)/shard_map/ppermute | solution.py:167
  11.2 1.3 %collective-permute-start.3 = (bf16[256,128]{1,0:T(8,128)(2,1)S(1)}, bf16[256,128]{1,0:T(8,128)(2,1)S(1)}, u32[]{:S(2)}, u32[]{:S(2)}) collective-permute-start(bf16[256,128]{1,0:T(8,128)(2,1)S(1)} %collective-permute-done.1.refs_1_), channel_id=1, source_target_pairs={{0,1},{1,0},{2,3},{3,2},{4,5},{5,4},{6,7},{7,6},{8,9},{9,8},{10,11... | collective-permute-start | bytes 196616 | tf_op jit(solution)/shard_map/ppermute | solution.py:175
  11.2 1.5 %collective-permute-start.5 = (bf16[256,128]{1,0:T(8,128)(2,1)S(1)}, bf16[256,128]{1,0:T(8,128)(2,1)S(1)}, u32[]{:S(2)}, u32[]{:S(2)}) collective-permute-start(bf16[256,128]{1,0:T(8,128)(2,1)S(1)} %collective-permute-done.2.refs_2_), channel_id=1, source_target_pairs={{0,1},{1,0},{2,3},{3,2},{4,5},{5,4},{6,7},{7,6},{8,9},{9,8},{10,11... | collective-permute-start | bytes 196616 | tf_op jit(solution)/shard_map/ppermute | solution.py:175
  16.5 1.4 %collective-permute-start.6 = (bf16[128,512]{1,0:T(8,128)(2,1)S(1)}, bf16[128,512]{1,0:T(8,128)(2,1)S(1)}, u32[]{:S(2)}, u32[]{:S(2)}) collective-permute-start(bf16[128,512]{1,0:T(8,128)(2,1)S(1)} %get-tuple-element.33), channel_id=1, source_target_pairs={{0,1},{1,0},{2,3},{3,2},{4,5},{5,4},{6,7},{7,6},{8,9},{9,8},{10,11... | collective-permute-start | bytes 393224 | tf_op jit(solution)/shard_map/ppermute | solution.py:167
  17.0 3.3 %collective-permute-start.9 = (bf16[128,512]{1,0:T(8,128)(2,1)S(1)}, bf16[128,512]{1,0:T(8,128)(2,1)S(1)}, u32[]{:S(2)}, u32[]{:S(2)}) collective-permute-start(bf16[128,512]{1,0:T(8,128)(2,1)S(1)} %get-tuple-element.38), channel_id=1, source_target_pairs={{0,1},{1,0},{2,3},{3,2},{4,5},{5,4},{6,7},{7,6},{8,9},{9,8},{10,11... | collective-permute-start | bytes 393224 | tf_op jit(solution)/shard_map/ppermute | solution.py:167
  17.9 5.6 %collective-permute-start.8 = (bf16[128,512]{1,0:T(8,128)(2,1)S(1)}, bf16[128,512]{1,0:T(8,128)(2,1)S(1)}, u32[]{:S(2)}, u32[]{:S(2)}) collective-permute-start(bf16[128,512]{1,0:T(8,128)(2,1)S(1)} %add_convert_fusion.2), channel_id=1, source_target_pairs={{0,2},{1,3},{2,0},{3,1},{4,6},{5,7},{6,4},{7,5},{8,10},{9,11},{10,... | collective-permute-start | bytes 393224 | tf_op jit(solution)/shard_map/ppermute | solution.py:167
  20.2 6.1 %collective-permute-start.7 = (bf16[128,1024]{1,0:T(8,128)(2,1)S(1)}, bf16[128,1024]{1,0:T(8,128)(2,1)S(1)}, u32[]{:S(2)}, u32[]{:S(2)}) collective-permute-start(bf16[128,1024]{1,0:T(8,128)(2,1)S(1)} %get-tuple-element.36), channel_id=1, source_target_pairs={{0,1},{1,0},{2,3},{3,2},{4,5},{5,4},{6,7},{7,6},{8,9},{9,8},{10,11... | collective-permute-start | bytes 786440 | tf_op jit(solution)/shard_map/ppermute | solution.py:167
  20.3 6.0 %collective-permute-start.10 = (bf16[128,512]{1,0:T(8,128)(2,1)S(1)}, bf16[128,512]{1,0:T(8,128)(2,1)S(1)}, u32[]{:S(2)}, u32[]{:S(2)}) collective-permute-start(bf16[128,512]{1,0:T(8,128)(2,1)S(1)} %add_convert_fusion.1), channel_id=1, source_target_pairs={{0,2},{1,3},{2,0},{3,1},{4,6},{5,7},{6,4},{7,5},{8,10},{9,11},{10,... | collective-permute-start | bytes 393224 | tf_op jit(solution)/shard_map/ppermute | solution.py:167

commit v19 on v12

--- a/solution.py
+++ b/solution.py
@@ -180,7 +180,7 @@
         out_specs=(vmem, vmem),
         scratch_shapes=[pltpu.SMEM(parents.shape, jnp.int32), pltpu.SemaphoreType.DMA((3,))],
         compiler_params=params,
-        cost_estimate=pl.CostEstimate(flops=8_000_000_000, bytes_accessed=130_000, transcendentals=0),
+        cost_estimate=pl.CostEstimate(flops=1_000_000, bytes_accessed=130_000, transcendentals=0),
     )(in_hbm(key_heads[:, 0, :]), in_hbm(value_heads[:, 0, :]), in_hbm(parents))
     if ctx_size == DIRECT_SIZE:
         columns = [swap(kv, "ctx", ctx_size, other) for other in (4, 2, 6)]
@@ -201,7 +201,7 @@
         in_specs=[vmem] * (3 + len(early)),
         out_specs=(vmem,) * 3,
         compiler_params=params,
-        cost_estimate=pl.CostEstimate(flops=130_000_000, bytes_accessed=1_000_000, transcendentals=260_000),
+        cost_estimate=pl.CostEstimate(flops=5000000000, bytes_accessed=1_000_000, transcendentals=260_000),
     )(reached, q, kv, *early)
 
     state = (m, l, acc)

time: 26.6 us -> 26.4 us (level)
  the two profiles are of different devices: /device:TPU:24 before, /device:TPU:26 now
where the time goes in v19:
time: 26.4 us; the launch traced here: 26.6 us
  starting transfers between devices  12.1 us (46%)
  Pallas kernels  6.43 us (24%)
  waiting for transfers between devices  5.92 us (22%)
  local copies, waits for them, and re-layouts  1.14 us (4%)
  other arithmetic  0.86 us (3%)
    ppermute x9, starting transfers between devices, swap(): return lax.ppermute(x, axis, [(i, i ^ other) for i in range(size)])  8.83 us
    ppermute x9, waiting for transfers between devices, swap(): return lax.ppermute(x, axis, [(i, i ^ other) for i in range(size)])  5.73 us
    ppermute x3, starting transfers between devices, forward(): return lax.ppermute(x, ('ctx', 'tp'), route)  3.27 us
    pallas_call x1, Pallas kernels, shards(): pl.pallas_call(functools.partial(own_block_kernel, early_xors), out_shape...  2.03 us
    pallas_call x1, Pallas kernels, shards(): pl.pallas_call(functools.partial(last_kernel, xors), out_shape=(jax.Shape...  1.21 us
    pallas_call x1, Pallas kernels, absorbed(): pl.pallas_call(functools.partial(others_kernel, xors), out_shape=state_sh...  1.21 us
    pallas_call x2, Pallas kernels, projected(): pl.pallas_call(functools.partial(project_pair, flip, part), out_shape=sha...  1.18 us
    transpose x1, local copies, waits for them, and re-layouts, shards(): q = jnp.transpose(query_heads, (1, 0, 2)).reshape(rows, head_dim)  1.14 us
  transfers between devices with their start and end apart: 12, of which 4 were waited for; matrix products, arithmetic and copies ran while one was open for 5% of the time, Pallas kernels for 17%

profile of v19, /device:TPU:26, one launch (start us, length us, event | category | flops | bytes accessed | tf_op | source)
XLA Modules:
  0.0 26.6 jit_solution(9308637429142814660)
XLA Ops:
  0.0 0.8 %shard_map.55 = (bf16[256,128]{1,0:T(8,128)(2,1)S(1)}, s32[8,128]{1,0:T(8,128)S(1)}) custom-call(bf16[128,128]{1,0:T(8,128)(2,1)} %bitcast.10, bf16[128,128]{1,0:T(8,128)(2,1)} %bitcast.11, s32[8]{0:T(128)} %parents_hbm.1), custom_call_target="tpu_custom_call" | custom-call | flops 1000000 | bytes 130000 | tf_op jit(solution)/shard_map/pallas_call | solution.py:173
  0.8 0.3 %collective-permute-start.3 = (bf16[256,128]{1,0:T(8,128)(2,1)S(1)}, bf16[256,128]{1,0:T(8,128)(2,1)S(1)}, u32[]{:S(2)}, u32[]{:S(2)}) collective-permute-start(bf16[256,128]{1,0:T(8,128)(2,1)S(1)} %get-tuple-element.22.kv_ref), channel_id=1, source_target_pairs={{0,24},{4,28},{8,16},{12,20},{16,8},{20,12},{24,0},{28,4},{1,25},{... | collective-permute-start | bytes 196616 | tf_op jit(solution)/shard_map/ppermute | solution.py:163
  1.1 0.7 %collective-permute-start.2 = (bf16[256,128]{1,0:T(8,128)(2,1)S(1)}, bf16[256,128]{1,0:T(8,128)(2,1)S(1)}, u32[]{:S(2)}, u32[]{:S(2)}) collective-permute-start(bf16[256,128]{1,0:T(8,128)(2,1)S(1)} %get-tuple-element.22.kv_ref), channel_id=1, source_target_pairs={{0,8},{4,12},{8,0},{12,4},{16,24},{20,28},{24,16},{28,20},{1,9},{5... | collective-permute-start | bytes 196616 | tf_op jit(solution)/shard_map/ppermute | solution.py:163
  1.8 3.5 %collective-permute-start.1 = (bf16[256,128]{1,0:T(8,128)(2,1)S(1)}, bf16[256,128]{1,0:T(8,128)(2,1)S(1)}, u32[]{:S(2)}, u32[]{:S(2)}) collective-permute-start(bf16[256,128]{1,0:T(8,128)(2,1)S(1)} %get-tuple-element.22.kv_ref), channel_id=1, source_target_pairs={{0,16},{4,20},{8,24},{12,28},{16,0},{20,4},{24,8},{28,12},{1,17},{... | collective-permute-start | bytes 196616 | tf_op jit(solution)/shard_map/ppermute | solution.py:163
  5.3 1.5 %collective-permute-start = (bf16[256,128]{1,0:T(8,128)(2,1)S(1)}, bf16[256,128]{1,0:T(8,128)(2,1)S(1)}, u32[]{:S(2)}, u32[]{:S(2)}) collective-permute-start(bf16[256,128]{1,0:T(8,128)(2,1)S(1)} %get-tuple-element.22.kv_ref), channel_id=1, source_target_pairs={{0,4},{4,0},{8,12},{12,8},{16,20},{20,16},{24,28},{28,24},{1,5},{5... | collective-permute-start | bytes 196616 | tf_op jit(solution)/shard_map/ppermute | solution.py:163
  6.8 0.0 slice-start
  6.8 1.1 %copy.12 = bf16[8,128,128]{2,1,0:T(8,128)(2,1)S(1)} copy(bf16[8,128,128]{2,0,1:T(8,128)(2,1)} %bitcast.9) | data formatting | bytes 524288 | tf_op jit(solution)/shard_map/transpose | solution.py:192
  7.9 0.0 collective-permute-done.3.refs_3_
  7.9 1.2 %collective-permute-start.5 = (bf16[256,128]{1,0:T(8,128)(2,1)S(1)}, bf16[256,128]{1,0:T(8,128)(2,1)S(1)}, u32[]{:S(2)}, u32[]{:S(2)}) collective-permute-start(bf16[256,128]{1,0:T(8,128)(2,1)S(1)} %collective-permute-done.3.refs_3_), channel_id=1, source_target_pairs={{0,1},{1,0},{2,3},{3,2},{4,5},{5,4},{6,7},{7,6},{8,9},{9,8},{10,11... | collective-permute-start | bytes 196616 | tf_op jit(solution)/shard_map/ppermute | solution.py:171
  9.2 0.0 collective-permute-done.2.refs_2_
  9.2 0.9 %collective-permute-start.4 = (bf16[256,128]{1,0:T(8,128)(2,1)S(1)}, bf16[256,128]{1,0:T(8,128)(2,1)S(1)}, u32[]{:S(2)}, u32[]{:S(2)}) collective-permute-start(bf16[256,128]{1,0:T(8,128)(2,1)S(1)} %collective-permute-done.2.refs_2_), channel_id=1, source_target_pairs={{0,1},{1,0},{2,3},{3,2},{4,5},{5,4},{6,7},{7,6},{8,12},{9,13},{10,... | collective-permute-start | bytes 196616 | tf_op jit(solution)/shard_map/ppermute | solution.py:171
  10.0 0.0 collective-permute-done.1.refs_1_
  10.0 1.2 %collective-permute-start.6 = (bf16[256,128]{1,0:T(8,128)(2,1)S(1)}, bf16[256,128]{1,0:T(8,128)(2,1)S(1)}, u32[]{:S(2)}, u32[]{:S(2)}) collective-permute-start(bf16[256,128]{1,0:T(8,128)(2,1)S(1)} %collective-permute-done.1.refs_1_), channel_id=1, source_target_pairs={{0,1},{1,0},{2,3},{3,2},{4,5},{5,4},{6,7},{7,6},{8,9},{9,8},{10,11... | collective-permute-start | bytes 196616 | tf_op jit(solution)/shard_map/ppermute | solution.py:171
  11.2 0.0 collective-permute-done.refs_0_
  11.2 0.0 slice-start.1
  11.2 2.0 %shard_map.56 = (f32[1,1024]{1,0:T(1,128)S(1)}, f32[1,1024]{1,0:T(1,128)S(1)}, f32[128,1024]{1,0:T(8,128)S(1)}) custom-call(s32[8,128]{1,0:T(8,128)S(1)} %get-tuple-element.21.reached_ref.tree_ref, bf16[1024,128]{1,0:T(8,128)(2,1)S(1)} %bitcast.6, bf16[256,128]{1,0:T(8,128)(2,1)S(1)} %get-tuple-element.22.kv_ref, ...), custom_call_target="tpu_custom_call" | custom-call | flops 5000000000 | bytes 1000000 | tf_op jit(solution)/shard_map/pallas_call | solution.py:194
  13.3 0.0 collective-permute-done.5.refs_1_
  13.3 0.2 collective-permute-done.4.refs_0_
  13.4 1.2 %shard_map.57 = (f32[1,1024]{1,0:T(1,128)S(1)}, f32[1,1024]{1,0:T(1,128)S(1)}, f32[128,1024]{1,0:T(8,128)S(1)}) custom-call(s32[8,128]{1,0:T(8,128)S(1)} %get-tuple-element.21.reached_ref.tree_ref, bf16[1024,128]{1,0:T(8,128)(2,1)S(1)} %bitcast.7, f32[1,1024]{1,0:T(1,128)S(1)} %get-tuple-element.23.m_in, ...), custom_call_target="tpu_custom_call", output_to_operand_aliasing={{0}: (2, {}), {1}: (3, {}), {2}: (4, {})} | custom-call | flops 270000000 | bytes 1000000 | tf_op jit(solution)/shard_map/pallas_call | solution.py:211
  14.7 0.0 collective-permute-done.6.refs_0_
  14.7 0.0 slice-done
  14.7 0.0 slice-done.1
  14.7 1.2 %shard_map.58 = (bf16[128,1024]{1,0:T(8,128)(2,1)S(1)}, bf16[128,512]{1,0:T(8,128)(2,1)S(1)}, f32[128,512]{1,0:T(8,128)S(1)}, f32[1,1024]{1,0:T(1,128)S(1)}, f32...) custom-call(s32[8,128]{1,0:T(8,128)S(1)} %get-tuple-element.21.reached_ref, ...), custom_call_target="tpu_custom_call", output_to_operand_aliasing={{3}: (2, {}), {4}: (3, {}), {5}: (4, {})} | custom-call | flops 1000000000 | bytes 10000000 | tf_op jit(solution)/shard_map/pallas_call | solution.py:231
  15.9 0.1 collective-permute-start.7
  16.0 0.5 %shard_map.60 = (bf16[128,512]{1,0:T(8,128)(2,1)S(1)}, f32[128,512]{1,0:T(8,128)S(1)}) custom-call(bf16[128,1024]{1,0:T(8,128)(2,1)S(1)} %get-tuple-element.32.att_ref, bf16[1024,4096]{1,0:T(8,128)(2,1)S(1)} %bitcast.5), custom_call_target="tpu_custom_call" | custom-call | flops 540000000 | bytes 4000000 | tf_op jit(solution)/shard_map/pallas_call | solution.py:242
  16.5 0.6 %collective-permute-start.10 = (bf16[128,512]{1,0:T(8,128)(2,1)S(1)}, bf16[128,512]{1,0:T(8,128)(2,1)S(1)}, u32[]{:S(2)}, u32[]{:S(2)}) collective-permute-start(bf16[128,512]{1,0:T(8,128)(2,1)S(1)} %get-tuple-element.36), channel_id=1, source_target_pairs={{0,1},{1,0},{2,3},{3,2},{4,5},{5,4},{6,7},{7,6},{8,9},{9,8},{10,11... | collective-permute-start | bytes 393224 | tf_op jit(solution)/shard_map/ppermute | solution.py:163
  17.0 0.3 %collective-permute-done.7 = bf16[128,512]{1,0:T(8,128)(2,1)S(1)} collective-permute-done((bf16[128,512]{1,0:T(8,128)(2,1)S(1)}, bf16[128,512]{1,0:T(8,128)(2,1)S(1)}, u32[]{:S(2)}, u32[]{:S(2)}) %collective-permute-start.7) | collective-permute-done | bytes 131104 | tf_op jit(solution)/shard_map/ppermute | solution.py:163
  17.4 0.6 %collective-permute-start.9 = (bf16[128,512]{1,0:T(8,128)(2,1)S(1)}, bf16[128,512]{1,0:T(8,128)(2,1)S(1)}, u32[]{:S(2)}, u32[]{:S(2)}) collective-permute-start(bf16[128,512]{1,0:T(8,128)(2,1)S(1)} %add_convert_fusion.2), channel_id=1, source_target_pairs={{0,2},{1,3},{2,0},{3,1},{4,6},{5,7},{6,4},{7,5},{8,10},{9,11},{10,... | collective-permute-start | bytes 393224 | tf_op jit(solution)/shard_map/ppermute | solution.py:163
  18.0 0.7 %shard_map.59 = (bf16[128,1024]{1,0:T(8,128)(2,1)S(1)}, f32[128,1024]{1,0:T(8,128)S(1)}) custom-call(bf16[128,1024]{1,0:T(8,128)(2,1)S(1)} %get-tuple-element.32.att_ref, bf16[1024,4096]{1,0:T(8,128)(2,1)S(1)} %bitcast.5), custom_call_target="tpu_custom_call" | custom-call | flops 540000000 | bytes 4000000 | tf_op jit(solution)/shard_map/pallas_call | solution.py:242
  18.7 0.1 collective-permute-start.8
  18.8 0.0 collective-permute-done.10
  18.8 1.6 %collective-permute-start.11 = (bf16[128,512]{1,0:T(8,128)(2,1)S(1)}, bf16[128,512]{1,0:T(8,128)(2,1)S(1)}, u32[]{:S(2)}, u32[]{:S(2)}) collective-permute-start(bf16[128,512]{1,0:T(8,128)(2,1)S(1)} %add_convert_fusion.1), channel_id=1, source_target_pairs={{0,2},{1,3},{2,0},{3,1},{4,6},{5,7},{6,4},{7,5},{8,10},{9,11},{10,... | collective-permute-start | bytes 393224 | tf_op jit(solution)/shard_map/ppermute | solution.py:163
  20.4 3.4 %collective-permute-done.9 = bf16[128,512]{1,0:T(8,128)(2,1)S(1)} collective-permute-done((bf16[128,512]{1,0:T(8,128)(2,1)S(1)}, bf16[128,512]{1,0:T(8,128)(2,1)S(1)}, u32[]{:S(2)}, u32[]{:S(2)}) %collective-permute-start.9) | collective-permute-done | bytes 131104 | tf_op jit(solution)/shard_map/ppermute | solution.py:163
  23.8 2.0 %collective-permute-done.11 = bf16[128,512]{1,0:T(8,128)(2,1)S(1)} collective-permute-done((bf16[128,512]{1,0:T(8,128)(2,1)S(1)}, bf16[128,512]{1,0:T(8,128)(2,1)S(1)}, u32[]{:S(2)}, u32[]{:S(2)}) %collective-permute-start.11) | collective-permute-done | bytes 131104 | tf_op jit(solution)/shard_map/ppermute | solution.py:163
  25.8 0.0 collective-permute-done.8
  25.8 0.8 %add_convert_fusion = bf16[128,1024]{1,0:T(8,128)(2,1)} fusion(f32[128,1024]{1,0:T(8,128)S(1)} %get-tuple-element.33, bf16[128,1024]{1,0:T(8,128)(2,1)S(1)} %collective-permute-done.8, bf16[128,512]{1,0:T(8,128)(2,1)S(1)} %collective-permute-done.11, bf16[128,512]{1,0:T(8,128)(2,1)S(1)} %collective-permute-done.9), kind=kLoop, calls=%fused_computation | loop fusion | flops 1048576 | bytes 1310720 | tf_op jit(solution)/shard_map/convert_element_type | solution.py:270
  (3 shorter events, 0.1 us)
Async XLA Ops:
  0.8 7.1 %collective-permute-start.3 = (bf16[256,128]{1,0:T(8,128)(2,1)S(1)}, bf16[256,128]{1,0:T(8,128)(2,1)S(1)}, u32[]{:S(2)}, u32[]{:S(2)}) collective-permute-start(bf16[256,128]{1,0:T(8,128)(2,1)S(1)} %get-tuple-element.22.kv_ref), channel_id=1, source_target_pairs={{0,24},{4,28},{8,16},{12,20},{16,8},{20,12},{24,0},{28,4},{1,25},{... | collective-permute-start | bytes 196616 | tf_op jit(solution)/shard_map/ppermute | solution.py:163
  1.1 8.1 %collective-permute-start.2 = (bf16[256,128]{1,0:T(8,128)(2,1)S(1)}, bf16[256,128]{1,0:T(8,128)(2,1)S(1)}, u32[]{:S(2)}, u32[]{:S(2)}) collective-permute-start(bf16[256,128]{1,0:T(8,128)(2,1)S(1)} %get-tuple-element.22.kv_ref), channel_id=1, source_target_pairs={{0,8},{4,12},{8,0},{12,4},{16,24},{20,28},{24,16},{28,20},{1,9},{5... | collective-permute-start | bytes 196616 | tf_op jit(solution)/shard_map/ppermute | solution.py:163
  1.8 8.3 %collective-permute-start.1 = (bf16[256,128]{1,0:T(8,128)(2,1)S(1)}, bf16[256,128]{1,0:T(8,128)(2,1)S(1)}, u32[]{:S(2)}, u32[]{:S(2)}) collective-permute-start(bf16[256,128]{1,0:T(8,128)(2,1)S(1)} %get-tuple-element.22.kv_ref), channel_id=1, source_target_pairs={{0,16},{4,20},{8,24},{12,28},{16,0},{20,4},{24,8},{28,12},{1,17},{... | collective-permute-start | bytes 196616 | tf_op jit(solution)/shard_map/ppermute | solution.py:163
  5.3 5.9 %collective-permute-start = (bf16[256,128]{1,0:T(8,128)(2,1)S(1)}, bf16[256,128]{1,0:T(8,128)(2,1)S(1)}, u32[]{:S(2)}, u32[]{:S(2)}) collective-permute-start(bf16[256,128]{1,0:T(8,128)(2,1)S(1)} %get-tuple-element.22.kv_ref), channel_id=1, source_target_pairs={{0,4},{4,0},{8,12},{12,8},{16,20},{20,16},{24,28},{28,24},{1,5},{5... | collective-permute-start | bytes 196616 | tf_op jit(solution)/shard_map/ppermute | solution.py:163
  6.8 7.9 %slice-start = ((s8[8388608]{0:T(1024)(128)(4,1)}), s8[4194304]{0:T(1024)(128)(4,1)S(1)}, s32[]{:S(2)}) async-start(s8[8388608]{0:T(1024)(128)(4,1)} %bitcast.4), calls=%async_computation | async-start | bytes 8388608
  7.9 5.3 %collective-permute-start.5 = (bf16[256,128]{1,0:T(8,128)(2,1)S(1)}, bf16[256,128]{1,0:T(8,128)(2,1)S(1)}, u32[]{:S(2)}, u32[]{:S(2)}) collective-permute-start(bf16[256,128]{1,0:T(8,128)(2,1)S(1)} %collective-permute-done.3.refs_3_), channel_id=1, source_target_pairs={{0,1},{1,0},{2,3},{3,2},{4,5},{5,4},{6,7},{7,6},{8,9},{9,8},{10,11... | collective-permute-start | bytes 196616 | tf_op jit(solution)/shard_map/ppermute | solution.py:171
  9.2 4.3 %collective-permute-start.4 = (bf16[256,128]{1,0:T(8,128)(2,1)S(1)}, bf16[256,128]{1,0:T(8,128)(2,1)S(1)}, u32[]{:S(2)}, u32[]{:S(2)}) collective-permute-start(bf16[256,128]{1,0:T(8,128)(2,1)S(1)} %collective-permute-done.2.refs_2_), channel_id=1, source_target_pairs={{0,1},{1,0},{2,3},{3,2},{4,5},{5,4},{6,7},{7,6},{8,12},{9,13},{10,... | collective-permute-start | bytes 196616 | tf_op jit(solution)/shard_map/ppermute | solution.py:171
  10.0 4.6 %collective-permute-start.6 = (bf16[256,128]{1,0:T(8,128)(2,1)S(1)}, bf16[256,128]{1,0:T(8,128)(2,1)S(1)}, u32[]{:S(2)}, u32[]{:S(2)}) collective-permute-start(bf16[256,128]{1,0:T(8,128)(2,1)S(1)} %collective-permute-done.1.refs_1_), channel_id=1, source_target_pairs={{0,1},{1,0},{2,3},{3,2},{4,5},{5,4},{6,7},{7,6},{8,9},{9,8},{10,11... | collective-permute-start | bytes 196616 | tf_op jit(solution)/shard_map/ppermute | solution.py:171
  11.2 3.5 %slice-start.1 = ((s8[8388608]{0:T(1024)(128)(4,1)}), s8[4194304]{0:T(1024)(128)(4,1)S(1)}, s32[]{:S(2)}) async-start(s8[8388608]{0:T(1024)(128)(4,1)} %bitcast.4), calls=%async_computation.1 | async-start | bytes 8388608
  15.9 1.4 %collective-permute-start.7 = (bf16[128,512]{1,0:T(8,128)(2,1)S(1)}, bf16[128,512]{1,0:T(8,128)(2,1)S(1)}, u32[]{:S(2)}, u32[]{:S(2)}) collective-permute-start(bf16[128,512]{1,0:T(8,128)(2,1)S(1)} %get-tuple-element.31), channel_id=1, source_target_pairs={{0,1},{1,0},{2,3},{3,2},{4,5},{5,4},{6,7},{7,6},{8,9},{9,8},{10,11... | collective-permute-start | bytes 393224 | tf_op jit(solution)/shard_map/ppermute | solution.py:163
  16.5 2.3 %collective-permute-start.10 = (bf16[128,512]{1,0:T(8,128)(2,1)S(1)}, bf16[128,512]{1,0:T(8,128)(2,1)S(1)}, u32[]{:S(2)}, u32[]{:S(2)}) collective-permute-start(bf16[128,512]{1,0:T(8,128)(2,1)S(1)} %get-tuple-element.36), channel_id=1, source_target_pairs={{0,1},{1,0},{2,3},{3,2},{4,5},{5,4},{6,7},{7,6},{8,9},{9,8},{10,11... | collective-permute-start | bytes 393224 | tf_op jit(solution)/shard_map/ppermute | solution.py:163
  17.4 6.4 %collective-permute-start.9 = (bf16[128,512]{1,0:T(8,128)(2,1)S(1)}, bf16[128,512]{1,0:T(8,128)(2,1)S(1)}, u32[]{:S(2)}, u32[]{:S(2)}) collective-permute-start(bf16[128,512]{1,0:T(8,128)(2,1)S(1)} %add_convert_fusion.2), channel_id=1, source_target_pairs={{0,2},{1,3},{2,0},{3,1},{4,6},{5,7},{6,4},{7,5},{8,10},{9,11},{10,... | collective-permute-start | bytes 393224 | tf_op jit(solution)/shard_map/ppermute | solution.py:163
  18.7 7.1 %collective-permute-start.8 = (bf16[128,1024]{1,0:T(8,128)(2,1)S(1)}, bf16[128,1024]{1,0:T(8,128)(2,1)S(1)}, u32[]{:S(2)}, u32[]{:S(2)}) collective-permute-start(bf16[128,1024]{1,0:T(8,128)(2,1)S(1)} %get-tuple-element.34), channel_id=1, source_target_pairs={{0,1},{1,0},{2,3},{3,2},{4,5},{5,4},{6,7},{7,6},{8,9},{9,8},{10,11... | collective-permute-start | bytes 786440 | tf_op jit(solution)/shard_map/ppermute | solution.py:163
  18.8 7.0 %collective-permute-start.11 = (bf16[128,512]{1,0:T(8,128)(2,1)S(1)}, bf16[128,512]{1,0:T(8,128)(2,1)S(1)}, u32[]{:S(2)}, u32[]{:S(2)}) collective-permute-start(bf16[128,512]{1,0:T(8,128)(2,1)S(1)} %add_convert_fusion.1), channel_id=1, source_target_pairs={{0,2},{1,3},{2,0},{3,1},{4,6},{5,7},{6,4},{7,5},{8,10},{9,11},{10,... | collective-permute-start | bytes 393224 | tf_op jit(solution)/shard_map/ppermute | solution.py:163

commit v20 on v19

--- a/solution.py
+++ b/solution.py
@@ -38,19 +38,20 @@
     return reached
 
 
-def pack_kernel(walk, k_hbm, v_hbm, parents_hbm, kv_ref, reached_ref, parents_ref, sems):
+def pack_kernel(walk, k_hbm, v_hbm, q_hbm, parents_hbm, kv_ref, q_ref, reached_ref, parents_ref, sems):
     copies = [
         pltpu.make_async_copy(parents_hbm, parents_ref, sems.at[0]),
         pltpu.make_async_copy(k_hbm, kv_ref.at[0:BLOCK, :], sems.at[1]),
         pltpu.make_async_copy(v_hbm, kv_ref.at[BLOCK:2 * BLOCK, :], sems.at[2]),
+        pltpu.make_async_copy(q_hbm, q_ref, sems.at[3]),
     ]
     for copy in copies:
         copy.start()
     copies[0].wait()
     reached = reached_mask(parents_ref) if walk else jnp.int32(0)
     reached_ref[...] = jnp.full(reached_ref.shape, reached, jnp.int32)
-    copies[1].wait()
-    copies[2].wait()
+    for copy in copies[1:]:
+        copy.wait()
 
 
 def project(att, w_ref, start, width):
@@ -170,18 +171,19 @@
                 route.append((i * tp_size + j, target[0] * tp_size + target[1]))
         return lax.ppermute(x, ("ctx", "tp"), route)
 
-    kv, reached = pl.pallas_call(
+    kv, queries, reached = pl.pallas_call(
         functools.partial(pack_kernel, ctx_size == DIRECT_SIZE),
         out_shape=(
             jax.ShapeDtypeStruct((2 * tok_rows, head_dim), jnp.bfloat16),
+            jax.ShapeDtypeStruct(query_heads.shape, jnp.bfloat16),
             jax.ShapeDtypeStruct((8, 128), jnp.int32),
         ),
-        in_specs=[hbm, hbm, hbm],
-        out_specs=(vmem, vmem),
-        scratch_shapes=[pltpu.SMEM(parents.shape, jnp.int32), pltpu.SemaphoreType.DMA((3,))],
+        in_specs=[hbm] * 4,
+        out_specs=(vmem,) * 3,
+        scratch_shapes=[pltpu.SMEM(parents.shape, jnp.int32), pltpu.SemaphoreType.DMA((4,))],
         compiler_params=params,
         cost_estimate=pl.CostEstimate(flops=1_000_000, bytes_accessed=130_000, transcendentals=0),
-    )(in_hbm(key_heads[:, 0, :]), in_hbm(value_heads[:, 0, :]), in_hbm(parents))
+    )(in_hbm(key_heads[:, 0, :]), in_hbm(value_heads[:, 0, :]), in_hbm(query_heads), in_hbm(parents))
     if ctx_size == DIRECT_SIZE:
         columns = [swap(kv, "ctx", ctx_size, other) for other in (4, 2, 6)]
         beside = swap(kv, "ctx", ctx_size, 1)
@@ -189,7 +191,7 @@
         early, early_xors = [beside, *columns], (1, 4, 2, 6)
     else:
         early, early_xors = [], ()
-    q = jnp.transpose(query_heads, (1, 0, 2)).reshape(rows, head_dim)
+    q = jnp.transpose(queries, (1, 0, 2)).reshape(rows, head_dim)
 
     m, l, acc = pl.pallas_call(
         functools.partial(own_block_kernel, early_xors),

time: 26.4 us -> 26.3 us (level); the launches traced: 26.6 us -> 25.8 us
  waiting for transfers between devices: 5.92 us -> 8.24 us
  Pallas kernels: 6.43 us -> 4.15 us
  local copies, waits for them, and re-layouts: 1.14 us -> 0.04 us
  starting transfers between devices: 12.1 us -> 12.4 us
    ppermute x3, waiting for transfers between devices: 0.19 us -> 1.67 us  [forward(): return lax.ppermute(x, ('ctx', 'tp'), route)]
    transpose x1, local copies, waits for them, and re-layouts: 1.14 us -> 0.04 us  [shards(): q = jnp.transpose(queries, (1, 0, 2)).reshape(rows, head_dim)]
    pallas_call x1, Pallas kernels: 2.03 us -> 1.03 us  [shards(): pl.pallas_call(functools.partial(own_block_kernel, early_xors), out_shape...]
    pallas_call x1, Pallas kernels: 1.21 us -> 0.21 us  [absorbed(): pl.pallas_call(functools.partial(others_kernel, xors), out_shape=state_sh...]
    ppermute x9, waiting for transfers between devices: 5.73 us -> 6.57 us  [swap(): return lax.ppermute(x, axis, [(i, i ^ other) for i in range(size)])]
    pallas_call x1, Pallas kernels: 1.21 us -> 0.7 us  [shards(): pl.pallas_call(functools.partial(last_kernel, xors), out_shape=(jax.Shape...]
    ppermute x3, starting transfers between devices: 3.27 us -> 3.55 us  [forward(): return lax.ppermute(x, ('ctx', 'tp'), route)]
  transfers between devices with their start and end apart: 12 -> 12, of which waited for: 4 -> 6; matrix products, arithmetic and copies ran while one was open for 5% -> 0% of each run, Pallas kernels for 17% -> 9%
where the time goes in v20:
time: 26.3 us; the launch traced here: 25.8 us
  starting transfers between devices  12.4 us (47%)
  waiting for transfers between devices  8.24 us (31%)
  Pallas kernels  4.15 us (16%)
  other arithmetic  0.86 us (3%)
    ppermute x9, starting transfers between devices, swap(): return lax.ppermute(x, axis, [(i, i ^ other) for i in range(size)])  8.82 us
    ppermute x9, waiting for transfers between devices, swap(): return lax.ppermute(x, axis, [(i, i ^ other) for i in range(size)])  6.57 us
    ppermute x3, starting transfers between devices, forward(): return lax.ppermute(x, ('ctx', 'tp'), route)  3.55 us
    ppermute x3, waiting for transfers between devices, forward(): return lax.ppermute(x, ('ctx', 'tp'), route)  1.67 us
    pallas_call x2, Pallas kernels, projected(): pl.pallas_call(functools.partial(project_pair, flip, part), out_shape=sha...  1.19 us
    pallas_call x1, Pallas kernels, shards(): pl.pallas_call(functools.partial(own_block_kernel, early_xors), out_shape...  1.03 us
    pallas_call x1, Pallas kernels, shards(): pl.pallas_call(functools.partial(pack_kernel, ctx_size == DIRECT_SIZE), o...  1.02 us
    convert_element_type x1, other arithmetic, shards(): (keep_near + near_in.astype(jnp.float32) + from_far).astype(jnp.bfloat16)  0.8 us
  transfers between devices with their start and end apart: 12, of which 6 were waited for; matrix products, arithmetic and copies ran while one was open for 0% of the time, Pallas kernels for 9%

profile of v20, /device:TPU:26, one launch (start us, length us, event | category | flops | bytes accessed | tf_op | source)
XLA Modules:
  0.0 25.8 jit_solution(5493081792049521797)
XLA Ops:
  0.0 1.0 %shard_map.55 = (bf16[256,128]{1,0:T(8,128)(2,1)S(1)}, bf16[128,8,128]{2,1,0:T(8,128)(2,1)S(1)}, s32[8,128]{1,0:T(8,128)S(1)}) custom-call(bf16[128,128]{1,0:T(8,128)(2,1)} %bitcast.10, bf16[128,128]{1,0:T(8,128)(2,1)} %bitcast.11, bf16[128,8,128]{2,1,0:T(8,128)(2,1)} %q_hbm.1, s32[8]{0:T(128)} %parents_hbm.1), custom_call_target="tpu_custom_call" | custom-call | flops 1000000 | bytes 130000 | tf_op jit(solution)/shard_map/pallas_call | solution.py:174
  1.0 0.3 %collective-permute-start.3 = (bf16[256,128]{1,0:T(8,128)(2,1)S(1)}, bf16[256,128]{1,0:T(8,128)(2,1)S(1)}, u32[]{:S(2)}, u32[]{:S(2)}) collective-permute-start(bf16[256,128]{1,0:T(8,128)(2,1)S(1)} %get-tuple-element.24.kv_ref), channel_id=1, source_target_pairs={{0,24},{4,28},{8,16},{12,20},{16,8},{20,12},{24,0},{28,4},{1,25},{... | collective-permute-start | bytes 196616 | tf_op jit(solution)/shard_map/ppermute | solution.py:164
  1.3 0.7 %collective-permute-start.2 = (bf16[256,128]{1,0:T(8,128)(2,1)S(1)}, bf16[256,128]{1,0:T(8,128)(2,1)S(1)}, u32[]{:S(2)}, u32[]{:S(2)}) collective-permute-start(bf16[256,128]{1,0:T(8,128)(2,1)S(1)} %get-tuple-element.24.kv_ref), channel_id=1, source_target_pairs={{0,8},{4,12},{8,0},{12,4},{16,24},{20,28},{24,16},{28,20},{1,9},{5... | collective-permute-start | bytes 196616 | tf_op jit(solution)/shard_map/ppermute | solution.py:164
  2.0 3.5 %collective-permute-start.1 = (bf16[256,128]{1,0:T(8,128)(2,1)S(1)}, bf16[256,128]{1,0:T(8,128)(2,1)S(1)}, u32[]{:S(2)}, u32[]{:S(2)}) collective-permute-start(bf16[256,128]{1,0:T(8,128)(2,1)S(1)} %get-tuple-element.24.kv_ref), channel_id=1, source_target_pairs={{0,16},{4,20},{8,24},{12,28},{16,0},{20,4},{24,8},{28,12},{1,17},{... | collective-permute-start | bytes 196616 | tf_op jit(solution)/shard_map/ppermute | solution.py:164
  5.5 1.5 %collective-permute-start = (bf16[256,128]{1,0:T(8,128)(2,1)S(1)}, bf16[256,128]{1,0:T(8,128)(2,1)S(1)}, u32[]{:S(2)}, u32[]{:S(2)}) collective-permute-start(bf16[256,128]{1,0:T(8,128)(2,1)S(1)} %get-tuple-element.24.kv_ref), channel_id=1, source_target_pairs={{0,4},{4,0},{8,12},{12,8},{16,20},{20,16},{24,28},{28,24},{1,5},{5... | collective-permute-start | bytes 196616 | tf_op jit(solution)/shard_map/ppermute | solution.py:164
  7.0 0.0 slice-start
  7.0 0.8 %collective-permute-done.3.refs_3_ = bf16[256,128]{1,0:T(8,128)(2,1)S(1)} collective-permute-done((bf16[256,128]{1,0:T(8,128)(2,1)S(1)}, bf16[256,128]{1,0:T(8,128)(2,1)S(1)}, u32[]{:S(2)}, u32[]{:S(2)}) %collective-permute-start.3) | collective-permute-done | bytes 65568 | tf_op jit(solution)/shard_map/ppermute | solution.py:164
  7.9 1.5 %collective-permute-start.5 = (bf16[256,128]{1,0:T(8,128)(2,1)S(1)}, bf16[256,128]{1,0:T(8,128)(2,1)S(1)}, u32[]{:S(2)}, u32[]{:S(2)}) collective-permute-start(bf16[256,128]{1,0:T(8,128)(2,1)S(1)} %collective-permute-done.3.refs_3_), channel_id=1, source_target_pairs={{0,1},{1,0},{2,3},{3,2},{4,5},{5,4},{6,7},{7,6},{8,9},{9,8},{10,11... | collective-permute-start | bytes 196616 | tf_op jit(solution)/shard_map/ppermute | solution.py:172
  9.4 0.0 collective-permute-done.2.refs_2_
  9.4 0.5 %collective-permute-start.4 = (bf16[256,128]{1,0:T(8,128)(2,1)S(1)}, bf16[256,128]{1,0:T(8,128)(2,1)S(1)}, u32[]{:S(2)}, u32[]{:S(2)}) collective-permute-start(bf16[256,128]{1,0:T(8,128)(2,1)S(1)} %collective-permute-done.2.refs_2_), channel_id=1, source_target_pairs={{0,1},{1,0},{2,3},{3,2},{4,5},{5,4},{6,7},{7,6},{8,12},{9,13},{10,... | collective-permute-start | bytes 196616 | tf_op jit(solution)/shard_map/ppermute | solution.py:172
  9.9 0.0 collective-permute-done.1.refs_1_
  9.9 1.5 %collective-permute-start.6 = (bf16[256,128]{1,0:T(8,128)(2,1)S(1)}, bf16[256,128]{1,0:T(8,128)(2,1)S(1)}, u32[]{:S(2)}, u32[]{:S(2)}) collective-permute-start(bf16[256,128]{1,0:T(8,128)(2,1)S(1)} %collective-permute-done.1.refs_1_), channel_id=1, source_target_pairs={{0,1},{1,0},{2,3},{3,2},{4,5},{5,4},{6,7},{7,6},{8,9},{9,8},{10,11... | collective-permute-start | bytes 196616 | tf_op jit(solution)/shard_map/ppermute | solution.py:172
  11.4 0.0 collective-permute-done.refs_0_
  11.4 0.0 slice-start.1
  11.4 1.0 %shard_map.56 = (f32[1,1024]{1,0:T(1,128)S(1)}, f32[1,1024]{1,0:T(1,128)S(1)}, f32[128,1024]{1,0:T(8,128)S(1)}) custom-call(s32[8,128]{1,0:T(8,128)S(1)} %get-tuple-element.22.reached_ref.tree_ref, bf16[1024,128]{1,0:T(8,128)(2,1)S(1)} %bitcast.6, bf16[256,128]{1,0:T(8,128)(2,1)S(1)} %get-tuple-element.24.kv_ref, ...), custom_call_target="tpu_custom_call" | custom-call | flops 5000000000 | bytes 1000000 | tf_op jit(solution)/shard_map/pallas_call | solution.py:196
  12.5 0.0 collective-permute-done.5.refs_1_
  12.5 1.2 %collective-permute-done.4.refs_0_ = bf16[256,128]{1,0:T(8,128)(2,1)S(1)} collective-permute-done((bf16[256,128]{1,0:T(8,128)(2,1)S(1)}, bf16[256,128]{1,0:T(8,128)(2,1)S(1)}, u32[]{:S(2)}, u32[]{:S(2)}) %collective-permute-start.4) | collective-permute-done | bytes 65568 | tf_op jit(solution)/shard_map/ppermute | solution.py:172
  13.7 0.2 shard_map.57
  13.9 0.5 %collective-permute-done.6.refs_0_ = bf16[256,128]{1,0:T(8,128)(2,1)S(1)} collective-permute-done((bf16[256,128]{1,0:T(8,128)(2,1)S(1)}, bf16[256,128]{1,0:T(8,128)(2,1)S(1)}, u32[]{:S(2)}, u32[]{:S(2)}) %collective-permute-start.6) | collective-permute-done | bytes 65568 | tf_op jit(solution)/shard_map/ppermute | solution.py:172
  14.4 0.0 slice-done
  14.4 0.0 slice-done.1
  14.4 0.7 %shard_map.58 = (bf16[128,1024]{1,0:T(8,128)(2,1)S(1)}, bf16[128,512]{1,0:T(8,128)(2,1)S(1)}, f32[128,512]{1,0:T(8,128)S(1)}, f32[1,1024]{1,0:T(1,128)S(1)}, f32...) custom-call(s32[8,128]{1,0:T(8,128)S(1)} %get-tuple-element.22.reached_ref, ...), custom_call_target="tpu_custom_call", output_to_operand_aliasing={{3}: (2, {}), {4}: (3, {}), {5}: (4, {})} | custom-call | flops 1000000000 | bytes 10000000 | tf_op jit(solution)/shard_map/pallas_call | solution.py:233
  15.1 0.1 collective-permute-start.7
  15.2 0.5 %shard_map.60 = (bf16[128,512]{1,0:T(8,128)(2,1)S(1)}, f32[128,512]{1,0:T(8,128)S(1)}) custom-call(bf16[128,1024]{1,0:T(8,128)(2,1)S(1)} %get-tuple-element.34.att_ref, bf16[1024,4096]{1,0:T(8,128)(2,1)S(1)} %bitcast.5), custom_call_target="tpu_custom_call" | custom-call | flops 540000000 | bytes 4000000 | tf_op jit(solution)/shard_map/pallas_call | solution.py:244
  15.6 0.5 %collective-permute-start.10 = (bf16[128,512]{1,0:T(8,128)(2,1)S(1)}, bf16[128,512]{1,0:T(8,128)(2,1)S(1)}, u32[]{:S(2)}, u32[]{:S(2)}) collective-permute-start(bf16[128,512]{1,0:T(8,128)(2,1)S(1)} %get-tuple-element.38), channel_id=1, source_target_pairs={{0,1},{1,0},{2,3},{3,2},{4,5},{5,4},{6,7},{7,6},{8,9},{9,8},{10,11... | collective-permute-start | bytes 393224 | tf_op jit(solution)/shard_map/ppermute | solution.py:164
  16.2 0.3 %collective-permute-done.7 = bf16[128,512]{1,0:T(8,128)(2,1)S(1)} collective-permute-done((bf16[128,512]{1,0:T(8,128)(2,1)S(1)}, bf16[128,512]{1,0:T(8,128)(2,1)S(1)}, u32[]{:S(2)}, u32[]{:S(2)}) %collective-permute-start.7) | collective-permute-done | bytes 131104 | tf_op jit(solution)/shard_map/ppermute | solution.py:164
  16.5 0.6 %collective-permute-start.9 = (bf16[128,512]{1,0:T(8,128)(2,1)S(1)}, bf16[128,512]{1,0:T(8,128)(2,1)S(1)}, u32[]{:S(2)}, u32[]{:S(2)}) collective-permute-start(bf16[128,512]{1,0:T(8,128)(2,1)S(1)} %add_convert_fusion.2), channel_id=1, source_target_pairs={{0,2},{1,3},{2,0},{3,1},{4,6},{5,7},{6,4},{7,5},{8,10},{9,11},{10,... | collective-permute-start | bytes 393224 | tf_op jit(solution)/shard_map/ppermute | solution.py:164
  17.1 0.7 %shard_map.59 = (bf16[128,1024]{1,0:T(8,128)(2,1)S(1)}, f32[128,1024]{1,0:T(8,128)S(1)}) custom-call(bf16[128,1024]{1,0:T(8,128)(2,1)S(1)} %get-tuple-element.34.att_ref, bf16[1024,4096]{1,0:T(8,128)(2,1)S(1)} %bitcast.5), custom_call_target="tpu_custom_call" | custom-call | flops 540000000 | bytes 4000000 | tf_op jit(solution)/shard_map/pallas_call | solution.py:244
  17.9 0.1 collective-permute-start.8
  18.0 0.0 collective-permute-done.10
  18.0 1.6 %collective-permute-start.11 = (bf16[128,512]{1,0:T(8,128)(2,1)S(1)}, bf16[128,512]{1,0:T(8,128)(2,1)S(1)}, u32[]{:S(2)}, u32[]{:S(2)}) collective-permute-start(bf16[128,512]{1,0:T(8,128)(2,1)S(1)} %add_convert_fusion.1), channel_id=1, source_target_pairs={{0,2},{1,3},{2,0},{3,1},{4,6},{5,7},{6,4},{7,5},{8,10},{9,11},{10,... | collective-permute-start | bytes 393224 | tf_op jit(solution)/shard_map/ppermute | solution.py:164
  19.6 3.4 %collective-permute-done.9 = bf16[128,512]{1,0:T(8,128)(2,1)S(1)} collective-permute-done((bf16[128,512]{1,0:T(8,128)(2,1)S(1)}, bf16[128,512]{1,0:T(8,128)(2,1)S(1)}, u32[]{:S(2)}, u32[]{:S(2)}) %collective-permute-start.9) | collective-permute-done | bytes 131104 | tf_op jit(solution)/shard_map/ppermute | solution.py:164
  22.9 2.0 %collective-permute-done.11 = bf16[128,512]{1,0:T(8,128)(2,1)S(1)} collective-permute-done((bf16[128,512]{1,0:T(8,128)(2,1)S(1)}, bf16[128,512]{1,0:T(8,128)(2,1)S(1)}, u32[]{:S(2)}, u32[]{:S(2)}) %collective-permute-start.11) | collective-permute-done | bytes 131104 | tf_op jit(solution)/shard_map/ppermute | solution.py:164
  25.0 0.0 collective-permute-done.8
  25.0 0.8 %add_convert_fusion = bf16[128,1024]{1,0:T(8,128)(2,1)} fusion(f32[128,1024]{1,0:T(8,128)S(1)} %get-tuple-element.35, bf16[128,1024]{1,0:T(8,128)(2,1)S(1)} %collective-permute-done.8, bf16[128,512]{1,0:T(8,128)(2,1)S(1)} %collective-permute-done.11, bf16[128,512]{1,0:T(8,128)(2,1)S(1)} %collective-permute-done.9), kind=kLoop, calls=%fused_computation | loop fusion | flops 1048576 | bytes 1310720 | tf_op jit(solution)/shard_map/convert_element_type | solution.py:272
  (4 shorter events, 0.1 us)
Async XLA Ops:
  1.0 6.8 %collective-permute-start.3 = (bf16[256,128]{1,0:T(8,128)(2,1)S(1)}, bf16[256,128]{1,0:T(8,128)(2,1)S(1)}, u32[]{:S(2)}, u32[]{:S(2)}) collective-permute-start(bf16[256,128]{1,0:T(8,128)(2,1)S(1)} %get-tuple-element.24.kv_ref), channel_id=1, source_target_pairs={{0,24},{4,28},{8,16},{12,20},{16,8},{20,12},{24,0},{28,4},{1,25},{... | collective-permute-start | bytes 196616 | tf_op jit(solution)/shard_map/ppermute | solution.py:164
  1.3 8.1 %collective-permute-start.2 = (bf16[256,128]{1,0:T(8,128)(2,1)S(1)}, bf16[256,128]{1,0:T(8,128)(2,1)S(1)}, u32[]{:S(2)}, u32[]{:S(2)}) collective-permute-start(bf16[256,128]{1,0:T(8,128)(2,1)S(1)} %get-tuple-element.24.kv_ref), channel_id=1, source_target_pairs={{0,8},{4,12},{8,0},{12,4},{16,24},{20,28},{24,16},{28,20},{1,9},{5... | collective-permute-start | bytes 196616 | tf_op jit(solution)/shard_map/ppermute | solution.py:164
  2.0 7.9 %collective-permute-start.1 = (bf16[256,128]{1,0:T(8,128)(2,1)S(1)}, bf16[256,128]{1,0:T(8,128)(2,1)S(1)}, u32[]{:S(2)}, u32[]{:S(2)}) collective-permute-start(bf16[256,128]{1,0:T(8,128)(2,1)S(1)} %get-tuple-element.24.kv_ref), channel_id=1, source_target_pairs={{0,16},{4,20},{8,24},{12,28},{16,0},{20,4},{24,8},{28,12},{1,17},{... | collective-permute-start | bytes 196616 | tf_op jit(solution)/shard_map/ppermute | solution.py:164
  5.5 5.9 %collective-permute-start = (bf16[256,128]{1,0:T(8,128)(2,1)S(1)}, bf16[256,128]{1,0:T(8,128)(2,1)S(1)}, u32[]{:S(2)}, u32[]{:S(2)}) collective-permute-start(bf16[256,128]{1,0:T(8,128)(2,1)S(1)} %get-tuple-element.24.kv_ref), channel_id=1, source_target_pairs={{0,4},{4,0},{8,12},{12,8},{16,20},{20,16},{24,28},{28,24},{1,5},{5... | collective-permute-start | bytes 196616 | tf_op jit(solution)/shard_map/ppermute | solution.py:164
  7.0 7.4 %slice-start = ((s8[8388608]{0:T(1024)(128)(4,1)}), s8[4194304]{0:T(1024)(128)(4,1)S(1)}, s32[]{:S(2)}) async-start(s8[8388608]{0:T(1024)(128)(4,1)} %bitcast.4), calls=%async_computation | async-start | bytes 8388608
  7.9 4.6 %collective-permute-start.5 = (bf16[256,128]{1,0:T(8,128)(2,1)S(1)}, bf16[256,128]{1,0:T(8,128)(2,1)S(1)}, u32[]{:S(2)}, u32[]{:S(2)}) collective-permute-start(bf16[256,128]{1,0:T(8,128)(2,1)S(1)} %collective-permute-done.3.refs_3_), channel_id=1, source_target_pairs={{0,1},{1,0},{2,3},{3,2},{4,5},{5,4},{6,7},{7,6},{8,9},{9,8},{10,11... | collective-permute-start | bytes 196616 | tf_op jit(solution)/shard_map/ppermute | solution.py:172
  9.4 4.3 %collective-permute-start.4 = (bf16[256,128]{1,0:T(8,128)(2,1)S(1)}, bf16[256,128]{1,0:T(8,128)(2,1)S(1)}, u32[]{:S(2)}, u32[]{:S(2)}) collective-permute-start(bf16[256,128]{1,0:T(8,128)(2,1)S(1)} %collective-permute-done.2.refs_2_), channel_id=1, source_target_pairs={{0,1},{1,0},{2,3},{3,2},{4,5},{5,4},{6,7},{7,6},{8,12},{9,13},{10,... | collective-permute-start | bytes 196616 | tf_op jit(solution)/shard_map/ppermute | solution.py:172
  9.9 4.5 %collective-permute-start.6 = (bf16[256,128]{1,0:T(8,128)(2,1)S(1)}, bf16[256,128]{1,0:T(8,128)(2,1)S(1)}, u32[]{:S(2)}, u32[]{:S(2)}) collective-permute-start(bf16[256,128]{1,0:T(8,128)(2,1)S(1)} %collective-permute-done.1.refs_1_), channel_id=1, source_target_pairs={{0,1},{1,0},{2,3},{3,2},{4,5},{5,4},{6,7},{7,6},{8,9},{9,8},{10,11... | collective-permute-start | bytes 196616 | tf_op jit(solution)/shard_map/ppermute | solution.py:172
  11.4 2.9 %slice-start.1 = ((s8[8388608]{0:T(1024)(128)(4,1)}), s8[4194304]{0:T(1024)(128)(4,1)S(1)}, s32[]{:S(2)}) async-start(s8[8388608]{0:T(1024)(128)(4,1)} %bitcast.4), calls=%async_computation.1 | async-start | bytes 8388608
  15.1 1.4 %collective-permute-start.7 = (bf16[128,512]{1,0:T(8,128)(2,1)S(1)}, bf16[128,512]{1,0:T(8,128)(2,1)S(1)}, u32[]{:S(2)}, u32[]{:S(2)}) collective-permute-start(bf16[128,512]{1,0:T(8,128)(2,1)S(1)} %get-tuple-element.33), channel_id=1, source_target_pairs={{0,1},{1,0},{2,3},{3,2},{4,5},{5,4},{6,7},{7,6},{8,9},{9,8},{10,11... | collective-permute-start | bytes 393224 | tf_op jit(solution)/shard_map/ppermute | solution.py:164
  15.6 2.3 %collective-permute-start.10 = (bf16[128,512]{1,0:T(8,128)(2,1)S(1)}, bf16[128,512]{1,0:T(8,128)(2,1)S(1)}, u32[]{:S(2)}, u32[]{:S(2)}) collective-permute-start(bf16[128,512]{1,0:T(8,128)(2,1)S(1)} %get-tuple-element.38), channel_id=1, source_target_pairs={{0,1},{1,0},{2,3},{3,2},{4,5},{5,4},{6,7},{7,6},{8,9},{9,8},{10,11... | collective-permute-start | bytes 393224 | tf_op jit(solution)/shard_map/ppermute | solution.py:164
  16.5 6.4 %collective-permute-start.9 = (bf16[128,512]{1,0:T(8,128)(2,1)S(1)}, bf16[128,512]{1,0:T(8,128)(2,1)S(1)}, u32[]{:S(2)}, u32[]{:S(2)}) collective-permute-start(bf16[128,512]{1,0:T(8,128)(2,1)S(1)} %add_convert_fusion.2), channel_id=1, source_target_pairs={{0,2},{1,3},{2,0},{3,1},{4,6},{5,7},{6,4},{7,5},{8,10},{9,11},{10,... | collective-permute-start | bytes 393224 | tf_op jit(solution)/shard_map/ppermute | solution.py:164
  17.9 7.1 %collective-permute-start.8 = (bf16[128,1024]{1,0:T(8,128)(2,1)S(1)}, bf16[128,1024]{1,0:T(8,128)(2,1)S(1)}, u32[]{:S(2)}, u32[]{:S(2)}) collective-permute-start(bf16[128,1024]{1,0:T(8,128)(2,1)S(1)} %get-tuple-element.36), channel_id=1, source_target_pairs={{0,1},{1,0},{2,3},{3,2},{4,5},{5,4},{6,7},{7,6},{8,9},{9,8},{10,11... | collective-permute-start | bytes 786440 | tf_op jit(solution)/shard_map/ppermute | solution.py:164
  18.0 7.0 %collective-permute-start.11 = (bf16[128,512]{1,0:T(8,128)(2,1)S(1)}, bf16[128,512]{1,0:T(8,128)(2,1)S(1)}, u32[]{:S(2)}, u32[]{:S(2)}) collective-permute-start(bf16[128,512]{1,0:T(8,128)(2,1)S(1)} %add_convert_fusion.1), channel_id=1, source_target_pairs={{0,2},{1,3},{2,0},{3,1},{4,6},{5,7},{6,4},{7,5},{8,10},{9,11},{10,... | collective-permute-start | bytes 393224 | tf_op jit(solution)/shard_map/ppermute | solution.py:164

commit v21 on v19

--- a/solution.py
+++ b/solution.py
@@ -218,7 +218,8 @@
                 cost_estimate=pl.CostEstimate(flops=270_000_000, bytes_accessed=1_000_000, transcendentals=500_000),
             )(reached, q, *state, *arrived)
 
-        state = absorbed(state, (3, 7), pairs[1:])
+        state = absorbed(state, (3,), pairs[1:2])
+        state = absorbed(state, (7,), pairs[2:])
         xors, pieces, tree, tree_spec = (5,), pairs[:1], reached, vmem
     else:
         xors, pieces, tree, tree_spec = (), [lax.all_gather(kv, "ctx", axis=0, tiled=True)], parents, smem

time: 26.4 us -> 26 us (0.985)
  the two profiles are of different devices: /device:TPU:26 before, /device:TPU:0 now
where the time goes in v21:
time: 26 us; the launch traced here: 25.5 us
  starting transfers between devices  10.5 us (40%)
  waiting for transfers between devices  8.37 us (32%)
  Pallas kernels  3.62 us (14%)
  local copies, waits for them, and re-layouts  2.08 us (8%)
  other arithmetic  0.86 us (3%)
    ppermute x9, starting transfers between devices, swap(): return lax.ppermute(x, axis, [(i, i ^ other) for i in range(size)])  10.4 us
    ppermute x9, waiting for transfers between devices, swap(): return lax.ppermute(x, axis, [(i, i ^ other) for i in range(size)])  8.11 us
    pallas_call x2, Pallas kernels, projected(): pl.pallas_call(functools.partial(project_pair, flip, part), out_shape=sha...  1.17 us
    transpose x1, local copies, waits for them, and re-layouts, shards(): q = jnp.transpose(query_heads, (1, 0, 2)).reshape(rows, head_dim)  1.14 us
    unnamed x4, local copies, waits for them, and re-layouts  0.94 us
    pallas_call x1, Pallas kernels, shards(): pl.pallas_call(functools.partial(pack_kernel, ctx_size == DIRECT_SIZE), o...  0.8 us
    convert_element_type x1, other arithmetic, shards(): (keep_near + near_in.astype(jnp.float32) + from_far).astype(jnp.bfloat16)  0.8 us
    pallas_call x1, Pallas kernels, shards(): pl.pallas_call(functools.partial(last_kernel, xors), out_shape=(jax.Shape...  0.7 us
  transfers between devices with their start and end apart: 12, of which 6 were waited for; matrix products, arithmetic and copies ran while one was open for 5% of the time, Pallas kernels for 8%

profile of v21, /device:TPU:0, one launch (start us, length us, event | category | flops | bytes accessed | tf_op | source)
XLA Modules:
  0.0 25.5 jit_solution(18199478872882386668)
XLA Ops:
  0.0 0.8 %shard_map.55 = (bf16[256,128]{1,0:T(8,128)(2,1)S(1)}, s32[8,128]{1,0:T(8,128)S(1)}) custom-call(bf16[128,128]{1,0:T(8,128)(2,1)} %bitcast.11, bf16[128,128]{1,0:T(8,128)(2,1)} %bitcast.12, s32[8]{0:T(128)} %parents_hbm.1), custom_call_target="tpu_custom_call" | custom-call | flops 1000000 | bytes 130000 | tf_op jit(solution)/shard_map/pallas_call | solution.py:173
  0.8 5.1 %collective-permute-start.3 = (bf16[256,128]{1,0:T(8,128)(2,1)S(1)}, bf16[256,128]{1,0:T(8,128)(2,1)S(1)}, u32[]{:S(2)}, u32[]{:S(2)}) collective-permute-start(bf16[256,128]{1,0:T(8,128)(2,1)S(1)} %get-tuple-element.25.kv_ref), channel_id=1, source_target_pairs={{0,24},{4,28},{8,16},{12,20},{16,8},{20,12},{24,0},{28,4},{1,25},{... | collective-permute-start | bytes 196616 | tf_op jit(solution)/shard_map/ppermute | solution.py:163
  5.9 0.0 collective-permute-start.2
  5.9 0.6 %collective-permute-start.1 = (bf16[256,128]{1,0:T(8,128)(2,1)S(1)}, bf16[256,128]{1,0:T(8,128)(2,1)S(1)}, u32[]{:S(2)}, u32[]{:S(2)}) collective-permute-start(bf16[256,128]{1,0:T(8,128)(2,1)S(1)} %get-tuple-element.25.kv_ref), channel_id=1, source_target_pairs={{0,16},{4,20},{8,24},{12,28},{16,0},{20,4},{24,8},{28,12},{1,17},{... | collective-permute-start | bytes 196616 | tf_op jit(solution)/shard_map/ppermute | solution.py:163
  6.6 1.7 %collective-permute-start = (bf16[256,128]{1,0:T(8,128)(2,1)S(1)}, bf16[256,128]{1,0:T(8,128)(2,1)S(1)}, u32[]{:S(2)}, u32[]{:S(2)}) collective-permute-start(bf16[256,128]{1,0:T(8,128)(2,1)S(1)} %get-tuple-element.25.kv_ref), channel_id=1, source_target_pairs={{0,4},{4,0},{8,12},{12,8},{16,20},{20,16},{24,28},{28,24},{1,5},{5... | collective-permute-start | bytes 196616 | tf_op jit(solution)/shard_map/ppermute | solution.py:163
  8.2 0.0 slice-start
  8.2 1.1 %copy.15 = bf16[8,128,128]{2,1,0:T(8,128)(2,1)S(1)} copy(bf16[8,128,128]{2,0,1:T(8,128)(2,1)} %bitcast.10) | data formatting | bytes 524288 | tf_op jit(solution)/shard_map/transpose | solution.py:192
  9.4 0.0 collective-permute-done.3.refs_3_
  9.4 0.1 collective-permute-start.5
  9.5 1.1 %collective-permute-done.2.refs_2_ = bf16[256,128]{1,0:T(8,128)(2,1)S(1)} collective-permute-done((bf16[256,128]{1,0:T(8,128)(2,1)S(1)}, bf16[256,128]{1,0:T(8,128)(2,1)S(1)}, u32[]{:S(2)}, u32[]{:S(2)}) %collective-permute-start.2) | collective-permute-done | bytes 65568 | tf_op jit(solution)/shard_map/ppermute | solution.py:163
  10.6 0.0 collective-permute-start.4
  10.6 1.0 %collective-permute-done.1.refs_1_ = bf16[256,128]{1,0:T(8,128)(2,1)S(1)} collective-permute-done((bf16[256,128]{1,0:T(8,128)(2,1)S(1)}, bf16[256,128]{1,0:T(8,128)(2,1)S(1)}, u32[]{:S(2)}, u32[]{:S(2)}) %collective-permute-start.1) | collective-permute-done | bytes 65568 | tf_op jit(solution)/shard_map/ppermute | solution.py:163
  11.6 0.0 collective-permute-start.6
  11.6 0.0 collective-permute-done.refs_0_
  11.6 0.0 slice-start.1
  11.6 0.5 %shard_map.56 = (f32[1,1024]{1,0:T(1,128)S(1)}, f32[1,1024]{1,0:T(1,128)S(1)}, f32[128,1024]{1,0:T(8,128)S(1)}) custom-call(s32[8,128]{1,0:T(8,128)S(1)} %get-tuple-element.24.reached_ref.tree_ref, bf16[1024,128]{1,0:T(8,128)(2,1)S(1)} %bitcast.6, bf16[256,128]{1,0:T(8,128)(2,1)S(1)} %get-tuple-element.25.kv_ref, ...), custom_call_target="tpu_custom_call" | custom-call | flops 5000000000 | bytes 1000000 | tf_op jit(solution)/shard_map/pallas_call | solution.py:194
  12.1 0.0 collective-permute-done.4.refs_0_
  12.1 0.2 shard_map.57
  12.3 0.0 collective-permute-done.5.refs_0_
  12.3 0.2 shard_map.58
  12.6 0.3 collective-permute-done.6.refs_0_
  12.8 0.0 slice-done
  12.8 0.9 %slice-done.1 = s8[4194304]{0:T(1024)(128)(4,1)S(1)} async-done(((s8[8388608]{0:T(1024)(128)(4,1)}), s8[4194304]{0:T(1024)(128)(4,1)S(1)}, s32[]{:S(2)}) %slice-start.1) | async-done | bytes 4194328
  13.8 0.7 %shard_map.59 = (bf16[128,1024]{1,0:T(8,128)(2,1)S(1)}, bf16[128,512]{1,0:T(8,128)(2,1)S(1)}, f32[128,512]{1,0:T(8,128)S(1)}, f32[1,1024]{1,0:T(1,128)S(1)}, f32...) custom-call(s32[8,128]{1,0:T(8,128)S(1)} %get-tuple-element.24.reached_ref, ...), custom_call_target="tpu_custom_call", output_to_operand_aliasing={{3}: (2, {}), {4}: (3, {}), {5}: (4, {})} | custom-call | flops 1000000000 | bytes 10000000 | tf_op jit(solution)/shard_map/pallas_call | solution.py:232
  14.5 0.6 %collective-permute-start.7 = (bf16[128,512]{1,0:T(8,128)(2,1)S(1)}, bf16[128,512]{1,0:T(8,128)(2,1)S(1)}, u32[]{:S(2)}, u32[]{:S(2)}) collective-permute-start(bf16[128,512]{1,0:T(8,128)(2,1)S(1)} %get-tuple-element.37), channel_id=1, source_target_pairs={{0,1},{1,0},{2,3},{3,2},{4,5},{5,4},{6,7},{7,6},{8,9},{9,8},{10,11... | collective-permute-start | bytes 393224 | tf_op jit(solution)/shard_map/ppermute | solution.py:163
  15.0 0.5 %shard_map.61 = (bf16[128,512]{1,0:T(8,128)(2,1)S(1)}, f32[128,512]{1,0:T(8,128)S(1)}) custom-call(bf16[128,1024]{1,0:T(8,128)(2,1)S(1)} %get-tuple-element.38.att_ref, bf16[1024,4096]{1,0:T(8,128)(2,1)S(1)} %bitcast.5), custom_call_target="tpu_custom_call" | custom-call | flops 540000000 | bytes 4000000 | tf_op jit(solution)/shard_map/pallas_call | solution.py:243
  15.5 0.1 collective-permute-start.10
  15.6 0.4 %collective-permute-done.7 = bf16[128,512]{1,0:T(8,128)(2,1)S(1)} collective-permute-done((bf16[128,512]{1,0:T(8,128)(2,1)S(1)}, bf16[128,512]{1,0:T(8,128)(2,1)S(1)}, u32[]{:S(2)}, u32[]{:S(2)}) %collective-permute-start.7) | collective-permute-done | bytes 131104 | tf_op jit(solution)/shard_map/ppermute | solution.py:163
  16.1 1.6 %collective-permute-start.9 = (bf16[128,512]{1,0:T(8,128)(2,1)S(1)}, bf16[128,512]{1,0:T(8,128)(2,1)S(1)}, u32[]{:S(2)}, u32[]{:S(2)}) collective-permute-start(bf16[128,512]{1,0:T(8,128)(2,1)S(1)} %add_convert_fusion.2), channel_id=1, source_target_pairs={{0,2},{1,3},{2,0},{3,1},{4,6},{5,7},{6,4},{7,5},{8,10},{9,11},{10,... | collective-permute-start | bytes 393224 | tf_op jit(solution)/shard_map/ppermute | solution.py:163
  17.6 0.7 %shard_map.60 = (bf16[128,1024]{1,0:T(8,128)(2,1)S(1)}, f32[128,1024]{1,0:T(8,128)S(1)}) custom-call(bf16[128,1024]{1,0:T(8,128)(2,1)S(1)} %get-tuple-element.38.att_ref, bf16[1024,4096]{1,0:T(8,128)(2,1)S(1)} %bitcast.5), custom_call_target="tpu_custom_call" | custom-call | flops 540000000 | bytes 4000000 | tf_op jit(solution)/shard_map/pallas_call | solution.py:243
  18.4 0.1 collective-permute-start.8
  18.5 0.0 collective-permute-done.10
  18.5 0.6 %collective-permute-start.11 = (bf16[128,512]{1,0:T(8,128)(2,1)S(1)}, bf16[128,512]{1,0:T(8,128)(2,1)S(1)}, u32[]{:S(2)}, u32[]{:S(2)}) collective-permute-start(bf16[128,512]{1,0:T(8,128)(2,1)S(1)} %add_convert_fusion.1), channel_id=1, source_target_pairs={{0,2},{1,3},{2,0},{3,1},{4,6},{5,7},{6,4},{7,5},{8,10},{9,11},{10,... | collective-permute-start | bytes 393224 | tf_op jit(solution)/shard_map/ppermute | solution.py:163
  19.1 2.9 %collective-permute-done.9 = bf16[128,512]{1,0:T(8,128)(2,1)S(1)} collective-permute-done((bf16[128,512]{1,0:T(8,128)(2,1)S(1)}, bf16[128,512]{1,0:T(8,128)(2,1)S(1)}, u32[]{:S(2)}, u32[]{:S(2)}) %collective-permute-start.9) | collective-permute-done | bytes 131104 | tf_op jit(solution)/shard_map/ppermute | solution.py:163
  22.1 2.6 %collective-permute-done.11 = bf16[128,512]{1,0:T(8,128)(2,1)S(1)} collective-permute-done((bf16[128,512]{1,0:T(8,128)(2,1)S(1)}, bf16[128,512]{1,0:T(8,128)(2,1)S(1)}, u32[]{:S(2)}, u32[]{:S(2)}) %collective-permute-start.11) | collective-permute-done | bytes 131104 | tf_op jit(solution)/shard_map/ppermute | solution.py:163
  24.7 0.0 collective-permute-done.8
  24.7 0.8 %add_convert_fusion = bf16[128,1024]{1,0:T(8,128)(2,1)} fusion(f32[128,1024]{1,0:T(8,128)S(1)} %get-tuple-element.39, bf16[128,1024]{1,0:T(8,128)(2,1)S(1)} %collective-permute-done.8, bf16[128,512]{1,0:T(8,128)(2,1)S(1)} %collective-permute-done.11, bf16[128,512]{1,0:T(8,128)(2,1)S(1)} %collective-permute-done.9), kind=kLoop, calls=%fused_computation | loop fusion | flops 1048576 | bytes 1310720 | tf_op jit(solution)/shard_map/convert_element_type | solution.py:271
  (3 shorter events, 0.1 us)
Async XLA Ops:
  0.8 8.6 %collective-permute-start.3 = (bf16[256,128]{1,0:T(8,128)(2,1)S(1)}, bf16[256,128]{1,0:T(8,128)(2,1)S(1)}, u32[]{:S(2)}, u32[]{:S(2)}) collective-permute-start(bf16[256,128]{1,0:T(8,128)(2,1)S(1)} %get-tuple-element.25.kv_ref), channel_id=1, source_target_pairs={{0,24},{4,28},{8,16},{12,20},{16,8},{20,12},{24,0},{28,4},{1,25},{... | collective-permute-start | bytes 196616 | tf_op jit(solution)/shard_map/ppermute | solution.py:163
  5.9 4.7 %collective-permute-start.2 = (bf16[256,128]{1,0:T(8,128)(2,1)S(1)}, bf16[256,128]{1,0:T(8,128)(2,1)S(1)}, u32[]{:S(2)}, u32[]{:S(2)}) collective-permute-start(bf16[256,128]{1,0:T(8,128)(2,1)S(1)} %get-tuple-element.25.kv_ref), channel_id=1, source_target_pairs={{0,8},{4,12},{8,0},{12,4},{16,24},{20,28},{24,16},{28,20},{1,9},{5... | collective-permute-start | bytes 196616 | tf_op jit(solution)/shard_map/ppermute | solution.py:163
  5.9 5.6 %collective-permute-start.1 = (bf16[256,128]{1,0:T(8,128)(2,1)S(1)}, bf16[256,128]{1,0:T(8,128)(2,1)S(1)}, u32[]{:S(2)}, u32[]{:S(2)}) collective-permute-start(bf16[256,128]{1,0:T(8,128)(2,1)S(1)} %get-tuple-element.25.kv_ref), channel_id=1, source_target_pairs={{0,16},{4,20},{8,24},{12,28},{16,0},{20,4},{24,8},{28,12},{1,17},{... | collective-permute-start | bytes 196616 | tf_op jit(solution)/shard_map/ppermute | solution.py:163
  6.6 5.0 %collective-permute-start = (bf16[256,128]{1,0:T(8,128)(2,1)S(1)}, bf16[256,128]{1,0:T(8,128)(2,1)S(1)}, u32[]{:S(2)}, u32[]{:S(2)}) collective-permute-start(bf16[256,128]{1,0:T(8,128)(2,1)S(1)} %get-tuple-element.25.kv_ref), channel_id=1, source_target_pairs={{0,4},{4,0},{8,12},{12,8},{16,20},{20,16},{24,28},{28,24},{1,5},{5... | collective-permute-start | bytes 196616 | tf_op jit(solution)/shard_map/ppermute | solution.py:163
  8.2 4.6 %slice-start = ((s8[8388608]{0:T(1024)(128)(4,1)}), s8[4194304]{0:T(1024)(128)(4,1)S(1)}, s32[]{:S(2)}) async-start(s8[8388608]{0:T(1024)(128)(4,1)} %bitcast.4), calls=%async_computation | async-start | bytes 8388608
  9.4 3.0 %collective-permute-start.5 = (bf16[256,128]{1,0:T(8,128)(2,1)S(1)}, bf16[256,128]{1,0:T(8,128)(2,1)S(1)}, u32[]{:S(2)}, u32[]{:S(2)}) collective-permute-start(bf16[256,128]{1,0:T(8,128)(2,1)S(1)} %collective-permute-done.3.refs_3_), channel_id=1, source_target_pairs={{0,1},{1,0},{2,3},{3,2},{4,5},{5,4},{6,7},{7,6},{8,9},{9,8},{10,11... | collective-permute-start | bytes 196616 | tf_op jit(solution)/shard_map/ppermute | solution.py:171
  10.6 1.5 %collective-permute-start.4 = (bf16[256,128]{1,0:T(8,128)(2,1)S(1)}, bf16[256,128]{1,0:T(8,128)(2,1)S(1)}, u32[]{:S(2)}, u32[]{:S(2)}) collective-permute-start(bf16[256,128]{1,0:T(8,128)(2,1)S(1)} %collective-permute-done.2.refs_2_), channel_id=1, source_target_pairs={{0,1},{1,0},{2,3},{3,2},{4,5},{5,4},{6,7},{7,6},{8,12},{9,13},{10,... | collective-permute-start | bytes 196616 | tf_op jit(solution)/shard_map/ppermute | solution.py:171
  11.6 1.3 %collective-permute-start.6 = (bf16[256,128]{1,0:T(8,128)(2,1)S(1)}, bf16[256,128]{1,0:T(8,128)(2,1)S(1)}, u32[]{:S(2)}, u32[]{:S(2)}) collective-permute-start(bf16[256,128]{1,0:T(8,128)(2,1)S(1)} %collective-permute-done.1.refs_1_), channel_id=1, source_target_pairs={{0,1},{1,0},{2,3},{3,2},{4,5},{5,4},{6,7},{7,6},{8,9},{9,8},{10,11... | collective-permute-start | bytes 196616 | tf_op jit(solution)/shard_map/ppermute | solution.py:171
  11.6 2.2 %slice-start.1 = ((s8[8388608]{0:T(1024)(128)(4,1)}), s8[4194304]{0:T(1024)(128)(4,1)S(1)}, s32[]{:S(2)}) async-start(s8[8388608]{0:T(1024)(128)(4,1)} %bitcast.4), calls=%async_computation.1 | async-start | bytes 8388608
  14.5 1.6 %collective-permute-start.7 = (bf16[128,512]{1,0:T(8,128)(2,1)S(1)}, bf16[128,512]{1,0:T(8,128)(2,1)S(1)}, u32[]{:S(2)}, u32[]{:S(2)}) collective-permute-start(bf16[128,512]{1,0:T(8,128)(2,1)S(1)} %get-tuple-element.37), channel_id=1, source_target_pairs={{0,1},{1,0},{2,3},{3,2},{4,5},{5,4},{6,7},{7,6},{8,9},{9,8},{10,11... | collective-permute-start | bytes 393224 | tf_op jit(solution)/shard_map/ppermute | solution.py:163
  15.5 3.0 %collective-permute-start.10 = (bf16[128,512]{1,0:T(8,128)(2,1)S(1)}, bf16[128,512]{1,0:T(8,128)(2,1)S(1)}, u32[]{:S(2)}, u32[]{:S(2)}) collective-permute-start(bf16[128,512]{1,0:T(8,128)(2,1)S(1)} %get-tuple-element.42), channel_id=1, source_target_pairs={{0,1},{1,0},{2,3},{3,2},{4,5},{5,4},{6,7},{7,6},{8,9},{9,8},{10,11... | collective-permute-start | bytes 393224 | tf_op jit(solution)/shard_map/ppermute | solution.py:163
  16.1 6.0 %collective-permute-start.9 = (bf16[128,512]{1,0:T(8,128)(2,1)S(1)}, bf16[128,512]{1,0:T(8,128)(2,1)S(1)}, u32[]{:S(2)}, u32[]{:S(2)}) collective-permute-start(bf16[128,512]{1,0:T(8,128)(2,1)S(1)} %add_convert_fusion.2), channel_id=1, source_target_pairs={{0,2},{1,3},{2,0},{3,1},{4,6},{5,7},{6,4},{7,5},{8,10},{9,11},{10,... | collective-permute-start | bytes 393224 | tf_op jit(solution)/shard_map/ppermute | solution.py:163
  18.4 6.3 %collective-permute-start.8 = (bf16[128,1024]{1,0:T(8,128)(2,1)S(1)}, bf16[128,1024]{1,0:T(8,128)(2,1)S(1)}, u32[]{:S(2)}, u32[]{:S(2)}) collective-permute-start(bf16[128,1024]{1,0:T(8,128)(2,1)S(1)} %get-tuple-element.40), channel_id=1, source_target_pairs={{0,1},{1,0},{2,3},{3,2},{4,5},{5,4},{6,7},{7,6},{8,9},{9,8},{10,11... | collective-permute-start | bytes 786440 | tf_op jit(solution)/shard_map/ppermute | solution.py:163
  18.5 6.2 %collective-permute-start.11 = (bf16[128,512]{1,0:T(8,128)(2,1)S(1)}, bf16[128,512]{1,0:T(8,128)(2,1)S(1)}, u32[]{:S(2)}, u32[]{:S(2)}) collective-permute-start(bf16[128,512]{1,0:T(8,128)(2,1)S(1)} %add_convert_fusion.1), channel_id=1, source_target_pairs={{0,2},{1,3},{2,0},{3,1},{4,6},{5,7},{6,4},{7,5},{8,10},{9,11},{10,... | collective-permute-start | bytes 393224 | tf_op jit(solution)/shard_map/ppermute | solution.py:163
